TPU v7x, 32 devices: a whole 2x2x4 slice. The times are simulated.
32 devices in a mesh: section: 2 (over x), fsdp: 4 (over y, core), tensor: 4 (over z).
Axes of the slice: x: 2, y: 2, z: 4, core: 2. Of those that a mesh axis runs over, the one named last changes fastest.
Arguments:
- inputs: bfloat16 [2, 4096, 1536], P(None, ('fsdp', 'tensor')), may hold values from -6 to 6
- doc_ids: int32 [2, 4, 1024], P(None, 'fsdp'), may hold values from 0 to 3, never falling along the last dimension, each value on 1 to 512 neighbouring positions
- cotangent: bfloat16 [2, 4096, 1536], P(None, ('fsdp', 'tensor')), may hold values from -6 to 6
- query_weight: bfloat16 [2, 1536, 1536], P('section', 'fsdp', 'tensor'), may hold values from -0.15625 to 0.15625
- key_weight: bfloat16 [2, 1536, 768], P('section', 'fsdp', 'tensor'), may hold values from -0.15625 to 0.15625
- value_weight: bfloat16 [2, 1536, 768], P('section', 'fsdp', 'tensor'), may hold values from -0.15625 to 0.15625
- output_weight: bfloat16 [2, 1536, 1536], P('section', 'tensor', 'fsdp'), may hold values from -0.4375 to 0.4375
- gate_weight: bfloat16 [2, 1536, 4096], P('section', 'fsdp', 'tensor'), may hold values from -0.15625 to 0.15625
- up_weight: bfloat16 [2, 1536, 4096], P('section', 'fsdp', 'tensor'), may hold values from -0.15625 to 0.15625
- down_weight: bfloat16 [2, 4096, 1536], P('section', 'tensor', 'fsdp'), may hold values from -0.09375 to 0.09375
- gains: bfloat16 [2, 2, 1536], P('section', None, ('fsdp', 'tensor')), may hold values from 0.099609375 to 1.8984375
Outputs:
- section_out: bfloat16 [2, 2, 4096, 1536], P('section', None, ('fsdp', 'tensor'))
- input_grads: float32 [2, 2, 4096, 1536], P('section', None, ('fsdp', 'tensor'))
- query_grad: float32 [2, 1536, 1536], P('section', 'fsdp', 'tensor')
- key_grad: float32 [2, 1536, 768], P('section', 'fsdp', 'tensor')
- value_grad: float32 [2, 1536, 768], P('section', 'fsdp', 'tensor')
- output_grad: float32 [2, 1536, 1536], P('section', 'tensor', 'fsdp')
- gate_grad: float32 [2, 1536, 4096], P('section', 'fsdp', 'tensor')
- up_grad: float32 [2, 1536, 4096], P('section', 'fsdp', 'tensor')
- down_grad: float32 [2, 4096, 1536], P('section', 'tensor', 'fsdp')
- gains_grad: float32 [2, 2, 1536], P('section', None, ('fsdp', 'tensor'))
Inputs may be any that keep to these rules, and one draw needn't show every extreme that they name: `doc_ids`: within each sequence the ids never fall; every document has 1 to half of 1024 tokens, and one has exactly that many.
All inputs are finite; a program needn't handle non-finite values.
Results may differ from a plain program's by a relative error of at most 0.035.
Values may be sent and summed in bfloat16 or wider, within the bound.
A program may use at most 320 MiB of HBM per device.

v0:
```python
import jax
import jax.numpy as jnp
from jax import lax
from jax.sharding import PartitionSpec as P

HD = 96


epsilon = 1e-05
rope_base = 100000.0


def shifted(block, axis, distance):
    devices = range(lax.axis_size(axis))
    route = [(i - distance, i) for i in devices if i - distance in devices]
    return lax.ppermute(block, axis, route)


def normalize(values, gain_row):
    return values * lax.rsqrt(jnp.mean(values * values, -1, keepdims=True) + epsilon) * gain_row


def norm_pullback(values, gain_row, upstream):
    norm_value, pullback = jax.vjp(normalize, values, gain_row)
    return pullback(upstream)


def turning(doc_rows):
    places = jnp.arange(doc_rows.shape[-1], dtype=jnp.int32)
    begins = jnp.concatenate(
        [jnp.ones(doc_rows.shape[:-1] + (1,), dtype=bool), doc_rows[..., 1:] != doc_rows[..., :-1]],
        -1,
    )
    starts = lax.cummax(jnp.where(begins, places, 0), axis=doc_rows.ndim - 1)
    positions = (places - starts).astype(jnp.float32)
    ladder = jnp.arange(HD // 2, dtype=jnp.float32)
    frequency = rope_base ** (-2.0 * ladder / HD)
    angles = positions[..., None] * frequency
    return (jnp.cos(angles)[:, :, None, :], jnp.sin(angles)[:, :, None, :])


def rotate(values, cosine, sine_part):
    half_size = values.shape[-1] // 2
    first_half = values[..., :half_size]
    second_half = values[..., half_size:]
    return jnp.concatenate(
        [
            first_half * cosine - second_half * sine_part,
            second_half * cosine + first_half * sine_part,
        ],
        -1,
    )


def matmul(left_side, right_side):
    return jnp.dot(left_side, right_side, preferred_element_type=jnp.float32)


def times_right_t(left_side, right_side):
    return lax.dot_general(
        left_side, right_side, (((1,), (1,)), ((), ())), preferred_element_type=jnp.float32
    )


def left_t_times(left_side, right_side):
    return lax.dot_general(
        left_side, right_side, (((0,), (0,)), ((), ())), preferred_element_type=jnp.float32
    )


def spread(rows_low):
    return lax.all_gather(rows_low, "tensor", axis=0, tiled=True)


def collect(partial_rows):
    return lax.psum_scatter(
        partial_rows.astype(jnp.bfloat16), "tensor", scatter_dimension=0, tiled=True
    ).astype(jnp.float32)


def score_block(query_rot, key_rot, doc_row):
    scores = jnp.einsum(
        "ahgd,bhd->hgab", query_rot, key_rot, preferred_element_type=jnp.float32
    ) * HD ** (-0.5)
    places = jnp.arange(doc_row.shape[0], dtype=jnp.int32)
    allowed = (places[None, :] <= places[:, None]) & (doc_row[None, :] == doc_row[:, None])
    return jnp.where(allowed[None, None], scores, -1e30)


def attend_forward(seq_block):
    query_rot, key_rot, value_low, doc_row = seq_block
    scores = score_block(query_rot, key_rot, doc_row)
    largest = jnp.max(scores, -1, keepdims=True)
    raised = jnp.exp(scores - largest)
    row_total = jnp.sum(raised, -1, keepdims=True)
    attn_probs = (raised / row_total).astype(jnp.bfloat16)
    mixed_seq = jnp.einsum(
        "hgab,bhd->ahgd", attn_probs, value_low, preferred_element_type=jnp.float32
    )
    return (mixed_seq.astype(jnp.bfloat16), largest + jnp.log(row_total))


def attend_backward(seq_block):
    query_rot, key_rot, value_low, doc_row, log_total, grad_mixed = seq_block
    scores = score_block(query_rot, key_rot, doc_row)
    attn_probs = jnp.exp(scores - log_total)
    grad_value = jnp.einsum(
        "hgab,ahgd->bhd",
        attn_probs.astype(jnp.bfloat16),
        grad_mixed,
        preferred_element_type=jnp.float32,
    )
    grad_probs = jnp.einsum(
        "ahgd,bhd->hgab", grad_mixed, value_low, preferred_element_type=jnp.float32
    )
    grad_scores = (
        attn_probs * (grad_probs - jnp.sum(attn_probs * grad_probs, -1, keepdims=True))
    ).astype(jnp.bfloat16)
    grad_query = jnp.einsum(
        "hgab,bhd->ahgd", grad_scores, key_rot, preferred_element_type=jnp.float32
    ) * HD ** (-0.5)
    grad_key = jnp.einsum(
        "hgab,ahgd->bhd", grad_scores, query_rot, preferred_element_type=jnp.float32
    ) * HD ** (-0.5)
    return (grad_query, grad_key, grad_value)


def layer_forward(hidden_in, weights, gain_pair, doc_rows):
    query_w, key_w, value_w, output_w, gate_w, up_w, down_w = weights
    seq_count, seq_len = doc_rows.shape
    heads_here = query_w.shape[1] // HD
    pairs_here = key_w.shape[1] // HD
    normed = normalize(hidden_in, gain_pair[0]).astype(jnp.bfloat16)
    whole_rows = spread(normed)
    cosine, sine_part = turning(doc_rows)
    query_rot = rotate(
        matmul(whole_rows, query_w).reshape(seq_count, seq_len, heads_here, HD), cosine, sine_part
    ).astype(jnp.bfloat16)
    key_rot = rotate(
        matmul(whole_rows, key_w).reshape(seq_count, seq_len, pairs_here, HD), cosine, sine_part
    ).astype(jnp.bfloat16)
    value_low = (
        matmul(whole_rows, value_w).astype(jnp.bfloat16).reshape(seq_count, seq_len, pairs_here, HD)
    )
    query_grouped = query_rot.reshape(seq_count, seq_len, pairs_here, heads_here // pairs_here, HD)
    mixed_all, log_total = lax.map(attend_forward, (query_grouped, key_rot, value_low, doc_rows))
    mixed_low = mixed_all.reshape(seq_count * seq_len, heads_here * HD)
    middle = hidden_in + collect(matmul(mixed_low, output_w))
    second = normalize(middle, gain_pair[1]).astype(jnp.bfloat16)
    second_whole = spread(second)
    gate_pre = matmul(second_whole, gate_w)
    up_pre = matmul(second_whole, up_w)
    hidden_low = (jax.nn.silu(gate_pre) * up_pre).astype(jnp.bfloat16)
    feed_out = matmul(hidden_low, down_w)
    result = middle + collect(feed_out)
    kept_set = (
        hidden_in,
        whole_rows,
        query_grouped,
        key_rot,
        value_low,
        log_total,
        mixed_low,
        middle,
        second_whole,
        gate_pre,
        up_pre,
        hidden_low,
    )
    return (result, kept_set)


def layer_backward(grad_out, kept_set, weights, gain_pair, doc_rows):
    (
        hidden_in,
        whole_rows,
        query_grouped,
        key_rot,
        value_low,
        log_total,
        mixed_low,
        middle,
        second_whole,
        gate_pre,
        up_pre,
        hidden_low,
    ) = kept_set
    query_w, key_w, value_w, output_w, gate_w, up_w, down_w = weights
    seq_count, seq_len = doc_rows.shape
    heads_here = query_w.shape[1] // HD
    pairs_here = key_w.shape[1] // HD
    grad_low = grad_out.astype(jnp.bfloat16)
    grad_whole = spread(grad_low)
    grad_hidden = times_right_t(grad_whole, down_w)
    sigmoid_gate = jax.nn.sigmoid(gate_pre)
    grad_gate = (
        grad_hidden * up_pre * sigmoid_gate * (1.0 + gate_pre * (1.0 - sigmoid_gate))
    ).astype(jnp.bfloat16)
    grad_up = (grad_hidden * gate_pre * sigmoid_gate).astype(jnp.bfloat16)
    second_terms = times_right_t(grad_gate, gate_w) + times_right_t(grad_up, up_w)
    grad_second = collect(second_terms)
    grad_middle_norm, grad_gain_two = norm_pullback(middle, gain_pair[1], grad_second)
    grad_middle = grad_out + grad_middle_norm
    grad_attn_whole = spread(grad_middle.astype(jnp.bfloat16))
    grad_mixed = times_right_t(grad_attn_whole, output_w).astype(jnp.bfloat16)
    grad_grouped = grad_mixed.reshape(seq_count, seq_len, pairs_here, heads_here // pairs_here, HD)
    grad_query, grad_key, grad_value = lax.map(
        attend_backward, (query_grouped, key_rot, value_low, doc_rows, log_total, grad_grouped)
    )
    cosine, sine_part = turning(doc_rows)
    grad_query = (
        rotate(grad_query.reshape(seq_count, seq_len, heads_here, HD), cosine, -sine_part)
        .astype(jnp.bfloat16)
        .reshape(seq_count * seq_len, heads_here * HD)
    )
    grad_key = (
        rotate(grad_key, cosine, -sine_part)
        .astype(jnp.bfloat16)
        .reshape(seq_count * seq_len, pairs_here * HD)
    )
    grad_value = grad_value.astype(jnp.bfloat16).reshape(seq_count * seq_len, pairs_here * HD)
    grad_normed = collect(
        times_right_t(grad_query, query_w)
        + times_right_t(grad_key, key_w)
        + times_right_t(grad_value, value_w)
    )
    grad_input_norm, grad_gain_one = norm_pullback(hidden_in, gain_pair[0], grad_normed)
    grad_input = grad_middle + grad_input_norm
    weight_terms = (
        left_t_times(whole_rows, grad_query),
        left_t_times(whole_rows, grad_key),
        left_t_times(whole_rows, grad_value),
        left_t_times(mixed_low, grad_attn_whole),
        left_t_times(second_whole, grad_gate),
        left_t_times(second_whole, grad_up),
        left_t_times(hidden_low, grad_whole),
    )
    return (grad_input, weight_terms, jnp.stack([grad_gain_one, grad_gain_two]))


def body(
    inputs,
    doc_ids,
    cotangent,
    query_weight,
    key_weight,
    value_weight,
    output_weight,
    gate_weight,
    up_weight,
    down_weight,
    gains,
):
    shards = (
        query_weight[0],
        key_weight[0],
        value_weight[0],
        output_weight[0],
        gate_weight[0],
        up_weight[0],
        down_weight[0],
    )
    weights = (
        lax.all_gather(shards[0], "fsdp", axis=0, tiled=True),
        lax.all_gather(shards[1], "fsdp", axis=0, tiled=True),
        lax.all_gather(shards[2], "fsdp", axis=0, tiled=True),
        lax.all_gather(shards[3], "fsdp", axis=1, tiled=True),
        lax.all_gather(shards[4], "fsdp", axis=0, tiled=True),
        lax.all_gather(shards[5], "fsdp", axis=0, tiled=True),
        lax.all_gather(shards[6], "fsdp", axis=1, tiled=True),
    )
    gain_pair = lax.all_gather(gains[0], ("fsdp", "tensor"), axis=1, tiled=True).astype(jnp.float32)
    section_index = lax.axis_index("section")
    first_section = section_index == 0
    micro_count = inputs.shape[0]
    tick_count = micro_count + 1
    arriving = jnp.zeros(inputs.shape[1:], jnp.bfloat16)
    produced = jnp.zeros(inputs.shape, jnp.bfloat16)
    kept_list = []
    for moment in range(tick_count):
        micro_slot = jnp.clip(moment - section_index, 0, micro_count - 1)
        is_live = (moment - section_index >= 0) & (moment - section_index < micro_count)
        fresh_rows = inputs[min(moment, micro_count - 1)]
        hidden_in = jnp.where(first_section, fresh_rows, arriving).astype(jnp.float32)
        doc_rows = lax.dynamic_index_in_dim(doc_ids, micro_slot, 0, keepdims=False)
        result, kept_set = layer_forward(hidden_in, weights, gain_pair, doc_rows)
        sent_rows = result.astype(jnp.bfloat16)
        produced = jnp.where(
            is_live, lax.dynamic_update_index_in_dim(produced, sent_rows, micro_slot, 0), produced
        )
        kept_list.append(kept_set)
        if moment < micro_count:
            arriving = shifted(sent_rows, "section", 1)
    stacked = jax.tree.map(lambda *members: jnp.stack(members), *kept_list)
    weights_back = (
        lax.all_gather(shards[0], "fsdp", axis=0, tiled=True),
        lax.all_gather(shards[1], "fsdp", axis=0, tiled=True),
        lax.all_gather(shards[2], "fsdp", axis=0, tiled=True),
        lax.all_gather(shards[3], "fsdp", axis=1, tiled=True),
        lax.all_gather(shards[4], "fsdp", axis=0, tiled=True),
        lax.all_gather(shards[5], "fsdp", axis=0, tiled=True),
        lax.all_gather(shards[6], "fsdp", axis=1, tiled=True),
    )
    full_sums = tuple((jnp.zeros(member.shape, jnp.float32) for member in weights[:4])) + tuple(
        (
            (
                jnp.zeros(
                    (member.shape[0] * lax.axis_size("fsdp"),) + member.shape[1:], jnp.float32
                )
                if number % 3 != 0
                else jnp.zeros(
                    (member.shape[0], member.shape[1] * lax.axis_size("fsdp")), jnp.float32
                )
            )
            for number, member in zip(range(4, 7), shards[4:])
        )
    )
    shard_sums = tuple((jnp.zeros(member.shape, jnp.float32) for member in shards))
    gain_sums = jnp.zeros(gain_pair.shape, jnp.float32)
    returning = jnp.zeros(inputs.shape[1:], jnp.bfloat16)
    grads_in = jnp.zeros(inputs.shape, jnp.float32)
    for moment in range(tick_count):
        micro_raw = moment - 1 + section_index
        micro_slot = jnp.clip(micro_raw, 0, micro_count - 1)
        is_live = (micro_raw >= 0) & (micro_raw < micro_count)
        saved_slot = jnp.clip(moment - 1 + 2 * section_index, 0, tick_count - 1)
        kept_set = jax.tree.map(
            lambda member: lax.dynamic_index_in_dim(member, saved_slot, 0, keepdims=False), stacked
        )
        given_grad = lax.dynamic_index_in_dim(cotangent, micro_slot, 0, keepdims=False)
        upstream = jnp.where(first_section, returning, given_grad).astype(jnp.float32)
        upstream = jnp.where(is_live, upstream, 0.0)
        doc_rows = lax.dynamic_index_in_dim(doc_ids, micro_slot, 0, keepdims=False)
        grad_input, weight_terms, gain_terms = layer_backward(
            upstream, kept_set, weights_back, gain_pair, doc_rows
        )
        gain_sums = gain_sums + gain_terms
        full_sums = tuple((running + share for running, share in zip(full_sums, weight_terms)))
        grads_in = jnp.where(
            is_live, lax.dynamic_update_index_in_dim(grads_in, grad_input, micro_slot, 0), grads_in
        )
        if moment < micro_count:
            returning = shifted(grad_input.astype(jnp.bfloat16), "section", -1)
    shard_sums = (
        lax.psum_scatter(
            full_sums[0].astype(jnp.bfloat16), "fsdp", scatter_dimension=0, tiled=True
        ).astype(jnp.float32),
        lax.psum_scatter(
            full_sums[1].astype(jnp.bfloat16), "fsdp", scatter_dimension=0, tiled=True
        ).astype(jnp.float32),
        lax.psum_scatter(
            full_sums[2].astype(jnp.bfloat16), "fsdp", scatter_dimension=0, tiled=True
        ).astype(jnp.float32),
        lax.psum_scatter(
            full_sums[3].astype(jnp.bfloat16), "fsdp", scatter_dimension=1, tiled=True
        ).astype(jnp.float32),
        lax.psum_scatter(
            full_sums[4].astype(jnp.bfloat16), "fsdp", scatter_dimension=0, tiled=True
        ).astype(jnp.float32),
        lax.psum_scatter(
            full_sums[5].astype(jnp.bfloat16), "fsdp", scatter_dimension=0, tiled=True
        ).astype(jnp.float32),
        lax.psum_scatter(
            full_sums[6].astype(jnp.bfloat16), "fsdp", scatter_dimension=1, tiled=True
        ).astype(jnp.float32),
    )
    gain_share = lax.psum_scatter(gain_sums, ("fsdp", "tensor"), scatter_dimension=1, tiled=True)
    results = (
        [produced[None], grads_in[None]]
        + [member[None] for member in shard_sums]
        + [gain_share[None]]
    )
    return tuple(results)


def solution(mesh):
    return jax.shard_map(
        body,
        mesh=mesh,
        in_specs=(
            P(None, ("fsdp", "tensor"), None),
            P(None, "fsdp", None),
            P(None, ("fsdp", "tensor"), None),
            P("section", "fsdp", "tensor"),
            P("section", "fsdp", "tensor"),
            P("section", "fsdp", "tensor"),
            P("section", "tensor", "fsdp"),
            P("section", "fsdp", "tensor"),
            P("section", "fsdp", "tensor"),
            P("section", "tensor", "fsdp"),
            P("section", None, ("fsdp", "tensor")),
        ),
        out_specs=(
            P("section", None, ("fsdp", "tensor"), None),
            P("section", None, ("fsdp", "tensor"), None),
            P("section", "fsdp", "tensor"),
            P("section", "fsdp", "tensor"),
            P("section", "fsdp", "tensor"),
            P("section", "tensor", "fsdp"),
            P("section", "fsdp", "tensor"),
            P("section", "fsdp", "tensor"),
            P("section", "tensor", "fsdp"),
            P("section", None, ("fsdp", "tensor")),
        ),
        check_vma=False,
    )
```

profile of v0, /device:TPU:1, one launch (start us, length us, event | category | flops | bytes accessed | tf_op | source)
XLA Modules:
  0.0 2338.3 jit_solution(13023552756553925203)
XLA Ops:
  8.7 36.9 %all-gather = bf16[1,2,1536]{1,0,2:T(2,128)(2,1)S(1)} all-gather(bf16[1,2,96]{1,0,2:T(2,128)(2,1)S(1)} %copy.58), channel_id=2, replica_groups=mesh['section'=2,'fsdp'=4,'tensor'=4] {'fsdp','tensor'}, dimensions={2}, use_global_device_ids=true | all-gather | bytes 6528 | tf_op jit(solution)/shard_map/all_gather | solution.py:272
  46.9 25.1 %slice_reduce_fusion = (f32[1536]{0:T(1024)S(1)}, f32[1536]{0:T(1024)S(1)}) fusion(f32[1,2,1536]{1,0,2:T(1,128)S(1)} %convert_element_type.666), kind=kLoop, calls=%fused_computation.388 | loop fusion | bytes 24576 | tf_op jit(solution)/shard_map/slice | solution.py:149
  107.6 31.7 %all-gather.26.cloned.1.call-done = bf16[1024,1536]{1,0:T(8,128)(2,1)} async-done(((bf16[256,1536]{1,0:T(8,128)(2,1)}), bf16[1024,1536]{1,0:T(8,128)(2,1)}) %all-gather.26.cloned.1.call-update) | async-done | bytes 3145744 | tf_op jit(solution)/shard_map/all_gather | solution.py:72
  164.2 58.3 %reduce-scatter.31.cloned.1.call-done = bf16[256,1536]{1,0:T(8,128)(2,1)} async-done(((bf16[1024,1536]{1,0:T(8,128)(2,1)}), bf16[256,1536]{1,0:T(8,128)(2,1)}) %reduce-scatter.31.cloned.1.call-update) | async-done | bytes 786448 | tf_op jit(solution)/shard_map/reduce_scatter | solution.py:76
  228.9 24.2 %all-gather.54.cloned.1.call-done = bf16[1,1536,1024]{2,1,0:T(8,128)(2,1)} async-done(((bf16[1,384,1024]{2,1,0:T(8,128)(2,1)}), bf16[1,1536,1024]{2,1,0:T(8,128)(2,1)}) %all-gather.54.cloned.1.call-update) | async-done | bytes 3145744 | tf_op jit(solution)/shard_map/all_gather | solution.py:268
  253.1 65.1 %all-gather.28.cloned.1.call-done = bf16[1024,1536]{1,0:T(8,128)(2,1)} async-done(((bf16[256,1536]{1,0:T(8,128)(2,1)}), bf16[1024,1536]{1,0:T(8,128)(2,1)}) %all-gather.28.cloned.1.call-update) | async-done | bytes 3145744 | tf_op jit(solution)/shard_map/all_gather | solution.py:72
  326.5 20.9 all-gather.56.cloned.1.call-done
  385.2 59.8 %reduce-scatter.33.cloned.1.call-done = bf16[256,1536]{1,0:T(8,128)(2,1)} async-done(((bf16[1024,1536]{1,0:T(8,128)(2,1)}), bf16[256,1536]{1,0:T(8,128)(2,1)}) %reduce-scatter.33.cloned.1.call-update) | async-done | bytes 786448 | tf_op jit(solution)/shard_map/reduce_scatter | solution.py:76
  472.5 63.4 %all-gather.30.cloned.1.call-done = bf16[1024,1536]{1,0:T(8,128)(2,1)} async-done(((bf16[256,1536]{1,0:T(8,128)(2,1)}), bf16[1024,1536]{1,0:T(8,128)(2,1)}) %all-gather.30.cloned.1.call-update) | async-done | bytes 3145744 | tf_op jit(solution)/shard_map/all_gather | solution.py:72
  559.3 58.9 %reduce-scatter.35.cloned.1.call-done = bf16[256,1536]{1,0:T(8,128)(2,1)} async-done(((bf16[1024,1536]{1,0:T(8,128)(2,1)}), bf16[256,1536]{1,0:T(8,128)(2,1)}) %reduce-scatter.35.cloned.1.call-update) | async-done | bytes 786448 | tf_op jit(solution)/shard_map/reduce_scatter | solution.py:76
  622.9 63.4 %all-gather.32.cloned.1.call-done = bf16[1024,1536]{1,0:T(8,128)(2,1)} async-done(((bf16[256,1536]{1,0:T(8,128)(2,1)}), bf16[1024,1536]{1,0:T(8,128)(2,1)}) %all-gather.32.cloned.1.call-update) | async-done | bytes 3145744 | tf_op jit(solution)/shard_map/all_gather | solution.py:72
  704.3 58.9 %reduce-scatter.37.cloned.1.call-done = bf16[256,1536]{1,0:T(8,128)(2,1)} async-done(((bf16[1024,1536]{1,0:T(8,128)(2,1)}), bf16[256,1536]{1,0:T(8,128)(2,1)}) %reduce-scatter.37.cloned.1.call-update) | async-done | bytes 786448 | tf_op jit(solution)/shard_map/reduce_scatter | solution.py:76
  790.2 63.6 %all-gather.34.cloned.1.call-done = bf16[1024,1536]{1,0:T(8,128)(2,1)} async-done(((bf16[256,1536]{1,0:T(8,128)(2,1)}), bf16[1024,1536]{1,0:T(8,128)(2,1)}) %all-gather.34.cloned.1.call-update) | async-done | bytes 3145744 | tf_op jit(solution)/shard_map/all_gather | solution.py:72
  876.3 58.9 %reduce-scatter.39.cloned.1.call-done = bf16[256,1536]{1,0:T(8,128)(2,1)} async-done(((bf16[1024,1536]{1,0:T(8,128)(2,1)}), bf16[256,1536]{1,0:T(8,128)(2,1)}) %reduce-scatter.39.cloned.1.call-update) | async-done | bytes 786448 | tf_op jit(solution)/shard_map/reduce_scatter | solution.py:76
  940.7 62.6 %all-gather.36.cloned.1.call-done = bf16[1024,1536]{1,0:T(8,128)(2,1)} async-done(((bf16[256,1536]{1,0:T(8,128)(2,1)}), bf16[1024,1536]{1,0:T(8,128)(2,1)}) %all-gather.36.cloned.1.call-update) | async-done | bytes 3145744 | tf_op jit(solution)/shard_map/all_gather | solution.py:72
  1026.3 40.6 %all-gather.38.cloned.1.call-done = bf16[1024,1536]{1,0:T(8,128)(2,1)} async-done(((bf16[256,1536]{1,0:T(8,128)(2,1)}), bf16[1024,1536]{1,0:T(8,128)(2,1)}) %all-gather.38.cloned.1.call-update) | async-done | bytes 3145744 | tf_op jit(solution)/shard_map/all_gather | solution.py:72
  1090.3 53.8 %reduce-scatter.43.cloned.1.call-done = bf16[256,1536]{1,0:T(8,128)(2,1)} async-done(((bf16[1024,1536]{1,0:T(8,128)(2,1)}), bf16[256,1536]{1,0:T(8,128)(2,1)}) %reduce-scatter.43.cloned.1.call-update) | async-done | bytes 786448 | tf_op jit(solution)/shard_map/reduce_scatter | solution.py:76
  1166.8 47.5 %all-gather.40.cloned.1.call-done = bf16[1024,1536]{1,0:T(8,128)(2,1)} async-done(((bf16[256,1536]{1,0:T(8,128)(2,1)}), bf16[1024,1536]{1,0:T(8,128)(2,1)}) %all-gather.40.cloned.1.call-update) | async-done | bytes 3145744 | tf_op jit(solution)/shard_map/all_gather | solution.py:72
  1270.0 53.7 %reduce-scatter.45.cloned.1.call-done = bf16[256,1536]{1,0:T(8,128)(2,1)} async-done(((bf16[1024,1536]{1,0:T(8,128)(2,1)}), bf16[256,1536]{1,0:T(8,128)(2,1)}) %reduce-scatter.45.cloned.1.call-update) | async-done | bytes 786448 | tf_op jit(solution)/shard_map/reduce_scatter | solution.py:76
  1354.3 63.8 %all-gather.42.cloned.1.call-done = bf16[1024,1536]{1,0:T(8,128)(2,1)} async-done(((bf16[256,1536]{1,0:T(8,128)(2,1)}), bf16[1024,1536]{1,0:T(8,128)(2,1)}) %all-gather.42.cloned.1.call-update) | async-done | bytes 3145744 | tf_op jit(solution)/shard_map/all_gather | solution.py:72
  1437.1 58.3 %reduce-scatter.47.cloned.1.call-done = bf16[256,1536]{1,0:T(8,128)(2,1)} async-done(((bf16[1024,1536]{1,0:T(8,128)(2,1)}), bf16[256,1536]{1,0:T(8,128)(2,1)}) %reduce-scatter.47.cloned.1.call-update) | async-done | bytes 786448 | tf_op jit(solution)/shard_map/reduce_scatter | solution.py:76
  1512.8 53.4 %all-gather.44.cloned.1.call-done = bf16[1024,1536]{1,0:T(8,128)(2,1)} async-done(((bf16[256,1536]{1,0:T(8,128)(2,1)}), bf16[1024,1536]{1,0:T(8,128)(2,1)}) %all-gather.44.cloned.1.call-update) | async-done | bytes 3145744 | tf_op jit(solution)/shard_map/all_gather | solution.py:72
  1618.7 58.3 %reduce-scatter.49.cloned.1.call-done = bf16[256,1536]{1,0:T(8,128)(2,1)} async-done(((bf16[1024,1536]{1,0:T(8,128)(2,1)}), bf16[256,1536]{1,0:T(8,128)(2,1)}) %reduce-scatter.49.cloned.1.call-update) | async-done | bytes 786448 | tf_op jit(solution)/shard_map/reduce_scatter | solution.py:76
  1704.8 64.0 %all-gather.46.cloned.1.call-done = bf16[1024,1536]{1,0:T(8,128)(2,1)} async-done(((bf16[256,1536]{1,0:T(8,128)(2,1)}), bf16[1024,1536]{1,0:T(8,128)(2,1)}) %all-gather.46.cloned.1.call-update) | async-done | bytes 3145744 | tf_op jit(solution)/shard_map/all_gather | solution.py:72
  1788.0 58.3 %reduce-scatter.51.cloned.1.call-done = bf16[256,1536]{1,0:T(8,128)(2,1)} async-done(((bf16[1024,1536]{1,0:T(8,128)(2,1)}), bf16[256,1536]{1,0:T(8,128)(2,1)}) %reduce-scatter.51.cloned.1.call-update) | async-done | bytes 786448 | tf_op jit(solution)/shard_map/reduce_scatter | solution.py:76
  2061.8 38.1 %reduce-scatter.59.cloned.1.call-done = bf16[384,1024]{1,0:T(8,128)(2,1)} async-done(((bf16[1536,1024]{1,0:T(8,128)(2,1)}), bf16[384,1024]{1,0:T(8,128)(2,1)}) %reduce-scatter.59.cloned.1.call-update) | async-done | bytes 786448 | tf_op jit(solution)/shard_map/reduce_scatter | solution.py:360
  2102.3 23.5 %reduce-scatter.61.cloned.1.call-done = bf16[384,192]{1,0:T(8,128)(2,1)} async-done(((bf16[1536,192]{1,0:T(8,128)(2,1)}), bf16[384,192]{1,0:T(8,128)(2,1)}) %reduce-scatter.61.cloned.1.call-update) | async-done | bytes 147472
  2126.9 24.6 %reduce-scatter.63.cloned.1.call-done = bf16[384,192]{1,0:T(8,128)(2,1)} async-done(((bf16[1536,192]{1,0:T(8,128)(2,1)}), bf16[384,192]{1,0:T(8,128)(2,1)}) %reduce-scatter.63.cloned.1.call-update) | async-done | bytes 147472
  2154.1 25.9 %reduce-scatter.65.cloned.1.call-done = bf16[384,384]{1,0:T(8,128)(2,1)} async-done(((bf16[1536,384]{1,0:T(8,128)(2,1)}), bf16[384,384]{1,0:T(8,128)(2,1)}) %reduce-scatter.65.cloned.1.call-update) | async-done | bytes 294928
  2182.0 26.3 %reduce-scatter.55.cloned.1.call-done = bf16[384,384]{1,0:T(8,128)(2,1)} async-done(((bf16[1536,384]{1,0:T(8,128)(2,1)}), bf16[384,384]{1,0:T(8,128)(2,1)}) %reduce-scatter.55.cloned.1.call-update) | async-done | bytes 294928 | tf_op jit(solution)/shard_map/reduce_scatter | solution.py:345
  2210.1 60.6 %reduce-scatter.53.cloned.1.call-done = bf16[256,1536]{1,0:T(8,128)(2,1)} async-done(((bf16[1024,1536]{1,0:T(8,128)(2,1)}), bf16[256,1536]{1,0:T(8,128)(2,1)}) %reduce-scatter.53.cloned.1.call-update) | async-done | bytes 786448 | tf_op jit(solution)/shard_map/reduce_scatter | solution.py:76
  2277.9 51.6 %reduce-scatter.69.cloned.1.call-done = f32[96,2]{1,0:T(8,128)} async-done(((f32[1536,2]{1,0:T(8,128)}), f32[96,2]{1,0:T(8,128)}) %reduce-scatter.69.cloned.1.call-update) | async-done | bytes 784
  (780 shorter events, 766.1 us)
Async XLA Ops:
  7.9 131.4 %all-gather.26.cloned.1.call-start = ((), (), s32[]{:S(2)}) async-start(), calls=%async_computation.20 | async-start | bytes 3932160 | tf_op jit(solution)/shard_map/all_gather | solution.py:72
  73.9 148.6 %reduce-scatter.31.cloned.1.call-start = ((), (), s32[]{:S(2)}) async-start(), calls=%async_computation.21 | async-start | bytes 3932160 | tf_op jit(solution)/shard_map/reduce_scatter | solution.py:76
  164.2 154.0 %all-gather.28.cloned.1.call-start = ((), (), s32[]{:S(2)}) async-start(), calls=%async_computation.22 | async-start | bytes 3932160 | tf_op jit(solution)/shard_map/all_gather | solution.py:72
  227.7 149.8 %all-gather.58.cloned.1.call-start = ((), (), s32[]{:S(2)}) async-start(), calls=%async_computation.51 | async-start | bytes 3932160 | tf_op jit(solution)/shard_map/all_gather | solution.py:270
  228.5 216.5 %reduce-scatter.33.cloned.1.call-start = ((), (), s32[]{:S(2)}) async-start(), calls=%async_computation.23 | async-start | bytes 3932160 | tf_op jit(solution)/shard_map/reduce_scatter | solution.py:76
  385.1 150.8 %all-gather.30.cloned.1.call-start = ((), (), s32[]{:S(2)}) async-start(), calls=%async_computation.24 | async-start | bytes 3932160 | tf_op jit(solution)/shard_map/all_gather | solution.py:72
  470.0 148.2 %reduce-scatter.35.cloned.1.call-start = ((), (), s32[]{:S(2)}) async-start(), calls=%async_computation.25 | async-start | bytes 3932160 | tf_op jit(solution)/shard_map/reduce_scatter | solution.py:76
  559.2 127.1 %all-gather.32.cloned.1.call-start = ((), (), s32[]{:S(2)}) async-start(), calls=%async_computation.26 | async-start | bytes 3932160 | tf_op jit(solution)/shard_map/all_gather | solution.py:72
  622.5 140.7 %reduce-scatter.37.cloned.1.call-start = ((), (), s32[]{:S(2)}) async-start(), calls=%async_computation.27 | async-start | bytes 3932160 | tf_op jit(solution)/shard_map/reduce_scatter | solution.py:76
  704.2 149.6 %all-gather.34.cloned.1.call-start = ((), (), s32[]{:S(2)}) async-start(), calls=%async_computation.28 | async-start | bytes 3932160 | tf_op jit(solution)/shard_map/all_gather | solution.py:72
  787.8 147.3 %reduce-scatter.39.cloned.1.call-start = ((), (), s32[]{:S(2)}) async-start(), calls=%async_computation.29 | async-start | bytes 3932160 | tf_op jit(solution)/shard_map/reduce_scatter | solution.py:76
  939.5 127.4 %all-gather.38.cloned.1.call-start = ((), (), s32[]{:S(2)}) async-start(), calls=%async_computation.32 | async-start | bytes 3932160 | tf_op jit(solution)/shard_map/all_gather | solution.py:72
  940.6 203.5 %reduce-scatter.43.cloned.1.call-start = ((), (), s32[]{:S(2)}) async-start(), calls=%async_computation.33 | async-start | bytes 3932160 | tf_op jit(solution)/shard_map/reduce_scatter | solution.py:76
  1085.2 129.1 %all-gather.40.cloned.1.call-start = ((), (), s32[]{:S(2)}) async-start(), calls=%async_computation.34 | async-start | bytes 3932160 | tf_op jit(solution)/shard_map/all_gather | solution.py:72
  1150.6 173.1 %reduce-scatter.45.cloned.1.call-start = ((), (), s32[]{:S(2)}) async-start(), calls=%async_computation.35 | async-start | bytes 3932160 | tf_op jit(solution)/shard_map/reduce_scatter | solution.py:76
  1264.8 153.3 %all-gather.42.cloned.1.call-start = ((), (), s32[]{:S(2)}) async-start(), calls=%async_computation.36 | async-start | bytes 3932160 | tf_op jit(solution)/shard_map/all_gather | solution.py:72
  1354.0 141.4 %reduce-scatter.47.cloned.1.call-start = ((), (), s32[]{:S(2)}) async-start(), calls=%async_computation.37 | async-start | bytes 3932160 | tf_op jit(solution)/shard_map/reduce_scatter | solution.py:76
  1436.4 129.7 %all-gather.44.cloned.1.call-start = ((), (), s32[]{:S(2)}) async-start(), calls=%async_computation.38 | async-start | bytes 3932160 | tf_op jit(solution)/shard_map/all_gather | solution.py:72
  1502.4 174.6 %reduce-scatter.49.cloned.1.call-start = ((), (), s32[]{:S(2)}) async-start(), calls=%async_computation.39 | async-start | bytes 3932160 | tf_op jit(solution)/shard_map/reduce_scatter | solution.py:76
  1618.1 150.7 %all-gather.46.cloned.1.call-start = ((), (), s32[]{:S(2)}) async-start(), calls=%async_computation.40 | async-start | bytes 3932160 | tf_op jit(solution)/shard_map/all_gather | solution.py:72
  1704.8 141.5 %reduce-scatter.51.cloned.1.call-start = ((), (), s32[]{:S(2)}) async-start(), calls=%async_computation.41 | async-start | bytes 3932160 | tf_op jit(solution)/shard_map/reduce_scatter | solution.py:76
  1787.3 155.2 %all-gather.48.cloned.1.call-start = ((), (), s32[]{:S(2)}) async-start(), calls=%async_computation.42 | async-start | bytes 3932160 | tf_op jit(solution)/shard_map/all_gather | solution.py:72
  1852.6 182.2 %reduce-scatter.41.cloned.1.call-start = ((), (), s32[]{:S(2)}) async-start(), calls=%async_computation.31 | async-start | bytes 3932160 | tf_op jit(solution)/shard_map/reduce_scatter | solution.py:76
  1860.3 183.1 %reduce-scatter.67.cloned.1.call-start = ((), (), s32[]{:S(2)}) async-start(), calls=%async_computation.55 | async-start | bytes 3932160
  1879.6 179.8 %reduce-scatter.57.cloned.1.call-start = ((), (), s32[]{:S(2)}) async-start(), calls=%async_computation.45 | async-start | bytes 3932160 | tf_op jit(solution)/shard_map/reduce_scatter | solution.py:357
  1898.5 201.4 %reduce-scatter.59.cloned.1.call-start = ((), (), s32[]{:S(2)}) async-start(), calls=%async_computation.46 | async-start | bytes 3932160 | tf_op jit(solution)/shard_map/reduce_scatter | solution.py:360
  1925.2 200.6 %reduce-scatter.61.cloned.1.call-start = ((), (), s32[]{:S(2)}) async-start(), calls=%async_computation.52 | async-start | bytes 983040
  1983.7 167.8 %reduce-scatter.63.cloned.1.call-start = ((), (), s32[]{:S(2)}) async-start(), calls=%async_computation.53 | async-start | bytes 983040
  2003.0 177.0 %reduce-scatter.65.cloned.1.call-start = ((), (), s32[]{:S(2)}) async-start(), calls=%async_computation.54 | async-start | bytes 1474560
  2011.6 196.7 %reduce-scatter.55.cloned.1.call-start = ((), (), s32[]{:S(2)}) async-start(), calls=%async_computation.44 | async-start | bytes 1474560 | tf_op jit(solution)/shard_map/reduce_scatter | solution.py:345
  2026.1 244.6 %reduce-scatter.53.cloned.1.call-start = ((), (), s32[]{:S(2)}) async-start(), calls=%async_computation.43 | async-start | bytes 3932160 | tf_op jit(solution)/shard_map/reduce_scatter | solution.py:76
  2032.3 297.2 %reduce-scatter.69.cloned.1.call-start = ((), (), s32[]{:S(2)}) async-start(), calls=%async_computation.56 | async-start | bytes 835584
  (217 other events, 4709.3 us)
Sparse Core Ops, SparseCore 0:
  73.3 65.9 all-gather.25
  163.7 58.7 reduce-scatter.30
  223.9 29.1 all-gather.53
  255.1 63.0 all-gather.27
  319.7 27.6 all-gather.55
  349.0 28.4 all-gather.57
  385.2 59.6 reduce-scatter.32
  470.1 65.7 all-gather.29
  559.3 58.7 reduce-scatter.34
  622.6 63.6 all-gather.31
  704.3 58.7 reduce-scatter.36
  787.9 65.8 all-gather.33
  876.3 58.7 reduce-scatter.38
  939.6 63.6 all-gather.35
  1004.7 62.1 all-gather.37
  1085.4 58.7 reduce-scatter.42
  1150.6 63.6 all-gather.39
  1264.9 58.7 reduce-scatter.44
  1354.2 63.8 all-gather.41
  1436.6 58.7 reduce-scatter.46
  1502.5 63.6 all-gather.43
  1618.2 58.7 reduce-scatter.48
  1704.9 63.8 all-gather.45
  1787.4 58.7 reduce-scatter.50
  1852.8 63.6 all-gather.47
  1919.3 58.7 reduce-scatter.40
  1980.7 38.1 reduce-scatter.66
  2021.4 37.9 reduce-scatter.56
  2061.9 37.9 reduce-scatter.58
  2182.6 25.7 reduce-scatter.54
  2210.6 60.0 reduce-scatter.52
  2274.5 54.8 reduce-scatter.68
  (5 shorter events, 109.4 us)
where the time goes:
time: 2350 us; the launch traced here: 2340 us
  waiting for transfers between devices  1600 us (68%)
  matrix products  397 us (17%)
  other arithmetic  184 us (8%)
  local copies, waits for them, and re-layouts  71.7 us (3%)
  blocking collectives  58.1 us (2%)
    reduce_scatter x12, waiting for transfers between devices, collect(): lax.psum_scatter(partial_rows.astype(jnp.bfloat16), 'tensor', scatter_dim...  638 us
    all_gather x12, waiting for transfers between devices, spread(): return lax.all_gather(rows_low, 'tensor', axis=0, tiled=True)  619 us
    unnamed x42, waiting for transfers between devices  129 us
    dot_general x21, matrix products, matmul(): return jnp.dot(left_side, right_side, preferred_element_type=jnp.float32)  91.7 us
    dot_general x21, matrix products, times_right_t(): lax.dot_general(left_side, right_side, (((1,), (1,)), ((), ())), preferre...  84.6 us
    dot_general x21, matrix products, left_t_times(): lax.dot_general(left_side, right_side, (((0,), (0,)), ((), ())), preferre...  70.4 us
    ppermute x4, waiting for transfers between devices, shifted(): return lax.ppermute(block, axis, route)  69.9 us
    another operation x17, other arithmetic, body(): stacked = jax.tree.map(lambda *members: jnp.stack(members), *kept_list)  52 us
  transfers between devices with their start and end apart: 41, of which 36 were waited for; matrix products, arithmetic and copies ran while one was open for 15% of the time, Pallas kernels for 0%

commit v1 on v0

v1 whole, which is shorter than its diff:
```python
import jax
import jax.numpy as jnp
import numpy as np
from jax import lax
from jax.sharding import PartitionSpec as P

HD = 96
epsilon = 1e-05
rope_base = 100000.0
AXES = ("section", "fsdp", "tensor")
bf16 = jnp.bfloat16
f32 = jnp.float32


class Grid:
    def __init__(self, mesh):
        self.X = mesh.shape["section"]
        self.C = 2
        self.Y = mesh.shape["fsdp"] // self.C
        self.Z = mesh.shape["tensor"]
        self.R = self.Y * self.Z
        self.places = [
            (x, y, c, z)
            for x in range(self.X)
            for y in range(self.Y)
            for c in range(self.C)
            for z in range(self.Z)
        ]

    def rank(self, place):
        x, y, c, z = place
        return ((x * self.Y + y) * self.C + c) * self.Z + z

    def send(self, block, route):
        pairs = []
        for place in self.places:
            goal = route(*place)
            if goal is not None:
                pairs.append((self.rank(place), self.rank(goal)))
        return lax.ppermute(block, AXES, pairs)

    def over_x(self, block):
        return self.send(block, lambda x, y, c, z: (1 - x, y, c, z))

    def over_c(self, block):
        return self.send(block, lambda x, y, c, z: (x, y, 1 - c, z))

    def place_of(self, p):
        p = p % self.R
        y, k = p // self.Z, p % self.Z
        return (y, k if y % 2 == 0 else self.Z - 1 - k)

    def pos_of(self, y, z):
        return y * self.Z + (z if y % 2 == 0 else self.Z - 1 - z)

    def turn(self, block, step):
        def route(x, y, c, z):
            yy, zz = self.place_of(self.pos_of(y, z) + step)
            return (x, yy, c, zz)

        return self.send(block, route)

    def me(self):
        x = lax.axis_index("section")
        f = lax.axis_index("fsdp")
        z = lax.axis_index("tensor")
        return x, f // self.C, f % self.C, z

    def my_pos(self):
        x, y, c, z = self.me()
        return y * self.Z + jnp.where(y % 2 == 0, z, self.Z - 1 - z)

    def dyn_place(self, p):
        p = (p + 2 * self.R) % self.R
        y, k = p // self.Z, p % self.Z
        return y, jnp.where(y % 2 == 0, k, self.Z - 1 - k)

    def ring_gather(self, block):
        found = [(0, block)]
        up = down = block
        ahead = self.R // 2
        for k in range(1, ahead + 1):
            up = self.turn(up, 1)
            found.append((-k, up))
            if k <= self.R - 1 - ahead:
                down = self.turn(down, -1)
                found.append((k, down))
        return found

    def ring_scatter(self, piece):
        ahead = self.R // 2
        behind = self.R - 1 - ahead
        up = down = None
        for k in range(ahead, 0, -1):
            term = piece(k)
            up = self.turn((term if up is None else term + up.astype(f32)).astype(bf16), 1)
            if k <= behind:
                term = piece(-k)
                down = self.turn((term if down is None else term + down.astype(f32)).astype(bf16), -1)
        return piece(0) + up.astype(f32) + down.astype(f32)


def matmul(a, b):
    return jnp.dot(a, b, preferred_element_type=f32)


def times_right_t(a, b):
    return lax.dot_general(a, b, (((1,), (1,)), ((), ())), preferred_element_type=f32)


def left_t_times(a, b):
    return lax.dot_general(a, b, (((0,), (0,)), ((), ())), preferred_element_type=f32)


def normalize(values, gain_row):
    return values * lax.rsqrt(jnp.mean(values * values, -1, keepdims=True) + epsilon) * gain_row


def norm_pullback(values, gain_row, upstream):
    _, pullback = jax.vjp(normalize, values, gain_row)
    return pullback(upstream)


def turning(doc_row):
    places = jnp.arange(doc_row.shape[-1], dtype=jnp.int32)
    begins = jnp.concatenate([jnp.ones((1,), dtype=bool), doc_row[1:] != doc_row[:-1]], -1)
    starts = lax.cummax(jnp.where(begins, places, 0), axis=0)
    positions = (places - starts).astype(f32)
    ladder = jnp.arange(HD // 2, dtype=f32)
    frequency = rope_base ** (-2.0 * ladder / HD)
    angles = positions[..., None] * frequency
    return jnp.cos(angles), jnp.sin(angles)


def rotate(values, cosine, sine_part):
    half = values.shape[-1] // 2
    a = values[..., :half]
    b = values[..., half:]
    return jnp.concatenate([a * cosine - b * sine_part, b * cosine + a * sine_part], -1)


def scores_of(query_rot, key_rot, allowed):
    scores = jnp.einsum("ahgd,bhd->hgab", query_rot, key_rot, preferred_element_type=f32)
    return jnp.where(allowed[None, None], scores * HD ** (-0.5), -1e30)


def attend_forward(query_rot, key_rot, value_low, allowed):
    scores = scores_of(query_rot, key_rot, allowed)
    largest = jnp.max(scores, -1, keepdims=True)
    raised = jnp.exp(scores - largest)
    row_total = jnp.sum(raised, -1, keepdims=True)
    probs = (raised / row_total).astype(bf16)
    mixed = jnp.einsum("hgab,bhd->ahgd", probs, value_low, preferred_element_type=f32)
    return mixed.astype(bf16), largest + jnp.log(row_total)


def attend_backward(query_rot, key_rot, value_low, allowed, log_total, grad_mixed):
    probs = jnp.exp(scores_of(query_rot, key_rot, allowed) - log_total)
    grad_value = jnp.einsum(
        "hgab,ahgd->bhd", probs.astype(bf16), grad_mixed, preferred_element_type=f32
    )
    grad_probs = jnp.einsum("ahgd,bhd->hgab", grad_mixed, value_low, preferred_element_type=f32)
    grad_scores = (
        probs * (grad_probs - jnp.sum(probs * grad_probs, -1, keepdims=True))
    ).astype(bf16)
    grad_query = jnp.einsum(
        "hgab,bhd->ahgd", grad_scores, key_rot, preferred_element_type=f32
    ) * HD ** (-0.5)
    grad_key = jnp.einsum(
        "hgab,ahgd->bhd", grad_scores, query_rot, preferred_element_type=f32
    ) * HD ** (-0.5)
    return grad_query, grad_key, grad_value


def spread(grid, block):
    far = grid.over_x(block)
    near = jnp.concatenate([block, grid.over_c(block)], 0)
    far = jnp.concatenate([far, grid.over_c(far)], 0)
    return near, far


def collect(grid, near, far):
    rows = near.shape[0] // 2
    passed = far[:rows] + grid.over_c(far[rows:].astype(bf16)).astype(f32)
    from_x = grid.over_x(passed.astype(bf16)).astype(f32)
    from_c = grid.over_c(near[rows:].astype(bf16)).astype(f32)
    return near[:rows] + from_c + from_x


def layer_forward(grid, hidden_in, weights, gain_pair, facts):
    cosine, sine_part, allowed = facts
    weight_qkv, weight_o, weight_g, weight_u, weight_d = weights
    heads = weight_o.shape[1] // HD
    pairs = heads // 2
    normed = normalize(hidden_in, gain_pair[0]).astype(bf16)
    near, far = spread(grid, normed)
    qkv = jnp.concatenate([matmul(near, weight_qkv), matmul(far, weight_qkv)], 0)
    length = qkv.shape[0]
    q_cols, k_cols = heads * HD, pairs * HD
    query_rot = rotate(qkv[:, :q_cols].reshape(length, heads, HD), cosine, sine_part).astype(bf16)
    key_rot = rotate(
        qkv[:, q_cols : q_cols + k_cols].reshape(length, pairs, HD), cosine, sine_part
    ).astype(bf16)
    value_low = qkv[:, q_cols + k_cols :].astype(bf16).reshape(length, pairs, HD)
    query_rot = query_rot.reshape(length, pairs, 2, HD)
    mixed, log_total = attend_forward(query_rot, key_rot, value_low, allowed)
    mixed = mixed.reshape(length, q_cols)
    half = length // 2
    part_far = times_right_t(mixed[half:], weight_o)
    part_near = times_right_t(mixed[:half], weight_o)
    middle = hidden_in + collect(grid, part_near, part_far)
    second = normalize(middle, gain_pair[1]).astype(bf16)
    near2, far2 = spread(grid, second)
    gates, ups, hiddens = [], [], []
    for part in (near2, far2):
        gate = matmul(part, weight_g)
        up = matmul(part, weight_u)
        gates.append(gate.astype(bf16))
        ups.append(up.astype(bf16))
        hiddens.append((jax.nn.silu(gate) * up).astype(bf16))
    part_far = matmul(hiddens[1], weight_d)
    part_near = matmul(hiddens[0], weight_d)
    result = middle + collect(grid, part_near, part_far)
    whole = jnp.concatenate([near, far], 0)
    whole2 = jnp.concatenate([near2, far2], 0)
    kept = (
        hidden_in, whole, query_rot, key_rot, value_low, log_total, mixed, middle, whole2,
        gates, ups, jnp.concatenate(hiddens, 0),
    )
    return result, kept


def layer_backward(grid, grad_out, kept, weights, gain_pair, facts):
    cosine, sine_part, allowed = facts
    weight_qkv, weight_o, weight_g, weight_u, weight_d = weights
    (
        hidden_in, whole, query_rot, key_rot, value_low, log_total, mixed, middle, whole2,
        gates, ups, hidden,
    ) = kept
    grad_low = grad_out.astype(bf16)
    near, far = spread(grid, grad_low)
    terms, grad_gs, grad_us = [], [], []
    for part, gate, up in zip((near, far), gates, ups):
        gate = gate.astype(f32)
        up = up.astype(f32)
        grad_hidden = times_right_t(part, weight_d)
        sig = jax.nn.sigmoid(gate)
        grad_gate = (grad_hidden * up * sig * (1.0 + gate * (1.0 - sig))).astype(bf16)
        grad_up = (grad_hidden * gate * sig).astype(bf16)
        terms.append(times_right_t(grad_gate, weight_g) + times_right_t(grad_up, weight_u))
        grad_gs.append(grad_gate)
        grad_us.append(grad_up)
    grad_second = collect(grid, terms[0], terms[1])
    down_term = left_t_times(hidden, jnp.concatenate([near, far], 0)).astype(bf16)
    gate_term = left_t_times(whole2, jnp.concatenate(grad_gs, 0)).astype(bf16)
    up_term = left_t_times(whole2, jnp.concatenate(grad_us, 0)).astype(bf16)
    grad_norm, gain_two = norm_pullback(middle, gain_pair[1], grad_second)
    grad_middle = grad_out + grad_norm
    near, far = spread(grid, grad_middle.astype(bf16))
    grad_attn = jnp.concatenate([near, far], 0)
    length = grad_attn.shape[0]
    half = length // 2
    grad_mixed = jnp.concatenate(
        [matmul(near, weight_o), matmul(far, weight_o)], 0
    ).astype(bf16)
    out_term = left_t_times(grad_attn, mixed).astype(bf16)
    pairs = key_rot.shape[1]
    grad_query, grad_key, grad_value = attend_backward(
        query_rot, key_rot, value_low, allowed, log_total,
        grad_mixed.reshape(length, pairs, 2, HD),
    )
    grad_query = rotate(grad_query.reshape(length, 2 * pairs, HD), cosine, -sine_part)
    grad_key = rotate(grad_key, cosine, -sine_part)
    grad_qkv = jnp.concatenate(
        [
            grad_query.astype(bf16).reshape(length, 2 * pairs * HD),
            grad_key.astype(bf16).reshape(length, pairs * HD),
            grad_value.astype(bf16).reshape(length, pairs * HD),
        ],
        1,
    )
    part_far = times_right_t(grad_qkv[half:], weight_qkv)
    part_near = times_right_t(grad_qkv[:half], weight_qkv)
    grad_normed = collect(grid, part_near, part_far)
    qkv_term = left_t_times(whole, grad_qkv).astype(bf16)
    grad_norm, gain_one = norm_pullback(hidden_in, gain_pair[0], grad_normed)
    grad_input = grad_middle + grad_norm
    return grad_input, (qkv_term, out_term, gate_term, up_term, down_term), jnp.stack([gain_one, gain_two])


def body(grid, inputs, doc_ids, cotangent, wq, wk, wv, wo, wg, wu, wd, gains):
    X, Y, C, Z = grid.X, grid.Y, grid.C, grid.Z
    x, y, c, z = grid.me()
    pos = grid.my_pos()
    micro, rows, width = inputs.shape
    depth = wq.shape[1]
    at_zero = x == 0

    def enter(block):
        def route(m):
            def go(x, y, c, z):
                if z % 2 != x:
                    return None
                return (x, y, z // 2, m * C + c)

            return go

        first, last = grid.send(block[0], route(0)), grid.send(block[1], route(1))
        return jnp.where(z // C == 0, first, last)

    def leave(block, section):
        def route(m):
            def go(x, y, c, z):
                if z // C != m:
                    return None
                return (section, y, z % C, 2 * c + x)

            return go

        return jnp.stack([grid.send(block, route(m)) for m in range(micro)])

    rows_in = enter(inputs)
    rows_cot = enter(cotangent)
    docs = lax.all_gather(doc_ids[:, 0], "fsdp", axis=0, tiled=False)
    doc_row = docs[y * C + z % C, z // C]
    length = doc_row.shape[0]
    places = jnp.arange(length, dtype=jnp.int32)
    cosine, sine_part = turning(doc_row)

    def in_my_order(rows_of):
        blocks = []
        for dx, dc in ((0, 0), (0, 1), (1, 0), (1, 1)):
            xx = x + dx - 2 * x * dx
            cc = c + dc - 2 * c * dc
            blocks.append(lax.dynamic_slice_in_dim(rows_of, (2 * cc + xx) * rows, rows, 0))
        return jnp.concatenate(blocks, 0)

    token = in_my_order(places)
    doc_mine = in_my_order(doc_row)
    cosine = in_my_order(cosine)[:, None, :]
    sine_part = in_my_order(sine_part)[:, None, :]
    allowed = (token[None, :] <= token[:, None]) & (doc_mine[None, :] == doc_mine[:, None])
    facts = (cosine, sine_part, allowed)

    gain_all = lax.all_gather(gains[0], AXES, axis=0, tiled=False)
    gain_all = gain_all.reshape(X, Y * C * Z, 2, -1).transpose(0, 2, 1, 3).reshape(X, 2, width).astype(f32)

    def cut(block, index, count, axis):
        size = block.shape[axis] // count
        return lax.dynamic_slice_in_dim(block, index * size, size, axis)

    def pack_attn(side):
        qkv = jnp.concatenate([cut(wq[0], side, 2, 1), cut(wk[0], side, 2, 1), cut(wv[0], side, 2, 1)], 1)
        return jnp.concatenate([qkv, cut(wo[0], side, 2, 0).T], 1)

    def pack_gu(side):
        return jnp.stack([cut(wg[0], side, 2, 1), cut(wu[0], side, 2, 1)])

    def both_layers(pack):
        kept = pack(x)
        came = grid.over_x(pack(1 - x))
        return jnp.where(at_zero, kept, came), jnp.where(at_zero, came, kept)

    attn_parts = both_layers(pack_attn)
    gu_parts = both_layers(pack_gu)
    down_parts = both_layers(lambda side: cut(wd[0], side, 2, 0))

    def sibling_join(mine, other, axis):
        came = grid.over_c(other)
        return jnp.where(
            c == 0,
            jnp.concatenate([mine, came], axis),
            jnp.concatenate([came, mine], axis),
        )

    def whole_attn(part):
        buffer = jnp.zeros((Y, Z) + part.shape, bf16)
        for offset, block in grid.ring_gather(part):
            yy, zz = grid.dyn_place(pos + offset)
            buffer = lax.dynamic_update_slice(buffer, block[None, None], (yy, zz, 0, 0))
        halves = Z // 2
        mine = lax.dynamic_slice_in_dim(buffer, c * halves, halves, 1)
        other = lax.dynamic_slice_in_dim(buffer, (1 - c) * halves, halves, 1)
        came = grid.over_c(other)
        both = jnp.where(c == 0, jnp.stack([mine, came], 1), jnp.stack([came, mine], 1))
        top = both.transpose(0, 1, 3, 2, 4).reshape(width, halves, -1)
        q_cols = wq.shape[2] // 2
        k_cols = wk.shape[2] // 2
        weight_qkv = jnp.concatenate(
            [
                top[:, :, :q_cols].reshape(width, -1),
                top[:, :, q_cols : q_cols + k_cols].reshape(width, -1),
                top[:, :, q_cols + k_cols : q_cols + 2 * k_cols].reshape(width, -1),
            ],
            1,
        )
        weight_o = top[:, :, q_cols + 2 * k_cols :].reshape(width, -1)
        return weight_qkv, weight_o

    def whole_ffn(gu_part, down_part):
        gu = sibling_join(cut(gu_part, c, 2, 2), cut(gu_part, 1 - c, 2, 2), 1)
        down = sibling_join(cut(down_part, c, 2, 0), cut(down_part, 1 - c, 2, 0), 1)
        units = down.shape[0]
        tall = C * depth
        weight_g = jnp.zeros((width, Z * units), bf16)
        weight_u = jnp.zeros((width, Z * units), bf16)
        weight_d = jnp.zeros((Z * units, width), bf16)
        for (offset, gu_block), (_, d_block) in zip(grid.ring_gather(gu), grid.ring_gather(down)):
            yy, zz = grid.dyn_place(pos + offset)
            weight_g = lax.dynamic_update_slice(weight_g, gu_block[0], (yy * tall, zz * units))
            weight_u = lax.dynamic_update_slice(weight_u, gu_block[1], (yy * tall, zz * units))
            weight_d = lax.dynamic_update_slice(weight_d, d_block, (zz * units, yy * tall))
        return weight_g, weight_u, weight_d

    weights = []
    for s in range(2):
        weights.append(whole_attn(attn_parts[s]) + whole_ffn(gu_parts[s], down_parts[s]))

    hidden = rows_in.astype(f32)
    kept, outs = [], []
    for s in range(2):
        result, keep = layer_forward(grid, hidden, weights[s], gain_all[s], facts)
        low = result.astype(bf16)
        outs.append(leave(low, s))
        kept.append(keep)
        hidden = low.astype(f32)
    produced = jnp.where(at_zero, outs[0], outs[1])

    upstream = rows_cot
    grads_in, gain_terms, sums = [None] * 2, [None] * 2, [None] * 2
    for s in (1, 0):
        grad_input, terms, gain_terms[s] = layer_backward(
            grid, upstream.astype(f32), kept[s], weights[s], gain_all[s], facts
        )
        upstream = grad_input.astype(bf16)
        grads_in[s] = leave(upstream, s)
        sums[s] = terms
    grads_in = jnp.where(at_zero, grads_in[0], grads_in[1]).astype(f32)

    def back_attn(qkv_term, out_term):
        halves = Z // 2
        q_cols = wq.shape[2] // 2
        k_cols = wk.shape[2] // 2
        nq, nk = halves * q_cols, halves * k_cols
        top = jnp.concatenate(
            [
                qkv_term[:, :nq].reshape(width, halves, q_cols),
                qkv_term[:, nq : nq + nk].reshape(width, halves, k_cols),
                qkv_term[:, nq + nk :].reshape(width, halves, k_cols),
                out_term.reshape(width, halves, q_cols),
            ],
            2,
        )
        both = top.reshape(Y, C, depth, halves, -1).transpose(0, 1, 3, 2, 4)
        mine = lax.dynamic_index_in_dim(both, c, 1, keepdims=False)
        other = lax.dynamic_index_in_dim(both, 1 - c, 1, keepdims=False)
        buffer = sibling_join(mine, other, 1)

        def piece(offset):
            yy, zz = grid.dyn_place(pos + offset)
            return lax.dynamic_slice(buffer, (yy, zz, 0, 0), (1, 1) + buffer.shape[2:])[0, 0].astype(f32)

        return grid.ring_scatter(piece)

    def back_ffn(gate_term, up_term, down_term):
        units = down_term.shape[0] // Z
        tall = C * depth

        def piece_gu(offset):
            yy, zz = grid.dyn_place(pos + offset)
            at = (yy * tall, zz * units)
            return jnp.stack(
                [lax.dynamic_slice(term, at, (tall, units)) for term in (gate_term, up_term)]
            ).astype(f32)

        def piece_d(offset):
            yy, zz = grid.dyn_place(pos + offset)
            return lax.dynamic_slice(down_term, (zz * units, yy * tall), (units, tall)).astype(f32)

        gu = grid.ring_scatter(piece_gu).astype(bf16)
        down = grid.ring_scatter(piece_d).astype(bf16)
        gu = sibling_join(cut(gu, c, 2, 1), cut(gu, 1 - c, 2, 1), 2)
        down = sibling_join(cut(down, c, 2, 1), cut(down, 1 - c, 2, 1), 0)
        return gu, down

    def home(terms, axis):
        kept_part = jnp.where(at_zero, terms[0], terms[1])
        came = grid.over_x(jnp.where(at_zero, terms[1], terms[0]))
        return jnp.where(
            at_zero,
            jnp.concatenate([kept_part, came], axis),
            jnp.concatenate([came, kept_part], axis),
        ).astype(f32)

    attn_back, gu_back, down_back = [None] * 2, [None] * 2, [None] * 2
    for s in (1, 0):
        gu_back[s], down_back[s] = back_ffn(*sums[s][2:])
        attn_back[s] = back_attn(*sums[s][:2]).astype(bf16)
    gu_home = home(gu_back, 2)
    down_home = home(down_back, 0)
    q_cols = wq.shape[2] // 2
    k_cols = wk.shape[2] // 2
    kept_part = jnp.where(at_zero, attn_back[0], attn_back[1])
    came = grid.over_x(jnp.where(at_zero, attn_back[1], attn_back[0]))
    left = jnp.where(at_zero, kept_part, came).astype(f32)
    right = jnp.where(at_zero, came, kept_part).astype(f32)
    cuts = [0, q_cols, q_cols + k_cols, q_cols + 2 * k_cols, q_cols * 2 + 2 * k_cols]
    query_home, key_home, value_home, out_home = [
        jnp.concatenate([left[:, a:b], right[:, a:b]], 1) for a, b in zip(cuts[:-1], cuts[1:])
    ]
    out_home = out_home.T

    gain_sum = jnp.stack(gain_terms)
    gain_sum = gain_sum.reshape(X, 2, Y * C * Z, -1).transpose(0, 2, 1, 3).reshape(X * Y * C * Z, -1)
    gain_share = lax.psum_scatter(gain_sum, AXES, scatter_dimension=0, tiled=True)
    gain_share = gain_share.reshape(1, 2, -1)
    return (
        produced[None],
        grads_in[None],
        query_home[None],
        key_home[None],
        value_home[None],
        out_home[None],
        gu_home[0][None],
        gu_home[1][None],
        down_home[None],
        gain_share,
    )


def solution(mesh):
    grid = Grid(mesh)

    def run(*arguments):
        return body(grid, *arguments)

    return jax.shard_map(
        run,
        mesh=mesh,
        in_specs=(
            P(None, ("fsdp", "tensor"), None),
            P(None, "fsdp", None),
            P(None, ("fsdp", "tensor"), None),
            P("section", "fsdp", "tensor"),
            P("section", "fsdp", "tensor"),
            P("section", "fsdp", "tensor"),
            P("section", "tensor", "fsdp"),
            P("section", "fsdp", "tensor"),
            P("section", "fsdp", "tensor"),
            P("section", "tensor", "fsdp"),
            P("section", None, ("fsdp", "tensor")),
        ),
        out_specs=(
            P("section", None, ("fsdp", "tensor"), None),
            P("section", None, ("fsdp", "tensor"), None),
            P("section", "fsdp", "tensor"),
            P("section", "fsdp", "tensor"),
            P("section", "fsdp", "tensor"),
            P("section", "tensor", "fsdp"),
            P("section", "fsdp", "tensor"),
            P("section", "fsdp", "tensor"),
            P("section", "tensor", "fsdp"),
            P("section", None, ("fsdp", "tensor")),
        ),
        check_vma=False,
    )
```

time: 2350 us -> 1310 us (0.56)
  waiting for transfers between devices: 1600 us -> 292 us
  starting transfers between devices: 12.9 us -> 211 us
  local copies, waits for them, and re-layouts: 71.7 us -> 259 us
  matrix products: 397 us -> 212 us
  blocking collectives: 58.1 us -> 140 us
    reduce_scatter x15 -> x0, waiting for transfers between devices: 713 us -> none  [the longest x12 638 us: collect(): lax.psum_scatter(partial_rows.astype(jnp.bfloat16), 'tensor', scatter_dim...]
    all_gather x17 -> x0, waiting for transfers between devices: 684 us -> none  [the longest x12 619 us: spread(): return lax.all_gather(rows_low, 'tensor', axis=0, tiled=True)]
    ppermute x4 -> x162, waiting for transfers between devices: 69.9 us -> 292 us  [send(): return lax.ppermute(block, AXES, pairs)]
    ppermute x4 -> x162, starting transfers between devices: 9.09 us -> 211 us  [send(): return lax.ppermute(block, AXES, pairs)]
    dot_general x75 -> x56, matrix products: 329 us -> 175 us  [the longest x10 43.5 us: left_t_times(): lax.dot_general(a, b, (((0,), (0,)), ((), ())), preferred_element_type=f32)]
    unnamed x42 -> x0, waiting for transfers between devices: 129 us -> none
    dynamic_update_slice x0 -> x46, local copies, waits for them, and re-layouts: none -> 77.2 us  [the longest x14 61.8 us: whole_ffn(): lax.dynamic_update_slice(weight_d, d_block, (zz * units, yy * tall))]
    dynamic_slice x1 -> x58, local copies, waits for them, and re-layouts: 0.01 us -> 66.2 us  [the longest x36 50.1 us: piece_gu(): lax.dynamic_slice(term, at, (tall, units))]
  transfers between devices with their start and end apart: 41 -> 162, of which waited for: 36 -> 40; matrix products, arithmetic and copies ran while one was open for 15% -> 49% of each run, Pallas kernels for 0% -> 0%
where the time goes in v1:
time: 1310 us; the launch traced here: 1290 us
  waiting for transfers between devices  292 us (22%)
  local copies, waits for them, and re-layouts  259 us (20%)
  matrix products  212 us (16%)
  starting transfers between devices  211 us (16%)
  other arithmetic  172 us (13%)
  blocking collectives  140 us (11%)
    ppermute x162, waiting for transfers between devices, send(): return lax.ppermute(block, AXES, pairs)  292 us
    ppermute x162, starting transfers between devices, send(): return lax.ppermute(block, AXES, pairs)  211 us
    all_gather x1, blocking collectives, body(): gain_all = lax.all_gather(gains[0], AXES, axis=0, tiled=False)  74.1 us
    dynamic_update_slice x14, local copies, waits for them, and re-layouts, whole_ffn(): lax.dynamic_update_slice(weight_d, d_block, (zz * units, yy * tall))  61.8 us
    unnamed x1, blocking collectives  55.5 us
    dynamic_slice x36, local copies, waits for them, and re-layouts, piece_gu(): lax.dynamic_slice(term, at, (tall, units))  50.1 us
    dot_general x10, matrix products, left_t_times(): lax.dot_general(a, b, (((0,), (0,)), ((), ())), preferred_element_type=f32)  43.5 us
    dot_general x20, matrix products, matmul(): return jnp.dot(a, b, preferred_element_type=f32)  41.9 us
  transfers between devices with their start and end apart: 162, of which 40 were waited for; matrix products, arithmetic and copies ran while one was open for 49% of the time, Pallas kernels for 0%

profile of v1, /device:TPU:1, one launch (start us, length us, event | category | flops | bytes accessed | tf_op | source)
XLA Modules:
  0.0 1292.2 jit_solution(17226244447758011857)
XLA Ops:
  15.3 7.7 collective-permute-start.1
  25.3 74.1 %all_gather.6 = bf16[32,2,96]{2,1,0:T(2,128)(2,1)S(1)} all-gather(bf16[1,2,96]{2,1,0:T(2,128)(2,1)S(1)} %copy-done.200), channel_id=1, replica_groups=mesh['section'=2,'fsdp'=4,'tensor'=4] {'section','fsdp','tensor'}, dimensions={0}, use_global_device_ids=true | all-gather | bytes 12672 | tf_op jit(solution)/shard_map/all_gather | solution.py:345
  100.1 10.2 all-gather
  133.0 25.5 %collective-permute-done.6 = bf16[384,576]{0,1:T(8,128)(2,1)S(1)} collective-permute-done((bf16[384,576]{0,1:T(8,128)(2,1)S(1)}, bf16[384,576]{0,1:T(8,128)(2,1)S(1)}, u32[]{:S(2)}, u32[]{:S(2)}) %collective-permute-start.6) | collective-permute-done | bytes 442400 | tf_op jit(solution)/shard_map/ppermute | solution.py:40
  160.1 8.9 collective-permute-done.8
  170.7 7.9 collective-permute-done.10
  205.7 7.7 collective-permute-done.47
  244.9 8.8 reshape.736
  274.7 7.6 fusion.364
  282.3 8.0 fusion.6
  398.0 8.8 reshape.745
  428.3 9.0 fusion.365
  437.3 8.0 fusion.7
  445.3 7.5 fusion.204
  472.2 8.8 collective-permute-done.70
  527.7 14.7 %collective-permute-done.64 = bf16[2,768,256]{2,1,0:T(8,128)(2,1)S(1)} collective-permute-done((bf16[2,768,256]{2,1,0:T(8,128)(2,1)S(1)}, bf16[2,768,256]{2,1,0:T(8,128)(2,1)S(1)}, u32[]{:S(2)}, u32[]{:S(2)}) %collective-permute-start.64) | collective-permute-done | bytes 786464 | tf_op jit(solution)/shard_map/ppermute | solution.py:40
  615.7 7.6 collective-permute-done.154
  636.2 14.0 %collective-permute-done.78 = bf16[256,1536]{1,0:T(8,128)(2,1)S(1)} collective-permute-done((bf16[256,1536]{1,0:T(8,128)(2,1)S(1)}, bf16[256,1536]{1,0:T(8,128)(2,1)S(1)}, u32[]{:S(2)}, u32[]{:S(2)}) %collective-permute-start.78) | collective-permute-done | bytes 786464 | tf_op jit(solution)/shard_map/ppermute | solution.py:40
  696.5 9.4 fusion.219
  705.9 13.1 %fusion.3 = (f32[2,2,1024]{2,1,0:T(2,128)S(1)}, f32[2,1024,1024,2]{2,1,3,0:T(8,128)}) fusion(f32[2,2,1024,1024]{2,3,1,0:T(8,128)} %get-tuple-element.247, f32[2,2,1024]{2,1,0:T(2,128)S(1)} %log_add_fusion.1, bf16[1024,2,96,1]{0,2,3,1:T(8,128)(2,1)S(1)} %bitcast.598, bf16[512,2,2,96]{0,3,2,1:T(8,128)(2,1)} %copy-done.70, bf16[512,2,2,96]{0,3,2,1:T(8,128)(2,1)S(1)} %fusion.225), kind=kOutput, calls=%fused_computation.7 | convolution fusion | flops 819458048 | bytes 34766848 | tf_op jit(solution)/shard_map/ahgd,bhd->hgab/dot_general | solution.py:162
  719.3 10.9 fusion.5
  804.3 19.2 %collective-permute-start.139 = (bf16[2,768,256]{2,1,0:T(8,128)(2,1)S(1)}, bf16[2,768,256]{2,1,0:T(8,128)(2,1)S(1)}, u32[]{:S(2)}, u32[]{:S(2)}) collective-permute-start(bf16[2,768,256]{2,1,0:T(8,128)(2,1)S(1)} %add_convert_fusion.3), channel_id=1, source_target_pairs={{0,1},{1,2},{2,3},{3,11},{4,5},{5,6},{6,7},{7,15},{8,0},{9,8},{10,... | collective-permute-start | bytes 2359304 | tf_op jit(solution)/shard_map/ppermute | solution.py:40
  831.9 9.7 collective-permute-done.142
  844.0 16.0 %collective-permute-start.97 = (bf16[256,1536]{1,0:T(8,128)(2,1)}, bf16[256,1536]{1,0:T(8,128)(2,1)S(1)}, u32[]{:S(2)}, u32[]{:S(2)}) collective-permute-start(bf16[256,1536]{1,0:T(8,128)(2,1)} %fusion.130), channel_id=1, source_target_pairs={{0,16},{1,17},{2,18},{3,19},{4,20},{5,21},{6,22},{7,23},{8,24},{9,... | collective-permute-start | bytes 2359304 | tf_op jit(solution)/shard_map/ppermute | solution.py:40
  934.2 22.9 %collective-permute-done.146 = bf16[256,768]{1,0:T(8,128)(2,1)S(1)} collective-permute-done((bf16[256,768]{1,0:T(8,128)(2,1)S(1)}, bf16[256,768]{1,0:T(8,128)(2,1)S(1)}, u32[]{:S(2)}, u32[]{:S(2)}) %collective-permute-start.146) | collective-permute-done | bytes 393248 | tf_op jit(solution)/shard_map/ppermute | solution.py:40
  1020.9 9.4 fusion.216
  1030.4 7.7 fusion
  1038.1 10.9 fusion.2
  1097.1 17.1 %collective-permute-done.134 = bf16[2,768,256]{2,1,0:T(8,128)(2,1)S(1)} collective-permute-done((bf16[2,768,256]{2,1,0:T(8,128)(2,1)S(1)}, bf16[2,768,256]{2,1,0:T(8,128)(2,1)S(1)}, u32[]{:S(2)}, u32[]{:S(2)}) %collective-permute-start.134) | collective-permute-done | bytes 786464 | tf_op jit(solution)/shard_map/ppermute | solution.py:40
  1120.0 10.1 collective-permute-done.112
  1193.4 31.5 %collective-permute-done.118 = bf16[384,576]{0,1:T(8,128)(2,1)} collective-permute-done((bf16[384,576]{0,1:T(8,128)(2,1)}, bf16[384,576]{0,1:T(8,128)(2,1)}, u32[]{:S(2)}, u32[]{:S(2)}) %collective-permute-start.118) | collective-permute-done | bytes 442400 | tf_op jit(solution)/shard_map/ppermute | solution.py:40
  1228.0 55.5 %all-reduce = f32[32,192]{1,0:T(8,128)S(1)} all-reduce(f32[32,192]{1,0:T(8,128)S(1)} %reshape.759), channel_id=3, replica_groups=mesh['section'=2,'fsdp'=4,'tensor'=4] {'section','fsdp','tensor'}, use_global_device_ids=true, to_apply=%region_20.21.clone | all-reduce | flops 6144 | bytes 49152
  (1153 shorter events, 797.7 us)
Async XLA Ops:
  2.4 114.4 %collective-permute-start.27 = (bf16[512,384]{1,0:T(8,128)(2,1)}, bf16[512,384]{1,0:T(8,128)(2,1)}, u32[]{:S(2)}, u32[]{:S(2)}) collective-permute-start(bf16[512,384]{1,0:T(8,128)(2,1)} %dynamic-slice_bitcast_fusion.10), channel_id=1, source_target_pairs={{0,16},{1,17},{2,18},{3,19},{4,20},{5,21},{6,22},{7,23},{8,24},{9,... | collective-permute-start | bytes 1179656 | tf_op jit(solution)/shard_map/ppermute | solution.py:40
  10.1 109.0 %collective-permute-start.3 = (bf16[384,576]{0,1:T(8,128)(2,1)}, bf16[384,576]{0,1:T(8,128)(2,1)S(1)}, u32[]{:S(2)}, u32[]{:S(2)}) collective-permute-start(bf16[384,576]{0,1:T(8,128)(2,1)} %pad_maximum_fusion.42), channel_id=1, source_target_pairs={{0,16},{1,17},{2,18},{3,19},{4,20},{5,21},{6,22},{7,23},{8,24},{9,... | collective-permute-start | bytes 1327112 | tf_op jit(solution)/shard_map/ppermute | solution.py:40
  12.6 112.5 %collective-permute-start.18 = (bf16[2,384,512]{2,1,0:T(8,128)(2,1)}, bf16[2,384,512]{2,1,0:T(8,128)(2,1)}, u32[]{:S(2)}, u32[]{:S(2)}) collective-permute-start(bf16[2,384,512]{2,1,0:T(8,128)(2,1)} %pad_maximum_fusion.18), channel_id=1, source_target_pairs={{0,16},{1,17},{2,18},{3,19},{4,20},{5,21},{6,22},{7,23},{8,24},{9,... | collective-permute-start | bytes 2359304 | tf_op jit(solution)/shard_map/ppermute | solution.py:40
  15.3 106.8 %collective-permute-start.1 = (bf16[256,1536]{1,0:T(8,128)(2,1)}, bf16[256,1536]{1,0:T(8,128)(2,1)}, u32[]{:S(2)}, u32[]{:S(2)}) collective-permute-start(bf16[256,1536]{1,0:T(8,128)(2,1)} %get-tuple-element.140), channel_id=1, source_target_pairs={{0,2},{2,6},{4,3},{6,7},{8,10},{10,14},{12,11},{14,15},{17,18},{19... | collective-permute-start | bytes 2359304 | tf_op jit(solution)/shard_map/ppermute | solution.py:40
  22.9 99.4 %collective-permute-start = (bf16[256,1536]{1,0:T(8,128)(2,1)}, bf16[256,1536]{1,0:T(8,128)(2,1)}, u32[]{:S(2)}, u32[]{:S(2)}) collective-permute-start(bf16[256,1536]{1,0:T(8,128)(2,1)} %get-tuple-element.141), channel_id=1, source_target_pairs={{0,0},{2,4},{4,1},{6,5},{8,8},{10,12},{12,9},{14,13},{17,16},{19,2... | collective-permute-start | bytes 2359304 | tf_op jit(solution)/shard_map/ppermute | solution.py:40
  122.1 61.1 %collective-permute-start.44 = (bf16[384,576]{0,1:T(8,128)(2,1)S(1)}, bf16[384,576]{0,1:T(8,128)(2,1)S(1)}, u32[]{:S(2)}, u32[]{:S(2)}) collective-permute-start(bf16[384,576]{0,1:T(8,128)(2,1)S(1)} %get-tuple-element.34), channel_id=1, source_target_pairs={{0,1},{1,2},{2,3},{3,11},{4,5},{5,6},{6,7},{7,15},{8,0},{9,8},{10,... | collective-permute-start | bytes 1327112 | tf_op jit(solution)/shard_map/ppermute | solution.py:40
  122.4 60.9 %collective-permute-start.45 = (bf16[384,576]{0,1:T(8,128)(2,1)S(1)}, bf16[384,576]{0,1:T(8,128)(2,1)S(1)}, u32[]{:S(2)}, u32[]{:S(2)}) collective-permute-start(bf16[384,576]{0,1:T(8,128)(2,1)S(1)} %get-tuple-element.34), channel_id=1, source_target_pairs={{0,8},{1,0},{2,1},{3,2},{4,12},{5,4},{6,5},{7,6},{8,9},{9,10},{10,... | collective-permute-start | bytes 1327112 | tf_op jit(solution)/shard_map/ppermute | solution.py:40
  125.1 58.6 %collective-permute-start.29 = (bf16[256,768]{1,0:T(8,128)(2,1)S(1)}, bf16[256,768]{1,0:T(8,128)(2,1)S(1)}, u32[]{:S(2)}, u32[]{:S(2)}) collective-permute-start(bf16[256,768]{1,0:T(8,128)(2,1)S(1)} %get-tuple-element.38), channel_id=1, source_target_pairs={{0,1},{1,2},{2,3},{3,11},{4,5},{5,6},{6,7},{7,15},{8,0},{9,8},{10,... | collective-permute-start | bytes 1179656 | tf_op jit(solution)/shard_map/ppermute | solution.py:40
  179.1 58.8 %collective-permute-start.11 = (bf16[2,2,384,576]{2,3,1,0:T(8,128)(2,1)S(1)}, bf16[2,2,384,576]{2,3,1,0:T(8,128)(2,1)S(1)}, u32[]{:S(2)}, u32[]{:S(2)}) collective-permute-start(bf16[2,2,384,576]{2,3,1,0:T(8,128)(2,1)S(1)} %get-tuple-element.78), channel_id=1, source_target_pairs={{0,4},{1,5},{2,6},{3,7},{4,0},{5,1},{6,2},{7,3},{8,12},{9,13},{10,... | collective-permute-start | bytes 5308424 | tf_op jit(solution)/shard_map/ppermute | solution.py:40
  226.8 75.7 %collective-permute-start.21 = (bf16[2,768,256]{2,1,0:T(8,128)(2,1)}, bf16[2,768,256]{2,1,0:T(8,128)(2,1)}, u32[]{:S(2)}, u32[]{:S(2)}) collective-permute-start(bf16[2,768,256]{2,1,0:T(8,128)(2,1)} %maximum_select_fusion.7), channel_id=1, source_target_pairs={{0,8},{1,0},{2,1},{3,2},{4,12},{5,4},{6,5},{7,6},{8,9},{9,10},{10,... | collective-permute-start | bytes 2359304 | tf_op jit(solution)/shard_map/ppermute | solution.py:40
  237.8 61.2 %collective-permute-start.48 = (bf16[384,576]{0,1:T(8,128)(2,1)}, bf16[384,576]{0,1:T(8,128)(2,1)}, u32[]{:S(2)}, u32[]{:S(2)}) collective-permute-start(bf16[384,576]{0,1:T(8,128)(2,1)} %collective-permute-done.46), channel_id=1, source_target_pairs={{0,1},{1,2},{2,3},{3,11},{4,5},{5,6},{6,7},{7,15},{8,0},{9,8},{10,... | collective-permute-start | bytes 1327112 | tf_op jit(solution)/shard_map/ppermute | solution.py:40
  369.9 84.1 %collective-permute-start.82 = (bf16[256,1536]{1,0:T(8,128)(2,1)}, bf16[256,1536]{1,0:T(8,128)(2,1)}, u32[]{:S(2)}, u32[]{:S(2)}) collective-permute-start(bf16[256,1536]{1,0:T(8,128)(2,1)} %get-tuple-element.136), channel_id=1, source_target_pairs={{0,2},{2,6},{4,3},{6,7},{8,10},{10,14},{12,11},{14,15},{17,18},{19... | collective-permute-start | bytes 2359304 | tf_op jit(solution)/shard_map/ppermute | solution.py:40
  376.5 79.1 %collective-permute-start.81 = (bf16[256,1536]{1,0:T(8,128)(2,1)}, bf16[256,1536]{1,0:T(8,128)(2,1)}, u32[]{:S(2)}, u32[]{:S(2)}) collective-permute-start(bf16[256,1536]{1,0:T(8,128)(2,1)} %get-tuple-element.137), channel_id=1, source_target_pairs={{0,0},{2,4},{4,1},{6,5},{8,8},{10,12},{12,9},{14,13},{17,16},{19,2... | collective-permute-start | bytes 2359304 | tf_op jit(solution)/shard_map/ppermute | solution.py:40
  558.0 77.8 %collective-permute-start.74 = (bf16[256,1536]{1,0:T(8,128)(2,1)}, bf16[256,1536]{1,0:T(8,128)(2,1)}, u32[]{:S(2)}, u32[]{:S(2)}) collective-permute-start(bf16[256,1536]{1,0:T(8,128)(2,1)} %slice.980), channel_id=1, source_target_pairs={{0,4},{1,5},{2,6},{3,7},{4,0},{5,1},{6,2},{7,3},{8,12},{9,13},{10,... | collective-permute-start | bytes 2359304 | tf_op jit(solution)/shard_map/ppermute | solution.py:40
  568.7 57.2 %collective-permute-start.84 = (bf16[256,1536]{1,0:T(8,128)(2,1)}, bf16[256,1536]{1,0:T(8,128)(2,1)S(1)}, u32[]{:S(2)}, u32[]{:S(2)}) collective-permute-start(bf16[256,1536]{1,0:T(8,128)(2,1)} %slice.978), channel_id=1, source_target_pairs={{0,4},{1,5},{2,6},{3,7},{4,0},{5,1},{6,2},{7,3},{8,12},{9,13},{10,... | collective-permute-start | bytes 2359304 | tf_op jit(solution)/shard_map/ppermute | solution.py:40
  582.6 78.2 %collective-permute-start.157 = (bf16[256,768]{1,0:T(8,128)(2,1)}, bf16[256,768]{1,0:T(8,128)(2,1)}, u32[]{:S(2)}, u32[]{:S(2)}) collective-permute-start(bf16[256,768]{1,0:T(8,128)(2,1)} %get-tuple-element.86), channel_id=1, source_target_pairs={{0,8},{1,0},{2,1},{3,2},{4,12},{5,4},{6,5},{7,6},{8,9},{9,10},{10,... | collective-permute-start | bytes 1179656 | tf_op jit(solution)/shard_map/ppermute | solution.py:40
  682.4 94.5 %collective-permute-start.141 = (bf16[2,768,256]{2,1,0:T(8,128)(2,1)}, bf16[2,768,256]{2,1,0:T(8,128)(2,1)}, u32[]{:S(2)}, u32[]{:S(2)}) collective-permute-start(bf16[2,768,256]{2,1,0:T(8,128)(2,1)} %add_convert_fusion.2), channel_id=1, source_target_pairs={{0,8},{1,0},{2,1},{3,2},{4,12},{5,4},{6,5},{7,6},{8,9},{9,10},{10,... | collective-permute-start | bytes 2359304 | tf_op jit(solution)/shard_map/ppermute | solution.py:40
  685.3 91.1 %collective-permute-start.156 = (bf16[256,768]{1,0:T(8,128)(2,1)}, bf16[256,768]{1,0:T(8,128)(2,1)}, u32[]{:S(2)}, u32[]{:S(2)}) collective-permute-start(bf16[256,768]{1,0:T(8,128)(2,1)} %get-tuple-element.83), channel_id=1, source_target_pairs={{0,1},{1,2},{2,3},{3,11},{4,5},{5,6},{6,7},{7,15},{8,0},{9,8},{10,... | collective-permute-start | bytes 1179656 | tf_op jit(solution)/shard_map/ppermute | solution.py:40
  687.3 91.9 %collective-permute-start.159 = (bf16[256,768]{1,0:T(8,128)(2,1)}, bf16[256,768]{1,0:T(8,128)(2,1)}, u32[]{:S(2)}, u32[]{:S(2)}) collective-permute-start(bf16[256,768]{1,0:T(8,128)(2,1)} %add_convert_fusion.13), channel_id=1, source_target_pairs={{0,8},{1,0},{2,1},{3,2},{4,12},{5,4},{6,5},{7,6},{8,9},{9,10},{10,... | collective-permute-start | bytes 1179656 | tf_op jit(solution)/shard_map/ppermute | solution.py:40
  690.9 91.7 %collective-permute-start.138 = (bf16[2,768,256]{2,1,0:T(8,128)(2,1)}, bf16[2,768,256]{2,1,0:T(8,128)(2,1)}, u32[]{:S(2)}, u32[]{:S(2)}) collective-permute-start(bf16[2,768,256]{2,1,0:T(8,128)(2,1)} %add_convert_fusion.4), channel_id=1, source_target_pairs={{0,1},{1,2},{2,3},{3,11},{4,5},{5,6},{6,7},{7,15},{8,0},{9,8},{10,... | collective-permute-start | bytes 2359304 | tf_op jit(solution)/shard_map/ppermute | solution.py:40
  881.2 91.2 %collective-permute-start.96 = (bf16[256,1536]{1,0:T(8,128)(2,1)}, bf16[256,1536]{1,0:T(8,128)(2,1)}, u32[]{:S(2)}, u32[]{:S(2)}) collective-permute-start(bf16[256,1536]{1,0:T(8,128)(2,1)} %slice.974), channel_id=1, source_target_pairs={{0,4},{1,5},{2,6},{3,7},{4,0},{5,1},{6,2},{7,3},{8,12},{9,13},{10,... | collective-permute-start | bytes 2359304 | tf_op jit(solution)/shard_map/ppermute | solution.py:40
  890.7 71.5 %collective-permute-start.149 = (bf16[256,768]{1,0:T(8,128)(2,1)}, bf16[256,768]{1,0:T(8,128)(2,1)}, u32[]{:S(2)}, u32[]{:S(2)}) collective-permute-start(bf16[256,768]{1,0:T(8,128)(2,1)} %get-tuple-element.82), channel_id=1, source_target_pairs={{0,8},{1,0},{2,1},{3,2},{4,12},{5,4},{6,5},{7,6},{8,9},{9,10},{10,... | collective-permute-start | bytes 1179656 | tf_op jit(solution)/shard_map/ppermute | solution.py:40
  1004.1 82.0 %collective-permute-start.160 = (bf16[256,384]{1,0:T(8,128)(2,1)}, bf16[256,384]{1,0:T(8,128)(2,1)}, u32[]{:S(2)}, u32[]{:S(2)}) collective-permute-start(bf16[256,384]{1,0:T(8,128)(2,1)} %get-tuple-element.210), channel_id=1, source_target_pairs={{0,4},{1,5},{2,6},{3,7},{4,0},{5,1},{6,2},{7,3},{8,12},{9,13},{10,... | collective-permute-start | bytes 589832 | tf_op jit(solution)/shard_map/ppermute | solution.py:40
  1006.9 132.5 %collective-permute-start.143 = (bf16[2,384,256]{2,1,0:T(8,128)(2,1)}, bf16[2,384,256]{2,1,0:T(8,128)(2,1)}, u32[]{:S(2)}, u32[]{:S(2)}) collective-permute-start(bf16[2,384,256]{2,1,0:T(8,128)(2,1)} %get-tuple-element.166), channel_id=1, source_target_pairs={{0,4},{1,5},{2,6},{3,7},{4,0},{5,1},{6,2},{7,3},{8,12},{9,13},{10,... | collective-permute-start | bytes 1179656 | tf_op jit(solution)/shard_map/ppermute | solution.py:40
  1010.8 72.7 %collective-permute-start.133 = (bf16[2,768,256]{2,1,0:T(8,128)(2,1)}, bf16[2,768,256]{2,1,0:T(8,128)(2,1)}, u32[]{:S(2)}, u32[]{:S(2)}) collective-permute-start(bf16[2,768,256]{2,1,0:T(8,128)(2,1)} %add_convert_fusion.8), channel_id=1, source_target_pairs={{0,8},{1,0},{2,1},{3,2},{4,12},{5,4},{6,5},{7,6},{8,9},{9,10},{10,... | collective-permute-start | bytes 2359304 | tf_op jit(solution)/shard_map/ppermute | solution.py:40
  1014.4 76.4 %collective-permute-start.130 = (bf16[2,768,256]{2,1,0:T(8,128)(2,1)}, bf16[2,768,256]{2,1,0:T(8,128)(2,1)}, u32[]{:S(2)}, u32[]{:S(2)}) collective-permute-start(bf16[2,768,256]{2,1,0:T(8,128)(2,1)} %add_convert_fusion.10), channel_id=1, source_target_pairs={{0,1},{1,2},{2,3},{3,11},{4,5},{5,6},{6,7},{7,15},{8,0},{9,8},{10,... | collective-permute-start | bytes 2359304 | tf_op jit(solution)/shard_map/ppermute | solution.py:40
  1017.5 70.2 %collective-permute-start.152 = (bf16[256,384]{1,0:T(8,128)(2,1)}, bf16[256,384]{1,0:T(8,128)(2,1)}, u32[]{:S(2)}, u32[]{:S(2)}) collective-permute-start(bf16[256,384]{1,0:T(8,128)(2,1)} %get-tuple-element.208), channel_id=1, source_target_pairs={{0,4},{1,5},{2,6},{3,7},{4,0},{5,1},{6,2},{7,3},{8,12},{9,13},{10,... | collective-permute-start | bytes 589832 | tf_op jit(solution)/shard_map/ppermute | solution.py:40
  1175.2 109.0 %collective-permute-start.110 = (bf16[256,1536]{1,0:T(8,128)(2,1)}, bf16[256,1536]{1,0:T(8,128)(2,1)}, u32[]{:S(2)}, u32[]{:S(2)}) collective-permute-start(bf16[256,1536]{1,0:T(8,128)(2,1)} %fusion.130), channel_id=1, source_target_pairs={{2,16},{3,20},{6,18},{7,22},{10,24},{11,28},{14,26},{15,30},{18,17... | collective-permute-start | bytes 2359304 | tf_op jit(solution)/shard_map/ppermute | solution.py:40
  1177.6 106.5 %collective-permute-start.109 = (bf16[256,1536]{1,0:T(8,128)(2,1)}, bf16[256,1536]{1,0:T(8,128)(2,1)}, u32[]{:S(2)}, u32[]{:S(2)}) collective-permute-start(bf16[256,1536]{1,0:T(8,128)(2,1)} %fusion.130), channel_id=1, source_target_pairs={{0,16},{1,20},{4,18},{5,22},{8,24},{9,28},{12,26},{13,30},{16,17},... | collective-permute-start | bytes 2359304 | tf_op jit(solution)/shard_map/ppermute | solution.py:40
  1184.6 99.5 %collective-permute-start.108 = (bf16[256,1536]{1,0:T(8,128)(2,1)}, bf16[256,1536]{1,0:T(8,128)(2,1)}, u32[]{:S(2)}, u32[]{:S(2)}) collective-permute-start(bf16[256,1536]{1,0:T(8,128)(2,1)} %fusion.133), channel_id=1, source_target_pairs={{2,0},{3,4},{6,2},{7,6},{10,8},{11,12},{14,10},{15,14},{18,1},{19,... | collective-permute-start | bytes 2359304 | tf_op jit(solution)/shard_map/ppermute | solution.py:40
  1185.9 98.2 %collective-permute-start.107 = (bf16[256,1536]{1,0:T(8,128)(2,1)}, bf16[256,1536]{1,0:T(8,128)(2,1)}, u32[]{:S(2)}, u32[]{:S(2)}) collective-permute-start(bf16[256,1536]{1,0:T(8,128)(2,1)} %fusion.133), channel_id=1, source_target_pairs={{0,0},{1,4},{4,2},{5,6},{8,8},{9,12},{12,10},{13,14},{16,1},{17,5}... | collective-permute-start | bytes 2359304 | tf_op jit(solution)/shard_map/ppermute | solution.py:40
  1227.8 60.2 %collective-permute-start.127 = (bf16[384,576]{0,1:T(8,128)(2,1)}, bf16[384,576]{0,1:T(8,128)(2,1)S(1)}, u32[]{:S(2)}, u32[]{:S(2)}) collective-permute-start(bf16[384,576]{0,1:T(8,128)(2,1)} %get-tuple-element.22), channel_id=1, source_target_pairs={{0,16},{1,17},{2,18},{3,19},{4,20},{5,21},{6,22},{7,23},{8,24},{9,... | collective-permute-start | bytes 1327112 | tf_op jit(solution)/shard_map/ppermute | solution.py:40
  (361 other events, 7034.2 us)

commit v2 on v1

v2 whole, which is shorter than its diff:
```python
import functools

import jax
import jax.numpy as jnp
import jax.experimental.pallas as pl
import jax.experimental.pallas.tpu as pltpu
from jax import lax
from jax.sharding import PartitionSpec as P

HD = 96
HP = 128
NEVER = -1e30
epsilon = 1e-05
rope_base = 100000.0
AXES = ("section", "fsdp", "tensor")
bf16 = jnp.bfloat16
f32 = jnp.float32


class Grid:
    def __init__(self, mesh):
        self.calls = 0
        self.X = mesh.shape["section"]
        self.C = 2
        self.Y = mesh.shape["fsdp"] // self.C
        self.Z = mesh.shape["tensor"]
        self.R = self.Y * self.Z
        self.places = [
            (x, y, c, z)
            for x in range(self.X)
            for y in range(self.Y)
            for c in range(self.C)
            for z in range(self.Z)
        ]

    def rank(self, place):
        x, y, c, z = place
        return ((x * self.Y + y) * self.C + c) * self.Z + z

    def send(self, block, route):
        pairs = []
        for place in self.places:
            goal = route(*place)
            if goal is not None:
                pairs.append((self.rank(place), self.rank(goal)))
        return lax.ppermute(block, AXES, pairs)

    def over_x(self, block):
        return self.send(block, lambda x, y, c, z: (1 - x, y, c, z))

    def over_c(self, block):
        return self.send(block, lambda x, y, c, z: (x, y, 1 - c, z))

    def hops(self):
        routes = [lambda x, y, c, z: (x, y, 1 - c, z)]
        for bit in range((self.Y - 1).bit_length()):
            routes.append(lambda x, y, c, z, bit=bit: (x, y ^ (1 << bit), c, z))
        for bit in range((self.Z - 1).bit_length()):
            routes.append(lambda x, y, c, z, bit=bit: (x, y, c, z ^ (1 << bit)))
        return routes

    def place_of(self, p):
        p = p % self.R
        y, k = p // self.Z, p % self.Z
        return (y, k if y % 2 == 0 else self.Z - 1 - k)

    def pos_of(self, y, z):
        return y * self.Z + (z if y % 2 == 0 else self.Z - 1 - z)

    def neighbour(self, way):
        yy, zz = self.dyn_place(self.my_pos() + way)
        return {"fsdp": yy * self.C + lax.axis_index("fsdp") % self.C, "tensor": zz}

    def me(self):
        x = lax.axis_index("section")
        f = lax.axis_index("fsdp")
        z = lax.axis_index("tensor")
        return x, f // self.C, f % self.C, z

    def my_pos(self):
        x, y, c, z = self.me()
        return y * self.Z + jnp.where(y % 2 == 0, z, self.Z - 1 - z)

    def dyn_place(self, p):
        p = (p + 2 * self.R) % self.R
        y, k = p // self.Z, p % self.Z
        return y, jnp.where(y % 2 == 0, k, self.Z - 1 - k)

def params(limit=56):
    return pltpu.CompilerParams(vmem_limit_bytes=limit * 1024 * 1024)


def whole_vmem(count):
    return [pl.BlockSpec(memory_space=pltpu.VMEM)] * count


def cost(micros):
    return pl.CostEstimate(flops=int(micros * 1.0e9), bytes_accessed=1 << 20, transcendentals=0)


def attn_join_kernel(grid, offsets, *refs):
    count = len(offsets)
    pieces = refs[:count]
    qkv_ref, out_ref, held, sems = refs[count:]
    pos = grid.my_pos()
    core = lax.axis_index("fsdp") % grid.C
    tall = held.shape[1]
    halves = grid.Z // 2

    def place(offset):
        yy, zz = grid.dyn_place(pos + offset)
        return yy, zz, zz // halves == core

    def fetch(i):
        return pltpu.make_async_copy(pieces[i], held.at[i], sems.at[i])

    for i, offset in enumerate(offsets):
        _, _, live = place(offset)

        @pl.when(live)
        def _():
            fetch(i).start()

    for i, offset in enumerate(offsets):
        yy, zz, live = place(offset)

        @pl.when(live)
        def _():
            fetch(i).wait()
            j = zz % halves
            rows = pl.ds(pl.multiple_of(yy * tall, tall), tall)
            q_at = pl.multiple_of(j * 2 * HP, HP)
            kv_at = pl.multiple_of(j * HP, HP)
            blank = jnp.zeros((tall, HP - HD), bf16)

            def head(n):
                return jnp.concatenate([held[i, :, n * HD : (n + 1) * HD], blank], 1)

            for h in range(2):
                qkv_ref[rows, pl.ds(q_at + h * HP, HP)] = head(h)
                out_ref[rows, pl.ds(q_at + h * HP, HP)] = head(4 + h)
            qkv_ref[rows, pl.ds(halves * 2 * HP + kv_at, HP)] = head(2)
            qkv_ref[rows, pl.ds(halves * 3 * HP + kv_at, HP)] = head(3)


def attn_join(grid, found, width):
    offsets = [o for o, _ in found]
    blocks = [b for _, b in found]
    halves = grid.Z // 2
    count = len(blocks)
    tall, cols = blocks[0].shape
    return pl.pallas_call(
        functools.partial(attn_join_kernel, grid, offsets),
        out_shape=(
            jax.ShapeDtypeStruct((width, halves * 4 * HP), bf16),
            jax.ShapeDtypeStruct((width, halves * 2 * HP), bf16),
        ),
        in_specs=[pl.BlockSpec(memory_space=pl.ANY)] * count,
        out_specs=whole_vmem(2),
        scratch_shapes=[pltpu.VMEM((count, tall, cols), bf16), pltpu.SemaphoreType.DMA((count,))],
        compiler_params=params(),
        cost_estimate=cost(5),
        name="attn_join",
    )(*blocks)


CHUNKS = 4


def add_came(term, came, n, size, starts, at=None):
    for ref, start, rows in zip(came, starts[0], starts[1]):
        first = start // size

        def added(ref=ref):
            block = ref[...] if at is None else ref[at]
            return term + block.astype(f32)

        if rows == size * CHUNKS:
            term = added()
        else:
            here = (n >= first) & (n < first + rows // size)
            block = ref[...] if at is None else ref[at]
            term = term + jnp.where(here, block.astype(f32), 0.0)
    return term


def came_spec(shape, start, size):
    lead = len(shape) - 2
    first, count = start // size, shape[-2] // size

    def index(n, at):
        return (0,) * lead + (jnp.clip(n - first, 0, count - 1), 0)

    return pl.BlockSpec(shape[:lead] + (size, shape[-1]), index)


def ffn_term_kernel(starts, at_ref, gate_ref, up_ref, down_ref, *refs):
    came, out = refs[:-1], refs[-1]
    n = pl.program_id(0)
    for m, term_ref in enumerate((gate_ref, up_ref, down_ref)):
        term = term_ref[...].astype(f32)
        out[m] = add_came(term, came, n, term.shape[0], starts, m).astype(bf16)


def ffn_term(at, terms, came, tall, units):
    size = tall // CHUNKS
    starts = ([start for _, start in came], [block.shape[1] for block, _ in came])
    return pl.pallas_call(
        functools.partial(ffn_term_kernel, starts),
        grid_spec=pltpu.PrefetchScalarGridSpec(
            num_scalar_prefetch=1,
            grid=(CHUNKS,),
            in_specs=[pl.BlockSpec((size, units), lambda n, at: (at[0] * CHUNKS + n, at[1]))] * 3
            + [came_spec(block.shape, start, size) for block, start in came],
            out_specs=pl.BlockSpec((3, size, units), lambda n, at: (0, n, 0)),
        ),
        out_shape=jax.ShapeDtypeStruct((3, tall, units), bf16),
        compiler_params=params(),
        cost_estimate=cost(3),
        name="ffn_term",
    )(at, *terms, *[block for block, _ in came])


def attn_term_kernel(halves, starts, at_ref, qkv_ref, out_ref, *refs):
    came, out = refs[:-1], refs[-1]
    n = pl.program_id(0)

    @pl.when(at_ref[2] != 0)
    def _():
        j = at_ref[1]
        q_at = pl.multiple_of(j * 2 * HP, HP)
        kv_at = pl.multiple_of(j * HP, HP)

        def part(ref, at):
            return ref[:, pl.ds(at, HP)][:, :HD].astype(f32)

        term = jnp.concatenate(
            [
                part(qkv_ref, q_at),
                part(qkv_ref, q_at + HP),
                part(qkv_ref, halves * 2 * HP + kv_at),
                part(qkv_ref, halves * 3 * HP + kv_at),
                part(out_ref, q_at),
                part(out_ref, q_at + HP),
            ],
            1,
        )
        out[...] = add_came(term, came, n, term.shape[0], starts).astype(bf16)


def attn_term(at, qkv_term, out_term, came, tall, halves):
    size = tall // CHUNKS
    starts = ([start for _, start in came], [block.shape[0] for block, _ in came])
    return pl.pallas_call(
        functools.partial(attn_term_kernel, halves, starts),
        grid_spec=pltpu.PrefetchScalarGridSpec(
            num_scalar_prefetch=1,
            grid=(CHUNKS,),
            in_specs=[
                pl.BlockSpec((size, qkv_term.shape[1]), lambda n, at: (at[0] * CHUNKS + n, 0)),
                pl.BlockSpec((size, out_term.shape[1]), lambda n, at: (at[0] * CHUNKS + n, 0)),
            ]
            + [came_spec(block.shape, start, size) for block, start in came],
            out_specs=pl.BlockSpec((size, 6 * HD), lambda n, at: (n, 0)),
        ),
        out_shape=jax.ShapeDtypeStruct((tall, 6 * HD), bf16),
        compiler_params=params(),
        cost_estimate=cost(3),
        name="attn_term",
    )(at, qkv_term, out_term, *[block for block, _ in came])


def swapped(values):
    lane = lax.broadcasted_iota(jnp.int32, values.shape, 1)
    half = HD // 2
    return jnp.where(lane < half, pltpu.roll(values, HP - half, 1), pltpu.roll(values, half, 1))


MESH = pl.DeviceIdType.MESH
NT = (((1,), (1,)), ((), ()))
PARTS = 2


def dot_nt(a, b):
    return lax.dot_general(a, b, NT, preferred_element_type=f32)


def greet(grid, sides, cycle):
    x, y, c, _ = grid.me()
    sib = {"fsdp": y * grid.C + 1 - c}
    over = {"section": 1 - x}
    others = [sib, over] if sides else []
    if cycle:
        others += [grid.neighbour(1), grid.neighbour(-1)]
    barrier = pltpu.get_barrier_semaphore()
    for other in others:
        pl.semaphore_signal(barrier, inc=1, device_id=other, device_id_type=MESH)
    pl.semaphore_wait(barrier, len(others))
    return sib, over


def remote(src, dst, sems, n, device):
    return pltpu.make_async_remote_copy(
        src_ref=src, dst_ref=dst, send_sem=sems.at[0, n], recv_sem=sems.at[1, n],
        device_id=device, device_id_type=MESH,
    )


def pieces_of(rows):
    size = rows // PARTS
    return [pl.ds(k * size, size) for k in range(PARTS)]


class Plan:
    def __init__(self):
        self.inputs, self.outs, self.stages, self.hooks = [], [], [], []

    def give(self, array):
        self.inputs.append(array)
        return ("in", len(self.inputs) - 1)

    def room(self, shape):
        self.outs.append(jax.ShapeDtypeStruct(shape, bf16))
        return ("out", len(self.outs) - 1)

    def move(self, stage, src, dst, way, offset, owned, cut=None, whole=False):
        while len(self.stages) <= stage:
            self.stages.append([])
        self.stages[stage].append((src, dst, way, offset, owned, cut, whole))

    def count(self):
        return sum(len(stage) for stage in self.stages)

    def settle(self, results):
        for hook in self.hooks:
            hook(lambda handle: self.inputs[handle[1]] if handle[0] == "in" else results[handle[1]])


class Background:
    def __init__(self, grid, plan, ins, outs, sems):
        self.stages, self.now, n = [], -1, 0
        pos = grid.my_pos()
        core = lax.axis_index("fsdp") % grid.C
        refs = {"in": ins, "out": outs}

        def live(owned, offset):
            if not owned:
                return None
            return grid.dyn_place(pos + offset)[1] // (grid.Z // 2) == core

        for stage in plan.stages:
            made = []
            for src, dst, way, offset, owned, cut, whole in stage:
                src_ref, dst_ref = refs[src[0]][src[1]], refs[dst[0]][dst[1]]
                if cut is not None:
                    src_ref = src_ref.at[cut]
                    if not whole:
                        dst_ref = dst_ref.at[cut]
                copy = remote(src_ref, dst_ref, sems, n, grid.neighbour(way))
                made.append((copy, live(owned, offset), live(owned, offset - way)))
                n += 1
            self.stages.append(made)

    @staticmethod
    def do(condition, action):
        if condition is None:
            action()
        else:
            pl.when(condition)(action)

    def advance(self):
        if 0 <= self.now < len(self.stages):
            for copy, _, come in self.stages[self.now]:
                self.do(come, copy.wait_recv)
        self.now += 1
        if self.now < len(self.stages):
            for copy, go, _ in self.stages[self.now]:
                self.do(go, copy.start)

    def finish(self):
        while self.now < len(self.stages):
            self.advance()
        for stage in self.stages:
            for copy, go, _ in stage:
                self.do(go, copy.wait_send)


class Gather:
    def __init__(self, grid, block, owned=False):
        self.grid, self.owned, self.shape = grid, owned, block.shape
        self.up = self.down = block
        self.k, self.total = 0, grid.R // 2
        self.found = [(0, block)]

    def left(self):
        return self.total - self.k

    def add(self, plan, stage, hops=None):
        hops = self.left() if hops is None else min(hops, self.left())
        if hops == 0:
            return
        one = self.up is self.down
        up = plan.give(self.up)
        down = up if one else plan.give(self.down)
        new = []
        for n in range(hops):
            self.k += 1
            k = self.k
            if k < self.total:
                to_up, to_down = plan.room(self.shape), plan.room(self.shape)
                plan.move(stage + n, up, to_up, 1, 1 - k, self.owned)
                plan.move(stage + n, down, to_down, -1, k - 1, self.owned)
                new += [(-k, to_up), (k, to_down)]
                up, down = to_up, to_down
            else:
                both = plan.room(self.shape)
                first, last = halves_cut(self.shape)
                plan.move(stage + n, up, both, 1, 1 - k, self.owned, first)
                plan.move(stage + n, down, both, -1, k - 1, self.owned, last)
                new += [(-k, both)]
                up = down = both

        def hook(get):
            self.up, self.down = get(up), get(down)
            self.found += [(offset, get(handle)) for offset, handle in new]

        plan.hooks.append(hook)


def halves_cut(shape):
    rows = shape[-2] // 2
    lead = (slice(None),) * (len(shape) - 2)
    return lead + (pl.ds(0, rows),), lead + (pl.ds(rows, rows),)


class Scatter:
    def __init__(self, grid, piece, shape, owned=False):
        self.grid, self.piece, self.shape, self.owned = grid, piece, shape, owned
        self.k = grid.R // 2
        self.up, self.down = [], []

    def left(self):
        return self.k

    def add(self, plan, stage):
        if self.k == 0:
            return
        k = self.k
        self.k -= 1
        rows = self.shape[-2] // 2
        if k == self.grid.R // 2:
            first, last = halves_cut(self.shape)
            half = self.shape[:-2] + (rows, self.shape[-1])
            block = plan.give(self.piece(k, []))
            to_up, to_down = plan.room(half), plan.room(half)
            plan.move(stage, block, to_up, 1, k, self.owned, first, True)
            plan.move(stage, block, to_down, -1, -k, self.owned, last, True)
            starts = (0, rows)
        else:
            up, down = plan.give(self.piece(k, self.up)), plan.give(self.piece(-k, self.down))
            to_up, to_down = plan.room(self.shape), plan.room(self.shape)
            plan.move(stage, up, to_up, 1, k, self.owned)
            plan.move(stage, down, to_down, -1, -k, self.owned)
            starts = (0, 0)

        def hook(get):
            self.up, self.down = [(get(to_up), starts[0])], [(get(to_down), starts[1])]

        plan.hooks.append(hook)

    def result(self):
        return self.piece(0, self.up + self.down)


def fused_call(grid, kernel, name, plan, inputs, in_specs, outs, out_specs, scratch, micros):
    plan = Plan() if plan is None else plan
    a, b, c, d = len(inputs), len(plan.inputs), len(outs), len(plan.outs)
    moves = plan.count()

    def whole(*refs):
        fg_in, bg_in = refs[:a], refs[a : a + b]
        fg_out, bg_out = refs[a + b : a + b + c], refs[a + b + c : a + b + c + d]
        rest = refs[a + b + c + d :]
        background = Background(grid, plan, bg_in, bg_out, rest[-1]) if moves else Background(grid, plan, (), (), None)
        kernel(background, bool(moves), *fg_in, *fg_out, *(rest[:-1] if moves else rest))

    number = grid.calls
    grid.calls += 1
    results = pl.pallas_call(
        whole,
        out_shape=tuple(outs) + tuple(plan.outs),
        in_specs=list(in_specs) + [ANY] * b,
        out_specs=tuple(out_specs) + (ANY,) * d,
        scratch_shapes=list(scratch) + ([pltpu.SemaphoreType.DMA((2, moves))] if moves else []),
        compiler_params=remote_params(number),
        cost_estimate=cost(micros),
        name=name,
    )(*inputs, *plan.inputs)
    plan.settle(results[c:])
    return results[:c]


def ring_call(grid, plan):
    if plan.count() == 0:
        return

    def kernel(background, cycle):
        greet(grid, False, True)
        background.advance()
        background.finish()

    fused_call(grid, kernel, "cycle", plan, (), (), (), (), (), 30 * len(plan.stages))


class Spread:
    sems = pltpu.SemaphoreType.DMA((2, 1 + 2 * PARTS))

    def __init__(self, rows_ref, sems, sib, over):
        cuts = pieces_of(rows_ref.shape[1])
        self.near = remote(rows_ref.at[0], rows_ref.at[1], sems, 0, sib)
        self.far = [
            remote(rows_ref.at[0, at], rows_ref.at[2, at], sems, 1 + k, over)
            for k, at in enumerate(cuts)
        ]
        self.relay = [
            remote(rows_ref.at[2, at], rows_ref.at[3, at], sems, 1 + PARTS + k, sib)
            for k, at in enumerate(cuts)
        ]

    def start(self):
        for copy in self.far:
            copy.start()
        self.near.start()

    def pass_on(self, k):
        self.far[k].wait_recv()
        self.relay[k].start()

    def end(self):
        self.near.wait_send()
        for copy in self.far + self.relay:
            copy.wait_send()


class Collect:
    sems = pltpu.SemaphoreType.DMA((2, 1 + 2 * PARTS))

    @staticmethod
    def scratch(rows, width):
        return [pltpu.VMEM((6, rows, width), bf16), Collect.sems]

    def __init__(self, hold, sems, sib, over):
        self.hold = hold
        self.cuts = pieces_of(hold.shape[1])
        self.near = remote(hold.at[0], hold.at[2], sems, 0, sib)
        self.side = [
            remote(hold.at[1, at], hold.at[3, at], sems, 1 + k, sib)
            for k, at in enumerate(self.cuts)
        ]
        self.over = [
            remote(hold.at[4, at], hold.at[5, at], sems, 1 + PARTS + k, over)
            for k, at in enumerate(self.cuts)
        ]

    def give_near(self, part):
        self.hold[0] = part.astype(bf16)
        self.near.start()

    def give_side(self, k, part):
        self.hold[1, self.cuts[k]] = part.astype(bf16)
        self.side[k].start()

    def give_over(self, k, part):
        self.side[k].wait_recv()
        self.hold[4, self.cuts[k]] = (part + self.hold[3, self.cuts[k]].astype(f32)).astype(bf16)
        self.over[k].start()

    def finish(self, part):
        self.near.wait_recv()
        part = part + self.hold[2].astype(f32)
        for copy in self.over:
            copy.wait_recv()
        return part + self.hold[5].astype(f32)

    def end(self):
        self.near.wait_send()
        for copy in self.side + self.over:
            copy.wait_send()


def normed_rows(values, gain_row):
    return values * lax.rsqrt(jnp.mean(values * values, -1, keepdims=True) + epsilon) * gain_row


def norm_back(values, gain_row, upstream):
    scale = lax.rsqrt(jnp.mean(values * values, -1, keepdims=True) + epsilon)
    unit = values * scale
    moved = upstream * gain_row
    grad = scale * (moved - unit * jnp.mean(moved * unit, -1, keepdims=True))
    gains = upstream * unit
    return grad, jnp.sum(gains.reshape(-1, 8, gains.shape[-1]), 0)


def remote_params(number, limit=58):
    return pltpu.CompilerParams(
        vmem_limit_bytes=limit * 1024 * 1024, collective_id=number, has_side_effects=True
    )


def shaped(*pairs):
    return tuple(jax.ShapeDtypeStruct(shape, dtype) for shape, dtype in pairs)


ANY = pl.BlockSpec(memory_space=pl.ANY)
VMEM = pl.BlockSpec(memory_space=pltpu.VMEM)


def qkv_kernel(
    grid, halves, background, cycle, h_ref, gain_ref, w_ref, cos_ref, sin_ref, all_ref, q_ref, k_ref, v_ref,
    rows_ref, sems, out_sem,
):
    rows = h_ref.shape[0]
    sib, over = greet(grid, True, cycle)
    background.advance()
    rows_ref[0] = normed_rows(h_ref[...].astype(f32), gain_ref[...]).astype(bf16)
    spread = Spread(rows_ref, sems, sib, over)
    spread.start()

    def work(slot, start, size):
        cosine, sine_part = cos_ref[slot, start : start + size], sin_ref[slot, start : start + size]
        at = slice(start, start + size)
        made = jnp.dot(rows_ref[slot, at], w_ref[...], preferred_element_type=f32)
        for h in range(3 * halves):
            one = made[:, h * HP : (h + 1) * HP]
            turned = (one * cosine + swapped(one) * sine_part).astype(bf16)
            if h < 2 * halves:
                q_ref[h, slot, at] = turned
            else:
                k_ref[h - 2 * halves, slot, at] = turned
        for h in range(halves):
            v_ref[h, slot, at] = made[:, (3 * halves + h) * HP : (3 * halves + h + 1) * HP].astype(bf16)

    work(0, 0, rows)
    spread.near.wait_recv()
    work(1, 0, rows)
    size = rows // PARTS
    for k in range(PARTS):
        spread.pass_on(k)
        work(2, k * size, size)
        spread.relay[k].wait_recv()
        work(3, k * size, size)
    out = pltpu.make_async_copy(rows_ref, all_ref, out_sem)
    out.start()
    out.wait()
    spread.end()
    background.finish()


def qkv_call(grid, plan, hidden, gain_row, weight, cosine, sine_part):
    rows, width = hidden.shape
    halves = grid.Z // 2
    shape = (halves, 4, rows, HP)
    return fused_call(
        grid, functools.partial(qkv_kernel, grid, halves), "qkv", plan,
        (hidden, gain_row, weight, cosine, sine_part), [VMEM] * 5,
        shaped(
            ((4, rows, width), bf16), ((2 * halves,) + shape[1:], bf16), (shape, bf16), (shape, bf16)
        ),
        (ANY, VMEM, VMEM, VMEM),
        [pltpu.VMEM((4, rows, width), bf16), Spread.sems, pltpu.SemaphoreType.DMA],
        28,
    )


def place_id(grid):
    x, _, c, _ = grid.me()
    return [2 * cc + xx for xx, cc in ((x, c), (x, 1 - c), (1 - x, c), (1 - x, 1 - c))]


def attend_kernel(
    grid, heads, background, cycle, h_ref, q_ref, k_ref, v_ref, tokk_ref, tokq_ref, from_ref, wo_ref,
    mid_ref, mixed_ref, lse_ref, top, total, acc, part, hold, sems,
):
    rows = h_ref.shape[0]
    scale = HD ** (-0.5)
    ids = place_id(grid)
    sib, over = greet(grid, True, cycle)
    background.advance()
    collect = Collect(hold, sems, sib, over)

    def attend(i):
        tok_q, begin = tokq_ref[i], from_ref[i]

        def block(j, first):
            tok_k = tokk_ref[j]
            allowed = (tok_k <= tok_q) & (tok_k >= begin)
            for h in range(heads):
                scores = dot_nt(q_ref[h, i], k_ref[h // 2, j])
                scores = jnp.where(allowed, scores * scale, NEVER)
                peak = jnp.max(scores, 1, keepdims=True)
                if not first:
                    before = top[h]
                    peak = jnp.maximum(peak, before)
                raised = jnp.exp(scores - peak)
                summed = jnp.sum(raised, 1, keepdims=True)
                got = jnp.dot(raised.astype(bf16), v_ref[h // 2, j], preferred_element_type=f32)
                if first:
                    total[h] = summed
                    acc[h] = got
                else:
                    shrink = jnp.exp(before - peak)
                    total[h] = total[h] * shrink + summed
                    acc[h] = acc[h] * shrink + got
                top[h] = peak

        block(i, True)
        for j in range(4):
            if j != i:
                pl.when((ids[j] < ids[i]) & (ids[j] >= ids[i] - 2))(functools.partial(block, j, False))
        for h in range(heads):
            mixed_ref[i, :, h * HP : (h + 1) * HP] = (acc[h] / total[h]).astype(bf16)
            log_total = top[h] + jnp.log(total[h])
            lse_ref[i, h] = jnp.transpose(jnp.broadcast_to(log_total, (rows, HP)))[:8]
        part[...] = dot_nt(mixed_ref[i], wo_ref[...])

    cuts = pieces_of(rows)
    attend(3)
    for k in range(PARTS):
        collect.give_side(k, part[cuts[k]])
    attend(2)
    for k in range(PARTS):
        collect.give_over(k, part[cuts[k]])
    attend(1)
    collect.give_near(part[...])
    attend(0)
    mid_ref[...] = collect.finish(part[...] + h_ref[...].astype(f32))
    collect.end()
    background.finish()


def attend_call(grid, plan, hidden, query, keys, values, facts, weight_o):
    rows, width = hidden.shape
    heads = query.shape[0]
    return fused_call(
        grid, functools.partial(attend_kernel, grid, heads), "attend", plan,
        (
            hidden, query, keys, values, facts["tok"][:, None, :], facts["tok"][:, :, None],
            facts["from"][:, :, None], weight_o,
        ),
        [VMEM] * 8,
        shaped(((rows, width), f32), ((4, rows, heads * HP), bf16), ((4, heads, 8, rows), f32)),
        (VMEM,) * 3,
        [
            pltpu.VMEM((heads, rows, 1), f32),
            pltpu.VMEM((heads, rows, 1), f32),
            pltpu.VMEM((heads, rows, HP), f32),
            pltpu.VMEM((rows, width), f32),
        ]
        + Collect.scratch(rows, width),
        32,
    )


def fetch_ffn(grid, offsets, pieces, held, sems):
    pos = grid.my_pos()
    _, tall, units = pieces[0].shape
    copies = []
    for i, offset in enumerate(offsets):
        yy, zz = grid.dyn_place(pos + offset)
        rows = pl.ds(pl.multiple_of(yy * tall, tall), tall)
        cols = pl.ds(pl.multiple_of(zz * units, units), units)
        copy = pltpu.make_async_copy(pieces[i], held.at[:, rows, cols], sems.at[i])
        copy.start()
        copies.append(copy)
    return copies


STEP = 512


def ffn_kernel(grid, offsets, background, cycle, mid_ref, gain_ref, *refs):
    count = len(offsets)
    pieces = refs[:count]
    (
        out_ref, all_ref, gate_ref, up_ref, hid_ref,
        held, w_sems, rows_ref, s_sems, part, hold, c_sems, out_sem,
    ) = refs[count:]
    rows, width = mid_ref.shape
    hidden = gate_ref.shape[2]
    fetched = fetch_ffn(grid, offsets, pieces, held, w_sems)
    sib, over = greet(grid, True, cycle)
    background.advance()
    rows_ref[0] = normed_rows(mid_ref[...], gain_ref[...]).astype(bf16)
    spread = Spread(rows_ref, s_sems, sib, over)
    collect = Collect(hold, c_sems, sib, over)
    spread.start()
    for copy in fetched:
        copy.wait()

    def work(slot, start, size):
        at = pl.ds(start, size)

        def tile(n, carry):
            cols = pl.ds(pl.multiple_of(n * STEP, STEP), STEP)
            some = rows_ref[slot, at]
            gate = jnp.dot(some, held[0, :, cols], preferred_element_type=f32)
            up = jnp.dot(some, held[1, :, cols], preferred_element_type=f32)
            gate_ref[slot, at, cols] = gate.astype(bf16)
            up_ref[slot, at, cols] = up.astype(bf16)
            hid_ref[slot, at, cols] = (gate * jax.nn.sigmoid(gate) * up).astype(bf16)
            return carry

        lax.fori_loop(0, hidden // STEP, tile, 0)

        def tile_down(n, carry):
            cols = pl.ds(pl.multiple_of(n * STEP, STEP), STEP)
            part[at, cols] = dot_nt(hid_ref[slot, at], held[2, cols])
            return carry

        lax.fori_loop(0, width // STEP, tile_down, 0)

    work(0, 0, rows)
    out_ref[...] = mid_ref[...] + part[...]
    spread.near.wait_recv()
    work(1, 0, rows)
    collect.give_near(part[...])
    cuts = pieces_of(rows)
    size = rows // PARTS
    for k in range(PARTS):
        spread.pass_on(k)
        spread.relay[k].wait_recv()
        work(3, k * size, size)
        collect.give_side(k, part[cuts[k]])
        work(2, k * size, size)
        collect.give_over(k, part[cuts[k]])
        background.advance()
    out = pltpu.make_async_copy(rows_ref, all_ref, out_sem)
    out.start()
    out_ref[...] = collect.finish(out_ref[...])
    out.wait()
    spread.end()
    collect.end()
    background.finish()


def ffn_call(grid, plan, middle, gain_row, found):
    rows, width = middle.shape
    offsets, blocks = [o for o, _ in found], [b for _, b in found]
    hidden = grid.Z * blocks[0].shape[2]
    return fused_call(
        grid, functools.partial(ffn_kernel, grid, offsets), "ffn", plan,
        (middle, gain_row, *blocks), [VMEM] * 2 + [ANY] * len(blocks),
        shaped(((rows, width), f32), ((4, rows, width), bf16), *[((4, rows, hidden), bf16)] * 3),
        (VMEM, ANY, VMEM, VMEM, VMEM),
        [
            pltpu.VMEM((3, width, hidden), bf16),
            pltpu.SemaphoreType.DMA((len(blocks),)),
            pltpu.VMEM((4, rows, width), bf16),
            Spread.sems,
            pltpu.VMEM((rows, width), f32),
        ]
        + Collect.scratch(rows, width)
        + [pltpu.SemaphoreType.DMA],
        44,
    )


def ffn_back_kernel(grid, offsets, background, cycle, g_ref, mid_ref, gain_ref, gate_ref, up_ref, *refs):
    count = len(offsets)
    pieces = refs[:count]
    (
        out_ref, gains_ref, all_ref, dgate_ref, dup_ref,
        held, w_sems, rows_ref, s_sems, part, own, hold, c_sems, out_sem,
    ) = refs[count:]
    rows, width = mid_ref.shape
    hidden = gate_ref.shape[2]
    fetched = fetch_ffn(grid, offsets, pieces, held, w_sems)
    sib, over = greet(grid, True, cycle)
    background.advance()
    rows_ref[0] = g_ref[...]
    spread = Spread(rows_ref, s_sems, sib, over)
    collect = Collect(hold, c_sems, sib, over)
    spread.start()
    for copy in fetched:
        copy.wait()

    def work(slot, start, size):
        at = pl.ds(start, size)

        def tile(n, carry):
            cols = pl.ds(pl.multiple_of(n * STEP, STEP), STEP)
            grad = jnp.dot(rows_ref[slot, at], held[2, :, cols], preferred_element_type=f32)
            gate = gate_ref[slot, at, cols].astype(f32)
            up = up_ref[slot, at, cols].astype(f32)
            sig = jax.nn.sigmoid(gate)
            dgate_ref[slot, at, cols] = (grad * up * sig * (1.0 + gate * (1.0 - sig))).astype(bf16)
            dup_ref[slot, at, cols] = (grad * gate * sig).astype(bf16)
            return carry

        lax.fori_loop(0, hidden // STEP, tile, 0)

        def tile_back(n, carry):
            cols = pl.ds(pl.multiple_of(n * STEP, STEP), STEP)
            part[at, cols] = dot_nt(dgate_ref[slot, at], held[0, cols]) + dot_nt(
                dup_ref[slot, at], held[1, cols]
            )
            return carry

        lax.fori_loop(0, width // STEP, tile_back, 0)

    work(0, 0, rows)
    own[...] = part[...]
    spread.near.wait_recv()
    work(1, 0, rows)
    collect.give_near(part[...])
    cuts = pieces_of(rows)
    size = rows // PARTS
    for k in range(PARTS):
        spread.pass_on(k)
        spread.relay[k].wait_recv()
        work(3, k * size, size)
        collect.give_side(k, part[cuts[k]])
        work(2, k * size, size)
        collect.give_over(k, part[cuts[k]])
    out = pltpu.make_async_copy(rows_ref, all_ref, out_sem)
    out.start()
    second = collect.finish(own[...])
    grad, gains = norm_back(mid_ref[...], gain_ref[...], second)
    out_ref[...] = g_ref[...].astype(f32) + grad
    gains_ref[...] = gains
    out.wait()
    spread.end()
    collect.end()
    background.finish()


def ffn_back_call(grid, plan, grad_out, middle, gain_row, gate, up, found):
    rows, width = middle.shape
    offsets, blocks = [o for o, _ in found], [b for _, b in found]
    hidden = gate.shape[2]
    return fused_call(
        grid, functools.partial(ffn_back_kernel, grid, offsets), "ffn_back", plan,
        (grad_out, middle, gain_row, gate, up, *blocks), [VMEM] * 5 + [ANY] * len(blocks),
        shaped(
            ((rows, width), f32), ((8, width), f32), ((4, rows, width), bf16),
            *[((4, rows, hidden), bf16)] * 2,
        ),
        (VMEM, VMEM, ANY, VMEM, VMEM),
        [
            pltpu.VMEM((3, width, hidden), bf16),
            pltpu.SemaphoreType.DMA((len(blocks),)),
            pltpu.VMEM((4, rows, width), bf16),
            Spread.sems,
            pltpu.VMEM((rows, width), f32),
            pltpu.VMEM((rows, width), f32),
        ]
        + Collect.scratch(rows, width)
        + [pltpu.SemaphoreType.DMA],
        44,
    )


def mixed_back_kernel(grid, background, cycle, g_ref, w_ref, all_ref, gm_ref, rows_ref, sems, out_sem):
    rows = g_ref.shape[0]
    sib, over = greet(grid, True, cycle)
    background.advance()
    rows_ref[0] = g_ref[...].astype(bf16)
    spread = Spread(rows_ref, sems, sib, over)
    spread.start()

    def work(slot, start, size):
        at = slice(start, start + size)
        made = jnp.dot(rows_ref[slot, at], w_ref[...], preferred_element_type=f32).astype(bf16)
        for h in range(gm_ref.shape[0]):
            gm_ref[h, slot, at] = made[:, h * HP : (h + 1) * HP]

    work(0, 0, rows)
    spread.near.wait_recv()
    work(1, 0, rows)
    size = rows // PARTS
    for k in range(PARTS):
        spread.pass_on(k)
        work(2, k * size, size)
        spread.relay[k].wait_recv()
        work(3, k * size, size)
    out = pltpu.make_async_copy(rows_ref, all_ref, out_sem)
    out.start()
    out.wait()
    spread.end()
    background.finish()


def mixed_back_call(grid, plan, grad_middle, weight_o):
    rows, width = grad_middle.shape
    heads = weight_o.shape[1] // HP
    return fused_call(
        grid, functools.partial(mixed_back_kernel, grid), "mixed_back", plan,
        (grad_middle, weight_o), [VMEM] * 2,
        shaped(((4, rows, width), bf16), ((heads, 4, rows, HP), bf16)), (ANY, VMEM),
        [pltpu.VMEM((4, rows, width), bf16), Spread.sems, pltpu.SemaphoreType.DMA],
        27,
    )


def normed_back_kernel(
    grid, background, cycle, dqkv_ref, w_ref, h_ref, gain_ref, gm_ref, out_ref, gains_ref, part, hold, sems
):
    rows = h_ref.shape[0]
    sib, over = greet(grid, True, cycle)
    background.advance()
    collect = Collect(hold, sems, sib, over)
    cuts = pieces_of(rows)

    def work(slot):
        part[...] = dot_nt(dqkv_ref[slot], w_ref[...])

    work(3)
    for k in range(PARTS):
        collect.give_side(k, part[cuts[k]])
    work(2)
    for k in range(PARTS):
        collect.give_over(k, part[cuts[k]])
    work(1)
    collect.give_near(part[...])
    work(0)
    grad, gains = norm_back(
        h_ref[...].astype(f32), gain_ref[...], collect.finish(part[...])
    )
    out_ref[...] = (gm_ref[...] + grad).astype(bf16)
    gains_ref[...] = gains
    collect.end()
    background.finish()


def normed_back_call(grid, plan, grad_qkv, weight, hidden, gain_row, grad_middle):
    rows, width = hidden.shape
    return fused_call(
        grid, functools.partial(normed_back_kernel, grid), "normed_back", plan,
        (grad_qkv, weight, hidden, gain_row, grad_middle), [VMEM] * 5,
        shaped(((rows, width), bf16), ((8, width), f32)), (VMEM, VMEM),
        [pltpu.VMEM((rows, width), f32)] + Collect.scratch(rows, width),
        27,
    )


def attend_back_kernel(
    grid, heads, background, cycle, q_ref, k_ref, v_ref, g_ref, m_ref, l_ref, tokc_ref, tokr_ref, from_ref,
    cos_ref, sin_ref, out_ref, key_sum, value_sum, query_sum, delta,
):
    rows = q_ref.shape[2]
    pairs = heads // 2
    scale = HD ** (-0.5)
    ids = place_id(grid)
    if cycle:
        greet(grid, False, True)
        background.advance()
    key_sum[...] = jnp.zeros_like(key_sum)
    value_sum[...] = jnp.zeros_like(value_sum)
    query_sum[...] = jnp.zeros_like(query_sum)

    def back(summed, at):
        one = summed * scale
        return (one * cos_ref[at] - swapped(one) * sin_ref[at]).astype(bf16)

    for i in range(4):
        for h in range(heads):
            product = g_ref[h, i].astype(f32) * m_ref[i, :, h * HP : (h + 1) * HP].astype(f32)
            summed = jnp.sum(product, 1, keepdims=True)
            delta[h] = jnp.transpose(jnp.broadcast_to(summed, (rows, HP)))[:8]

        def block(j):
            allowed = (tokc_ref[j] <= tokr_ref[i]) & (tokc_ref[j] >= from_ref[i])
            for h in range(heads):
                query, upstream = q_ref[h, i], g_ref[h, i]
                key, value = k_ref[h // 2, j], v_ref[h // 2, j]
                scores = jnp.where(allowed, dot_nt(key, query) * scale, NEVER)
                probs = jnp.exp(scores - l_ref[i, h, 0:1])
                value_sum[h // 2, j] += jnp.dot(
                    probs.astype(bf16), upstream, preferred_element_type=f32
                )
                grad_scores = (probs * (dot_nt(value, upstream) - delta[h, 0:1])).astype(bf16)
                key_sum[h // 2, j] += jnp.dot(grad_scores, query, preferred_element_type=f32)
                query_sum[h, i] += lax.dot_general(
                    grad_scores, key, (((0,), (0,)), ((), ())), preferred_element_type=f32
                )

        for j in range(4):
            if i == j:
                block(j)
            else:
                pl.when((ids[j] < ids[i]) & (ids[j] >= ids[i] - 2))(functools.partial(block, j))

    for i in range(4):
        for h in range(heads):
            out_ref[i, :, h * HP : (h + 1) * HP] = back(query_sum[h, i], i)
        for h in range(pairs):
            at = heads + h
            out_ref[i, :, at * HP : (at + 1) * HP] = back(key_sum[h, i], i)
            at = heads + pairs + h
            out_ref[i, :, at * HP : (at + 1) * HP] = value_sum[h, i].astype(bf16)
    if cycle:
        background.finish()


def attend_back_call(grid, plan, query, keys, values, upstream, mixed, lse, facts):
    heads, _, rows, _ = query.shape
    pairs = heads // 2
    return fused_call(
        grid, functools.partial(attend_back_kernel, grid, heads), "attend_back", plan,
        (
            query, keys, values, upstream, mixed, lse, facts["tok"][:, :, None],
            facts["tok"][:, None, :], facts["from"][:, None, :], facts["cos"], facts["sin"],
        ),
        [VMEM] * 11,
        shaped(((4, rows, 2 * heads * HP), bf16)), (VMEM,),
        [
            pltpu.VMEM((pairs, 4, rows, HP), f32),
            pltpu.VMEM((pairs, 4, rows, HP), f32),
            pltpu.VMEM((heads, 4, rows, HP), f32),
            pltpu.VMEM((heads, 8, rows), f32),
        ],
        19,
    )[0]


def left_t_times(a, b):
    return lax.dot_general(a, b, (((0,), (0,)), ((), ())), preferred_element_type=f32)


def turning(doc_row):
    places = jnp.arange(doc_row.shape[-1], dtype=jnp.int32)
    begins = jnp.concatenate([jnp.ones((1,), dtype=bool), doc_row[1:] != doc_row[:-1]], -1)
    starts = lax.cummax(jnp.where(begins, places, 0), axis=0)
    positions = (places - starts).astype(f32)
    ladder = jnp.arange(HD // 2, dtype=f32)
    frequency = rope_base ** (-2.0 * ladder / HD)
    angles = positions[..., None] * frequency
    cosine, sine_part = jnp.cos(angles), jnp.sin(angles)
    blank = jnp.zeros((doc_row.shape[0], HP - HD), f32)
    return (
        starts,
        jnp.concatenate([cosine, cosine, blank], -1),
        jnp.concatenate([-sine_part, sine_part, blank], -1),
    )


def layer_forward(grid, hidden_in, attn, ffn, next_attn, gain_pair, facts):
    weight_qkv, weight_o = attn
    plan = Plan()
    ffn.add(plan, 0, 1)
    whole, query, keys, values = qkv_call(
        grid, plan, hidden_in, gain_pair[0:1], weight_qkv, facts["cos"], facts["sin"]
    )
    plan = Plan()
    ffn.add(plan, 0, 1)
    middle, mixed, lse = attend_call(grid, plan, hidden_in, query, keys, values, facts, weight_o)
    plan = Plan()
    ffn.add(plan, 0)
    ring_call(grid, plan)
    plan = Plan()
    if next_attn is not None:
        next_attn.add(plan, 0)
    result, whole2, gate, up, hidden = ffn_call(grid, plan, middle, gain_pair[1:2], ffn.found)
    kept = (hidden_in, whole, query, keys, values, lse, mixed, middle, whole2, gate, up, hidden)
    return result.astype(bf16), kept


def flat(blocks):
    return blocks.reshape(-1, blocks.shape[-1])


def layer_backward(grid, grad_out, kept, attn, ffn, gain_pair, facts, running, sum_ffn, sum_attn):
    weight_qkv, weight_o = attn
    hidden_in, whole, query, keys, values, lse, mixed, middle, whole2, gate, up, hidden = kept

    def plan():
        made = Plan()
        for ring in running:
            ring.add(made, 0)
        return made

    grad_middle, gain_two, grad_whole, grad_gate, grad_up = ffn_back_call(
        grid, plan(), grad_out, middle, gain_pair[1:2], gate, up, ffn.found
    )
    down_term = left_t_times(flat(grad_whole), flat(hidden)).astype(bf16)
    gate_term = left_t_times(flat(whole2), flat(grad_gate)).astype(bf16)
    up_term = left_t_times(flat(whole2), flat(grad_up)).astype(bf16)
    running.append(sum_ffn(gate_term, up_term, down_term))
    grad_attn, grad_mixed = mixed_back_call(grid, plan(), grad_middle, weight_o)
    grad_qkv = attend_back_call(grid, plan(), query, keys, values, grad_mixed, mixed, lse, facts)
    grad_input, gain_one = normed_back_call(
        grid, plan(), grad_qkv, weight_qkv, hidden_in, gain_pair[0:1], grad_middle
    )
    out_term = left_t_times(flat(grad_attn), flat(mixed)).astype(bf16)
    qkv_term = left_t_times(flat(whole), flat(grad_qkv)).astype(bf16)
    running.append(sum_attn(qkv_term, out_term))
    gains = jnp.stack([jnp.sum(gain_one, 0), jnp.sum(gain_two, 0)])
    return grad_input, gains


def body(grid, inputs, doc_ids, cotangent, wq, wk, wv, wo, wg, wu, wd, gains):
    X, Y, C, Z = grid.X, grid.Y, grid.C, grid.Z
    x, y, c, z = grid.me()
    pos = grid.my_pos()
    micro, rows, width = inputs.shape
    depth = wq.shape[1]
    at_zero = x == 0

    def enter(block):
        def route(m):
            def go(x, y, c, z):
                if z % 2 != x:
                    return None
                return (x, y, z // 2, m * C + c)

            return go

        first, last = grid.send(block[0], route(0)), grid.send(block[1], route(1))
        return jnp.where(z // C == 0, first, last)

    def leave(block, section):
        def route(m):
            def go(x, y, c, z):
                if z // C != m:
                    return None
                return (section, y, z % C, 2 * c + x)

            return go

        return jnp.stack([grid.send(block, route(m)) for m in range(micro)])

    rows_in = enter(inputs)
    rows_cot = enter(cotangent)
    docs = grid.over_c(doc_ids)
    docs = jnp.where(c == z % C, doc_ids, docs)[:, 0]
    doc_row = lax.dynamic_index_in_dim(docs, z // C, 0, keepdims=False)
    length = doc_row.shape[0]
    starts, cosine, sine_part = turning(doc_row)
    ids = place_id(grid)

    def in_my_order(rows_of):
        return jnp.stack(
            [lax.dynamic_slice_in_dim(rows_of, ids[n] * rows, rows, 0) for n in range(4)]
        )

    facts = {
        "tok": in_my_order(jnp.arange(length, dtype=jnp.int32)),
        "from": in_my_order(starts),
        "cos": in_my_order(cosine),
        "sin": in_my_order(sine_part),
    }

    mine = (y * C + c) * Z + z
    table = lax.dynamic_update_slice(
        jnp.zeros((Y * C * Z,) + gains.shape[1:], bf16), gains, (mine, 0, 0)
    )
    for hop in grid.hops():
        table = table + grid.send(table, hop)
    gain_own = table.transpose(1, 0, 2).reshape(2, width)
    gain_other = grid.over_x(gain_own)
    gain_all = [
        jnp.where(at_zero, gain_own, gain_other).astype(f32),
        jnp.where(at_zero, gain_other, gain_own).astype(f32),
    ]

    def cut(block, index, count, axis):
        size = block.shape[axis] // count
        return lax.dynamic_slice_in_dim(block, index * size, size, axis)

    def pack_attn(side):
        qkv = jnp.concatenate([cut(wq[0], side, 2, 1), cut(wk[0], side, 2, 1), cut(wv[0], side, 2, 1)], 1)
        return jnp.concatenate([qkv, cut(wo[0], side, 2, 0).T], 1)

    def pack_ffn(side):
        return jnp.stack([cut(wg[0], side, 2, 1), cut(wu[0], side, 2, 1), cut(wd[0], side, 2, 0).T])

    def both_layers(pack):
        kept = pack(x)
        came = grid.over_x(pack(1 - x))
        return jnp.where(at_zero, kept, came), jnp.where(at_zero, came, kept)

    def sibling_join(mine, other, axis):
        came = grid.over_c(other)
        return jnp.where(
            c == 0,
            jnp.concatenate([mine, came], axis),
            jnp.concatenate([came, mine], axis),
        )

    halves = Z // 2
    tall = C * depth
    owner = lambda z: z // halves
    units = wg.shape[2] // 4
    attn_parts = both_layers(pack_attn)
    ffn_parts = both_layers(pack_ffn)

    def whole_attn(part):
        came = grid.send(part, lambda x, y, c, z: (x, y, 1 - c, z) if owner(z) != c else None)
        both = jnp.where(
            c == 0, jnp.concatenate([part, came], 0), jnp.concatenate([came, part], 0)
        )
        return Gather(grid, both, True)

    def whole_ffn(part):
        block = sibling_join(cut(part, c, 2, 2), cut(part, 1 - c, 2, 2), 1)
        return Gather(grid, block)

    attn = [whole_attn(attn_parts[s]) for s in range(2)]
    ffn = [whole_ffn(ffn_parts[s]) for s in range(2)]
    plan = Plan()
    attn[0].add(plan, 0)
    ring_call(grid, plan)

    hidden = rows_in
    kept, outs, joined = [], [], []
    for s in range(2):
        joined.append(attn_join(grid, attn[s].found, width))
        hidden, keep = layer_forward(
            grid, hidden, joined[s], ffn[s], attn[s + 1] if s == 0 else None, gain_all[s], facts
        )
        outs.append(leave(hidden, s))
        kept.append(keep)
    produced = jnp.where(at_zero, outs[0], outs[1])

    def spot(offset):
        yy, zz = grid.dyn_place(pos + offset)
        live = (zz // halves == c).astype(jnp.int32)
        return yy, zz, live

    def sum_ffn(*terms):
        def piece(offset, came):
            yy, zz, _ = spot(offset)
            at = jnp.stack([yy, zz]).astype(jnp.int32)
            return ffn_term(at, terms, came, tall, units)

        return Scatter(grid, piece, (3, tall, units))

    def sum_attn(qkv_term, out_term):
        def piece(offset, came):
            yy, zz, live = spot(offset)
            at = jnp.stack([yy, zz % halves, live]).astype(jnp.int32)
            return attn_term(at, qkv_term, out_term, came, tall, halves)

        return Scatter(grid, piece, (tall, 6 * HD), True)

    upstream = rows_cot
    grads_in, gain_terms, running = [None] * 2, [None] * 2, []
    for s in (1, 0):
        upstream, gain_terms[s] = layer_backward(
            grid, upstream, kept[s], joined[s], ffn[s], gain_all[s], facts, running, sum_ffn, sum_attn
        )
        grads_in[s] = leave(upstream, s)
    while any(ring.left() for ring in running):
        plan = Plan()
        for ring in running:
            ring.add(plan, 0)
        ring_call(grid, plan)
    ffn_sum = [running[2].result(), running[0].result()]
    attn_sum = [running[3].result(), running[1].result()]
    grads_in = jnp.where(at_zero, grads_in[0], grads_in[1]).astype(f32)

    def back_attn(total):
        mine = cut(total, c, 2, 0)
        came = grid.send(
            cut(total, 1 - c, 2, 0), lambda x, y, c, z: (x, y, 1 - c, z) if owner(z) == c else None
        )
        return jnp.where(z // halves == c, mine, came)

    def back_ffn(total):
        return sibling_join(cut(total, c, 2, 1), cut(total, 1 - c, 2, 1), 2)

    def home(terms):
        kept_part = jnp.where(at_zero, terms[0], terms[1])
        came = grid.over_x(jnp.where(at_zero, terms[1], terms[0]))
        return jnp.where(at_zero, kept_part, came).astype(f32), jnp.where(at_zero, came, kept_part).astype(f32)

    attn_back, ffn_back = [None] * 2, [None] * 2
    for s in (1, 0):
        ffn_back[s] = back_ffn(ffn_sum[s])
        attn_back[s] = back_attn(attn_sum[s])
    ffn_home = jnp.concatenate(home(ffn_back), 2)
    q_cols = wq.shape[2] // 2
    k_cols = wk.shape[2] // 2
    left, right = home(attn_back)
    cuts = [0, q_cols, q_cols + k_cols, q_cols + 2 * k_cols, q_cols * 2 + 2 * k_cols]
    query_home, key_home, value_home, out_home = [
        jnp.concatenate([left[:, a:b], right[:, a:b]], 1) for a, b in zip(cuts[:-1], cuts[1:])
    ]
    out_home = out_home.T

    gain_kept = jnp.where(at_zero, gain_terms[0], gain_terms[1])
    gain_sum = gain_kept + grid.over_x(jnp.where(at_zero, gain_terms[1], gain_terms[0]))
    for hop in grid.hops():
        gain_sum = gain_sum + grid.send(gain_sum, hop)
    share = width // (Y * C * Z)
    gain_share = lax.dynamic_slice_in_dim(gain_sum, mine * share, share, 1)[None]
    return (
        produced[None],
        grads_in[None],
        query_home[None],
        key_home[None],
        value_home[None],
        out_home[None],
        ffn_home[0][None],
        ffn_home[1][None],
        ffn_home[2].T[None],
        gain_share,
    )


def solution(mesh):
    grid = Grid(mesh)

    def run(*arguments):
        grid.calls = 0
        return body(grid, *arguments)

    return jax.shard_map(
        run,
        mesh=mesh,
        in_specs=(
            P(None, ("fsdp", "tensor"), None),
            P(None, "fsdp", None),
            P(None, ("fsdp", "tensor"), None),
            P("section", "fsdp", "tensor"),
            P("section", "fsdp", "tensor"),
            P("section", "fsdp", "tensor"),
            P("section", "tensor", "fsdp"),
            P("section", "fsdp", "tensor"),
            P("section", "fsdp", "tensor"),
            P("section", "tensor", "fsdp"),
            P("section", None, ("fsdp", "tensor")),
        ),
        out_specs=(
            P("section", None, ("fsdp", "tensor"), None),
            P("section", None, ("fsdp", "tensor"), None),
            P("section", "fsdp", "tensor"),
            P("section", "fsdp", "tensor"),
            P("section", "fsdp", "tensor"),
            P("section", "tensor", "fsdp"),
            P("section", "fsdp", "tensor"),
            P("section", "fsdp", "tensor"),
            P("section", "tensor", "fsdp"),
            P("section", None, ("fsdp", "tensor")),
        ),
        check_vma=False,
    )
```

time: 1310 us -> 1280 us (0.977)
  Pallas kernels: 0 us -> 957 us
  local copies, waits for them, and re-layouts: 259 us -> 33 us
  waiting for transfers between devices: 292 us -> 90.7 us
  matrix products: 212 us -> 53.6 us
  blocking collectives: 140 us -> 0 us
  starting transfers between devices: 211 us -> 73.4 us
  other arithmetic: 172 us -> 48.5 us
    pallas_call x0 -> x55, Pallas kernels: none -> 957 us  [the longest x21 801 us: fused_call(): pl.pallas_call(whole, out_shape=tuple(outs) + tuple(plan.outs), in_specs=...]
    ppermute x162 -> x35, waiting for transfers between devices: 292 us -> 90.7 us  [send(): return lax.ppermute(block, AXES, pairs)]
    dot_general x52 -> x0, matrix products: 169 us -> none  [the longest x20 41.9 us: matmul(): return jnp.dot(a, b, preferred_element_type=f32)]
    ppermute x162 -> x35, starting transfers between devices: 211 us -> 73.4 us  [send(): return lax.ppermute(block, AXES, pairs)]
    all_gather x2 -> x0, blocking collectives: 84.3 us -> none  [the longest x1 74.1 us: body(): gain_all = lax.all_gather(gains[0], AXES, axis=0, tiled=False)]
    convert_element_type x51 -> x4, other arithmetic: 88.4 us -> 4.94 us  [the longest x2 4.79 us: layer_forward(): return (result.astype(bf16), kept)]
    dynamic_update_slice x46 -> x1, local copies, waits for them, and re-layouts: 77.2 us -> 0.01 us  [body(): lax.dynamic_update_slice(jnp.zeros((Y * C * Z,) + gains.shape[1:], bf16),...]
    unnamed x1 -> x0, blocking collectives: 55.5 us -> none
  transfers between devices with their start and end apart: 162 -> 35, of which waited for: 40 -> 9; matrix products, arithmetic and copies ran while one was open for 49% -> 9% of each run, Pallas kernels for 0% -> 64%
where the time goes in v2:
time: 1280 us; the launch traced here: 1260 us
  Pallas kernels  957 us (75%)
  waiting for transfers between devices  90.7 us (7%)
  starting transfers between devices  73.4 us (6%)
  matrix products  53.6 us (4%)
  other arithmetic  48.5 us (4%)
  local copies, waits for them, and re-layouts  33 us (3%)
    pallas_call x21, Pallas kernels, fused_call(): pl.pallas_call(whole, out_shape=tuple(outs) + tuple(plan.outs), in_specs=...  801 us
    ppermute x35, waiting for transfers between devices, send(): return lax.ppermute(block, AXES, pairs)  90.7 us
    ppermute x35, starting transfers between devices, send(): return lax.ppermute(block, AXES, pairs)  73.4 us
    pallas_call x16, Pallas kernels, attn_term(): pl.pallas_call(functools.partial(attn_term_kernel, halves, starts), grid_...  72.8 us
    pallas_call x16, Pallas kernels, ffn_term(): pl.pallas_call(functools.partial(ffn_term_kernel, starts), grid_spec=pltp...  72.2 us
    dot_general x10, matrix products, left_t_times(): lax.dot_general(a, b, (((0,), (0,)), ((), ())), preferred_element_type=f32)  53.6 us
  transfers between devices with their start and end apart: 35, of which 9 were waited for; matrix products, arithmetic and copies ran while one was open for 9% of the time, Pallas kernels for 64%

profile of v2, /device:TPU:1, one launch (start us, length us, event | category | flops | bytes accessed | tf_op | source)
XLA Modules:
  0.0 1258.5 jit_solution(12502505934070116408)
XLA Ops:
  37.3 10.1 collective-permute-done.4
  53.5 7.1 collective-permute-start.18
  68.2 8.9 collective-permute-done.18
  77.1 12.2 collective-permute-done.19
  91.5 42.5 %cycle.7 = (bf16[768,576]{1,0:T(8,128)(2,1)}, bf16[768,576]{1,0:T(8,128)(2,1)}, bf16[768,576]{1,0:T(8,128)(2,1)}, bf16[768,576]{1,0:T(8,128)(2,1)}, bf16[768,576...) custom-call(bf16[768,576]{1,0:T(8,128)(2,1)} %maximum_select_fusion.6.refs_0_), custom_call_target="tpu_custom_call" | custom-call | flops 120000004096 | bytes 1048576 | tf_op jit(solution)/shard_map/cycle/pallas_call | solution.py:489
  145.9 40.8 %qkv.2 = (bf16[4,256,1536]{2,1,0:T(8,128)(2,1)}, bf16[4,4,256,128]{3,2,1,0:T(8,128)(2,1)}, bf16[2,4,256,128]{3,2,1,0:T(8,128)(2,1)}, bf16[2,4,256,128]{3,2,1,0:T...) custom-call(bf16[256,1536]{1,0:T(8,128)(2,1)} %broadcast_select_fusion.7.refs_0_.refs_2_, ...), custom_call_target="tpu_custom_call" | custom-call | flops 28000000000 | bytes 1048576 | tf_op jit(solution)/shard_map/qkv/pallas_call | solution.py:489
  186.7 33.8 %attend.2 = (f32[256,1536]{1,0:T(8,128)}, bf16[4,256,512]{2,1,0:T(8,128)(2,1)}, f32[4,4,8,256]{3,2,1,0:T(8,128)}, bf16[3,768,256]{2,1,0:T(8,128)(2,1)}, bf16[3,768,256]{2,1,0:T(8,128)(2,1)}) custom-call(bf16[256,1536]{1,0:T(8,128)(2,1)} %broadcast_select_fusion.7.refs_0_.refs_2_, bf16[4,4,256,128]{3,2,1,0:T(8,128)(2,1)} %get-tuple-element.126.refs_1_.refs_0_, ...), custom_call_target="tpu_custom_call" | custom-call | flops 32000000000 | bytes 1048576 | tf_op jit(solution)/shard_map/attend/pallas_call | solution.py:489
  220.5 41.0 %cycle.8 = (bf16[3,768,256]{2,1,0:T(8,128)(2,1)}, bf16[3,768,256]{2,1,0:T(8,128)(2,1)}, bf16[3,768,256]{2,1,0:T(8,128)(2,1)}) custom-call(bf16[3,768,256]{2,1,0:T(8,128)(2,1)} %get-tuple-element.133.refs_0_.refs_5_.refs_8_, bf16[3,768,256]{2,1,0:T(8,128)(2,1)} %get-tuple-element.134.refs_1_.refs_6_.refs_9_), custom_call_target="tpu_custom_call" | custom-call | flops 60000002048 | bytes 1048576 | tf_op jit(solution)/shard_map/cycle/pallas_call | solution.py:489
  261.5 59.5 %ffn.2 = (f32[256,1536]{1,0:T(8,128)}, bf16[4,256,1536]{2,1,0:T(8,128)(2,1)}, bf16[4,256,1024]{2,1,0:T(8,128)(2,1)}, bf16[4,256,1024]{2,1,0:T(8,128)(2,1)}, bf16...) custom-call(f32[256,1536]{1,0:T(8,128)} %get-tuple-element.132.refs_, ...), custom_call_target="tpu_custom_call" | custom-call | flops 44000002048 | bytes 1048576 | tf_op jit(solution)/shard_map/ffn/pallas_call | solution.py:489
  331.6 31.8 %qkv.3 = (bf16[4,256,1536]{2,1,0:T(8,128)(2,1)}, bf16[4,4,256,128]{3,2,1,0:T(8,128)(2,1)}, bf16[2,4,256,128]{3,2,1,0:T(8,128)(2,1)}, bf16[2,4,256,128]{3,2,1,0:T...) custom-call(bf16[256,1536]{1,0:T(8,128)(2,1)} %convert_element_type.85.refs_0_.refs_2_, ...), custom_call_target="tpu_custom_call" | custom-call | flops 28000000000 | bytes 1048576 | tf_op jit(solution)/shard_map/qkv/pallas_call | solution.py:489
  363.4 32.7 %attend.3 = (f32[256,1536]{1,0:T(8,128)}, bf16[4,256,512]{2,1,0:T(8,128)(2,1)}, f32[4,4,8,256]{3,2,1,0:T(8,128)}, bf16[3,768,256]{2,1,0:T(8,128)(2,1)}, bf16[3,768,256]{2,1,0:T(8,128)(2,1)}) custom-call(bf16[256,1536]{1,0:T(8,128)(2,1)} %convert_element_type.85.refs_0_.refs_2_, bf16[4,4,256,128]{3,2,1,0:T(8,128)(2,1)} %get-tuple-element.147.refs_1_.refs_0_, ...), custom_call_target="tpu_custom_call" | custom-call | flops 32000000000 | bytes 1048576 | tf_op jit(solution)/shard_map/attend/pallas_call | solution.py:489
  396.1 40.7 %cycle.9 = (bf16[3,768,256]{2,1,0:T(8,128)(2,1)}, bf16[3,768,256]{2,1,0:T(8,128)(2,1)}, bf16[3,768,256]{2,1,0:T(8,128)(2,1)}) custom-call(bf16[3,768,256]{2,1,0:T(8,128)(2,1)} %get-tuple-element.154.refs_0_.refs_5_.refs_8_, bf16[3,768,256]{2,1,0:T(8,128)(2,1)} %get-tuple-element.155.refs_1_.refs_6_.refs_9_), custom_call_target="tpu_custom_call" | custom-call | flops 60000002048 | bytes 1048576 | tf_op jit(solution)/shard_map/cycle/pallas_call | solution.py:489
  436.8 45.0 %ffn.3 = (f32[256,1536]{1,0:T(8,128)}, bf16[4,256,1536]{2,1,0:T(8,128)(2,1)}, bf16[4,256,1024]{2,1,0:T(8,128)(2,1)}, bf16[4,256,1024]{2,1,0:T(8,128)(2,1)}, bf16[4,256,1024]{2,1,0:T(8,128)(2,1)}) custom-call(f32[256,1536]{1,0:T(8,128)} %get-tuple-element.153.refs_0_.refs_1_, f32[1,1536]{1,0:T(1,128)} %get-tuple-element.304.refs_1_.refs_2_, ...), custom_call_target="tpu_custom_call" | custom-call | flops 44000002048 | bytes 1048576 | tf_op jit(solution)/shard_map/ffn/pallas_call | solution.py:489
  490.4 79.9 %ffn_back.2 = (f32[256,1536]{1,0:T(8,128)}, f32[8,1536]{1,0:T(8,128)}, bf16[4,256,1536]{2,1,0:T(8,128)(2,1)}, bf16[4,256,1024]{2,1,0:T(8,128)(2,1)}, bf16[4,256,1024]{2,1,0:T(8,128)(2,1)}) custom-call(bf16[256,1536]{1,0:T(8,128)(2,1)} %broadcast_select_fusion.6.refs_0_, f32[256,1536]{1,0:T(8,128)} %get-tuple-element.153.refs_0_.refs_1_, ...), custom_call_target="tpu_custom_call" | custom-call | flops 44000002048 | bytes 1048576 | tf_op jit(solution)/shard_map/ffn_back/pallas_call | solution.py:489
  570.3 6.6 bitcast_convert_fusion.6.up_ref
  591.3 26.0 %mixed_back.2 = (bf16[4,256,1536]{2,1,0:T(8,128)(2,1)}, bf16[4,4,256,128]{3,2,1,0:T(8,128)(2,1)}, bf16[3,384,256]{2,1,0:T(8,128)(2,1)}, bf16[3,384,256]{2,1,0:T(8,128)(2,1)}) custom-call(f32[256,1536]{1,0:T(8,128)} %get-tuple-element.162.refs_0_.refs_4_, bf16[1536,512]{1,0:T(8,128)(2,1)} %get-tuple-element.150.refs_7_.refs_1_, ...), custom_call_target="tpu_custom_call" | custom-call | flops 27000000512 | bytes 1048576 | tf_op jit(solution)/shard_map/mixed_back/pallas_call | solution.py:489
  631.2 32.1 %attend_back.2 = (bf16[4,256,1024]{2,1,0:T(8,128)(2,1)}, bf16[3,768,256]{2,1,0:T(8,128)(2,1)}, bf16[3,768,256]{2,1,0:T(8,128)(2,1)}) custom-call(bf16[4,4,256,128]{3,2,1,0:T(8,128)(2,1)} %get-tuple-element.147.refs_1_.refs_0_, bf16[2,4,256,128]{3,2,1,0:T(8,128)(2,1)} %get-tuple-element.148.refs_2_.refs_1_, ...), custom_call_target="tpu_custom_call" | custom-call | flops 19000000512 | bytes 1048576 | tf_op jit(solution)/shard_map/attend_back/pallas_call | solution.py:489
  663.3 6.7 bitcast_convert_fusion.4.qkv_ref
  679.0 31.9 %normed_back.2 = (bf16[256,1536]{1,0:T(8,128)(2,1)}, f32[8,1536]{1,0:T(8,128)}, bf16[3,768,256]{2,1,0:T(8,128)(2,1)}, bf16[3,768,256]{2,1,0:T(8,128)(2,1)}) custom-call(bf16[4,256,1024]{2,1,0:T(8,128)(2,1)} %get-tuple-element.173.refs_0_, bf16[1536,1024]{1,0:T(8,128)(2,1)} %get-tuple-element.146.refs_2_.refs_1_, ...), custom_call_target="tpu_custom_call" | custom-call | flops 27000000512 | bytes 1048576 | tf_op jit(solution)/shard_map/normed_back/pallas_call | solution.py:489
  724.3 45.2 %ffn_back.3 = (f32[256,1536]{1,0:T(8,128)}, f32[8,1536]{1,0:T(8,128)}, bf16[4,256,1536]{2,1,0:T(8,128)(2,1)}, bf16[4,256,1024]{2,1,0:T(8,128)(2,1)}, bf16[4,256,...) custom-call(bf16[256,1536]{1,0:T(8,128)(2,1)} %get-tuple-element.176, ...), custom_call_target="tpu_custom_call" | custom-call | flops 44000002048 | bytes 1048576 | tf_op jit(solution)/shard_map/ffn_back/pallas_call | solution.py:489
  769.6 6.6 bitcast_convert_fusion.2.up_ref
  799.5 34.8 %mixed_back.3 = (bf16[4,256,1536]{2,1,0:T(8,128)(2,1)}, bf16[4,4,256,128]{3,2,1,0:T(8,128)(2,1)}, bf16[768,576]{1,0:T(8,128)(2,1)}, bf16[768,576]{1,0:T(8,128)(2...) custom-call(f32[256,1536]{1,0:T(8,128)} %get-tuple-element.183.refs_0_.refs_4_, ...), custom_call_target="tpu_custom_call" | custom-call | flops 27000000512 | bytes 1048576 | tf_op jit(solution)/shard_map/mixed_back/pallas_call | solution.py:489
  852.5 46.9 %attend_back.3 = (bf16[4,256,1024]{2,1,0:T(8,128)(2,1)}, bf16[768,576]{1,0:T(8,128)(2,1)}, bf16[768,576]{1,0:T(8,128)(2,1)}, bf16[3,768,256]{2,1,0:T(8,128)(2,1)}, bf16[3,768,256]{2,1,0:T(8,128)(2,1)}) custom-call(bf16[4,4,256,128]{3,2,1,0:T(8,128)(2,1)} %get-tuple-element.126.refs_1_.refs_0_, bf16[2,4,256,128]{3,2,1,0:T(8,128)(2,1)} %get-tuple-element.127.refs_2_.refs_1_, ...), custom_call_target="tpu_custom_call" | custom-call | flops 19000000512 | bytes 1048576 | tf_op jit(solution)/shard_map/attend_back/pallas_call | solution.py:489
  917.3 40.0 %normed_back.3 = (bf16[256,1536]{1,0:T(8,128)(2,1)}, f32[8,1536]{1,0:T(8,128)}, bf16[768,576]{1,0:T(8,128)(2,1)}, bf16[768,576]{1,0:T(8,128)(2,1)}, bf16[3,768,2...) custom-call(bf16[4,256,1024]{2,1,0:T(8,128)(2,1)} %get-tuple-element.198.refs_0_, ...), custom_call_target="tpu_custom_call" | custom-call | flops 27000000512 | bytes 1048576 | tf_op jit(solution)/shard_map/normed_back/pallas_call | solution.py:489
  991.1 49.9 %cycle.10 = (bf16[3,768,256]{2,1,0:T(8,128)(2,1)}, bf16[3,768,256]{2,1,0:T(8,128)(2,1)}, bf16[384,576]{1,0:T(8,128)(2,1)}, bf16[384,576]{1,0:T(8,128)(2,1)}) custom-call(bf16[3,768,256]{2,1,0:T(8,128)(2,1)} %ffn_term.28.refs_0_, bf16[3,768,256]{2,1,0:T(8,128)(2,1)} %ffn_term.29.refs_1_, bf16[768,576]{1,0:T(8,128)(2,1)} %attn_term.23.refs_2_), custom_call_target="tpu_custom_call" | custom-call | flops 30000001024 | bytes 1048576 | tf_op jit(solution)/shard_map/cycle/pallas_call | solution.py:489
  1050.4 19.6 %cycle.11 = (bf16[768,576]{1,0:T(8,128)(2,1)}, bf16[768,576]{1,0:T(8,128)(2,1)}) custom-call(bf16[768,576]{1,0:T(8,128)(2,1)} %attn_term.24.refs_0_, bf16[768,576]{1,0:T(8,128)(2,1)} %attn_term.25.refs_1_), custom_call_target="tpu_custom_call" | custom-call | flops 30000001024 | bytes 1048576 | tf_op jit(solution)/shard_map/cycle/pallas_call | solution.py:489
  1079.2 18.3 %cycle.12 = (bf16[768,576]{1,0:T(8,128)(2,1)}, bf16[768,576]{1,0:T(8,128)(2,1)}) custom-call(bf16[768,576]{1,0:T(8,128)(2,1)} %attn_term.26.refs_0_, bf16[768,576]{1,0:T(8,128)(2,1)} %attn_term.27.refs_1_), custom_call_target="tpu_custom_call" | custom-call | flops 30000001024 | bytes 1048576 | tf_op jit(solution)/shard_map/cycle/pallas_call | solution.py:489
  1106.4 8.3 cycle.13
  1115.4 14.6 %collective-permute-start.31 = (f32[2,1536]{1,0:T(2,128)S(1)}, f32[2,1536]{1,0:T(2,128)S(1)}, u32[]{:S(2)}, u32[]{:S(2)}) collective-permute-start(f32[2,1536]{1,0:T(2,128)S(1)} %select_add_fusion), channel_id=1, source_target_pairs={{0,4},{1,5},{2,6},{3,7},{4,0},{5,1},{6,2},{7,3},{8,12},{9,13},{10,... | collective-permute-start | bytes 36872 | tf_op jit(solution)/shard_map/ppermute | solution.py:46
  1182.5 8.1 collective-permute-done.14
  1193.8 37.6 %collective-permute-done.20 = bf16[256,1536]{1,0:T(8,128)(2,1)S(1)} collective-permute-done((bf16[256,1536]{1,0:T(8,128)(2,1)}, bf16[256,1536]{1,0:T(8,128)(2,1)S(1)}, u32[]{:S(2)}, u32[]{:S(2)}) %collective-permute-start.20) | collective-permute-done | bytes 786464 | tf_op jit(solution)/shard_map/ppermute | solution.py:46
  1243.3 8.6 collective-permute-done.29
  (322 shorter events, 328.4 us)
Async XLA Ops:
  4.5 130.9 %collective-permute-start.10 = (bf16[3,384,512]{2,1,0:T(8,128)(2,1)}, bf16[3,384,512]{2,1,0:T(8,128)(2,1)}, u32[]{:S(2)}, u32[]{:S(2)}) collective-permute-start(bf16[3,384,512]{2,1,0:T(8,128)(2,1)} %pad_maximum_fusion.1), channel_id=1, source_target_pairs={{0,16},{1,17},{2,18},{3,19},{4,20},{5,21},{6,22},{7,23},{8,24},{9,... | collective-permute-start | bytes 3538952 | tf_op jit(solution)/shard_map/ppermute | solution.py:46
  6.5 23.9 %collective-permute-start.9 = (s32[2,1,1024]{2,1,0:T(1,128)}, s32[2,1,1024]{2,1,0:T(1,128)}, u32[]{:S(2)}, u32[]{:S(2)}) collective-permute-start(s32[2,1,1024]{2,1,0:T(1,128)} %param.12), channel_id=1, source_target_pairs={{0,4},{1,5},{2,6},{3,7},{4,0},{5,1},{6,2},{7,3},{8,12},{9,13},{10,... | collective-permute-start | bytes 24584 | tf_op jit(solution)/shard_map/ppermute | solution.py:46
  11.1 50.7 %collective-permute-start.7 = (bf16[384,576]{1,0:T(8,128)(2,1)}, bf16[384,576]{1,0:T(8,128)(2,1)}, u32[]{:S(2)}, u32[]{:S(2)}) collective-permute-start(bf16[384,576]{1,0:T(8,128)(2,1)} %pad_maximum_fusion.5), channel_id=1, source_target_pairs={{0,16},{1,17},{2,18},{3,19},{4,20},{5,21},{6,22},{7,23},{8,24},{9,... | collective-permute-start | bytes 1327112 | tf_op jit(solution)/shard_map/ppermute | solution.py:46
  11.2 16.4 %collective-permute-start.2 = (bf16[16,2,96]{2,1,0:T(2,128)(2,1)S(1)}, bf16[16,2,96]{2,1,0:T(2,128)(2,1)S(1)}, u32[]{:S(2)}, u32[]{:S(2)}) collective-permute-start(bf16[16,2,96]{2,1,0:T(2,128)(2,1)S(1)} %constant_dynamic-update-slice_fusion.1), channel_id=1, source_target_pairs={{0,4},{1,5},{2,6},{3,7},{4,0},{5,1},{6,2},{7,3},{8,12},{9,13},{10,... | collective-permute-start | bytes 18440 | tf_op jit(solution)/shard_map/ppermute | solution.py:46
  12.5 52.0 %collective-permute-start = (bf16[256,1536]{1,0:T(8,128)(2,1)}, bf16[256,1536]{1,0:T(8,128)(2,1)S(1)}, u32[]{:S(2)}, u32[]{:S(2)}) collective-permute-start(bf16[256,1536]{1,0:T(8,128)(2,1)} %get-tuple-element.261), channel_id=1, source_target_pairs={{0,0},{2,4},{4,1},{6,5},{8,8},{10,12},{12,9},{14,13},{17,16},{19,2... | collective-permute-start | bytes 2359304 | tf_op jit(solution)/shard_map/ppermute | solution.py:46
  27.6 38.3 %collective-permute-start.1 = (bf16[256,1536]{1,0:T(8,128)(2,1)S(1)}, bf16[256,1536]{1,0:T(8,128)(2,1)S(1)}, u32[]{:S(2)}, u32[]{:S(2)}) collective-permute-start(bf16[256,1536]{1,0:T(8,128)(2,1)S(1)} %copy-done.14), channel_id=1, source_target_pairs={{0,2},{2,6},{4,3},{6,7},{8,10},{10,14},{12,11},{14,15},{17,18},{19... | collective-permute-start | bytes 2359304 | tf_op jit(solution)/shard_map/ppermute | solution.py:46
  30.4 6.0 collective-permute-start.3
  36.4 11.0 collective-permute-start.4
  53.5 23.6 %collective-permute-start.18 = (bf16[256,1536]{1,0:T(8,128)(2,1)}, bf16[256,1536]{1,0:T(8,128)(2,1)S(1)}, u32[]{:S(2)}, u32[]{:S(2)}) collective-permute-start(bf16[256,1536]{1,0:T(8,128)(2,1)} %get-tuple-element.259), channel_id=1, source_target_pairs={{0,0},{2,4},{4,1},{6,5},{8,8},{10,12},{12,9},{14,13},{17,16},{19,2... | collective-permute-start | bytes 2359304 | tf_op jit(solution)/shard_map/ppermute | solution.py:46
  61.9 27.4 %collective-permute-start.19 = (bf16[256,1536]{1,0:T(8,128)(2,1)}, bf16[256,1536]{1,0:T(8,128)(2,1)S(1)}, u32[]{:S(2)}, u32[]{:S(2)}) collective-permute-start(bf16[256,1536]{1,0:T(8,128)(2,1)} %get-tuple-element.258), channel_id=1, source_target_pairs={{0,2},{2,6},{4,3},{6,7},{8,10},{10,14},{12,11},{14,15},{17,18},{19... | collective-permute-start | bytes 2359304 | tf_op jit(solution)/shard_map/ppermute | solution.py:46
  64.5 25.7 %collective-permute-start.8 = (bf16[384,576]{1,0:T(8,128)(2,1)S(1)}, bf16[384,576]{1,0:T(8,128)(2,1)S(1)}, u32[]{:S(2)}, u32[]{:S(2)}) collective-permute-start(bf16[384,576]{1,0:T(8,128)(2,1)S(1)} %get-tuple-element.273), channel_id=1, source_target_pairs={{2,6},{3,7},{4,0},{5,1},{10,14},{11,15},{12,8},{13,9},{18,22},{19,... | collective-permute-start | bytes 1327112 | tf_op jit(solution)/shard_map/ppermute | solution.py:46
  65.9 68.2 %collective-permute-start.12 = (bf16[384,576]{1,0:T(8,128)(2,1)S(1)}, bf16[384,576]{1,0:T(8,128)(2,1)S(1)}, u32[]{:S(2)}, u32[]{:S(2)}) collective-permute-start(bf16[384,576]{1,0:T(8,128)(2,1)S(1)} %get-tuple-element.272), channel_id=1, source_target_pairs={{2,6},{3,7},{4,0},{5,1},{10,14},{11,15},{12,8},{13,9},{18,22},{19,... | collective-permute-start | bytes 1327112 | tf_op jit(solution)/shard_map/ppermute | solution.py:46
  137.0 7.6 collective-permute-start.11
  143.7 185.4 %collective-permute-start.15 = (bf16[3,384,256]{2,1,0:T(8,128)(2,1)}, bf16[3,384,256]{2,1,0:T(8,128)(2,1)}, u32[]{:S(2)}, u32[]{:S(2)}) collective-permute-start(bf16[3,384,256]{2,1,0:T(8,128)(2,1)} %get-tuple-element.269), channel_id=1, source_target_pairs={{0,4},{1,5},{2,6},{3,7},{4,0},{5,1},{6,2},{7,3},{8,12},{9,13},{10,... | collective-permute-start | bytes 1769480 | tf_op jit(solution)/shard_map/ppermute | solution.py:46
  484.2 689.3 %collective-permute-start.16 = (bf16[256,1536]{1,0:T(8,128)(2,1)}, bf16[256,1536]{1,0:T(8,128)(2,1)}, u32[]{:S(2)}, u32[]{:S(2)}) collective-permute-start(bf16[256,1536]{1,0:T(8,128)(2,1)} %convert_element_type.87), channel_id=1, source_target_pairs={{0,16},{1,20},{4,18},{5,22},{8,24},{9,28},{12,26},{13,30},{16,17},... | collective-permute-start | bytes 2359304 | tf_op jit(solution)/shard_map/ppermute | solution.py:46
  488.8 686.1 %collective-permute-start.17 = (bf16[256,1536]{1,0:T(8,128)(2,1)}, bf16[256,1536]{1,0:T(8,128)(2,1)}, u32[]{:S(2)}, u32[]{:S(2)}) collective-permute-start(bf16[256,1536]{1,0:T(8,128)(2,1)} %convert_element_type.87), channel_id=1, source_target_pairs={{2,16},{3,20},{6,18},{7,22},{10,24},{11,28},{14,26},{15,30},{18,17... | collective-permute-start | bytes 2359304 | tf_op jit(solution)/shard_map/ppermute | solution.py:46
  959.5 155.1 %collective-permute-start.30 = (f32[2,1536]{1,0:T(2,128)}, f32[2,1536]{1,0:T(2,128)}, u32[]{:S(2)}, u32[]{:S(2)}) collective-permute-start(f32[2,1536]{1,0:T(2,128)} %broadcast_select_fusion.12), channel_id=1, source_target_pairs={{0,16},{1,17},{2,18},{3,19},{4,20},{5,21},{6,22},{7,23},{8,24},{9,... | collective-permute-start | bytes 36872 | tf_op jit(solution)/shard_map/ppermute | solution.py:46
  985.4 167.5 %collective-permute-start.25 = (bf16[384,576]{1,0:T(8,128)(2,1)}, bf16[384,576]{1,0:T(8,128)(2,1)}, u32[]{:S(2)}, u32[]{:S(2)}) collective-permute-start(bf16[384,576]{1,0:T(8,128)(2,1)} %constant_dynamic-slice_fusion.7), channel_id=1, source_target_pairs={{0,4},{1,5},{6,2},{7,3},{8,12},{9,13},{14,10},{15,11},{16,20},{17,... | collective-permute-start | bytes 1327112 | tf_op jit(solution)/shard_map/ppermute | solution.py:46
  1115.4 19.2 %collective-permute-start.31 = (f32[2,1536]{1,0:T(2,128)S(1)}, f32[2,1536]{1,0:T(2,128)S(1)}, u32[]{:S(2)}, u32[]{:S(2)}) collective-permute-start(f32[2,1536]{1,0:T(2,128)S(1)} %select_add_fusion), channel_id=1, source_target_pairs={{0,4},{1,5},{2,6},{3,7},{4,0},{5,1},{6,2},{7,3},{8,12},{9,13},{10,... | collective-permute-start | bytes 36872 | tf_op jit(solution)/shard_map/ppermute | solution.py:46
  1135.3 3.8 collective-permute-start.32
  1137.7 28.1 %collective-permute-start.24 = (bf16[384,576]{1,0:T(8,128)(2,1)S(1)}, bf16[384,576]{1,0:T(8,128)(2,1)S(1)}, u32[]{:S(2)}, u32[]{:S(2)}) collective-permute-start(bf16[384,576]{1,0:T(8,128)(2,1)S(1)} %constant_dynamic-slice_fusion.8), channel_id=1, source_target_pairs={{0,4},{1,5},{6,2},{7,3},{8,12},{9,13},{14,10},{15,11},{16,20},{17,... | collective-permute-start | bytes 1327112 | tf_op jit(solution)/shard_map/ppermute | solution.py:46
  1139.2 6.1 collective-permute-start.33
  1145.2 3.6 collective-permute-start.34
  1148.8 29.7 %collective-permute-start.13 = (bf16[256,1536]{1,0:T(8,128)(2,1)}, bf16[256,1536]{1,0:T(8,128)(2,1)}, u32[]{:S(2)}, u32[]{:S(2)}) collective-permute-start(bf16[256,1536]{1,0:T(8,128)(2,1)} %convert_element_type.85.refs_0_.refs_2_), channel_id=1, source_target_pairs={{0,0},{1,4},{4,2},{5,6},{8,8},{9,12},{12,10},{13,14},{16,1},{17,5}... | collective-permute-start | bytes 2359304 | tf_op jit(solution)/shard_map/ppermute | solution.py:46
  1152.9 13.0 %collective-permute-start.27 = (bf16[3,384,256]{2,1,0:T(8,128)(2,1)S(1)}, bf16[3,384,256]{2,1,0:T(8,128)(2,1)S(1)}, u32[]{:S(2)}, u32[]{:S(2)}) collective-permute-start(bf16[3,384,256]{2,1,0:T(8,128)(2,1)S(1)} %get-tuple-element.264), channel_id=1, source_target_pairs={{0,4},{1,5},{2,6},{3,7},{4,0},{5,1},{6,2},{7,3},{8,12},{9,13},{10,... | collective-permute-start | bytes 1769480 | tf_op jit(solution)/shard_map/ppermute | solution.py:46
  1166.6 24.0 %collective-permute-start.14 = (bf16[256,1536]{1,0:T(8,128)(2,1)}, bf16[256,1536]{1,0:T(8,128)(2,1)}, u32[]{:S(2)}, u32[]{:S(2)}) collective-permute-start(bf16[256,1536]{1,0:T(8,128)(2,1)} %convert_element_type.85.refs_0_.refs_2_), channel_id=1, source_target_pairs={{2,0},{3,4},{6,2},{7,6},{10,8},{11,12},{14,10},{15,14},{18,1},{19,... | collective-permute-start | bytes 2359304 | tf_op jit(solution)/shard_map/ppermute | solution.py:46
  1168.5 62.9 %collective-permute-start.20 = (bf16[256,1536]{1,0:T(8,128)(2,1)}, bf16[256,1536]{1,0:T(8,128)(2,1)S(1)}, u32[]{:S(2)}, u32[]{:S(2)}) collective-permute-start(bf16[256,1536]{1,0:T(8,128)(2,1)} %get-tuple-element.203), channel_id=1, source_target_pairs={{0,0},{1,4},{4,2},{5,6},{8,8},{9,12},{12,10},{13,14},{16,1},{17,5}... | collective-permute-start | bytes 2359304 | tf_op jit(solution)/shard_map/ppermute | solution.py:46
  1173.6 57.8 %collective-permute-start.21 = (bf16[256,1536]{1,0:T(8,128)(2,1)}, bf16[256,1536]{1,0:T(8,128)(2,1)S(1)}, u32[]{:S(2)}, u32[]{:S(2)}) collective-permute-start(bf16[256,1536]{1,0:T(8,128)(2,1)} %get-tuple-element.203), channel_id=1, source_target_pairs={{2,0},{3,4},{6,2},{7,6},{10,8},{11,12},{14,10},{15,14},{18,1},{19,... | collective-permute-start | bytes 2359304 | tf_op jit(solution)/shard_map/ppermute | solution.py:46
  1174.9 56.5 %collective-permute-start.22 = (bf16[256,1536]{1,0:T(8,128)(2,1)}, bf16[256,1536]{1,0:T(8,128)(2,1)S(1)}, u32[]{:S(2)}, u32[]{:S(2)}) collective-permute-start(bf16[256,1536]{1,0:T(8,128)(2,1)} %get-tuple-element.176.refs_0_), channel_id=1, source_target_pairs={{0,16},{1,20},{4,18},{5,22},{8,24},{9,28},{12,26},{13,30},{16,17},... | collective-permute-start | bytes 2359304 | tf_op jit(solution)/shard_map/ppermute | solution.py:46
  1178.5 53.0 %collective-permute-start.23 = (bf16[256,1536]{1,0:T(8,128)(2,1)}, bf16[256,1536]{1,0:T(8,128)(2,1)S(1)}, u32[]{:S(2)}, u32[]{:S(2)}) collective-permute-start(bf16[256,1536]{1,0:T(8,128)(2,1)} %get-tuple-element.176.refs_0_), channel_id=1, source_target_pairs={{2,16},{3,20},{6,18},{7,22},{10,24},{11,28},{14,26},{15,30},{18,17... | collective-permute-start | bytes 2359304 | tf_op jit(solution)/shard_map/ppermute | solution.py:46
  1190.5 42.9 %collective-permute-start.26 = (bf16[384,576]{1,0:T(8,128)(2,1)S(1)}, bf16[384,576]{1,0:T(8,128)(2,1)S(1)}, u32[]{:S(2)}, u32[]{:S(2)}) collective-permute-start(bf16[384,576]{1,0:T(8,128)(2,1)S(1)} %get-tuple-element.246), channel_id=1, source_target_pairs={{0,16},{1,17},{2,18},{3,19},{4,20},{5,21},{6,22},{7,23},{8,24},{9,... | collective-permute-start | bytes 1327112 | tf_op jit(solution)/shard_map/ppermute | solution.py:46
  1231.4 20.4 %collective-permute-start.29 = (bf16[3,384,512]{2,1,0:T(8,128)(2,1)}, bf16[3,384,512]{2,1,0:T(8,128)(2,1)}, u32[]{:S(2)}, u32[]{:S(2)}) collective-permute-start(bf16[3,384,512]{2,1,0:T(8,128)(2,1)} %broadcast_select_fusion.2), channel_id=1, source_target_pairs={{0,16},{1,17},{2,18},{3,19},{4,20},{5,21},{6,22},{7,23},{8,24},{9,... | collective-permute-start | bytes 3538952 | tf_op jit(solution)/shard_map/ppermute | solution.py:46
  (53 other events, 669.5 us)

commit v3 on v2

v3 whole, which is shorter than its diff:
```python
import functools

import jax
import jax.numpy as jnp
import jax.experimental.pallas as pl
import jax.experimental.pallas.tpu as pltpu
from jax import lax
from jax.sharding import PartitionSpec as P

HD = 96
HP = 128
NEVER = -1e30
epsilon = 1e-05
rope_base = 100000.0
AXES = ("section", "fsdp", "tensor")
bf16 = jnp.bfloat16
f32 = jnp.float32


class Grid:
    def __init__(self, mesh):
        self.calls = 0
        self.X = mesh.shape["section"]
        self.C = 2
        self.Y = mesh.shape["fsdp"] // self.C
        self.Z = mesh.shape["tensor"]
        self.R = self.Y * self.Z
        self.places = [
            (x, y, c, z)
            for x in range(self.X)
            for y in range(self.Y)
            for c in range(self.C)
            for z in range(self.Z)
        ]

    def rank(self, place):
        x, y, c, z = place
        return ((x * self.Y + y) * self.C + c) * self.Z + z

    def send(self, block, route):
        pairs = []
        for place in self.places:
            goal = route(*place)
            if goal is not None:
                pairs.append((self.rank(place), self.rank(goal)))
        return lax.ppermute(block, AXES, pairs)

    def over_x(self, block):
        return self.send(block, lambda x, y, c, z: (1 - x, y, c, z))

    def over_c(self, block):
        return self.send(block, lambda x, y, c, z: (x, y, 1 - c, z))

    def hops(self):
        routes = [lambda x, y, c, z: (x, y, 1 - c, z)]
        for bit in range((self.Y - 1).bit_length()):
            routes.append(lambda x, y, c, z, bit=bit: (x, y ^ (1 << bit), c, z))
        for bit in range((self.Z - 1).bit_length()):
            routes.append(lambda x, y, c, z, bit=bit: (x, y, c, z ^ (1 << bit)))
        return routes

    def place_of(self, p):
        p = p % self.R
        y, k = p // self.Z, p % self.Z
        return (y, k if y % 2 == 0 else self.Z - 1 - k)

    def pos_of(self, y, z):
        return y * self.Z + (z if y % 2 == 0 else self.Z - 1 - z)

    def neighbour(self, way):
        yy, zz = self.dyn_place(self.my_pos() + way)
        return {"fsdp": yy * self.C + lax.axis_index("fsdp") % self.C, "tensor": zz}

    def me(self):
        x = lax.axis_index("section")
        f = lax.axis_index("fsdp")
        z = lax.axis_index("tensor")
        return x, f // self.C, f % self.C, z

    def my_pos(self):
        x, y, c, z = self.me()
        return y * self.Z + jnp.where(y % 2 == 0, z, self.Z - 1 - z)

    def dyn_place(self, p):
        p = (p + 2 * self.R) % self.R
        y, k = p // self.Z, p % self.Z
        return y, jnp.where(y % 2 == 0, k, self.Z - 1 - k)

def params(limit=56):
    return pltpu.CompilerParams(vmem_limit_bytes=limit * 1024 * 1024)


def whole_vmem(count):
    return [pl.BlockSpec(memory_space=pltpu.VMEM)] * count


def cost(micros):
    return pl.CostEstimate(flops=int(micros * 1.0e9), bytes_accessed=1 << 20, transcendentals=0)


def swapped(values):
    lane = lax.broadcasted_iota(jnp.int32, values.shape, 1)
    half = HD // 2
    return jnp.where(lane < half, pltpu.roll(values, HP - half, 1), pltpu.roll(values, half, 1))


MESH = pl.DeviceIdType.MESH
NT = (((1,), (1,)), ((), ()))
PARTS = 2


def dot_nt(a, b):
    return lax.dot_general(a, b, NT, preferred_element_type=f32)


def partners(grid):
    x, y, c, _ = grid.me()
    return (
        {"fsdp": y * grid.C + 1 - c},
        {"section": 1 - x},
        {"section": 1 - x, "fsdp": y * grid.C + 1 - c},
    )


def greet(grid, sides, cycle):
    others = list(partners(grid)[:sides])
    if cycle:
        others += [grid.neighbour(1), grid.neighbour(-1)]
    barrier = pltpu.get_barrier_semaphore()
    for other in others:
        pl.semaphore_signal(barrier, inc=1, device_id=other, device_id_type=MESH)
    pl.semaphore_wait(barrier, len(others))
    return partners(grid)


def remote(src, dst, sems, n, device):
    return pltpu.make_async_remote_copy(
        src_ref=src, dst_ref=dst, send_sem=sems.at[0, n], recv_sem=sems.at[1, n],
        device_id=device, device_id_type=MESH,
    )


def pieces_of(rows):
    size = rows // PARTS
    return [pl.ds(k * size, size) for k in range(PARTS)]


def start_all(copies):
    for copy in copies:
        copy.start()


def wait_all(copies):
    for copy in copies:
        copy.wait()


class Plan:
    def __init__(self):
        self.inputs, self.outs, self.lands, self.stages, self.hooks = [], [], [], [], []
        self.slots, self.makes, self.totals, self.moves, self.copies = [], [], [], 0, 1

    def give(self, array):
        for n, known in enumerate(self.inputs):
            if known is array:
                return ("in", n)
        self.inputs.append(array)
        return ("in", len(self.inputs) - 1)

    def room(self, shape):
        self.outs.append(jax.ShapeDtypeStruct(shape, bf16))
        return ("out", len(self.outs) - 1)

    def land(self, shape):
        self.lands.append(shape)
        return ("land", len(self.lands) - 1)

    def slot(self, key, shape):
        if (key, shape) not in self.slots:
            self.slots.append((key, shape))
        return self.slots.index((key, shape))

    def make(self, stage, key, shape, parts, offset, owned):
        slot = self.slot(key, shape)
        made = []
        for places, came in parts:
            copies = [(self.give(array), src, dst) for array, src, dst in places]
            joins = [(h if isinstance(h, tuple) else self.give(h), at) for h, at in came]
            made.append((copies, joins))
        self.copies = max(self.copies, sum(len(c) + len(j) for c, j in made))
        self.makes.append((stage, slot, made, offset, owned))
        return ("make", len(self.makes) - 1)

    def move(self, stage, src, dst, way, offset, owned, cut, part=0, needs=None):
        while len(self.stages) <= stage:
            self.stages.append([])
        self.stages[stage].append((self.moves, src, dst, way, offset, owned, cut, part, needs))
        self.moves += 1
        return self.moves - 1

    def scratch(self):
        if not self.moves:
            return []
        held = [pltpu.VMEM(shape, bf16) for _, shape in self.slots for _ in range(2)]
        held += [pltpu.VMEM(shape, bf16) for shape in self.lands]
        sems = [pltpu.SemaphoreType.DMA((2, self.moves))]
        if self.slots:
            sems.append(pltpu.SemaphoreType.DMA((len(self.slots), self.copies)))
        return held + sems

    def settle(self, results):
        for hook in self.hooks:
            hook(lambda handle: self.inputs[handle[1]] if handle[0] == "in" else results[handle[1]])


class Background:
    def __init__(self, grid, plan, ins, outs, rest):
        self.stages, self.totals, self.now, self.sent = [], [], -1, 0
        if not plan.moves:
            return
        pos = grid.my_pos()
        core = lax.axis_index("fsdp") % grid.C
        count = 2 * len(plan.slots)
        held, lands = rest[:count], rest[count : count + len(plan.lands)]
        sems = rest[count + len(plan.lands)]
        local = rest[-1]
        self.refs = {"in": ins, "out": outs, "land": lands}

        def live(owned, offset):
            if not owned:
                return None
            return grid.dyn_place(pos + offset)[1] // (grid.Z // 2) == core

        def built(slot, made, offset, owned):
            term, more = held[2 * slot], held[2 * slot + 1]
            yy, zz = grid.dyn_place(pos + offset)
            n, parts = 0, []
            for copies, joins in made:
                fetches, adds = [], []
                for handle, src, dst in copies:
                    ref = self.refs[handle[0]][handle[1]].at[src(yy, zz)]
                    fetches.append(pltpu.make_async_copy(ref, term.at[dst], local.at[slot, n]))
                    n += 1
                for handle, at in joins:
                    ref = self.refs[handle[0]][handle[1]]
                    if handle[0] == "land":
                        adds.append((None, ref, at))
                    else:
                        copy = pltpu.make_async_copy(ref.at[at], more.at[at], local.at[slot, n])
                        adds.append((copy, more, at))
                    n += 1
                parts.append((fetches, adds, term, handle_early(joins)))
            return parts, live(owned, offset)

        def handle_early(joins):
            return all(handle[0] == "in" for handle, _ in joins)

        self.makes = [[] for _ in plan.stages]
        buffers = []
        for stage, slot, made, offset, owned in plan.makes:
            parts, alive = built(slot, made, offset, owned)
            self.makes[stage].append((parts, alive))
            buffers.append((held[2 * slot], parts, alive))
        for slot, made, owned in plan.totals:
            self.totals.append((held[2 * slot],) + built(slot, made, 0, owned))
        self.all = {}
        for stage in plan.stages:
            row = []
            for number, src, dst, way, offset, owned, cut, part, needs in stage:
                put = None
                if src[0] == "make":
                    src_ref, parts, alive = buffers[src[1]]
                    put = (parts[part], alive)
                else:
                    src_ref = self.refs[src[0]][src[1]]
                dst_ref = self.refs[dst[0]][dst[1]]
                copy = remote(src_ref.at[cut], dst_ref.at[cut], sems, number, grid.neighbour(way))
                self.all[number] = (copy, live(owned, offset), live(owned, offset - way))
                row.append((number, put, needs))
            self.stages.append(row)
        self.come, self.put_done = set(), set()

    @staticmethod
    def do(condition, action):
        if condition is None:
            action()
        else:
            pl.when(condition)(action)

    def fetch(self, stage):
        if stage < len(self.stages):
            for parts, alive in self.makes[stage]:
                for fetches, adds, _, early in parts:
                    copies = fetches + [copy for copy, _, _ in adds if copy is not None and early]
                    self.do(alive, functools.partial(start_all, copies))

    def begin(self):
        self.fetch(0)
        for _, parts, alive in self.totals:
            for fetches, _, _, _ in parts:
                self.do(alive, functools.partial(start_all, fetches))

    @staticmethod
    def put(part, started=True):
        fetches, adds, term, early = part
        wait_all(fetches)
        for copy, ref, at in adds:
            if copy is not None:
                if not (early and started):
                    copy.start()
                copy.wait()
            term[at] = (term[at].astype(f32) + ref[at].astype(f32)).astype(bf16)

    def arrive(self, number):
        if number is not None and number not in self.come:
            self.come.add(number)
            copy, _, come = self.all[number]
            self.do(come, copy.wait_recv)

    def advance(self):
        self.now += 1
        if self.now < len(self.stages):
            for number, put, needs in self.stages[self.now]:
                for need in needs or ():
                    self.arrive(need)
                if put is not None and id(put[0]) not in self.put_done:
                    self.put_done.add(id(put[0]))
                    self.do(put[1], functools.partial(self.put, put[0]))
                copy, go, _ = self.all[number]
                self.do(go, copy.start)
            if self.now + 1 < len(self.stages):
                self.wait_sends(self.now)
                self.fetch(self.now + 1)
        if self.now >= len(self.stages):
            for row in self.stages:
                for number, _, _ in row:
                    self.arrive(number)

    def arrived(self, stage):
        for row in self.stages[: stage + 1]:
            for number, _, _ in row:
                self.arrive(number)

    def wait_sends(self, stage):
        while self.sent < stage:
            for number, _, _ in self.stages[self.sent]:
                copy, go, _ = self.all[number]
                self.do(go, copy.wait_send)
            self.sent += 1

    def finish(self):
        while self.now < len(self.stages):
            self.advance()
        self.wait_sends(len(self.stages))


class Gather:
    def __init__(self, grid, shape, cuts, owned=False):
        self.grid, self.owned, self.shape, self.cuts = grid, owned, shape, cuts
        self.k, self.total = 0, grid.R // 2

    def begin(self, plan):
        room = plan.room(self.shape)
        self.up = self.down = room

        def hook(get):
            self.found = [(0, get(room))]
            if self.k == 0:
                self.up = self.down = get(room)

        plan.hooks.append(hook)
        return room

    def left(self):
        return self.total - self.k

    def add(self, plan, stage, hops=None):
        hops = self.left() if hops is None else min(hops, self.left())
        if hops == 0:
            return
        one = self.up is self.down
        up = self.up if isinstance(self.up, tuple) else plan.give(self.up)
        down = up if one else plan.give(self.down)
        new = []
        before = [(None, None)] * len(self.cuts)
        for n in range(hops):
            self.k += 1
            k = self.k
            last = k == self.total
            to_up = plan.room(self.shape)
            to_down = to_up if last else plan.room(self.shape)
            now = []
            for (cut, first, second), (need_up, need_down) in zip(self.cuts, before):
                pair = (first, second) if last else (cut, cut)
                moved = []
                for src, dst, way, part, need in (
                    (up, to_up, 1, pair[0], need_up), (down, to_down, -1, pair[1], need_down)
                ):
                    moved.append(
                        None
                        if part is None
                        else plan.move(
                            stage + n, src, dst, way, -way * (k - 1), self.owned, part,
                            needs=(need,),
                        )
                    )
                now.append(tuple(moved))
            before = now
            new.append((-k, to_up))
            if not last:
                new.append((k, to_down))
            up, down = to_up, to_down

        def hook(get):
            self.up, self.down = get(up), get(down)
            self.found += [(offset, get(handle)) for offset, handle in new]

        plan.hooks.append(hook)


class Scatter:
    def __init__(self, grid, parts, shape, owned=False):
        self.grid, self.parts, self.shape, self.owned = grid, parts, shape, owned
        self.k = grid.R // 2
        self.held = {1: None, -1: None}

    def left(self):
        return self.k

    def came(self, way, n):
        if self.held[way] is None:
            return []
        block, column = self.held[way]
        at = self.parts[n][0][column]
        return [] if at is None else [(block, at)]

    def add(self, plan, stage, steps=1, final=False):
        steps = min(steps, self.k)
        before = {way: [None] * len(self.parts) for way in (1, -1)}
        for n in range(steps):
            k = self.k
            self.k -= 1
            room = plan.land if n < steps - 1 or final else plan.room
            rooms = {way: room(self.shape) for way in (1, -1)}
            halves = k == self.grid.R // 2
            blocks = {}
            for way in (1, -1):
                if halves and way == -1:
                    blocks[way] = blocks[1]
                    continue
                parts = [(places, self.came(way, m)) for m, (_, places) in enumerate(self.parts)]
                blocks[way] = plan.make(
                    stage + n, (id(self), way, n % 2), self.shape, parts, way * k, self.owned
                )
            now = {1: [], -1: []}
            for m, (cuts, _) in enumerate(self.parts):
                for way in (1, -1):
                    column = (1 if way == 1 else 2) if halves else 0
                    moved = None
                    if cuts[column] is not None:
                        moved = plan.move(
                            stage + n, blocks[way], rooms[way], way, way * k, self.owned, cuts[column],
                            m, (before[way][m],),
                        )
                    now[way].append(moved)
            before = now
            self.held = {
                way: (rooms[way], (1 if way == 1 else 2) if halves else 0) for way in (1, -1)
            }

        def hook(get):
            self.held = {
                way: (get(block), column) if block[0] == "out" else (None, column)
                for way, (block, column) in self.held.items()
            }

        if steps:
            plan.hooks.append(hook)

    def total(self, plan):
        parts = [
            (places, self.came(1, m) + self.came(-1, m)) for m, (_, places) in enumerate(self.parts)
        ]
        slot = plan.slot(("total", id(self)), self.shape)
        made = []
        for places, came in parts:
            copies = [(plan.give(array), src, dst) for array, src, dst in places]
            joins = [(h if isinstance(h, tuple) else plan.give(h), at) for h, at in came]
            made.append((copies, joins))
        plan.copies = max(plan.copies, sum(len(c) + len(j) for c, j in made))
        plan.totals.append((slot, made, self.owned))


def fused_call(grid, kernel, name, plan, inputs, in_specs, outs, out_specs, scratch, micros):
    plan = Plan() if plan is None else plan
    a, b, c, d = len(inputs), len(plan.inputs), len(outs), len(plan.outs)
    moves = plan.moves

    def whole(*refs):
        fg_in, bg_in = refs[:a], refs[a : a + b]
        fg_out, bg_out = refs[a + b : a + b + c], refs[a + b + c : a + b + c + d]
        rest = refs[a + b + c + d :]
        own = len(scratch)
        background = Background(grid, plan, bg_in, bg_out, rest[own:])
        kernel(background, bool(moves), *fg_in, *fg_out, *rest[:own])

    number = grid.calls
    grid.calls += 1
    results = pl.pallas_call(
        whole,
        out_shape=tuple(outs) + tuple(plan.outs),
        in_specs=list(in_specs) + [ANY] * b,
        out_specs=tuple(out_specs) + (ANY,) * d,
        scratch_shapes=list(scratch) + plan.scratch(),
        compiler_params=remote_params(number),
        cost_estimate=cost(micros),
        name=name,
    )(*inputs, *plan.inputs)
    plan.settle(results[c:])
    return results[:c]


class Spread:
    sems = pltpu.SemaphoreType.DMA((2, 1 + 2 * PARTS))

    def __init__(self, rows_ref, sems, sib, over):
        cuts = pieces_of(rows_ref.shape[1])
        self.near = remote(rows_ref.at[0], rows_ref.at[1], sems, 0, sib)
        self.far = [
            remote(rows_ref.at[0, at], rows_ref.at[2, at], sems, 1 + k, over)
            for k, at in enumerate(cuts)
        ]
        self.relay = [
            remote(rows_ref.at[2, at], rows_ref.at[3, at], sems, 1 + PARTS + k, sib)
            for k, at in enumerate(cuts)
        ]

    def start(self):
        for copy in self.far:
            copy.start()
        self.near.start()

    def pass_on(self, k):
        self.far[k].wait_recv()
        self.relay[k].start()

    def end(self):
        self.near.wait_send()
        for copy in self.far + self.relay:
            copy.wait_send()


class Collect:
    sems = pltpu.SemaphoreType.DMA((2, 1 + 2 * PARTS))

    @staticmethod
    def scratch(rows, width):
        return [pltpu.VMEM((6, rows, width), bf16), Collect.sems]

    def __init__(self, hold, sems, sib, over):
        self.hold = hold
        self.cuts = pieces_of(hold.shape[1])
        self.near = remote(hold.at[0], hold.at[2], sems, 0, sib)
        self.side = [
            remote(hold.at[1, at], hold.at[3, at], sems, 1 + k, sib)
            for k, at in enumerate(self.cuts)
        ]
        self.over = [
            remote(hold.at[4, at], hold.at[5, at], sems, 1 + PARTS + k, over)
            for k, at in enumerate(self.cuts)
        ]

    def give_near(self, part):
        self.hold[0] = part.astype(bf16)
        self.near.start()

    def give_side(self, k, part):
        self.hold[1, self.cuts[k]] = part.astype(bf16)
        self.side[k].start()

    def give_over(self, k, part):
        self.side[k].wait_recv()
        self.hold[4, self.cuts[k]] = (part + self.hold[3, self.cuts[k]].astype(f32)).astype(bf16)
        self.over[k].start()

    def finish(self, part):
        self.near.wait_recv()
        part = part + self.hold[2].astype(f32)
        for copy in self.over:
            copy.wait_recv()
        return part + self.hold[5].astype(f32)

    def end(self):
        self.near.wait_send()
        for copy in self.side + self.over:
            copy.wait_send()


def normed_rows(values, gain_row):
    return values * lax.rsqrt(jnp.mean(values * values, -1, keepdims=True) + epsilon) * gain_row


def norm_back(values, gain_row, upstream):
    scale = lax.rsqrt(jnp.mean(values * values, -1, keepdims=True) + epsilon)
    unit = values * scale
    moved = upstream * gain_row
    grad = scale * (moved - unit * jnp.mean(moved * unit, -1, keepdims=True))
    gains = upstream * unit
    return grad, jnp.sum(gains.reshape(-1, 8, gains.shape[-1]), 0)


def remote_params(number, limit=58):
    return pltpu.CompilerParams(
        vmem_limit_bytes=limit * 1024 * 1024, collective_id=number, has_side_effects=True
    )


def shaped(*pairs):
    return tuple(jax.ShapeDtypeStruct(shape, dtype) for shape, dtype in pairs)


ANY = pl.BlockSpec(memory_space=pl.ANY)
VMEM = pl.BlockSpec(memory_space=pltpu.VMEM)


def attn_kernel(
    grid, heads, offsets, background, cycle, h_ref, gain_ref, cos_ref, sin_ref, tokk_ref, tokq_ref,
    from_ref, *refs,
):
    pieces = refs[: len(offsets)]
    (
        all_ref, q_ref, k_ref, v_ref, mid_ref, mixed_ref, lse_ref,
        held, w_sems, wo_ref, wo_sems, rows_ref, s_sems, out_sem, top, total, acc, part, hold, c_sems,
    ) = refs[len(offsets) :]
    rows = h_ref.shape[0]
    halves = heads // 2
    scale = HD ** (-0.5)
    ids = place_id(grid)
    background.begin()
    fetched = fetch_attn(grid, offsets, pieces, held, None, w_sems)
    fetched_out = fetch_attn(grid, offsets, pieces, None, wo_ref, wo_sems)
    sib, over, _ = greet(grid, 2, cycle)
    rows_ref[0] = normed_rows(h_ref[...].astype(f32), gain_ref[...]).astype(bf16)
    spread = Spread(rows_ref, s_sems, sib, over)
    spread.start()
    background.advance()
    end_fetch(fetched)

    def work(slot, start, size):
        cosine, sine_part = cos_ref[slot, start : start + size], sin_ref[slot, start : start + size]
        at = slice(start, start + size)
        made = jnp.dot(rows_ref[slot, at], held[...], preferred_element_type=f32)
        for h in range(3 * halves):
            one = made[:, h * HP : (h + 1) * HP]
            turned = (one * cosine + swapped(one) * sine_part).astype(bf16)
            if h < 2 * halves:
                q_ref[h, slot, at] = turned
            else:
                k_ref[h - 2 * halves, slot, at] = turned
        for h in range(halves):
            v_ref[h, slot, at] = made[:, (3 * halves + h) * HP : (3 * halves + h + 1) * HP].astype(bf16)

    work(0, 0, rows)
    spread.near.wait_recv()
    work(1, 0, rows)
    size = rows // PARTS
    for k in range(PARTS):
        spread.pass_on(k)
        work(2, k * size, size)
        spread.relay[k].wait_recv()
        work(3, k * size, size)
    out = pltpu.make_async_copy(rows_ref, all_ref, out_sem)
    out.start()
    end_fetch(fetched_out)
    collect = Collect(hold, c_sems, sib, over)

    def attend(i):
        tok_q, begin = tokq_ref[i], from_ref[i]

        def block(j, first):
            tok_k = tokk_ref[j]
            allowed = (tok_k <= tok_q) & (tok_k >= begin)
            for h in range(heads):
                scores = dot_nt(q_ref[h, i], k_ref[h // 2, j])
                scores = jnp.where(allowed, scores * scale, NEVER)
                peak = jnp.max(scores, 1, keepdims=True)
                if not first:
                    before = top[h]
                    peak = jnp.maximum(peak, before)
                raised = jnp.exp(scores - peak)
                summed = jnp.sum(raised, 1, keepdims=True)
                got = jnp.dot(raised.astype(bf16), v_ref[h // 2, j], preferred_element_type=f32)
                if first:
                    total[h] = summed
                    acc[h] = got
                else:
                    shrink = jnp.exp(before - peak)
                    total[h] = total[h] * shrink + summed
                    acc[h] = acc[h] * shrink + got
                top[h] = peak

        block(i, True)
        for j in range(4):
            if j != i:
                pl.when((ids[j] < ids[i]) & (ids[j] >= ids[i] - 2))(functools.partial(block, j, False))
        for h in range(heads):
            mixed_ref[i, :, h * HP : (h + 1) * HP] = (acc[h] / total[h]).astype(bf16)
            log_total = top[h] + jnp.log(total[h])
            lse_ref[i, h] = jnp.transpose(jnp.broadcast_to(log_total, (rows, HP)))[:8]
        part[...] = dot_nt(mixed_ref[i], wo_ref[...])

    cuts = pieces_of(rows)
    attend(3)
    for k in range(PARTS):
        collect.give_side(k, part[cuts[k]])
    background.advance()
    attend(2)
    for k in range(PARTS):
        collect.give_over(k, part[cuts[k]])
    attend(1)
    collect.give_near(part[...])
    attend(0)
    mid_ref[...] = collect.finish(part[...] + h_ref[...].astype(f32))
    background.advance()
    out.wait()
    spread.end()
    collect.end()
    background.finish()


def attn_call(grid, plan, hidden, gain_row, facts, found):
    rows, width = hidden.shape
    halves = grid.Z // 2
    heads = 2 * halves
    offsets, blocks = apart(found)
    shape = (halves, 4, rows, HP)
    return fused_call(
        grid, functools.partial(attn_kernel, grid, heads, offsets), "attn", plan,
        (
            hidden, gain_row, facts["cos"], facts["sin"], facts["tok"][:, None, :],
            facts["tok"][:, :, None], facts["from"][:, :, None], *blocks,
        ),
        [VMEM] * 7 + [ANY] * len(blocks),
        shaped(
            ((4, rows, width), bf16), ((heads,) + shape[1:], bf16), (shape, bf16), (shape, bf16),
            ((rows, width), f32), ((4, rows, heads * HP), bf16), ((4, heads, 8, rows), f32),
        ),
        (ANY,) + (VMEM,) * 6,
        [
            pltpu.VMEM((width, 4 * halves * HP), bf16), fetch_sems(found),
            pltpu.VMEM((width, heads * HP), bf16), fetch_sems(found),
            pltpu.VMEM((4, rows, width), bf16), Spread.sems, pltpu.SemaphoreType.DMA,
            pltpu.VMEM((heads, rows, 1), f32),
            pltpu.VMEM((heads, rows, 1), f32),
            pltpu.VMEM((heads, rows, HP), f32),
            pltpu.VMEM((rows, width), f32),
        ]
        + Collect.scratch(rows, width),
        60,
    )


def fetch_attn(grid, offsets, pieces, qkv, out, sems):
    pos = grid.my_pos()
    core = lax.axis_index("fsdp") % grid.C
    halves = grid.Z // 2
    tall = pieces[0].shape[0]
    fetched = []
    for i, offset in enumerate(offsets):
        yy, zz = grid.dyn_place(pos + offset)
        j = zz % halves
        rows = pl.ds(pl.multiple_of(yy * tall, tall), tall)

        def copy(n, first, width, ref, at):
            return pltpu.make_async_copy(
                pieces[i].at[:, pl.ds(first * HP, width * HP)],
                ref.at[rows, pl.ds(pl.multiple_of(at * HP, HP), width * HP)],
                sems.at[i, n],
            )

        if out is None:
            copies = [
                copy(0, 0, 2, qkv, 2 * j),
                copy(1, 2, 1, qkv, 2 * halves + j),
                copy(2, 3, 1, qkv, 3 * halves + j),
            ]
        else:
            copies = [copy(0, 4, 2, out, 2 * j)]
        live = zz // halves == core
        pl.when(live)(functools.partial(start_all, copies))
        fetched.append((live, copies))
    return fetched


def end_fetch(fetched):
    for live, copies in fetched:
        pl.when(live)(functools.partial(wait_all, copies))


def fetch_sems(found):
    return pltpu.SemaphoreType.DMA((len(found), 3))


def apart(found):
    return [offset for offset, _ in found], [block for _, block in found]


def place_id(grid):
    x, _, c, z = grid.me()
    return [2 * cc + (xx + z) % 2 for xx, cc in ((x, c), (x, 1 - c), (1 - x, c), (1 - x, 1 - c))]


def fetch_ffn(grid, offsets, pieces, held, sems):
    pos = grid.my_pos()
    _, tall, units = pieces[0].shape
    copies = []
    for i, offset in enumerate(offsets):
        yy, zz = grid.dyn_place(pos + offset)
        rows = pl.ds(pl.multiple_of(yy * tall, tall), tall)
        cols = pl.ds(pl.multiple_of(zz * units, units), units)
        copy = pltpu.make_async_copy(pieces[i], held.at[:, rows, cols], sems.at[i])
        copy.start()
        copies.append(copy)
    return copies


STEP = 512


def ffn_kernel(grid, offsets, background, cycle, mid_ref, gain_ref, *refs):
    count = len(offsets)
    pieces = refs[:count]
    (
        out_ref, all_ref, gate_ref, up_ref, hid_ref,
        held, w_sems, rows_ref, s_sems, part, own, hold, c_sems, out_sem,
    ) = refs[count:]
    rows, width = mid_ref.shape
    hidden = gate_ref.shape[2]
    background.begin()
    fetched = fetch_ffn(grid, offsets, pieces, held, w_sems)
    sib, over, _ = greet(grid, 2, cycle)
    rows_ref[0] = normed_rows(mid_ref[...], gain_ref[...]).astype(bf16)
    spread = Spread(rows_ref, s_sems, sib, over)
    collect = Collect(hold, c_sems, sib, over)
    spread.start()
    background.advance()
    for copy in fetched:
        copy.wait()

    def work(slot, start, size):
        at = pl.ds(start, size)

        def tile(n, carry):
            cols = pl.ds(pl.multiple_of(n * STEP, STEP), STEP)
            some = rows_ref[slot, at]
            gate = jnp.dot(some, held[0, :, cols], preferred_element_type=f32)
            up = jnp.dot(some, held[1, :, cols], preferred_element_type=f32)
            gate_ref[slot, at, cols] = gate.astype(bf16)
            up_ref[slot, at, cols] = up.astype(bf16)
            hid_ref[slot, at, cols] = (gate * jax.nn.sigmoid(gate) * up).astype(bf16)
            return carry

        lax.fori_loop(0, hidden // STEP, tile, 0)

        def tile_down(n, carry):
            cols = pl.ds(pl.multiple_of(n * STEP, STEP), STEP)
            part[at, cols] = dot_nt(hid_ref[slot, at], held[2, cols])
            return carry

        lax.fori_loop(0, width // STEP, tile_down, 0)

    work(0, 0, rows)
    own[...] = mid_ref[...] + part[...]
    spread.near.wait_recv()
    work(1, 0, rows)
    collect.give_near(part[...])
    cuts = pieces_of(rows)
    size = rows // PARTS
    for k in range(PARTS):
        spread.pass_on(k)
        if k:
            background.advance()
        spread.relay[k].wait_recv()
        work(3, k * size, size)
        collect.give_side(k, part[cuts[k]])
        work(2, k * size, size)
        collect.give_over(k, part[cuts[k]])
    background.advance()
    out = pltpu.make_async_copy(rows_ref, all_ref, out_sem)
    out.start()
    out_ref[...] = collect.finish(own[...]).astype(bf16)
    out.wait()
    spread.end()
    collect.end()
    background.finish()


def ffn_call(grid, plan, middle, gain_row, found):
    rows, width = middle.shape
    offsets, blocks = [o for o, _ in found], [b for _, b in found]
    hidden = grid.Z * blocks[0].shape[2]
    return fused_call(
        grid, functools.partial(ffn_kernel, grid, offsets), "ffn", plan,
        (middle, gain_row, *blocks), [VMEM] * 2 + [ANY] * len(blocks),
        shaped(((rows, width), bf16), ((4, rows, width), bf16), *[((4, rows, hidden), bf16)] * 3),
        (VMEM, ANY, VMEM, VMEM, VMEM),
        [
            pltpu.VMEM((3, width, hidden), bf16),
            pltpu.SemaphoreType.DMA((len(blocks),)),
            pltpu.VMEM((4, rows, width), bf16),
            Spread.sems,
            pltpu.VMEM((rows, width), f32),
            pltpu.VMEM((rows, width), f32),
        ]
        + Collect.scratch(rows, width)
        + [pltpu.SemaphoreType.DMA],
        44,
    )


TN = (((0,), (0,)), ((), ()))


def weight_terms(out, left, right, step=512):
    whole = right[...].reshape(-1, right.shape[-1])

    def tile(n, carry):
        cols = pl.ds(pl.multiple_of(n * step, step), step)
        some = left[:, :, cols].reshape(-1, step)
        out[cols, :] = lax.dot_general(some, whole, TN, preferred_element_type=f32).astype(bf16)
        return carry

    lax.fori_loop(0, left.shape[-1] // step, tile, 0)


def ffn_back_kernel(
    grid, offsets, background, cycle, g_ref, mid_ref, gain_ref, gate_ref, up_ref, hid_ref, whole_ref, *refs
):
    count = len(offsets)
    pieces = refs[:count]
    (
        out_ref, gains_ref, terms_ref,
        held, w_sems, rows_ref, s_sems, dgate_ref, dup_ref, part, own, hold, c_sems, out_sems,
    ) = refs[count:]
    rows, width = mid_ref.shape
    hidden = gate_ref.shape[2]
    background.begin()
    fetched = fetch_ffn(grid, offsets, pieces, held, w_sems)
    sib, over, _ = greet(grid, 2, cycle)
    rows_ref[0] = g_ref[...]
    spread = Spread(rows_ref, s_sems, sib, over)
    collect = Collect(hold, c_sems, sib, over)
    spread.start()
    background.advance()
    wait_all(fetched)

    def work(slot, start, size):
        at = pl.ds(start, size)

        def tile(n, carry):
            cols = pl.ds(pl.multiple_of(n * STEP, STEP), STEP)
            grad = jnp.dot(rows_ref[slot, at], held[2, :, cols], preferred_element_type=f32)
            gate = gate_ref[slot, at, cols].astype(f32)
            up = up_ref[slot, at, cols].astype(f32)
            sig = jax.nn.sigmoid(gate)
            dgate_ref[slot, at, cols] = (grad * up * sig * (1.0 + gate * (1.0 - sig))).astype(bf16)
            dup_ref[slot, at, cols] = (grad * gate * sig).astype(bf16)
            return carry

        lax.fori_loop(0, hidden // STEP, tile, 0)

        def tile_back(n, carry):
            cols = pl.ds(pl.multiple_of(n * STEP, STEP), STEP)
            part[at, cols] = dot_nt(dgate_ref[slot, at], held[0, cols]) + dot_nt(
                dup_ref[slot, at], held[1, cols]
            )
            return carry

        lax.fori_loop(0, width // STEP, tile_back, 0)

    work(0, 0, rows)
    own[...] = part[...]
    spread.near.wait_recv()
    work(1, 0, rows)
    collect.give_near(part[...])
    cuts = pieces_of(rows)
    size = rows // PARTS
    for k in range(PARTS):
        spread.pass_on(k)
        if k:
            background.advance()
        spread.relay[k].wait_recv()
        work(3, k * size, size)
        collect.give_side(k, part[cuts[k]])
        work(2, k * size, size)
        collect.give_over(k, part[cuts[k]])
    outs = []
    for m, (left, right) in enumerate(
        ((rows_ref, hid_ref), (whole_ref, dgate_ref), (whole_ref, dup_ref))
    ):
        n = (m + 2) % 3
        weight_terms(held.at[n], left, right)
        outs.append(pltpu.make_async_copy(held.at[n], terms_ref.at[n], out_sems.at[n]))
        outs[-1].start()
        if m == 0:
            background.advance()
    second = collect.finish(own[...])
    grad, gains = norm_back(mid_ref[...], gain_ref[...], second)
    out_ref[...] = g_ref[...].astype(f32) + grad
    gains_ref[...] = gains
    background.advance()
    wait_all(outs)
    spread.end()
    collect.end()
    background.finish()


def ffn_back_call(grid, plan, grad_out, middle, gain_row, gate, up, hidden_low, whole, found):
    rows, width = middle.shape
    offsets, blocks = apart(found)
    hidden = gate.shape[2]
    return fused_call(
        grid, functools.partial(ffn_back_kernel, grid, offsets), "ffn_back", plan,
        (grad_out, middle, gain_row, gate, up, hidden_low, whole, *blocks),
        [VMEM] * 7 + [ANY] * len(blocks),
        shaped(((rows, width), f32), ((8, width), f32), ((3, width, hidden), bf16)),
        (VMEM, VMEM, ANY),
        [
            pltpu.VMEM((3, width, hidden), bf16),
            pltpu.SemaphoreType.DMA((len(blocks),)),
            pltpu.VMEM((4, rows, width), bf16),
            Spread.sems,
            pltpu.VMEM((4, rows, hidden), bf16),
            pltpu.VMEM((4, rows, hidden), bf16),
            pltpu.VMEM((rows, width), f32),
            pltpu.VMEM((rows, width), f32),
        ]
        + Collect.scratch(rows, width)
        + [pltpu.SemaphoreType.DMA((3,))],
        60,
    )


def attn_back_kernel(
    grid, heads, offsets, background, cycle, g_ref, h_ref, gain_ref, cos_ref, sin_ref, q_ref, k_ref,
    v_ref, m_ref, l_ref, tokc_ref, tokr_ref, from_ref, whole_ref, *refs,
):
    pieces = refs[: len(offsets)]
    (
        out_ref, gains_ref, qkv_term, out_term,
        held, w_sems, wo_ref, wo_sems, rows_ref, s_sems, gm_ref, dqkv_ref,
        key_sum, value_sum, query_sum, delta, part, hold, c_sems,
    ) = refs[len(offsets) :]
    rows = g_ref.shape[0]
    pairs = heads // 2
    scale = HD ** (-0.5)
    ids = place_id(grid)
    background.begin()
    fetched_out = fetch_attn(grid, offsets, pieces, None, wo_ref, wo_sems)
    fetched = fetch_attn(grid, offsets, pieces, held, None, w_sems)
    sib, over, _ = greet(grid, 2, cycle)
    rows_ref[0] = g_ref[...].astype(bf16)
    spread = Spread(rows_ref, s_sems, sib, over)
    spread.start()
    background.advance()
    end_fetch(fetched_out)

    def work(slot, start, size):
        at = slice(start, start + size)
        made = jnp.dot(rows_ref[slot, at], wo_ref[...], preferred_element_type=f32).astype(bf16)
        for h in range(heads):
            gm_ref[h, slot, at] = made[:, h * HP : (h + 1) * HP]

    key_sum[...] = jnp.zeros_like(key_sum)
    value_sum[...] = jnp.zeros_like(value_sum)
    query_sum[...] = jnp.zeros_like(query_sum)

    def attend_back(i):
        for h in range(heads):
            product = gm_ref[h, i].astype(f32) * m_ref[i, :, h * HP : (h + 1) * HP].astype(f32)
            summed = jnp.sum(product, 1, keepdims=True)
            delta[h] = jnp.transpose(jnp.broadcast_to(summed, (rows, HP)))[:8]

        def block(j):
            allowed = (tokc_ref[j] <= tokr_ref[i]) & (tokc_ref[j] >= from_ref[i])
            for h in range(heads):
                query, upstream = q_ref[h, i], gm_ref[h, i]
                key, value = k_ref[h // 2, j], v_ref[h // 2, j]
                scores = jnp.where(allowed, dot_nt(key, query) * scale, NEVER)
                probs = jnp.exp(scores - l_ref[i, h, 0:1])
                value_sum[h // 2, j] += jnp.dot(
                    probs.astype(bf16), upstream, preferred_element_type=f32
                )
                grad_scores = (probs * (dot_nt(value, upstream) - delta[h, 0:1])).astype(bf16)
                key_sum[h // 2, j] += jnp.dot(grad_scores, query, preferred_element_type=f32)
                query_sum[h, i] += lax.dot_general(
                    grad_scores, key, TN, preferred_element_type=f32
                )

        for j in range(4):
            if i == j:
                block(j)
            else:
                pl.when((ids[j] < ids[i]) & (ids[j] >= ids[i] - 2))(functools.partial(block, j))

    work(0, 0, rows)
    spread.near.wait_recv()
    work(1, 0, rows)
    attend_back(0)
    attend_back(1)
    size = rows // PARTS
    for k in range(PARTS):
        spread.pass_on(k)
        work(2, k * size, size)
        spread.relay[k].wait_recv()
        work(3, k * size, size)
    background.advance()
    attend_back(2)
    attend_back(3)

    def back(summed, at):
        one = summed * scale
        return (one * cos_ref[at] - swapped(one) * sin_ref[at]).astype(bf16)

    collect = Collect(hold, c_sems, sib, over)
    cuts = pieces_of(rows)
    end_fetch(fetched)

    def work_back(i):
        for h in range(heads):
            dqkv_ref[i, :, h * HP : (h + 1) * HP] = back(query_sum[h, i], i)
        for h in range(pairs):
            at = heads + h
            dqkv_ref[i, :, at * HP : (at + 1) * HP] = back(key_sum[h, i], i)
            at = heads + pairs + h
            dqkv_ref[i, :, at * HP : (at + 1) * HP] = value_sum[h, i].astype(bf16)
        part[...] = dot_nt(dqkv_ref[i], held[...])

    work_back(3)
    for k in range(PARTS):
        collect.give_side(k, part[cuts[k]])
    work_back(2)
    for k in range(PARTS):
        collect.give_over(k, part[cuts[k]])
    background.advance()
    work_back(1)
    collect.give_near(part[...])
    work_back(0)
    weight_terms(out_term, rows_ref, m_ref)
    weight_terms(qkv_term, whole_ref, dqkv_ref)
    grad, gains = norm_back(h_ref[...].astype(f32), gain_ref[...], collect.finish(part[...]))
    out_ref[...] = (g_ref[...] + grad).astype(bf16)
    gains_ref[...] = gains
    background.advance()
    spread.end()
    collect.end()
    background.finish()


def attn_back_call(grid, plan, grad_middle, hidden, gain_row, facts, kept, found):
    whole, query, keys, values, mixed, lse = kept
    rows, width = hidden.shape
    heads = query.shape[0]
    pairs = heads // 2
    offsets, blocks = apart(found)
    return fused_call(
        grid, functools.partial(attn_back_kernel, grid, heads, offsets), "attn_back", plan,
        (
            grad_middle, hidden, gain_row, facts["cos"], facts["sin"], query, keys, values, mixed, lse,
            facts["tok"][:, :, None], facts["tok"][:, None, :], facts["from"][:, None, :], whole,
            *blocks,
        ),
        [VMEM] * 14 + [ANY] * len(blocks),
        shaped(
            ((rows, width), bf16), ((8, width), f32), ((width, 2 * heads * HP), bf16),
            ((width, heads * HP), bf16),
        ),
        (VMEM,) * 4,
        [
            pltpu.VMEM((width, 2 * heads * HP), bf16), fetch_sems(found),
            pltpu.VMEM((width, heads * HP), bf16), fetch_sems(found),
            pltpu.VMEM((4, rows, width), bf16), Spread.sems,
            pltpu.VMEM((heads, 4, rows, HP), bf16),
            pltpu.VMEM((4, rows, 2 * heads * HP), bf16),
            pltpu.VMEM((pairs, 4, rows, HP), f32),
            pltpu.VMEM((pairs, 4, rows, HP), f32),
            pltpu.VMEM((heads, 4, rows, HP), f32),
            pltpu.VMEM((heads, 8, rows), f32),
            pltpu.VMEM((rows, width), f32),
        ]
        + Collect.scratch(rows, width),
        80,
    )


def start_kernel(grid, joins, early, background, cycle, attn_ref, ffn_ref, sems, local):
    x, _, c, z = grid.me()
    mine = z // (grid.Z // 2) == c
    attn_to = [background.refs[h[0]][h[1]] for h in joins[0]]
    ffn_to = [background.refs[h[0]][h[1]] for h in joins[1]]
    depth = attn_ref.shape[1]
    rows = pl.ds(pl.multiple_of(c * depth, depth), depth)
    sib, over, diag = greet(grid, 3, cycle)
    everything = []
    for layer in range(2):
        to = attn_to[layer].at[rows]
        moves = [
            (mine, pltpu.make_async_copy(attn_ref.at[layer], to, local.at[0])),
            (~mine, remote(attn_ref.at[layer], to, sems, 0, sib)),
            (mine, remote(attn_ref.at[1 - layer], to, sems, 1, over)),
            (~mine, remote(attn_ref.at[1 - layer], to, sems, 2, diag)),
        ]
        into = ffn_to[layer].at[:, rows]
        quarter = lambda side, core: ffn_ref.at[2 * side + core]
        parts = [
            remote(quarter(1 - layer, c), into, sems, 4, over),
            remote(quarter(1 - layer, 1 - c), into, sems, 5, diag),
            remote(quarter(layer, 1 - c), into, sems, 3, sib),
            pltpu.make_async_copy(quarter(layer, c), into, local.at[1]),
        ]
        everything.append((moves, parts))

        @pl.when(x == layer)
        def _():
            for condition, copy in moves:
                pl.when(condition)(copy.start)

    (own, to_sib, to_over, to_diag), parts = [copy for _, copy in moves], parts

    @pl.when(mine)
    def _():
        own.wait()
        to_over.wait_send()
        for copy in (to_sib, to_over, to_diag):
            copy.wait_recv()

    @pl.when(~mine)
    def _():
        to_sib.wait_send()
        to_diag.wait_send()

    background.advance()
    for layer in range(2):
        pl.when(x == layer)(functools.partial(start_all, everything[layer][1]))
    for n in range(early):
        background.advance()
    wait_all(parts)
    background.finish()


def start_call(grid, plan, joins, early, attn_pack, ffn_pack):
    fused_call(
        grid, functools.partial(start_kernel, grid, joins, early), "start", plan,
        (attn_pack, ffn_pack), [ANY] * 2, (), (),
        [pltpu.SemaphoreType.DMA((2, 6)), pltpu.SemaphoreType.DMA((2,))], 70,
    )


def tail_kernel(
    grid, ready, background, cycle, ffn_own, ffn_came, attn_own, attn_came, sems, local
):
    x, _, c, z = grid.me()
    mine = z // (grid.Z // 2) == c
    depth = attn_own.shape[0]
    rows = pl.ds(pl.multiple_of(c * depth, depth), depth)
    other = pl.ds(pl.multiple_of((1 - c) * depth, depth), depth)
    background.begin()
    sib, over, diag = greet(grid, 3, cycle)
    background.advance()

    def home(n, layer, heads):
        term, parts, alive = background.totals[n]
        for part in parts:
            background.do(alive, functools.partial(background.put, part, False))
        if heads:
            keep = (term.at[rows], attn_own)
            moves = [
                remote(term.at[other], attn_own, sems, 3, sib),
                remote(term.at[rows], attn_came, sems, 4, over),
                remote(term.at[other], attn_came, sems, 5, diag),
            ]
        else:
            keep = (term.at[:, rows], ffn_own.at[c])
            moves = [
                remote(term.at[:, other], ffn_own.at[c], sems, 0, sib),
                remote(term.at[:, rows], ffn_came.at[c], sems, 1, over),
                remote(term.at[:, other], ffn_came.at[c], sems, 2, diag),
            ]
        stay = pltpu.make_async_copy(*keep, local.at[1 if heads else 0])
        here = x == layer
        there = x != layer
        if heads:
            here, there = here & mine, there & mine

        @pl.when(here)
        def _():
            stay.start()
            moves[0].start()

        @pl.when(there)
        def _():
            moves[1].start()
            moves[2].start()

        return stay, moves

    done = {}
    waiting = list(enumerate(ready))
    while waiting or background.now < len(background.stages):
        for n, (layer, heads, stage) in list(waiting):
            if stage < background.now:
                background.arrived(stage)
                done[heads] = home(n, layer, heads)
                waiting.remove((n, (layer, heads, stage)))
        if background.now < len(background.stages):
            background.advance()
    background.finish()
    stay, moves = done[False]
    stay.wait()
    for copy in moves:
        copy.wait()
    stay, moves = done[True]

    @pl.when(mine)
    def _():
        stay.wait()
        for copy in moves:
            copy.wait_send()
        moves[1].wait_recv()

    @pl.when(~mine)
    def _():
        moves[0].wait_recv()
        moves[2].wait_recv()


def tail_call(grid, plan, ready, depth, units):
    return fused_call(
        grid, functools.partial(tail_kernel, grid, ready), "tail", plan, (), (),
        shaped(*[((2, 3, depth, units), bf16)] * 2, *[((depth, 6 * HP), bf16)] * 2), (ANY,) * 4,
        [pltpu.SemaphoreType.DMA((2, 6)), pltpu.SemaphoreType.DMA((2,))], 60,
    )


def turning(doc_row):
    places = jnp.arange(doc_row.shape[-1], dtype=jnp.int32)
    begins = jnp.concatenate([jnp.ones((1,), dtype=bool), doc_row[1:] != doc_row[:-1]], -1)
    starts = lax.cummax(jnp.where(begins, places, 0), axis=0)
    positions = (places - starts).astype(f32)
    ladder = jnp.arange(HD // 2, dtype=f32)
    frequency = rope_base ** (-2.0 * ladder / HD)
    angles = positions[..., None] * frequency
    cosine, sine_part = jnp.cos(angles), jnp.sin(angles)
    blank = jnp.zeros((doc_row.shape[0], HP - HD), f32)
    return (
        starts,
        jnp.concatenate([cosine, cosine, blank], -1),
        jnp.concatenate([-sine_part, sine_part, blank], -1),
    )


def after(value, *others):
    return lax.optimization_barrier((value,) + others)[0]


def layer_forward(grid, hidden_in, attn, ffn, nexts, gain_pair, facts, before_ffn):
    plan = Plan()
    ffn.add(plan, 0)
    whole, query, keys, values, middle, mixed, lse = attn_call(
        grid, plan, hidden_in, gain_pair[0:1], facts, attn.found
    )
    plan = Plan()
    if nexts:
        nexts[0].add(plan, 0)
        nexts[1].add(plan, max(0, len(plan.stages) - 2), 1)
    result, whole2, gate, up, hidden = ffn_call(
        grid, plan, middle, after(gain_pair[1:2], *before_ffn), ffn.found
    )
    kept = (hidden_in, (whole, query, keys, values, mixed, lse), middle, whole2, gate, up, hidden)
    return result, kept


def layer_backward(grid, grad_out, kept, attn, ffn, gain_pair, facts, running, sum_ffn, sum_attn, leaving):
    hidden_in, kept_attn, middle, whole2, gate, up, hidden = kept
    plan = Plan()
    for ring in running:
        ring.add(plan, 0, min(4, ring.left()))
    grad_middle, gain_two, terms = ffn_back_call(
        grid, plan, grad_out, middle, gain_pair[1:2], gate, up, hidden, whole2, ffn.found
    )
    sums = sum_ffn(terms)
    running.append(sums)
    plan = Plan()
    sums.add(plan, 0, 3)
    grad_input, gain_one, qkv_term, out_term = attn_back_call(
        grid, plan, grad_middle, hidden_in, after(gain_pair[0:1], *leaving), facts, kept_attn, attn.found
    )
    running.append(sum_attn(qkv_term, out_term))
    gains = jnp.stack([jnp.sum(gain_one, 0), jnp.sum(gain_two, 0)])
    return grad_input, gains


def body(grid, inputs, doc_ids, cotangent, wq, wk, wv, wo, wg, wu, wd, gains):
    X, Y, C, Z = grid.X, grid.Y, grid.C, grid.Z
    x, y, c, z = grid.me()
    pos = grid.my_pos()
    micro, rows, width = inputs.shape
    depth = wq.shape[1]
    at_zero = x == 0

    def enter(block):
        def route(m):
            def go(x, y, c, z):
                if z % 2 != (x + m * C + c) % 2:
                    return None
                return (x, y, z // 2, m * C + c)

            return go

        first, last = grid.send(block[0], route(0)), grid.send(block[1], route(1))
        return jnp.where(z // C == 0, first, last)

    def leave(block, section):
        def route(m):
            def go(x, y, c, z):
                if z // C != m:
                    return None
                return (section, y, z % C, 2 * c + (x + z) % 2)

            return go

        return [grid.send(block, route(m)) for m in range(micro)]

    rows_in = enter(inputs)
    docs = grid.over_c(doc_ids)
    docs = jnp.where(c == z % C, doc_ids, docs)[:, 0]
    doc_row = lax.dynamic_index_in_dim(docs, z // C, 0, keepdims=False)
    length = doc_row.shape[0]
    starts, cosine, sine_part = turning(doc_row)
    ids = place_id(grid)

    def in_my_order(rows_of):
        return jnp.stack(
            [lax.dynamic_slice_in_dim(rows_of, ids[n] * rows, rows, 0) for n in range(4)]
        )

    facts = {
        "tok": in_my_order(jnp.arange(length, dtype=jnp.int32)),
        "from": in_my_order(starts),
        "cos": in_my_order(cosine),
        "sin": in_my_order(sine_part),
    }

    mine = (y * C + c) * Z + z
    table = lax.dynamic_update_slice(
        jnp.zeros((Y * C * Z,) + gains.shape[1:], bf16), gains, (mine, 0, 0)
    )
    for hop in grid.hops():
        table = table + grid.send(table, hop)
    gain_own = table.transpose(1, 0, 2).reshape(2, width)
    gain_other = grid.over_x(gain_own)
    gain_all = [
        jnp.where(at_zero, gain_own, gain_other).astype(f32),
        jnp.where(at_zero, gain_other, gain_own).astype(f32),
    ]

    def cut(block, index, count, axis):
        size = block.shape[axis] // count
        return lax.dynamic_slice_in_dim(block, index * size, size, axis)

    def heads_of(block):
        split = block.reshape(block.shape[0], -1, HD)
        return jnp.pad(split, ((0, 0), (0, 0), (0, HP - HD))).reshape(block.shape[0], -1)

    def pack_attn(side):
        parts = [cut(wq[0], side, 2, 1), cut(wk[0], side, 2, 1), cut(wv[0], side, 2, 1)]
        return heads_of(jnp.concatenate(parts + [cut(wo[0], side, 2, 0).T], 1))

    def pack_ffn(quarter):
        return jnp.stack(
            [cut(wg[0], quarter, 4, 1), cut(wu[0], quarter, 4, 1), cut(wd[0], quarter, 4, 0).T]
        )

    halves = Z // 2
    tall = C * depth
    units = wg.shape[2] // 4
    upper, lower = pl.ds(0, tall // 2), pl.ds(tall // 2, tall // 2)
    attn_cuts = [((upper,), (upper,), None), ((lower,), None, (lower,))]
    ffn_cuts = [((m,), (m, upper), (m, lower)) for m in range(3)]
    attn = [Gather(grid, (tall, 6 * HP), attn_cuts, True) for _ in range(2)]
    ffn = [Gather(grid, (3, tall, units), ffn_cuts) for _ in range(2)]
    plan = Plan()
    joins = [[ring.begin(plan) for ring in rings] for rings in (attn, ffn)]
    attn[0].add(plan, 0)
    ffn[0].add(plan, max(0, len(plan.stages) - 2), 1)
    start_call(
        grid, plan, joins, max(0, len(plan.stages) - 3), jnp.stack([pack_attn(0), pack_attn(1)]),
        jnp.stack([pack_ffn(quarter) for quarter in range(4)]),
    )

    hidden = rows_in
    kept = []
    for s in range(2):
        nexts = (attn[1], ffn[1]) if s == 0 else None
        if s == 1:
            rows_cot = enter(after(cotangent, hidden))
        hidden, keep = layer_forward(
            grid, hidden, attn[s], ffn[s], nexts, gain_all[s], facts, (rows_cot,) if s == 1 else ()
        )
        kept.append(keep)
    outs = [leave(after(kept[1][0], hidden), 0), leave(hidden, 1)]

    def sum_ffn(terms):
        def block(m):
            return lambda yy, zz: (
                m,
                pl.ds(pl.multiple_of(yy * tall, tall), tall),
                pl.ds(pl.multiple_of(zz * units, units), units),
            )

        parts = [(cuts, [(terms, block(m), (m,))]) for m, cuts in enumerate(ffn_cuts)]
        return Scatter(grid, parts, (3, tall, units))

    def sum_attn(qkv_term, out_term):
        size = tall // 2

        def block(row, first, count):
            def at(yy, zz):
                here = (first + count * (zz % halves)) * HP
                return (
                    pl.ds(pl.multiple_of(yy * tall + row, size), size),
                    pl.ds(pl.multiple_of(here, HP), count * HP),
                )

            return at

        parts = []
        for cuts, rows_at, row in ((attn_cuts[0], upper, 0), (attn_cuts[1], lower, size)):
            parts.append(
                (
                    cuts,
                    [
                        (qkv_term, block(row, 0, 2), (rows_at, pl.ds(0, 2 * HP))),
                        (qkv_term, block(row, 2 * halves, 1), (rows_at, pl.ds(2 * HP, HP))),
                        (qkv_term, block(row, 3 * halves, 1), (rows_at, pl.ds(3 * HP, HP))),
                        (out_term, block(row, 0, 2), (rows_at, pl.ds(4 * HP, 2 * HP))),
                    ],
                )
            )
        return Scatter(grid, parts, (tall, 6 * HP), True)

    upstream = rows_cot
    gain_terms, running = [None] * 2, []
    leaving = outs[0] + outs[1]
    for s in (1, 0):
        upstream, gain_terms[s] = layer_backward(
            grid, upstream, kept[s], attn[s], ffn[s], gain_all[s], facts, running, sum_ffn, sum_attn, leaving
        )
        leaving = leave(upstream, s)
        if s == 1:
            upper_grads = leaving
    grads_in = [leaving, upper_grads]
    produced = jnp.where(at_zero, jnp.stack(outs[0]), jnp.stack(outs[1]))
    plan = Plan()
    ready = []
    for n, ring in enumerate(running):
        left = ring.left()
        ring.add(plan, 0, left, True)
        ready.append((1 - n // 2, n % 2 == 1, left - 1))
    for ring in running:
        ring.total(plan)
    ffn_own, ffn_came, attn_own, attn_came = tail_call(grid, plan, ready, depth, units)
    grads_in = jnp.where(at_zero, jnp.stack(grads_in[0]), jnp.stack(grads_in[1])).astype(f32)

    def in_order(own, came):
        return jnp.where(at_zero, own, came), jnp.where(at_zero, came, own)

    ffn_home = jnp.concatenate([half[core] for half in in_order(ffn_own, ffn_came) for core in range(C)], 2)
    ffn_home = ffn_home.astype(f32)
    sides = in_order(attn_own, attn_came)
    query_home, key_home, value_home, out_home = [
        jnp.concatenate(
            [side[:, h * HP : h * HP + HD] for side in sides for h in some], 1
        ).astype(f32)
        for some in ((0, 1), (2,), (3,), (4, 5))
    ]
    out_home = out_home.T

    gain_kept = jnp.where(at_zero, gain_terms[0], gain_terms[1])
    gain_sum = gain_kept + grid.over_x(jnp.where(at_zero, gain_terms[1], gain_terms[0]))
    for hop in grid.hops():
        gain_sum = gain_sum + grid.send(gain_sum, hop)
    share = width // (Y * C * Z)
    gain_share = lax.dynamic_slice_in_dim(gain_sum, mine * share, share, 1)[None]
    return (
        produced[None],
        grads_in[None],
        query_home[None],
        key_home[None],
        value_home[None],
        out_home[None],
        ffn_home[0][None],
        ffn_home[1][None],
        ffn_home[2].T[None],
        gain_share,
    )


def solution(mesh):
    grid = Grid(mesh)

    def run(*arguments):
        grid.calls = 0
        return body(grid, *arguments)

    return jax.shard_map(
        run,
        mesh=mesh,
        in_specs=(
            P(None, ("fsdp", "tensor"), None),
            P(None, "fsdp", None),
            P(None, ("fsdp", "tensor"), None),
            P("section", "fsdp", "tensor"),
            P("section", "fsdp", "tensor"),
            P("section", "fsdp", "tensor"),
            P("section", "tensor", "fsdp"),
            P("section", "fsdp", "tensor"),
            P("section", "fsdp", "tensor"),
            P("section", "tensor", "fsdp"),
            P("section", None, ("fsdp", "tensor")),
        ),
        out_specs=(
            P("section", None, ("fsdp", "tensor"), None),
            P("section", None, ("fsdp", "tensor"), None),
            P("section", "fsdp", "tensor"),
            P("section", "fsdp", "tensor"),
            P("section", "fsdp", "tensor"),
            P("section", "tensor", "fsdp"),
            P("section", "fsdp", "tensor"),
            P("section", "fsdp", "tensor"),
            P("section", "tensor", "fsdp"),
            P("section", None, ("fsdp", "tensor")),
        ),
        check_vma=False,
    )
```

time: 1280 us -> 930 us (0.73)
  Pallas kernels: 957 us -> 820 us
  waiting for transfers between devices: 90.7 us -> 5.28 us
  matrix products: 53.6 us -> 0 us
  starting transfers between devices: 73.4 us -> 35.9 us
  other arithmetic: 48.5 us -> 22.6 us
    pallas_call x34 -> x0, Pallas kernels: 156 us -> none  [the longest x16 72.8 us: attn_term(): pl.pallas_call(functools.partial(attn_term_kernel, halves, starts), grid_...]
    ppermute x35 -> x23, waiting for transfers between devices: 90.7 us -> 5.28 us  [send(): return lax.ppermute(block, AXES, pairs)]
    dot_general x10 -> x0, matrix products: 53.6 us -> none  [left_t_times(): lax.dot_general(a, b, (((0,), (0,)), ((), ())), preferred_element_type=f32)]
    ppermute x35 -> x23, starting transfers between devices: 73.4 us -> 35.9 us  [send(): return lax.ppermute(block, AXES, pairs)]
    pallas_call x21 -> x10, Pallas kernels: 801 us -> 820 us  [fused_call(): pl.pallas_call(whole, out_shape=tuple(outs) + tuple(plan.outs), in_specs=...]
    select_n x10 -> x3, other arithmetic: 17.7 us -> 4.42 us  [the longest x1 2.78 us: body(): produced = jnp.where(at_zero, jnp.stack(outs[0]), jnp.stack(outs[1]))]
  transfers between devices with their start and end apart: 35 -> 23, of which waited for: 9 -> 5; matrix products, arithmetic and copies ran while one was open for 9% -> 5% of each run, Pallas kernels for 64% -> 48%
where the time goes in v3:
time: 930 us; the launch traced here: 916 us
  Pallas kernels  820 us (88%)
  starting transfers between devices  35.9 us (4%)
  local copies, waits for them, and re-layouts  30.3 us (3%)
  other arithmetic  22.6 us (2%)
    pallas_call x10, Pallas kernels, fused_call(): pl.pallas_call(whole, out_shape=tuple(outs) + tuple(plan.outs), in_specs=...  820 us
    ppermute x23, starting transfers between devices, send(): return lax.ppermute(block, AXES, pairs)  35.9 us
  transfers between devices with their start and end apart: 23, of which 5 were waited for; matrix products, arithmetic and copies ran while one was open for 5% of the time, Pallas kernels for 48%

profile of v3, /device:TPU:1, one launch (start us, length us, event | category | flops | bytes accessed | tf_op | source)
XLA Modules:
  0.0 916.2 jit_solution(15356214276153646331)
XLA Ops:
  1.9 2.6 slice_bitcast_fusion.3
  7.9 2.2 slice_bitcast_fusion.16
  11.7 1.7 copy.57
  13.5 1.7 copy.59
  15.2 1.7 copy.58
  17.0 1.7 copy.60
  21.3 1.7 pad_maximum_fusion.refs_1_
  23.0 99.9 %start.1 = (bf16[768,768]{1,0:T(8,128)(2,1)}, bf16[768,768]{1,0:T(8,128)(2,1)}, bf16[3,768,256]{2,1,0:T(8,128)(2,1)}, bf16[3,768,256]{2,1,0:T(8,128)(2,1)}, bf16...) custom-call(bf16[2,384,768]{2,1,0:T(8,128)(2,1)} %pad_maximum_fusion, ...), custom_call_target="tpu_custom_call" | custom-call | flops 70000001024 | bytes 1048576 | tf_op jit(solution)/shard_map/start/pallas_call | solution.py:509
  126.5 1.9 fusion.1
  132.3 3.3 collective-permute-start.5
  136.8 1.7 collective-permute-start.6
  142.3 74.2 %attn.2 = (bf16[4,256,1536]{2,1,0:T(8,128)(2,1)}, bf16[4,4,256,128]{3,2,1,0:T(8,128)(2,1)}, bf16[2,4,256,128]{3,2,1,0:T(8,128)(2,1)}, bf16[2,4,256,128]{3,2,1,0:...) custom-call(bf16[256,1536]{1,0:T(8,128)(2,1)} %broadcast_select_fusi, ...), custom_call_target="tpu_custom_call" | custom-call | flops 60000002048 | bytes 1048576 | tf_op jit(solution)/shard_map/attn/pallas_call | solution.py:509
  216.5 86.7 %ffn.2 = (bf16[256,1536]{1,0:T(8,128)(2,1)}, bf16[4,256,1536]{2,1,0:T(8,128)(2,1)}, bf16[4,256,1024]{2,1,0:T(8,128)(2,1)}, bf16[4,256,1024]{2,1,0:T(8,128)(2,1)}...) custom-call(f32[256,1536]{1,0:T(8,128)} %get-tuple-element.107.refs_, ...), custom_call_target="tpu_custom_call" | custom-call | flops 44000002048 | bytes 1048576 | tf_op jit(solution)/shard_map/ffn/pallas_call | solution.py:509
  304.1 1.7 collective-permute-start.8
  305.8 89.3 %attn.3 = (bf16[4,256,1536]{2,1,0:T(8,128)(2,1)}, bf16[4,4,256,128]{3,2,1,0:T(8,128)(2,1)}, bf16[2,4,256,128]{3,2,1,0:T(8,128)(2,1)}, bf16[2,4,256,128]{3,2,1,0:...) custom-call(bf16[256,1536]{1,0:T(8,128)(2,1)} %get-tuple-element.135, ...), custom_call_target="tpu_custom_call" | custom-call | flops 60000002048 | bytes 1048576 | tf_op jit(solution)/shard_map/attn/pallas_call | solution.py:509
  396.1 41.2 %ffn.3 = (bf16[256,1536]{1,0:T(8,128)(2,1)}, bf16[4,256,1536]{2,1,0:T(8,128)(2,1)}, bf16[4,256,1024]{2,1,0:T(8,128)(2,1)}, bf16[4,256,1024]{2,1,0:T(8,128)(2,1)}, bf16[4,256,1024]{2,1,0:T(8,128)(2,1)}) custom-call(f32[256,1536]{1,0:T(8,128)} %get-tuple-element.126.refs_0_.refs_1_, f32[1,1536]{1,0:T(1,128)} %get-tuple-element.128.refs_1_.refs_2_, ...), custom_call_target="tpu_custom_call" | custom-call | flops 44000002048 | bytes 1048576 | tf_op jit(solution)/shard_map/ffn/pallas_call | solution.py:509
  438.6 5.7 collective-permute-start.10
  445.1 3.9 collective-permute-start.12
  449.0 54.1 %ffn_back.2 = (f32[256,1536]{1,0:T(8,128)}, f32[8,1536]{1,0:T(8,128)}, bf16[3,1536,1024]{2,1,0:T(8,128)(2,1)}) custom-call(bf16[256,1536]{1,0:T(8,128)(2,1)} %broadcast_select_fusion.2.refs_0_, f32[256,1536]{1,0:T(8,128)} %get-tuple-element.126.refs_0_.refs_1_, f32[1,1536]{1,0:T(1,128)} %get-tuple-element.128.refs_1_.refs_2_, ...), custom_call_target="tpu_custom_call" | custom-call | flops 60000002048 | bytes 1048576 | tf_op jit(solution)/shard_map/ffn_back/pallas_call | solution.py:509
  504.6 90.0 %attn_back.2 = (bf16[256,1536]{1,0:T(8,128)(2,1)}, f32[8,1536]{1,0:T(8,128)}, bf16[1536,1024]{1,0:T(8,128)(2,1)}, bf16[1536,512]{1,0:T(8,128)(2,1)}, bf16[3,768,...) custom-call(f32[256,1536]{1,0:T(8,128)} %get-tuple-element.140.refs_0_, ...), custom_call_target="tpu_custom_call" | custom-call | flops 80000000000 | bytes 1048576 | tf_op jit(solution)/shard_map/attn_back/pallas_call | solution.py:509
  595.4 3.0 collective-permute-start.14
  598.5 85.8 %ffn_back.3 = (f32[256,1536]{1,0:T(8,128)}, f32[8,1536]{1,0:T(8,128)}, bf16[3,1536,1024]{2,1,0:T(8,128)(2,1)}, bf16[3,768,256]{2,1,0:T(8,128)(2,1)}, bf16[3,768,...) custom-call(bf16[256,1536]{1,0:T(8,128)(2,1)} %get-tuple-element.149.refs_0_, ...), custom_call_target="tpu_custom_call" | custom-call | flops 60000002048 | bytes 1048576 | tf_op jit(solution)/shard_map/ffn_back/pallas_call | solution.py:509
  685.7 2.8 maximum_select_fusion
  688.5 90.3 %attn_back.3 = (bf16[256,1536]{1,0:T(8,128)(2,1)}, f32[8,1536]{1,0:T(8,128)}, bf16[1536,1024]{1,0:T(8,128)(2,1)}, bf16[1536,512]{1,0:T(8,128)(2,1)}, bf16[3,768,...) custom-call(f32[256,1536]{1,0:T(8,128)} %get-tuple-element.158.refs_0_, ...), custom_call_target="tpu_custom_call" | custom-call | flops 80000000000 | bytes 1048576 | tf_op jit(solution)/shard_map/attn_back/pallas_call | solution.py:509
  780.2 5.1 collective-permute-start.16
  785.3 108.7 %tail.1 = (bf16[2,3,384,256]{3,2,1,0:T(8,128)(2,1)}, bf16[2,3,384,256]{3,2,1,0:T(8,128)(2,1)}, bf16[384,768]{1,0:T(8,128)(2,1)}, bf16[384,768]{1,0:T(8,128)(2,1)}) custom-call(bf16[3,1536,1024]{2,1,0:T(8,128)(2,1)} %get-tuple-element.166.refs_22_.refs_0_, bf16[3,768,256]{2,1,0:T(8,128)(2,1)} %get-tuple-element.168.refs_1_, ...), custom_call_target="tpu_custom_call" | custom-call | flops 60000002048 | bytes 1048576 | tf_op jit(solution)/shard_map/tail/pallas_call | solution.py:509
  894.1 1.5 broadcast_select_fusion.5
  897.6 2.2 slice_bitcast_fusion
  902.4 1.5 collective-permute-done.20
  905.1 1.4 collective-permute-done.21
  910.4 1.6 copy.56
  912.6 3.3 fusion
  (191 shorter events, 39.9 us)
Async XLA Ops:
  1.4 5.4 copy-start.23
  1.4 123.4 %collective-permute-start.2 = (bf16[16,2,96]{2,1,0:T(2,128)(2,1)S(1)}, bf16[16,2,96]{2,1,0:T(2,128)(2,1)S(1)}, u32[]{:S(2)}, u32[]{:S(2)}) collective-permute-start(bf16[16,2,96]{2,1,0:T(2,128)(2,1)S(1)} %constant_dynamic-update-slice_fusion.1), channel_id=1, source_target_pairs={{0,4},{1,5},{2,6},{3,7},{4,0},{5,1},{6,2},{7,3},{8,12},{9,13},{10,... | collective-permute-start | bytes 18440 | tf_op jit(solution)/shard_map/ppermute | solution.py:46
  1.5 123.6 %collective-permute-start.7 = (s32[2,1,1024]{2,1,0:T(1,128)}, s32[2,1,1024]{2,1,0:T(1,128)}, u32[]{:S(2)}, u32[]{:S(2)}) collective-permute-start(s32[2,1,1024]{2,1,0:T(1,128)} %param.12), channel_id=1, source_target_pairs={{0,4},{1,5},{2,6},{3,7},{4,0},{5,1},{6,2},{7,3},{8,12},{9,13},{10,... | collective-permute-start | bytes 24584 | tf_op jit(solution)/shard_map/ppermute | solution.py:46
  4.5 136.8 %collective-permute-start.1 = (bf16[256,1536]{1,0:T(8,128)(2,1)}, bf16[256,1536]{1,0:T(8,128)(2,1)S(1)}, u32[]{:S(2)}, u32[]{:S(2)}) collective-permute-start(bf16[256,1536]{1,0:T(8,128)(2,1)} %get-tuple-element.213), channel_id=1, source_target_pairs={{0,2},{2,6},{5,3},{7,7},{8,10},{10,14},{13,11},{15,15},{17,18},{19... | collective-permute-start | bytes 2359304 | tf_op jit(solution)/shard_map/ppermute | solution.py:46
  5.4 135.9 %collective-permute-start = (bf16[256,1536]{1,0:T(8,128)(2,1)}, bf16[256,1536]{1,0:T(8,128)(2,1)S(1)}, u32[]{:S(2)}, u32[]{:S(2)}) collective-permute-start(bf16[256,1536]{1,0:T(8,128)(2,1)} %get-tuple-element.214), channel_id=1, source_target_pairs={{0,0},{2,4},{5,1},{7,5},{8,8},{10,12},{13,9},{15,13},{17,16},{19,2... | collective-permute-start | bytes 2359304 | tf_op jit(solution)/shard_map/ppermute | solution.py:46
  23.0 101.7 %copy-start.33 = (bf16[1,2,96]{2,1,0:T(2,128)(2,1)S(1)}, bf16[1,2,96]{2,1,0:T(2,128)(2,1)}, u32[]{:S(2)}) copy-start(bf16[1,2,96]{2,1,0:T(2,128)(2,1)} %param.21) | copy-start | bytes 1156
  23.0 102.0 %copy-start.32 = (s32[2,1,1024]{2,1,0:T(1,128)S(1)}, s32[2,1,1024]{2,1,0:T(1,128)}, u32[]{:S(2)}) copy-start(s32[2,1,1024]{2,1,0:T(1,128)} %param.12) | copy-start | bytes 24580
  124.7 5.0 collective-permute-start.3
  129.7 2.6 collective-permute-start.4
  132.3 4.3 collective-permute-start.5
  136.8 3.3 collective-permute-start.6
  216.5 86.8 %copy-start = (bf16[2,256,1536]{2,1,0:T(8,128)(2,1)S(1)}, bf16[2,256,1536]{2,1,0:T(8,128)(2,1)}, u32[]{:S(2)}) copy-start(bf16[2,256,1536]{2,1,0:T(8,128)(2,1)} %param.13) | copy-start | bytes 4718596
  303.4 91.7 %collective-permute-start.9 = (bf16[256,1536]{1,0:T(8,128)(2,1)S(1)}, bf16[256,1536]{1,0:T(8,128)(2,1)S(1)}, u32[]{:S(2)}, u32[]{:S(2)}) collective-permute-start(bf16[256,1536]{1,0:T(8,128)(2,1)S(1)} %get-tuple-element.211), channel_id=1, source_target_pairs={{0,2},{2,6},{5,3},{7,7},{8,10},{10,14},{13,11},{15,15},{17,18},{19... | collective-permute-start | bytes 2359304 | tf_op jit(solution)/shard_map/ppermute | solution.py:46
  304.1 91.0 %collective-permute-start.8 = (bf16[256,1536]{1,0:T(8,128)(2,1)S(1)}, bf16[256,1536]{1,0:T(8,128)(2,1)S(1)}, u32[]{:S(2)}, u32[]{:S(2)}) collective-permute-start(bf16[256,1536]{1,0:T(8,128)(2,1)S(1)} %get-tuple-element.212), channel_id=1, source_target_pairs={{0,0},{2,4},{5,1},{7,5},{8,8},{10,12},{13,9},{15,13},{17,16},{19,2... | collective-permute-start | bytes 2359304 | tf_op jit(solution)/shard_map/ppermute | solution.py:46
  437.3 67.3 %collective-permute-start.11 = (bf16[256,1536]{1,0:T(8,128)(2,1)}, bf16[256,1536]{1,0:T(8,128)(2,1)S(1)}, u32[]{:S(2)}, u32[]{:S(2)}) collective-permute-start(bf16[256,1536]{1,0:T(8,128)(2,1)} %get-tuple-element.135.refs_0_.refs_1_), channel_id=1, source_target_pairs={{2,0},{3,5},{6,2},{7,7},{10,8},{11,13},{14,10},{15,15},{18,1},{19,... | collective-permute-start | bytes 2359304 | tf_op jit(solution)/shard_map/ppermute | solution.py:46
  438.6 66.0 %collective-permute-start.10 = (bf16[256,1536]{1,0:T(8,128)(2,1)}, bf16[256,1536]{1,0:T(8,128)(2,1)S(1)}, u32[]{:S(2)}, u32[]{:S(2)}) collective-permute-start(bf16[256,1536]{1,0:T(8,128)(2,1)} %get-tuple-element.135.refs_0_.refs_1_), channel_id=1, source_target_pairs={{0,0},{1,5},{4,2},{5,7},{8,8},{9,13},{12,10},{13,15},{16,1},{17,4}... | collective-permute-start | bytes 2359304 | tf_op jit(solution)/shard_map/ppermute | solution.py:46
  444.4 60.2 %collective-permute-start.13 = (bf16[256,1536]{1,0:T(8,128)(2,1)}, bf16[256,1536]{1,0:T(8,128)(2,1)S(1)}, u32[]{:S(2)}, u32[]{:S(2)}) collective-permute-start(bf16[256,1536]{1,0:T(8,128)(2,1)} %get-tuple-element.134), channel_id=1, source_target_pairs={{2,16},{3,21},{6,18},{7,23},{10,24},{11,29},{14,26},{15,31},{18,17... | collective-permute-start | bytes 2359304 | tf_op jit(solution)/shard_map/ppermute | solution.py:46
  445.1 59.5 %collective-permute-start.12 = (bf16[256,1536]{1,0:T(8,128)(2,1)}, bf16[256,1536]{1,0:T(8,128)(2,1)S(1)}, u32[]{:S(2)}, u32[]{:S(2)}) collective-permute-start(bf16[256,1536]{1,0:T(8,128)(2,1)} %get-tuple-element.134), channel_id=1, source_target_pairs={{0,16},{1,21},{4,18},{5,23},{8,24},{9,29},{12,26},{13,31},{16,17},... | collective-permute-start | bytes 2359304 | tf_op jit(solution)/shard_map/ppermute | solution.py:46
  504.6 90.1 %copy-start.7 = (bf16[256,1536]{1,0:T(8,128)(2,1)}, bf16[256,1536]{1,0:T(8,128)(2,1)S(1)}, u32[]{:S(2)}) copy-start(bf16[256,1536]{1,0:T(8,128)(2,1)S(1)} %collective-permute-done.13) | copy-start | bytes 2359300
  504.6 90.1 %copy-start.8 = (bf16[256,1536]{1,0:T(8,128)(2,1)}, bf16[256,1536]{1,0:T(8,128)(2,1)S(1)}, u32[]{:S(2)}) copy-start(bf16[256,1536]{1,0:T(8,128)(2,1)S(1)} %collective-permute-done.12) | copy-start | bytes 2359300
  594.7 93.9 %collective-permute-start.15 = (bf16[256,1536]{1,0:T(8,128)(2,1)}, bf16[256,1536]{1,0:T(8,128)(2,1)S(1)}, u32[]{:S(2)}, u32[]{:S(2)}) collective-permute-start(bf16[256,1536]{1,0:T(8,128)(2,1)} %get-tuple-element.149.refs_0_), channel_id=1, source_target_pairs={{2,16},{3,21},{6,18},{7,23},{10,24},{11,29},{14,26},{15,31},{18,17... | collective-permute-start | bytes 2359304 | tf_op jit(solution)/shard_map/ppermute | solution.py:46
  595.4 93.1 %collective-permute-start.14 = (bf16[256,1536]{1,0:T(8,128)(2,1)}, bf16[256,1536]{1,0:T(8,128)(2,1)S(1)}, u32[]{:S(2)}, u32[]{:S(2)}) collective-permute-start(bf16[256,1536]{1,0:T(8,128)(2,1)} %get-tuple-element.149.refs_0_), channel_id=1, source_target_pairs={{0,16},{1,21},{4,18},{5,23},{8,24},{9,29},{12,26},{13,31},{16,17},... | collective-permute-start | bytes 2359304 | tf_op jit(solution)/shard_map/ppermute | solution.py:46
  598.4 86.7 %copy-start.31 = (f32[8,1536]{1,0:T(8,128)S(1)}, f32[8,1536]{1,0:T(8,128)}, u32[]{:S(2)}) copy-start(f32[8,1536]{1,0:T(8,128)} %get-tuple-element.182) | copy-start | bytes 147460
  688.5 90.3 %copy-start.3 = (bf16[256,1536]{1,0:T(8,128)(2,1)}, bf16[256,1536]{1,0:T(8,128)(2,1)S(1)}, u32[]{:S(2)}) copy-start(bf16[256,1536]{1,0:T(8,128)(2,1)S(1)} %collective-permute-done.15) | copy-start | bytes 2359300
  688.5 90.3 %copy-start.5 = (bf16[256,1536]{1,0:T(8,128)(2,1)}, bf16[256,1536]{1,0:T(8,128)(2,1)S(1)}, u32[]{:S(2)}) copy-start(bf16[256,1536]{1,0:T(8,128)(2,1)S(1)} %collective-permute-done.14) | copy-start | bytes 2359300
  778.9 133.8 %collective-permute-start.17 = (bf16[256,1536]{1,0:T(8,128)(2,1)}, bf16[256,1536]{1,0:T(8,128)(2,1)}, u32[]{:S(2)}, u32[]{:S(2)}) collective-permute-start(bf16[256,1536]{1,0:T(8,128)(2,1)} %get-tuple-element.167), channel_id=1, source_target_pairs={{2,0},{3,5},{6,2},{7,7},{10,8},{11,13},{14,10},{15,15},{18,1},{19,... | collective-permute-start | bytes 2359304 | tf_op jit(solution)/shard_map/ppermute | solution.py:46
  780.2 132.5 %collective-permute-start.16 = (bf16[256,1536]{1,0:T(8,128)(2,1)}, bf16[256,1536]{1,0:T(8,128)(2,1)}, u32[]{:S(2)}, u32[]{:S(2)}) collective-permute-start(bf16[256,1536]{1,0:T(8,128)(2,1)} %get-tuple-element.167), channel_id=1, source_target_pairs={{0,0},{1,5},{4,2},{5,7},{8,8},{9,13},{12,10},{13,15},{16,1},{17,4}... | collective-permute-start | bytes 2359304 | tf_op jit(solution)/shard_map/ppermute | solution.py:46
  896.5 3.4 collective-permute-start.18
  900.0 1.2 collective-permute-start.19
  901.2 2.6 collective-permute-start.20
  903.9 2.6 collective-permute-start.21
  906.5 5.5 collective-permute-start.22
  (25 other events, 56.4 us)

commit v4 on v3

--- a/solution.py
+++ b/solution.py
@@ -10,6 +10,7 @@
 HD = 96
 HP = 128
 NEVER = -1e30
+BLOCK = 4 * HD + 2 * HP
 epsilon = 1e-05
 rope_base = 100000.0
 AXES = ("section", "fsdp", "tensor")
@@ -51,14 +52,6 @@
     def over_c(self, block):
         return self.send(block, lambda x, y, c, z: (x, y, 1 - c, z))
 
-    def hops(self):
-        routes = [lambda x, y, c, z: (x, y, 1 - c, z)]
-        for bit in range((self.Y - 1).bit_length()):
-            routes.append(lambda x, y, c, z, bit=bit: (x, y ^ (1 << bit), c, z))
-        for bit in range((self.Z - 1).bit_length()):
-            routes.append(lambda x, y, c, z, bit=bit: (x, y, c, z ^ (1 << bit)))
-        return routes
-
     def place_of(self, p):
         p = p % self.R
         y, k = p // self.Z, p % self.Z
@@ -122,15 +115,37 @@
     )
 
 
-def greet(grid, sides, cycle):
-    others = list(partners(grid)[:sides])
+def doubling(grid):
+    _, y, c, z = grid.me()
+    found = []
+    for bit in range((grid.Y - 1).bit_length()):
+        step = 1 << bit
+        found.append({"fsdp": (y + step * (1 - 2 * ((y // step) % 2))) * grid.C + c})
+    for bit in range((grid.Z - 1).bit_length()):
+        step = 1 << bit
+        found.append({"tensor": z + step * (1 - 2 * ((z // step) % 2))})
+    return found
+
+
+def greet(grid, sides, cycle, more=(), meanwhile=lambda: None):
+    others = list(partners(grid)[:sides]) + list(more)
     if cycle:
         others += [grid.neighbour(1), grid.neighbour(-1)]
     barrier = pltpu.get_barrier_semaphore()
     for other in others:
         pl.semaphore_signal(barrier, inc=1, device_id=other, device_id_type=MESH)
+    meanwhile()
     pl.semaphore_wait(barrier, len(others))
     return partners(grid)
+
+
+def sum_over(table, land, sems, others):
+    for n, other in enumerate(others):
+        copy = remote(table.at[n], land.at[n], sems, n, other)
+        copy.start()
+        copy.wait()
+        table[n + 1] = table[n] + land[n]
+        yield n
 
 
 def remote(src, dst, sems, n, device):
@@ -520,6 +535,14 @@
     return results[:c]
 
 
+def load(sources, places, sems):
+    copies = [
+        pltpu.make_async_copy(src, dst, sems.at[n]) for n, (src, dst) in enumerate(zip(sources, places))
+    ]
+    start_all(copies)
+    return copies
+
+
 class Spread:
     sems = pltpu.SemaphoreType.DMA((2, 1 + 2 * PARTS))
 
@@ -630,21 +653,20 @@
     pieces = refs[: len(offsets)]
     (
         all_ref, q_ref, k_ref, v_ref, mid_ref, mixed_ref, lse_ref,
-        held, w_sems, wo_ref, wo_sems, rows_ref, s_sems, out_sem, top, total, acc, part, hold, c_sems,
+        stage, w_sems, held, wo_ref, rows_ref, s_sems, out_sem, top, total, acc, part, hold, c_sems,
     ) = refs[len(offsets) :]
     rows = h_ref.shape[0]
     halves = heads // 2
     scale = HD ** (-0.5)
     ids = place_id(grid)
     background.begin()
-    fetched = fetch_attn(grid, offsets, pieces, held, None, w_sems)
-    fetched_out = fetch_attn(grid, offsets, pieces, None, wo_ref, wo_sems)
+    fetched = fetch_attn(grid, offsets, pieces, stage, w_sems)
     sib, over, _ = greet(grid, 2, cycle)
     rows_ref[0] = normed_rows(h_ref[...].astype(f32), gain_ref[...]).astype(bf16)
     spread = Spread(rows_ref, s_sems, sib, over)
     spread.start()
     background.advance()
-    end_fetch(fetched)
+    end_fetch(grid, fetched, stage, held, wo_ref)
 
     def work(slot, start, size):
         cosine, sine_part = cos_ref[slot, start : start + size], sin_ref[slot, start : start + size]
@@ -671,7 +693,6 @@
         work(3, k * size, size)
     out = pltpu.make_async_copy(rows_ref, all_ref, out_sem)
     out.start()
-    end_fetch(fetched_out)
     collect = Collect(hold, c_sems, sib, over)
 
     def attend(i):
@@ -747,8 +768,7 @@
         ),
         (ANY,) + (VMEM,) * 6,
         [
-            pltpu.VMEM((width, 4 * halves * HP), bf16), fetch_sems(found),
-            pltpu.VMEM((width, heads * HP), bf16), fetch_sems(found),
+            *attn_weights(grid, found, width),
             pltpu.VMEM((4, rows, width), bf16), Spread.sems, pltpu.SemaphoreType.DMA,
             pltpu.VMEM((heads, rows, 1), f32),
             pltpu.VMEM((heads, rows, 1), f32),
@@ -760,45 +780,45 @@
     )
 
 
-def fetch_attn(grid, offsets, pieces, qkv, out, sems):
+def fetch_attn(grid, offsets, pieces, stage, sems):
     pos = grid.my_pos()
     core = lax.axis_index("fsdp") % grid.C
     halves = grid.Z // 2
-    tall = pieces[0].shape[0]
     fetched = []
     for i, offset in enumerate(offsets):
         yy, zz = grid.dyn_place(pos + offset)
-        j = zz % halves
-        rows = pl.ds(pl.multiple_of(yy * tall, tall), tall)
-
-        def copy(n, first, width, ref, at):
-            return pltpu.make_async_copy(
-                pieces[i].at[:, pl.ds(first * HP, width * HP)],
-                ref.at[rows, pl.ds(pl.multiple_of(at * HP, HP), width * HP)],
-                sems.at[i, n],
-            )
-
-        if out is None:
-            copies = [
-                copy(0, 0, 2, qkv, 2 * j),
-                copy(1, 2, 1, qkv, 2 * halves + j),
-                copy(2, 3, 1, qkv, 3 * halves + j),
-            ]
-        else:
-            copies = [copy(0, 4, 2, out, 2 * j)]
+        copy = pltpu.make_async_copy(pieces[i], stage.at[yy * halves + zz % halves], sems.at[i])
         live = zz // halves == core
-        pl.when(live)(functools.partial(start_all, copies))
-        fetched.append((live, copies))
+        pl.when(live)(copy.start)
+        fetched.append((live, copy))
     return fetched
 
 
-def end_fetch(fetched):
-    for live, copies in fetched:
-        pl.when(live)(functools.partial(wait_all, copies))
-
-
-def fetch_sems(found):
-    return pltpu.SemaphoreType.DMA((len(found), 3))
+def end_fetch(grid, fetched, stage, qkv, out):
+    for live, copy in fetched:
+        pl.when(live)(copy.wait)
+    halves = grid.Z // 2
+    tall = stage.shape[1]
+    blank = jnp.zeros((tall, HP - HD), bf16)
+    for yy in range(grid.Y):
+        rows = slice(yy * tall, (yy + 1) * tall)
+        for j in range(halves):
+            block = stage.at[yy * halves + j]
+            places = [(qkv, 2 * j), (qkv, 2 * j + 1), (qkv, 2 * halves + j), (qkv, 3 * halves + j)]
+            places += [(out, 2 * j), (out, 2 * j + 1)]
+            for n, (ref, at) in enumerate(places):
+                head = block[:, n * HD : (n + 1) * HD]
+                ref[rows, at * HP : (at + 1) * HP] = jnp.concatenate([head, blank], 1)
+
+
+def attn_weights(grid, found, width):
+    tall, halves = found[0][1].shape[0], grid.Z // 2
+    return [
+        pltpu.VMEM((grid.Y * halves, tall, BLOCK), bf16),
+        pltpu.SemaphoreType.DMA((len(found),)),
+        pltpu.VMEM((width, 4 * halves * HP), bf16),
+        pltpu.VMEM((width, 2 * halves * HP), bf16),
+    ]
 
 
 def apart(found):
@@ -831,11 +851,19 @@
     count = len(offsets)
     pieces = refs[:count]
     (
-        out_ref, all_ref, gate_ref, up_ref, hid_ref,
+        out_ref, all_ref, *stored,
         held, w_sems, rows_ref, s_sems, part, own, hold, c_sems, out_sem,
+        gate_ref, up_ref, hid_ref, g_sems,
     ) = refs[count:]
     rows, width = mid_ref.shape
     hidden = gate_ref.shape[2]
+    writes = []
+
+    def store(slot):
+        for n, (src, dst) in enumerate(zip((gate_ref, up_ref, hid_ref), stored)):
+            writes.append(pltpu.make_async_copy(src.at[slot], dst.at[slot], g_sems.at[n, slot]))
+            writes[-1].start()
+
     background.begin()
     fetched = fetch_ffn(grid, offsets, pieces, held, w_sems)
     sib, over, _ = greet(grid, 2, cycle)
@@ -870,9 +898,11 @@
         lax.fori_loop(0, width // STEP, tile_down, 0)
 
     work(0, 0, rows)
+    store(0)
     own[...] = mid_ref[...] + part[...]
     spread.near.wait_recv()
     work(1, 0, rows)
+    store(1)
     collect.give_near(part[...])
     cuts = pieces_of(rows)
     size = rows // PARTS
@@ -885,11 +915,14 @@
         collect.give_side(k, part[cuts[k]])
         work(2, k * size, size)
         collect.give_over(k, part[cuts[k]])
+    store(2)
+    store(3)
     background.advance()
     out = pltpu.make_async_copy(rows_ref, all_ref, out_sem)
     out.start()
     out_ref[...] = collect.finish(own[...]).astype(bf16)
     out.wait()
+    wait_all(writes)
     spread.end()
     collect.end()
     background.finish()
@@ -903,7 +936,7 @@
         grid, functools.partial(ffn_kernel, grid, offsets), "ffn", plan,
         (middle, gain_row, *blocks), [VMEM] * 2 + [ANY] * len(blocks),
         shaped(((rows, width), bf16), ((4, rows, width), bf16), *[((4, rows, hidden), bf16)] * 3),
-        (VMEM, ANY, VMEM, VMEM, VMEM),
+        (VMEM,) + (ANY,) * 4,
         [
             pltpu.VMEM((3, width, hidden), bf16),
             pltpu.SemaphoreType.DMA((len(blocks),)),
@@ -913,7 +946,9 @@
             pltpu.VMEM((rows, width), f32),
         ]
         + Collect.scratch(rows, width)
-        + [pltpu.SemaphoreType.DMA],
+        + [pltpu.SemaphoreType.DMA]
+        + [pltpu.VMEM((4, rows, hidden), bf16)] * 3
+        + [pltpu.SemaphoreType.DMA((3, 4))],
         44,
     )
 
@@ -934,16 +969,18 @@
 
 
 def ffn_back_kernel(
-    grid, offsets, background, cycle, g_ref, mid_ref, gain_ref, gate_ref, up_ref, hid_ref, whole_ref, *refs
+    grid, offsets, background, cycle, g_ref, mid_ref, gain_ref, *refs
 ):
     count = len(offsets)
-    pieces = refs[:count]
+    sources, pieces = refs[:4], refs[4 : 4 + count]
     (
         out_ref, gains_ref, terms_ref,
         held, w_sems, rows_ref, s_sems, dgate_ref, dup_ref, part, own, hold, c_sems, out_sems,
-    ) = refs[count:]
+        gate_ref, up_ref, hid_ref, whole_ref, in_sems,
+    ) = refs[4 + count :]
     rows, width = mid_ref.shape
     hidden = gate_ref.shape[2]
+    loads = load(sources, (gate_ref, up_ref, hid_ref, whole_ref), in_sems)
     background.begin()
     fetched = fetch_ffn(grid, offsets, pieces, held, w_sems)
     sib, over, _ = greet(grid, 2, cycle)
@@ -952,7 +989,7 @@
     collect = Collect(hold, c_sems, sib, over)
     spread.start()
     background.advance()
-    wait_all(fetched)
+    wait_all(fetched + loads[:2])
 
     def work(slot, start, size):
         at = pl.ds(start, size)
@@ -994,6 +1031,7 @@
         collect.give_side(k, part[cuts[k]])
         work(2, k * size, size)
         collect.give_over(k, part[cuts[k]])
+    wait_all(loads[2:])
     outs = []
     for m, (left, right) in enumerate(
         ((rows_ref, hid_ref), (whole_ref, dgate_ref), (whole_ref, dup_ref))
@@ -1022,7 +1060,7 @@
     return fused_call(
         grid, functools.partial(ffn_back_kernel, grid, offsets), "ffn_back", plan,
         (grad_out, middle, gain_row, gate, up, hidden_low, whole, *blocks),
-        [VMEM] * 7 + [ANY] * len(blocks),
+        [VMEM] * 3 + [ANY] * (4 + len(blocks)),
         shaped(((rows, width), f32), ((8, width), f32), ((3, width, hidden), bf16)),
         (VMEM, VMEM, ANY),
         [
@@ -1036,34 +1074,37 @@
             pltpu.VMEM((rows, width), f32),
         ]
         + Collect.scratch(rows, width)
-        + [pltpu.SemaphoreType.DMA((3,))],
+        + [pltpu.SemaphoreType.DMA((3,))]
+        + [pltpu.VMEM((4, rows, hidden), bf16)] * 3
+        + [pltpu.VMEM((4, rows, width), bf16), pltpu.SemaphoreType.DMA((4,))],
         60,
     )
 
 
 def attn_back_kernel(
-    grid, heads, offsets, background, cycle, g_ref, h_ref, gain_ref, cos_ref, sin_ref, q_ref, k_ref,
-    v_ref, m_ref, l_ref, tokc_ref, tokr_ref, from_ref, whole_ref, *refs,
+    grid, heads, offsets, background, cycle, g_ref, h_ref, gain_ref, l_ref, tokc_ref, tokr_ref,
+    from_ref, *refs,
 ):
-    pieces = refs[: len(offsets)]
+    sources, pieces = refs[:7], refs[7 : 7 + len(offsets)]
     (
         out_ref, gains_ref, qkv_term, out_term,
-        held, w_sems, wo_ref, wo_sems, rows_ref, s_sems, gm_ref, dqkv_ref,
+        stage, w_sems, held, wo_ref, rows_ref, s_sems, gm_ref, dqkv_ref, low_ref, low_m,
         key_sum, value_sum, query_sum, delta, part, hold, c_sems,
-    ) = refs[len(offsets) :]
+        q_ref, k_ref, v_ref, m_ref, cos_ref, sin_ref, whole_ref, in_sems,
+    ) = refs[7 + len(offsets) :]
     rows = g_ref.shape[0]
     pairs = heads // 2
     scale = HD ** (-0.5)
     ids = place_id(grid)
     background.begin()
-    fetched_out = fetch_attn(grid, offsets, pieces, None, wo_ref, wo_sems)
-    fetched = fetch_attn(grid, offsets, pieces, held, None, w_sems)
+    fetched = fetch_attn(grid, offsets, pieces, stage, w_sems)
+    loads = load(sources, (q_ref, k_ref, v_ref, m_ref, cos_ref, sin_ref, whole_ref), in_sems)
     sib, over, _ = greet(grid, 2, cycle)
     rows_ref[0] = g_ref[...].astype(bf16)
     spread = Spread(rows_ref, s_sems, sib, over)
     spread.start()
     background.advance()
-    end_fetch(fetched_out)
+    end_fetch(grid, fetched, stage, held, wo_ref)
 
     def work(slot, start, size):
         at = slice(start, start + size)
@@ -1106,6 +1147,7 @@
     work(0, 0, rows)
     spread.near.wait_recv()
     work(1, 0, rows)
+    wait_all(loads[:4])
     attend_back(0)
     attend_back(1)
     size = rows // PARTS
@@ -1124,16 +1166,19 @@
 
     collect = Collect(hold, c_sems, sib, over)
     cuts = pieces_of(rows)
-    end_fetch(fetched)
+    wait_all(loads[4:])
 
     def work_back(i):
-        for h in range(heads):
-            dqkv_ref[i, :, h * HP : (h + 1) * HP] = back(query_sum[h, i], i)
-        for h in range(pairs):
-            at = heads + h
-            dqkv_ref[i, :, at * HP : (at + 1) * HP] = back(key_sum[h, i], i)
-            at = heads + pairs + h
-            dqkv_ref[i, :, at * HP : (at + 1) * HP] = value_sum[h, i].astype(bf16)
+        for at in range(2 * heads):
+            if at < heads:
+                made, low = back(query_sum[at, i], i), at // 2 * 4 + at % 2
+            elif at < heads + pairs:
+                made, low = back(key_sum[at - heads, i], i), (at - heads) * 4 + 2
+            else:
+                h = at - heads - pairs
+                made, low = value_sum[h, i].astype(bf16), h * 4 + 3
+            dqkv_ref[i, :, at * HP : (at + 1) * HP] = made
+            low_ref[i, :, low * HD : (low + 1) * HD] = made[:, :HD]
         part[...] = dot_nt(dqkv_ref[i], held[...])
 
     work_back(3)
@@ -1146,8 +1191,13 @@
     work_back(1)
     collect.give_near(part[...])
     work_back(0)
-    weight_terms(out_term, rows_ref, m_ref)
-    weight_terms(qkv_term, whole_ref, dqkv_ref)
+    low_m[...] = jnp.zeros_like(low_m)
+    for i in range(4):
+        for h in range(heads):
+            at = h // 2 * 2 * HP + h % 2 * HD
+            low_m[i, :, at : at + HD] = m_ref[i, :, h * HP : h * HP + HD]
+    weight_terms(out_term, rows_ref, low_m)
+    weight_terms(qkv_term, whole_ref, low_ref)
     grad, gains = norm_back(h_ref[...].astype(f32), gain_ref[...], collect.finish(part[...]))
     out_ref[...] = (g_ref[...] + grad).astype(bf16)
     gains_ref[...] = gains
@@ -1166,41 +1216,68 @@
     return fused_call(
         grid, functools.partial(attn_back_kernel, grid, heads, offsets), "attn_back", plan,
         (
-            grad_middle, hidden, gain_row, facts["cos"], facts["sin"], query, keys, values, mixed, lse,
-            facts["tok"][:, :, None], facts["tok"][:, None, :], facts["from"][:, None, :], whole,
+            grad_middle, hidden, gain_row, lse, facts["tok"][:, :, None], facts["tok"][:, None, :],
+            facts["from"][:, None, :], query, keys, values, mixed, facts["cos"], facts["sin"], whole,
             *blocks,
         ),
-        [VMEM] * 14 + [ANY] * len(blocks),
+        [VMEM] * 7 + [ANY] * (7 + len(blocks)),
         shaped(
-            ((rows, width), bf16), ((8, width), f32), ((width, 2 * heads * HP), bf16),
+            ((rows, width), bf16), ((8, width), f32), ((width, 2 * heads * HD), bf16),
             ((width, heads * HP), bf16),
         ),
         (VMEM,) * 4,
         [
-            pltpu.VMEM((width, 2 * heads * HP), bf16), fetch_sems(found),
-            pltpu.VMEM((width, heads * HP), bf16), fetch_sems(found),
+            *attn_weights(grid, found, width),
             pltpu.VMEM((4, rows, width), bf16), Spread.sems,
             pltpu.VMEM((heads, 4, rows, HP), bf16),
             pltpu.VMEM((4, rows, 2 * heads * HP), bf16),
+            pltpu.VMEM((4, rows, 2 * heads * HD), bf16),
+            pltpu.VMEM((4, rows, heads * HP), bf16),
             pltpu.VMEM((pairs, 4, rows, HP), f32),
             pltpu.VMEM((pairs, 4, rows, HP), f32),
             pltpu.VMEM((heads, 4, rows, HP), f32),
             pltpu.VMEM((heads, 8, rows), f32),
             pltpu.VMEM((rows, width), f32),
         ]
-        + Collect.scratch(rows, width),
+        + Collect.scratch(rows, width)
+        + [
+            pltpu.VMEM((heads, 4, rows, HP), bf16),
+            pltpu.VMEM((pairs, 4, rows, HP), bf16),
+            pltpu.VMEM((pairs, 4, rows, HP), bf16),
+            pltpu.VMEM((4, rows, heads * HP), bf16),
+            pltpu.VMEM((4, rows, HP), f32),
+            pltpu.VMEM((4, rows, HP), f32),
+            pltpu.VMEM((4, rows, width), bf16),
+            pltpu.SemaphoreType.DMA((7,)),
+        ],
         80,
     )
 
 
-def start_kernel(grid, joins, early, background, cycle, attn_ref, ffn_ref, sems, local):
-    x, _, c, z = grid.me()
+def start_kernel(
+    grid, joins, early, background, cycle, wq, wk, wv, wo, wg, wu, wd, gains_ref, all_gains,
+    attn_ref, ffn_ref, sems, local, table, land, t_sems,
+):
+    x, y, c, z = grid.me()
     mine = z // (grid.Z // 2) == c
     attn_to = [background.refs[h[0]][h[1]] for h in joins[0]]
     ffn_to = [background.refs[h[0]][h[1]] for h in joins[1]]
     depth = attn_ref.shape[1]
+    units = ffn_ref.shape[3]
     rows = pl.ds(pl.multiple_of(c * depth, depth), depth)
-    sib, over, diag = greet(grid, 3, cycle)
+
+    def pack():
+        for side in range(2):
+            heads = [wq[0, :, 2 * side * HD : 2 * (side + 1) * HD]]
+            heads += [ref[0, :, side * HD : (side + 1) * HD] for ref in (wk, wv)]
+            heads.append(
+                jnp.transpose(wo[0, 2 * side * HD : 2 * (side + 1) * HD].astype(f32)).astype(bf16)
+            )
+            heads.append(jnp.zeros((depth, BLOCK - 6 * HD), bf16))
+            attn_ref[side] = jnp.concatenate(heads, 1)
+
+    others = doubling(grid)
+    sib, over, diag = greet(grid, 3, cycle, others, pack)
     everything = []
     for layer in range(2):
         to = attn_to[layer].at[rows]
@@ -1225,14 +1302,20 @@
             for condition, copy in moves:
                 pl.when(condition)(copy.start)
 
+    for q in range(4):
+        cols = slice(q * units, (q + 1) * units)
+        ffn_ref[q, 0] = wg[0, :, cols]
+        ffn_ref[q, 1] = wu[0, :, cols]
+        ffn_ref[q, 2] = jnp.transpose(wd[0, cols].astype(f32)).astype(bf16)
+
     (own, to_sib, to_over, to_diag), parts = [copy for _, copy in moves], parts
 
     @pl.when(mine)
     def _():
+        for copy in (to_sib, to_over, to_diag):
+            copy.wait_recv()
         own.wait()
         to_over.wait_send()
-        for copy in (to_sib, to_over, to_diag):
-            copy.wait_recv()
 
     @pl.when(~mine)
     def _():
@@ -1242,22 +1325,54 @@
     background.advance()
     for layer in range(2):
         pl.when(x == layer)(functools.partial(start_all, everything[layer][1]))
+    shares = grid.Y * grid.C * grid.Z
+    share = gains_ref.shape[2]
+    table[0] = jnp.zeros_like(table[0])
+    padded = jnp.concatenate([gains_ref[0].astype(f32), jnp.zeros((2, HP - share), f32)], 1)
+    table[0, (y * grid.C + c) * grid.Z + z, :2, :] = padded
+    for n in sum_over(table, land, t_sems, [sib] + others):
+        if n % 2 == 1 and early:
+            background.advance()
+            early -= 1
+    last = len(others) + 1
+    copy = remote(table.at[last], land.at[last], t_sems, last, over)
+    copy.start()
+    copy.wait()
+    for p in range(shares):
+        own, other = table[last, p, :2, :share], land[last, p, :2, :share]
+        at = slice(p * share, (p + 1) * share)
+        all_gains[0, :, at] = jnp.where(x == 0, own, other)
+        all_gains[1, :, at] = jnp.where(x == 0, other, own)
     for n in range(early):
         background.advance()
     wait_all(parts)
     background.finish()
 
 
-def start_call(grid, plan, joins, early, attn_pack, ffn_pack):
-    fused_call(
+def start_call(grid, plan, joins, early, shards, gains):
+    depth, width = shards[0].shape[1], grid.Y * grid.C * shards[0].shape[1]
+    units = shards[4].shape[2] // 4
+    hops = len(doubling(grid)) + 1
+    table = (hops + 1, grid.Y * grid.C * grid.Z, 8, HP)
+    return fused_call(
         grid, functools.partial(start_kernel, grid, joins, early), "start", plan,
-        (attn_pack, ffn_pack), [ANY] * 2, (), (),
-        [pltpu.SemaphoreType.DMA((2, 6)), pltpu.SemaphoreType.DMA((2,))], 70,
-    )
+        (*shards, gains), [VMEM] * 8, shaped(((2, 2, width), f32)), (VMEM,),
+        [
+            pltpu.VMEM((2, depth, BLOCK), bf16),
+            pltpu.VMEM((4, 3, depth, units), bf16),
+            pltpu.SemaphoreType.DMA((2, 6)),
+            pltpu.SemaphoreType.DMA((2,)),
+            pltpu.VMEM(table, f32),
+            pltpu.VMEM(table, f32),
+            pltpu.SemaphoreType.DMA((2, hops + 1)),
+        ],
+        70,
+    )[0]
 
 
 def tail_kernel(
-    grid, ready, background, cycle, ffn_own, ffn_came, attn_own, attn_came, sems, local
+    grid, ready, background, cycle, one_0, two_0, one_1, two_1, ffn_own, ffn_came, attn_own, attn_came,
+    gain_out, sems, local, table, land, t_sems,
 ):
     x, _, c, z = grid.me()
     mine = z // (grid.Z // 2) == c
@@ -1265,8 +1380,14 @@
     rows = pl.ds(pl.multiple_of(c * depth, depth), depth)
     other = pl.ds(pl.multiple_of((1 - c) * depth, depth), depth)
     background.begin()
-    sib, over, diag = greet(grid, 3, cycle)
+    others = doubling(grid)
+    sib, over, diag = greet(grid, 3, cycle, others)
     background.advance()
+    table[0] = jnp.concatenate(
+        [jnp.sum(ref[...], 0, keepdims=True) for ref in (one_0, two_0, one_1, two_1)]
+        + [jnp.zeros((4, table.shape[2]), f32)],
+        0,
+    )
 
     def home(n, layer, heads):
         term, parts, alive = background.totals[n]
@@ -1306,14 +1427,20 @@
 
     done = {}
     waiting = list(enumerate(ready))
+    hops = sum_over(table, land, t_sems, [over, sib] + others)
     while waiting or background.now < len(background.stages):
         for n, (layer, heads, stage) in list(waiting):
             if stage < background.now:
                 background.arrived(stage)
                 done[heads] = home(n, layer, heads)
                 waiting.remove((n, (layer, heads, stage)))
+        next(hops, None)
+        next(hops, None)
         if background.now < len(background.stages):
             background.advance()
+    for _ in hops:
+        pass
+    gain_out[...] = table[len(others) + 2]
     background.finish()
     stay, moves = done[False]
     stay.wait()
@@ -1334,12 +1461,68 @@
         moves[2].wait_recv()
 
 
-def tail_call(grid, plan, ready, depth, units):
+def tail_call(grid, plan, ready, gain_rows, depth, units):
+    width = gain_rows[0].shape[1]
+    hops = len(doubling(grid)) + 2
+    table = (hops + 1, 8, width)
     return fused_call(
-        grid, functools.partial(tail_kernel, grid, ready), "tail", plan, (), (),
-        shaped(*[((2, 3, depth, units), bf16)] * 2, *[((depth, 6 * HP), bf16)] * 2), (ANY,) * 4,
-        [pltpu.SemaphoreType.DMA((2, 6)), pltpu.SemaphoreType.DMA((2,))], 60,
+        grid, functools.partial(tail_kernel, grid, ready), "tail", plan, gain_rows, [VMEM] * 4,
+        shaped(
+            *[((2, 3, depth, units), bf16)] * 2, *[((depth, BLOCK), bf16)] * 2, ((8, width), f32)
+        ),
+        (ANY,) * 4 + (VMEM,),
+        [
+            pltpu.SemaphoreType.DMA((2, 6)),
+            pltpu.SemaphoreType.DMA((2,)),
+            pltpu.VMEM(table, f32),
+            pltpu.VMEM(table, f32),
+            pltpu.SemaphoreType.DMA((2, hops)),
+        ],
+        60,
     )
+
+
+def finish_kernel(
+    ffn_own, ffn_came, attn_own, attn_came, query, key, value, out, gate, up, down
+):
+    x = lax.axis_index("section")
+    units = ffn_own.shape[3]
+
+    def put(side, ffn_ref, attn_ref):
+        for core in range(2):
+            at = slice((2 * side + core) * units, (2 * side + core + 1) * units)
+            gate[:, at] = ffn_ref[core, 0].astype(f32)
+            up[:, at] = ffn_ref[core, 1].astype(f32)
+            down[at] = jnp.transpose(ffn_ref[core, 2].astype(f32))
+
+        def head(n):
+            return attn_ref[:, n * HD : (n + 1) * HD].astype(f32)
+
+        for h in range(2):
+            at = slice((2 * side + h) * HD, (2 * side + h + 1) * HD)
+            query[:, at] = head(h)
+            out[at] = jnp.transpose(head(4 + h))
+        key[:, side * HD : (side + 1) * HD] = head(2)
+        value[:, side * HD : (side + 1) * HD] = head(3)
+
+    for layer in range(2):
+
+        @pl.when(x == layer)
+        def _():
+            put(layer, ffn_own, attn_own)
+            put(1 - layer, ffn_came, attn_came)
+
+
+def finish_call(blocks, shards):
+    return pl.pallas_call(
+        finish_kernel,
+        out_shape=tuple(jax.ShapeDtypeStruct(shard.shape[1:], f32) for shard in shards),
+        in_specs=[VMEM] * 4,
+        out_specs=(VMEM,) * 7,
+        compiler_params=params(),
+        cost_estimate=cost(6),
+        name="finish",
+    )(*blocks)
 
 
 def turning(doc_row):
@@ -1363,7 +1546,7 @@
     return lax.optimization_barrier((value,) + others)[0]
 
 
-def layer_forward(grid, hidden_in, attn, ffn, nexts, gain_pair, facts, before_ffn):
+def layer_forward(grid, hidden_in, attn, ffn, nexts, gain_pair, facts):
     plan = Plan()
     ffn.add(plan, 0)
     whole, query, keys, values, middle, mixed, lse = attn_call(
@@ -1373,9 +1556,7 @@
     if nexts:
         nexts[0].add(plan, 0)
         nexts[1].add(plan, max(0, len(plan.stages) - 2), 1)
-    result, whole2, gate, up, hidden = ffn_call(
-        grid, plan, middle, after(gain_pair[1:2], *before_ffn), ffn.found
-    )
+    result, whole2, gate, up, hidden = ffn_call(grid, plan, middle, gain_pair[1:2], ffn.found)
     kept = (hidden_in, (whole, query, keys, values, mixed, lse), middle, whole2, gate, up, hidden)
     return result, kept
 
@@ -1396,8 +1577,7 @@
         grid, plan, grad_middle, hidden_in, after(gain_pair[0:1], *leaving), facts, kept_attn, attn.found
     )
     running.append(sum_attn(qkv_term, out_term))
-    gains = jnp.stack([jnp.sum(gain_one, 0), jnp.sum(gain_two, 0)])
-    return grad_input, gains
+    return grad_input, (gain_one, gain_two)
 
 
 def body(grid, inputs, doc_ids, cotangent, wq, wk, wv, wo, wg, wu, wd, gains):
@@ -1451,64 +1631,29 @@
         "sin": in_my_order(sine_part),
     }
 
-    mine = (y * C + c) * Z + z
-    table = lax.dynamic_update_slice(
-        jnp.zeros((Y * C * Z,) + gains.shape[1:], bf16), gains, (mine, 0, 0)
-    )
-    for hop in grid.hops():
-        table = table + grid.send(table, hop)
-    gain_own = table.transpose(1, 0, 2).reshape(2, width)
-    gain_other = grid.over_x(gain_own)
-    gain_all = [
-        jnp.where(at_zero, gain_own, gain_other).astype(f32),
-        jnp.where(at_zero, gain_other, gain_own).astype(f32),
-    ]
-
-    def cut(block, index, count, axis):
-        size = block.shape[axis] // count
-        return lax.dynamic_slice_in_dim(block, index * size, size, axis)
-
-    def heads_of(block):
-        split = block.reshape(block.shape[0], -1, HD)
-        return jnp.pad(split, ((0, 0), (0, 0), (0, HP - HD))).reshape(block.shape[0], -1)
-
-    def pack_attn(side):
-        parts = [cut(wq[0], side, 2, 1), cut(wk[0], side, 2, 1), cut(wv[0], side, 2, 1)]
-        return heads_of(jnp.concatenate(parts + [cut(wo[0], side, 2, 0).T], 1))
-
-    def pack_ffn(quarter):
-        return jnp.stack(
-            [cut(wg[0], quarter, 4, 1), cut(wu[0], quarter, 4, 1), cut(wd[0], quarter, 4, 0).T]
-        )
-
     halves = Z // 2
     tall = C * depth
     units = wg.shape[2] // 4
     upper, lower = pl.ds(0, tall // 2), pl.ds(tall // 2, tall // 2)
     attn_cuts = [((upper,), (upper,), None), ((lower,), None, (lower,))]
     ffn_cuts = [((m,), (m, upper), (m, lower)) for m in range(3)]
-    attn = [Gather(grid, (tall, 6 * HP), attn_cuts, True) for _ in range(2)]
+    attn = [Gather(grid, (tall, BLOCK), attn_cuts, True) for _ in range(2)]
     ffn = [Gather(grid, (3, tall, units), ffn_cuts) for _ in range(2)]
     plan = Plan()
     joins = [[ring.begin(plan) for ring in rings] for rings in (attn, ffn)]
     attn[0].add(plan, 0)
     ffn[0].add(plan, max(0, len(plan.stages) - 2), 1)
-    start_call(
-        grid, plan, joins, max(0, len(plan.stages) - 3), jnp.stack([pack_attn(0), pack_attn(1)]),
-        jnp.stack([pack_ffn(quarter) for quarter in range(4)]),
-    )
+    shards = (wq, wk, wv, wo, wg, wu, wd)
+    gain_all = start_call(grid, plan, joins, max(0, len(plan.stages) - 3), shards, gains)
 
     hidden = rows_in
     kept = []
     for s in range(2):
         nexts = (attn[1], ffn[1]) if s == 0 else None
-        if s == 1:
-            rows_cot = enter(after(cotangent, hidden))
-        hidden, keep = layer_forward(
-            grid, hidden, attn[s], ffn[s], nexts, gain_all[s], facts, (rows_cot,) if s == 1 else ()
-        )
+        hidden, keep = layer_forward(grid, hidden, attn[s], ffn[s], nexts, gain_all[s], facts)
         kept.append(keep)
-    outs = [leave(after(kept[1][0], hidden), 0), leave(hidden, 1)]
+    rows_cot = enter(after(cotangent, kept[1][2]))
+    outs = [leave(after(kept[1][0], hidden, rows_cot), 0), leave(after(hidden, rows_cot), 1)]
 
     def sum_ffn(terms):
         def block(m):
@@ -1524,15 +1669,11 @@
     def sum_attn(qkv_term, out_term):
         size = tall // 2
 
-        def block(row, first, count):
-            def at(yy, zz):
-                here = (first + count * (zz % halves)) * HP
-                return (
-                    pl.ds(pl.multiple_of(yy * tall + row, size), size),
-                    pl.ds(pl.multiple_of(here, HP), count * HP),
-                )
-
-            return at
+        def block(row, count):
+            return lambda yy, zz: (
+                pl.ds(pl.multiple_of(yy * tall + row, size), size),
+                pl.ds(pl.multiple_of(zz % halves * count, HP), count),
+            )
 
         parts = []
         for cuts, rows_at, row in ((attn_cuts[0], upper, 0), (attn_cuts[1], lower, size)):
@@ -1540,14 +1681,12 @@
                 (
                     cuts,
                     [
-                        (qkv_term, block(row, 0, 2), (rows_at, pl.ds(0, 2 * HP))),
-                        (qkv_term, block(row, 2 * halves, 1), (rows_at, pl.ds(2 * HP, HP))),
-                        (qkv_term, block(row, 3 * halves, 1), (rows_at, pl.ds(3 * HP, HP))),
-                        (out_term, block(row, 0, 2), (rows_at, pl.ds(4 * HP, 2 * HP))),
+                        (qkv_term, block(row, 4 * HD), (rows_at, pl.ds(0, 4 * HD))),
+                        (out_term, block(row, 2 * HP), (rows_at, pl.ds(4 * HD, 2 * HP))),
                     ],
                 )
             )
-        return Scatter(grid, parts, (tall, 6 * HP), True)
+        return Scatter(grid, parts, (tall, BLOCK), True)
 
     upstream = rows_cot
     gain_terms, running = [None] * 2, []
@@ -1563,45 +1702,22 @@
     produced = jnp.where(at_zero, jnp.stack(outs[0]), jnp.stack(outs[1]))
     plan = Plan()
     ready = []
-    for n, ring in enumerate(running):
-        left = ring.left()
-        ring.add(plan, 0, left, True)
+    for n in (1, 3, 0, 2):
+        left = running[n].left()
+        running[n].add(plan, 0, left, True)
         ready.append((1 - n // 2, n % 2 == 1, left - 1))
-    for ring in running:
-        ring.total(plan)
-    ffn_own, ffn_came, attn_own, attn_came = tail_call(grid, plan, ready, depth, units)
+        running[n].total(plan)
+    *blocks, gain_sum = tail_call(grid, plan, ready, gain_terms[0] + gain_terms[1], depth, units)
     grads_in = jnp.where(at_zero, jnp.stack(grads_in[0]), jnp.stack(grads_in[1])).astype(f32)
 
-    def in_order(own, came):
-        return jnp.where(at_zero, own, came), jnp.where(at_zero, came, own)
-
-    ffn_home = jnp.concatenate([half[core] for half in in_order(ffn_own, ffn_came) for core in range(C)], 2)
-    ffn_home = ffn_home.astype(f32)
-    sides = in_order(attn_own, attn_came)
-    query_home, key_home, value_home, out_home = [
-        jnp.concatenate(
-            [side[:, h * HP : h * HP + HD] for side in sides for h in some], 1
-        ).astype(f32)
-        for some in ((0, 1), (2,), (3,), (4, 5))
-    ]
-    out_home = out_home.T
-
-    gain_kept = jnp.where(at_zero, gain_terms[0], gain_terms[1])
-    gain_sum = gain_kept + grid.over_x(jnp.where(at_zero, gain_terms[1], gain_terms[0]))
-    for hop in grid.hops():
-        gain_sum = gain_sum + grid.send(gain_sum, hop)
-    share = width // (Y * C * Z)
-    gain_share = lax.dynamic_slice_in_dim(gain_sum, mine * share, share, 1)[None]
+    terms = finish_call(blocks, shards)
+    share = gains.shape[2]
+    mine = (y * C + c) * Z + z
+    gain_share = lax.dynamic_slice(gain_sum, (2 * x, mine * share), (2, share))[None]
     return (
         produced[None],
         grads_in[None],
-        query_home[None],
-        key_home[None],
-        value_home[None],
-        out_home[None],
-        ffn_home[0][None],
-        ffn_home[1][None],
-        ffn_home[2].T[None],
+        *[term[None] for term in terms],
         gain_share,
     )
 

time: 930 us -> 846 us (0.910)
  Pallas kernels: 820 us -> 781 us
  local copies, waits for them, and re-layouts: 30.3 us -> 14.2 us
  other arithmetic: 22.6 us -> 9.79 us
    pallas_call x10, Pallas kernels: 820 us -> 776 us  [fused_call(): pl.pallas_call(whole, out_shape=tuple(outs) + tuple(plan.outs), in_specs=...]
    ppermute x23 -> x13, starting transfers between devices: 35.9 us -> 28.7 us  [send(): return lax.ppermute(block, AXES, pairs)]
  transfers between devices with their start and end apart: 23 -> 13, of which waited for: 5 -> 0; matrix products, arithmetic and copies ran while one was open for 5% -> 2% of each run, Pallas kernels for 48% -> 46%
where the time goes in v4:
time: 846 us; the launch traced here: 836 us
  Pallas kernels  781 us (92%)
  starting transfers between devices  28.7 us (3%)
  local copies, waits for them, and re-layouts  14.2 us (2%)
  other arithmetic  9.79 us (1%)
    pallas_call x10, Pallas kernels, fused_call(): pl.pallas_call(whole, out_shape=tuple(outs) + tuple(plan.outs), in_specs=...  776 us
    ppermute x13, starting transfers between devices, send(): return lax.ppermute(block, AXES, pairs)  28.7 us
  transfers between devices with their start and end apart: 13, of which 0 were waited for; matrix products, arithmetic and copies ran while one was open for 2% of the time, Pallas kernels for 46%

profile of v4, /device:TPU:1, one launch (start us, length us, event | category | flops | bytes accessed | tf_op | source)
XLA Modules:
  0.0 835.6 jit_solution(13438007828435696375)
XLA Ops:
  0.8 1.5 slice_bitcast_fusion.2
  3.0 1.3 collective-permute-start
  6.0 102.0 %start.1 = (f32[2,2,1536]{2,1,0:T(2,128)}, bf16[768,640]{1,0:T(8,128)(2,1)}, bf16[768,640]{1,0:T(8,128)(2,1)}, bf16[3,768,256]{2,1,0:T(8,128)(2,1)}, bf16[3,768,...) custom-call(bf16[1,384,384]{2,1,0:T(8,128)(2,1)} %refs_0_.1, ...), custom_call_target="tpu_custom_call" | custom-call | flops 70000001024 | bytes 1048576 | tf_op jit(solution)/shard_map/start/pallas_call | solution.py:524
  108.0 1.4 slice_bitcast_fusion.4
  110.4 1.0 copy.33.refs_5_.refs_4_
  113.0 1.0 copy.34.refs_6_
  114.0 1.9 fusion.1
  116.3 0.8 pad_maximum_fusion.1.refs_3_.refs_12_
  118.0 1.0 broadcast_select_fusion.1.refs_0_.refs_1_
  119.0 72.2 %attn.2 = (bf16[4,256,1536]{2,1,0:T(8,128)(2,1)}, bf16[4,4,256,128]{3,2,1,0:T(8,128)(2,1)}, bf16[2,4,256,128]{3,2,1,0:T(8,128)(2,1)}, bf16[2,4,256,128]{3,2,1,0:...) custom-call(bf16[256,1536]{1,0:T(8,128)(2,1)} %broadcast_select_fusi, ...), custom_call_target="tpu_custom_call" | custom-call | flops 60000002048 | bytes 1048576 | tf_op jit(solution)/shard_map/attn/pallas_call | solution.py:524
  191.2 77.6 %ffn.2 = (bf16[256,1536]{1,0:T(8,128)(2,1)}, bf16[4,256,1536]{2,1,0:T(8,128)(2,1)}, bf16[4,256,1024]{2,1,0:T(8,128)(2,1)}, bf16[4,256,1024]{2,1,0:T(8,128)(2,1)}...) custom-call(f32[256,1536]{1,0:T(8,128)} %get-tuple-element.117.refs_, ...), custom_call_target="tpu_custom_call" | custom-call | flops 44000002048 | bytes 1048576 | tf_op jit(solution)/shard_map/ffn/pallas_call | solution.py:524
  268.8 72.6 %attn.3 = (bf16[4,256,1536]{2,1,0:T(8,128)(2,1)}, bf16[4,4,256,128]{3,2,1,0:T(8,128)(2,1)}, bf16[2,4,256,128]{3,2,1,0:T(8,128)(2,1)}, bf16[2,4,256,128]{3,2,1,0:...) custom-call(bf16[256,1536]{1,0:T(8,128)(2,1)} %get-tuple-element.144, ...), custom_call_target="tpu_custom_call" | custom-call | flops 60000002048 | bytes 1048576 | tf_op jit(solution)/shard_map/attn/pallas_call | solution.py:524
  342.2 1.7 collective-permute-start.3
  343.9 43.1 %ffn.3 = (bf16[256,1536]{1,0:T(8,128)(2,1)}, bf16[4,256,1536]{2,1,0:T(8,128)(2,1)}, bf16[4,256,1024]{2,1,0:T(8,128)(2,1)}, bf16[4,256,1024]{2,1,0:T(8,128)(2,1)}, bf16[4,256,1024]{2,1,0:T(8,128)(2,1)}) custom-call(f32[256,1536]{1,0:T(8,128)} %get-tuple-element.136.refs_0_.refs_1_, f32[1,1536]{1,0:T(1,128)} %get-tuple-element.236.refs_1_.refs_2_, ...), custom_call_target="tpu_custom_call" | custom-call | flops 44000002048 | bytes 1048576 | tf_op jit(solution)/shard_map/ffn/pallas_call | solution.py:524
  387.1 1.0 broadcast_select_fusion.refs_0_
  388.4 1.3 collective-permute-start.6
  389.7 5.7 collective-permute-start.5
  396.2 3.7 collective-permute-start.7
  399.9 53.1 %ffn_back.2 = (f32[256,1536]{1,0:T(8,128)}, f32[8,1536]{1,0:T(8,128)}, bf16[3,1536,1024]{2,1,0:T(8,128)(2,1)}) custom-call(bf16[256,1536]{1,0:T(8,128)(2,1)} %broadcast_select_fusion.refs_0_, f32[256,1536]{1,0:T(8,128)} %get-tuple-element.136.refs_0_.refs_1_, f32[1,1536]{1,0:T(1,128)} %get-tuple-element.236.refs_1_.refs_2_, ...), custom_call_target="tpu_custom_call" | custom-call | flops 60000002048 | bytes 1048576 | tf_op jit(solution)/shard_map/ffn_back/pallas_call | solution.py:524
  453.0 84.1 %attn_back.2 = (bf16[256,1536]{1,0:T(8,128)(2,1)}, f32[8,1536]{1,0:T(8,128)}, bf16[1536,768]{1,0:T(8,128)(2,1)}, bf16[1536,512]{1,0:T(8,128)(2,1)}, bf16[3,768,2...) custom-call(f32[256,1536]{1,0:T(8,128)} %get-tuple-element.150.refs_0_, ...), custom_call_target="tpu_custom_call" | custom-call | flops 80000000000 | bytes 1048576 | tf_op jit(solution)/shard_map/attn_back/pallas_call | solution.py:524
  537.8 5.4 collective-permute-start.9
  543.2 75.5 %ffn_back.3 = (f32[256,1536]{1,0:T(8,128)}, f32[8,1536]{1,0:T(8,128)}, bf16[3,1536,1024]{2,1,0:T(8,128)(2,1)}, bf16[3,768,256]{2,1,0:T(8,128)(2,1)}, bf16[3,768,...) custom-call(bf16[256,1536]{1,0:T(8,128)(2,1)} %get-tuple-element.159.refs_0_, ...), custom_call_target="tpu_custom_call" | custom-call | flops 60000002048 | bytes 1048576 | tf_op jit(solution)/shard_map/ffn_back/pallas_call | solution.py:524
  618.6 1.4 maximum_select_fusion
  620.1 87.6 %attn_back.3 = (bf16[256,1536]{1,0:T(8,128)(2,1)}, f32[8,1536]{1,0:T(8,128)}, bf16[1536,768]{1,0:T(8,128)(2,1)}, bf16[1536,512]{1,0:T(8,128)(2,1)}, bf16[3,768,2...) custom-call(f32[256,1536]{1,0:T(8,128)} %get-tuple-element.168.refs_0_, ...), custom_call_target="tpu_custom_call" | custom-call | flops 80000000000 | bytes 1048576 | tf_op jit(solution)/shard_map/attn_back/pallas_call | solution.py:524
  707.7 1.3 collective-permute-start.12
  709.0 5.4 collective-permute-start.11
  714.4 107.9 %tail.1 = (bf16[2,3,384,256]{3,2,1,0:T(8,128)(2,1)}, bf16[2,3,384,256]{3,2,1,0:T(8,128)(2,1)}, bf16[384,640]{1,0:T(8,128)(2,1)}, bf16[384,640]{1,0:T(8,128)(2,1)}, f32[8,1536]{1,0:T(8,128)}) custom-call(f32[8,1536]{1,0:T(8,128)} %get-tuple-element.178.refs_0_, f32[8,1536]{1,0:T(8,128)} %get-tuple-element.179.refs_1_, f32[8,1536]{1,0:T(8,128)} %get-tuple-element.180.refs_2_, ...), custom_call_target="tpu_custom_call" | custom-call | flops 60000002048 | bytes 1048576 | tf_op jit(solution)/shard_map/tail/pallas_call | solution.py:524
  822.3 5.8 finish.1
  828.1 1.9 copy.39
  830.0 1.9 copy.40
  831.9 1.3 dynamic-slice_bitcast_fusion.8
  833.2 1.9 fusion
  (66 shorter events, 8.9 us)
Async XLA Ops:
  0.6 3.7 copy-start.5
  0.7 4.5 copy-start.6
  0.7 110.8 %collective-permute-start.2 = (s32[2,1,1024]{2,1,0:T(1,128)}, s32[2,1,1024]{2,1,0:T(1,128)S(1)}, u32[]{:S(2)}, u32[]{:S(2)}) collective-permute-start(s32[2,1,1024]{2,1,0:T(1,128)} %param.12), channel_id=1, source_target_pairs={{0,4},{1,5},{2,6},{3,7},{4,0},{5,1},{6,2},{7,3},{8,12},{9,13},{10,... | collective-permute-start | bytes 24584 | tf_op jit(solution)/shard_map/ppermute | solution.py:47
  2.3 115.7 %collective-permute-start.1 = (bf16[256,1536]{1,0:T(8,128)(2,1)S(1)}, bf16[256,1536]{1,0:T(8,128)(2,1)S(1)}, u32[]{:S(2)}, u32[]{:S(2)}) collective-permute-start(bf16[256,1536]{1,0:T(8,128)(2,1)S(1)} %get-tuple-element.226), channel_id=1, source_target_pairs={{0,2},{2,6},{5,3},{7,7},{8,10},{10,14},{13,11},{15,15},{17,18},{19... | collective-permute-start | bytes 2359304 | tf_op jit(solution)/shard_map/ppermute | solution.py:47
  3.0 115.0 %collective-permute-start = (bf16[256,1536]{1,0:T(8,128)(2,1)S(1)}, bf16[256,1536]{1,0:T(8,128)(2,1)S(1)}, u32[]{:S(2)}, u32[]{:S(2)}) collective-permute-start(bf16[256,1536]{1,0:T(8,128)(2,1)S(1)} %get-tuple-element.227), channel_id=1, source_target_pairs={{0,0},{2,4},{5,1},{7,5},{8,8},{10,12},{13,9},{15,13},{17,16},{19,2... | collective-permute-start | bytes 2359304 | tf_op jit(solution)/shard_map/ppermute | solution.py:47
  6.0 105.5 %copy-start.7 = (s32[2,1,1024]{2,1,0:T(1,128)S(1)}, s32[2,1,1024]{2,1,0:T(1,128)}, u32[]{:S(2)}) copy-start(s32[2,1,1024]{2,1,0:T(1,128)} %param.12) | copy-start | bytes 24580
  268.7 72.6 %copy-start = (bf16[2,256,1536]{2,1,0:T(8,128)(2,1)S(1)}, bf16[2,256,1536]{2,1,0:T(8,128)(2,1)}, u32[]{:S(2)}) copy-start(bf16[2,256,1536]{2,1,0:T(8,128)(2,1)} %param.13) | copy-start | bytes 4718596
  341.5 45.6 %collective-permute-start.4 = (bf16[256,1536]{1,0:T(8,128)(2,1)S(1)}, bf16[256,1536]{1,0:T(8,128)(2,1)S(1)}, u32[]{:S(2)}, u32[]{:S(2)}) collective-permute-start(bf16[256,1536]{1,0:T(8,128)(2,1)S(1)} %get-tuple-element.224), channel_id=1, source_target_pairs={{0,2},{2,6},{5,3},{7,7},{8,10},{10,14},{13,11},{15,15},{17,18},{19... | collective-permute-start | bytes 2359304 | tf_op jit(solution)/shard_map/ppermute | solution.py:47
  342.2 44.8 %collective-permute-start.3 = (bf16[256,1536]{1,0:T(8,128)(2,1)S(1)}, bf16[256,1536]{1,0:T(8,128)(2,1)S(1)}, u32[]{:S(2)}, u32[]{:S(2)}) collective-permute-start(bf16[256,1536]{1,0:T(8,128)(2,1)S(1)} %get-tuple-element.225), channel_id=1, source_target_pairs={{0,0},{2,4},{5,1},{7,5},{8,8},{10,12},{13,9},{15,13},{17,16},{19,2... | collective-permute-start | bytes 2359304 | tf_op jit(solution)/shard_map/ppermute | solution.py:47
  387.1 1.4 copy-start.8
  388.4 64.5 %collective-permute-start.6 = (bf16[256,1536]{1,0:T(8,128)(2,1)S(1)}, bf16[256,1536]{1,0:T(8,128)(2,1)S(1)}, u32[]{:S(2)}, u32[]{:S(2)}) collective-permute-start(bf16[256,1536]{1,0:T(8,128)(2,1)S(1)} %copy-done.8), channel_id=1, source_target_pairs={{2,0},{3,5},{6,2},{7,7},{10,8},{11,13},{14,10},{15,15},{18,1},{19,... | collective-permute-start | bytes 2359304 | tf_op jit(solution)/shard_map/ppermute | solution.py:47
  389.7 63.2 %collective-permute-start.5 = (bf16[256,1536]{1,0:T(8,128)(2,1)S(1)}, bf16[256,1536]{1,0:T(8,128)(2,1)S(1)}, u32[]{:S(2)}, u32[]{:S(2)}) collective-permute-start(bf16[256,1536]{1,0:T(8,128)(2,1)S(1)} %copy-done.8), channel_id=1, source_target_pairs={{0,0},{1,5},{4,2},{5,7},{8,8},{9,13},{12,10},{13,15},{16,1},{17,4}... | collective-permute-start | bytes 2359304 | tf_op jit(solution)/shard_map/ppermute | solution.py:47
  395.4 57.5 %collective-permute-start.8 = (bf16[256,1536]{1,0:T(8,128)(2,1)}, bf16[256,1536]{1,0:T(8,128)(2,1)S(1)}, u32[]{:S(2)}, u32[]{:S(2)}) collective-permute-start(bf16[256,1536]{1,0:T(8,128)(2,1)} %get-tuple-element.145), channel_id=1, source_target_pairs={{2,16},{3,21},{6,18},{7,23},{10,24},{11,29},{14,26},{15,31},{18,17... | collective-permute-start | bytes 2359304 | tf_op jit(solution)/shard_map/ppermute | solution.py:47
  396.2 56.8 %collective-permute-start.7 = (bf16[256,1536]{1,0:T(8,128)(2,1)}, bf16[256,1536]{1,0:T(8,128)(2,1)S(1)}, u32[]{:S(2)}, u32[]{:S(2)}) collective-permute-start(bf16[256,1536]{1,0:T(8,128)(2,1)} %get-tuple-element.145), channel_id=1, source_target_pairs={{0,16},{1,21},{4,18},{5,23},{8,24},{9,29},{12,26},{13,31},{16,17},... | collective-permute-start | bytes 2359304 | tf_op jit(solution)/shard_map/ppermute | solution.py:47
  537.0 83.0 %collective-permute-start.10 = (bf16[256,1536]{1,0:T(8,128)(2,1)}, bf16[256,1536]{1,0:T(8,128)(2,1)S(1)}, u32[]{:S(2)}, u32[]{:S(2)}) collective-permute-start(bf16[256,1536]{1,0:T(8,128)(2,1)} %get-tuple-element.159.refs_0_), channel_id=1, source_target_pairs={{2,16},{3,21},{6,18},{7,23},{10,24},{11,29},{14,26},{15,31},{18,17... | collective-permute-start | bytes 2359304 | tf_op jit(solution)/shard_map/ppermute | solution.py:47
  537.8 82.3 %collective-permute-start.9 = (bf16[256,1536]{1,0:T(8,128)(2,1)}, bf16[256,1536]{1,0:T(8,128)(2,1)S(1)}, u32[]{:S(2)}, u32[]{:S(2)}) collective-permute-start(bf16[256,1536]{1,0:T(8,128)(2,1)} %get-tuple-element.159.refs_0_), channel_id=1, source_target_pairs={{0,16},{1,21},{4,18},{5,23},{8,24},{9,29},{12,26},{13,31},{16,17},... | collective-permute-start | bytes 2359304 | tf_op jit(solution)/shard_map/ppermute | solution.py:47
  620.0 87.6 %copy-start.1 = (bf16[256,1536]{1,0:T(8,128)(2,1)}, bf16[256,1536]{1,0:T(8,128)(2,1)S(1)}, u32[]{:S(2)}) copy-start(bf16[256,1536]{1,0:T(8,128)(2,1)S(1)} %collective-permute-done.10) | copy-start | bytes 2359300
  620.1 87.6 %copy-start.3 = (bf16[256,1536]{1,0:T(8,128)(2,1)}, bf16[256,1536]{1,0:T(8,128)(2,1)S(1)}, u32[]{:S(2)}) copy-start(bf16[256,1536]{1,0:T(8,128)(2,1)S(1)} %collective-permute-done.9) | copy-start | bytes 2359300
  707.7 125.5 %collective-permute-start.12 = (bf16[256,1536]{1,0:T(8,128)(2,1)}, bf16[256,1536]{1,0:T(8,128)(2,1)S(1)}, u32[]{:S(2)}, u32[]{:S(2)}) collective-permute-start(bf16[256,1536]{1,0:T(8,128)(2,1)} %get-tuple-element.177), channel_id=1, source_target_pairs={{2,0},{3,5},{6,2},{7,7},{10,8},{11,13},{14,10},{15,15},{18,1},{19,... | collective-permute-start | bytes 2359304 | tf_op jit(solution)/shard_map/ppermute | solution.py:47
  709.0 124.2 %collective-permute-start.11 = (bf16[256,1536]{1,0:T(8,128)(2,1)}, bf16[256,1536]{1,0:T(8,128)(2,1)S(1)}, u32[]{:S(2)}, u32[]{:S(2)}) collective-permute-start(bf16[256,1536]{1,0:T(8,128)(2,1)} %get-tuple-element.177), channel_id=1, source_target_pairs={{0,0},{1,5},{4,2},{5,7},{8,8},{9,13},{12,10},{13,15},{16,1},{17,4}... | collective-permute-start | bytes 2359304 | tf_op jit(solution)/shard_map/ppermute | solution.py:47
  822.3 10.9 %copy-start.4 = (bf16[256,1536]{1,0:T(8,128)(2,1)S(1)}, bf16[256,1536]{1,0:T(8,128)(2,1)}, u32[]{:S(2)}) copy-start(bf16[256,1536]{1,0:T(8,128)(2,1)} %copy-done.3) | copy-start | bytes 2359300
  828.1 5.1 copy-start.2

commit v5 on v4

--- a/solution.py
+++ b/solution.py
@@ -2,15 +2,17 @@
 
 import jax
 import jax.numpy as jnp
+import numpy as np
 import jax.experimental.pallas as pl
 import jax.experimental.pallas.tpu as pltpu
 from jax import lax
 from jax.sharding import PartitionSpec as P
 
 HD = 96
+DOCS = 4
 HP = 128
 NEVER = -1e30
-BLOCK = 4 * HD + 2 * HP
+BLOCK = 4 * HD
 epsilon = 1e-05
 rope_base = 100000.0
 AXES = ("section", "fsdp", "tensor")
@@ -758,8 +760,8 @@
     return fused_call(
         grid, functools.partial(attn_kernel, grid, heads, offsets), "attn", plan,
         (
-            hidden, gain_row, facts["cos"], facts["sin"], facts["tok"][:, None, :],
-            facts["tok"][:, :, None], facts["from"][:, :, None], *blocks,
+            hidden, gain_row, facts["cos"], facts["sin"], facts["tok_row"], facts["tok_col"],
+            facts["from_col"], *blocks,
         ),
         [VMEM] * 7 + [ANY] * len(blocks),
         shaped(
@@ -798,17 +800,24 @@
     for live, copy in fetched:
         pl.when(live)(copy.wait)
     halves = grid.Z // 2
-    tall = stage.shape[1]
-    blank = jnp.zeros((tall, HP - HD), bf16)
+    share_rows = stage.shape[1] // grid.C
+    depth = share_rows * 2 // 3
+    half = depth // 2
+
+    def put(ref, first, count, at, head):
+        blank = jnp.zeros((count, HP - HD), bf16)
+        ref[first : first + count, at * HP : (at + 1) * HP] = jnp.concatenate([head, blank], 1)
+
     for yy in range(grid.Y):
-        rows = slice(yy * tall, (yy + 1) * tall)
         for j in range(halves):
             block = stage.at[yy * halves + j]
-            places = [(qkv, 2 * j), (qkv, 2 * j + 1), (qkv, 2 * halves + j), (qkv, 3 * halves + j)]
-            places += [(out, 2 * j), (out, 2 * j + 1)]
-            for n, (ref, at) in enumerate(places):
-                head = block[:, n * HD : (n + 1) * HD]
-                ref[rows, at * HP : (at + 1) * HP] = jnp.concatenate([head, blank], 1)
+            for core in range(grid.C):
+                first, base = (yy * grid.C + core) * depth, core * share_rows
+                for n, at in enumerate((2 * j, 2 * j + 1, 2 * halves + j, 3 * halves + j)):
+                    put(qkv, first, depth, at, block[base : base + depth, n * HD : (n + 1) * HD])
+                for n in range(4):
+                    head = block[base + depth : base + share_rows, n * HD : (n + 1) * HD]
+                    put(out, first + n // 2 * half, half, 2 * j + n % 2, head)
 
 
 def attn_weights(grid, found, width):
@@ -904,6 +913,7 @@
     work(1, 0, rows)
     store(1)
     collect.give_near(part[...])
+    background.advance()
     cuts = pieces_of(rows)
     size = rows // PARTS
     for k in range(PARTS):
@@ -1020,6 +1030,7 @@
     spread.near.wait_recv()
     work(1, 0, rows)
     collect.give_near(part[...])
+    background.advance()
     cuts = pieces_of(rows)
     size = rows // PARTS
     for k in range(PARTS):
@@ -1031,6 +1042,7 @@
         collect.give_side(k, part[cuts[k]])
         work(2, k * size, size)
         collect.give_over(k, part[cuts[k]])
+    background.advance()
     wait_all(loads[2:])
     outs = []
     for m, (left, right) in enumerate(
@@ -1040,8 +1052,6 @@
         weight_terms(held.at[n], left, right)
         outs.append(pltpu.make_async_copy(held.at[n], terms_ref.at[n], out_sems.at[n]))
         outs[-1].start()
-        if m == 0:
-            background.advance()
     second = collect.finish(own[...])
     grad, gains = norm_back(mid_ref[...], gain_ref[...], second)
     out_ref[...] = g_ref[...].astype(f32) + grad
@@ -1088,7 +1098,7 @@
     sources, pieces = refs[:7], refs[7 : 7 + len(offsets)]
     (
         out_ref, gains_ref, qkv_term, out_term,
-        stage, w_sems, held, wo_ref, rows_ref, s_sems, gm_ref, dqkv_ref, low_ref, low_m,
+        stage, w_sems, held, wo_ref, rows_ref, s_sems, gm_ref, dqkv_ref, low_ref, low_m, whole_out,
         key_sum, value_sum, query_sum, delta, part, hold, c_sems,
         q_ref, k_ref, v_ref, m_ref, cos_ref, sin_ref, whole_ref, in_sems,
     ) = refs[7 + len(offsets) :]
@@ -1150,13 +1160,13 @@
     wait_all(loads[:4])
     attend_back(0)
     attend_back(1)
+    background.advance()
     size = rows // PARTS
     for k in range(PARTS):
         spread.pass_on(k)
         work(2, k * size, size)
         spread.relay[k].wait_recv()
         work(3, k * size, size)
-    background.advance()
     attend_back(2)
     attend_back(3)
 
@@ -1187,17 +1197,22 @@
     work_back(2)
     for k in range(PARTS):
         collect.give_over(k, part[cuts[k]])
-    background.advance()
     work_back(1)
     collect.give_near(part[...])
     work_back(0)
-    low_m[...] = jnp.zeros_like(low_m)
     for i in range(4):
         for h in range(heads):
-            at = h // 2 * 2 * HP + h % 2 * HD
-            low_m[i, :, at : at + HD] = m_ref[i, :, h * HP : h * HP + HD]
-    weight_terms(out_term, rows_ref, low_m)
+            low_m[i, :, h * HD : (h + 1) * HD] = m_ref[i, :, h * HP : h * HP + HD]
+    weight_terms(whole_out, rows_ref, low_m)
+    half = out_term.shape[2]
+    for n in range(out_term.shape[0]):
+        for j in range(pairs):
+            cols = slice(2 * j * HD, 2 * (j + 1) * HD)
+            out_term[n, j] = jnp.concatenate(
+                [whole_out[(2 * n + k) * half : (2 * n + k + 1) * half, cols] for k in range(2)], 1
+            )
     weight_terms(qkv_term, whole_ref, low_ref)
+    background.advance()
     grad, gains = norm_back(h_ref[...].astype(f32), gain_ref[...], collect.finish(part[...]))
     out_ref[...] = (g_ref[...] + grad).astype(bf16)
     gains_ref[...] = gains
@@ -1210,20 +1225,21 @@
 def attn_back_call(grid, plan, grad_middle, hidden, gain_row, facts, kept, found):
     whole, query, keys, values, mixed, lse = kept
     rows, width = hidden.shape
+    depth = width // (grid.Y * grid.C)
     heads = query.shape[0]
     pairs = heads // 2
     offsets, blocks = apart(found)
     return fused_call(
         grid, functools.partial(attn_back_kernel, grid, heads, offsets), "attn_back", plan,
         (
-            grad_middle, hidden, gain_row, lse, facts["tok"][:, :, None], facts["tok"][:, None, :],
-            facts["from"][:, None, :], query, keys, values, mixed, facts["cos"], facts["sin"], whole,
+            grad_middle, hidden, gain_row, lse, facts["tok_col"], facts["tok_row"],
+            facts["from_row"], query, keys, values, mixed, facts["cos"], facts["sin"], whole,
             *blocks,
         ),
         [VMEM] * 7 + [ANY] * (7 + len(blocks)),
         shaped(
             ((rows, width), bf16), ((8, width), f32), ((width, 2 * heads * HD), bf16),
-            ((width, heads * HP), bf16),
+            ((width // depth, pairs, depth // 2, BLOCK), bf16),
         ),
         (VMEM,) * 4,
         [
@@ -1232,7 +1248,8 @@
             pltpu.VMEM((heads, 4, rows, HP), bf16),
             pltpu.VMEM((4, rows, 2 * heads * HP), bf16),
             pltpu.VMEM((4, rows, 2 * heads * HD), bf16),
-            pltpu.VMEM((4, rows, heads * HP), bf16),
+            pltpu.VMEM((4, rows, heads * HD), bf16),
+            pltpu.VMEM((width, heads * HD), bf16),
             pltpu.VMEM((pairs, 4, rows, HP), f32),
             pltpu.VMEM((pairs, 4, rows, HP), f32),
             pltpu.VMEM((heads, 4, rows, HP), f32),
@@ -1255,32 +1272,32 @@
 
 
 def start_kernel(
-    grid, joins, early, background, cycle, wq, wk, wv, wo, wg, wu, wd, gains_ref, all_gains,
-    attn_ref, ffn_ref, sems, local, table, land, t_sems,
+    grid, joins, early, background, cycle, wq, wk, wv, wo, wg, wu, wd, gains_ref, docs_ref, freq_ref,
+    all_gains, cos_ref, sin_ref, tok_row, from_row, tok_col, from_col,
+    attn_ref, ffn_ref, sems, local, table, land, t_sems, docs_land, begins, d_sems,
 ):
     x, y, c, z = grid.me()
     mine = z // (grid.Z // 2) == c
     attn_to = [background.refs[h[0]][h[1]] for h in joins[0]]
     ffn_to = [background.refs[h[0]][h[1]] for h in joins[1]]
-    depth = attn_ref.shape[1]
-    units = ffn_ref.shape[3]
+    depth, units = ffn_ref.shape[2:]
+    share_rows = attn_ref.shape[1]
     rows = pl.ds(pl.multiple_of(c * depth, depth), depth)
+    attn_rows = pl.ds(pl.multiple_of(c * share_rows, share_rows), share_rows)
 
     def pack():
         for side in range(2):
             heads = [wq[0, :, 2 * side * HD : 2 * (side + 1) * HD]]
             heads += [ref[0, :, side * HD : (side + 1) * HD] for ref in (wk, wv)]
-            heads.append(
-                jnp.transpose(wo[0, 2 * side * HD : 2 * (side + 1) * HD].astype(f32)).astype(bf16)
-            )
-            heads.append(jnp.zeros((depth, BLOCK - 6 * HD), bf16))
-            attn_ref[side] = jnp.concatenate(heads, 1)
+            turned = jnp.transpose(wo[0, 2 * side * HD : 2 * (side + 1) * HD].astype(f32)).astype(bf16)
+            attn_ref[side, :depth] = jnp.concatenate(heads, 1)
+            attn_ref[side, depth:] = jnp.concatenate([turned[: depth // 2], turned[depth // 2 :]], 1)
 
     others = doubling(grid)
     sib, over, diag = greet(grid, 3, cycle, others, pack)
     everything = []
     for layer in range(2):
-        to = attn_to[layer].at[rows]
+        to = attn_to[layer].at[attn_rows]
         moves = [
             (mine, pltpu.make_async_copy(attn_ref.at[layer], to, local.at[0])),
             (~mine, remote(attn_ref.at[layer], to, sems, 0, sib)),
@@ -1330,6 +1347,8 @@
     table[0] = jnp.zeros_like(table[0])
     padded = jnp.concatenate([gains_ref[0].astype(f32), jnp.zeros((2, HP - share), f32)], 1)
     table[0, (y * grid.C + c) * grid.Z + z, :2, :] = padded
+    docs = remote(docs_ref, docs_land, d_sems, 0, sib)
+    docs.start()
     for n in sum_over(table, land, t_sems, [sib] + others):
         if n % 2 == 1 and early:
             background.advance()
@@ -1338,6 +1357,32 @@
     copy = remote(table.at[last], land.at[last], t_sems, last, over)
     copy.start()
     copy.wait()
+    docs.wait()
+    both = jnp.where(z % grid.C == c, docs_ref[...], docs_land[...])
+    doc = jnp.where(z // grid.C == 0, both[0], both[1])
+    begin = jnp.zeros_like(doc)
+    for value in range(1, DOCS):
+        before = jnp.sum((doc < value).astype(f32), (0, 1), keepdims=True).astype(jnp.int32)
+        begin = jnp.where(doc == value, before, begin)
+    begins[...] = begin
+    size = tok_row.shape[2]
+    per = size // HP
+    lane = lax.broadcasted_iota(jnp.int32, (size, HP), 1)
+    for n, quarter in enumerate(place_id(grid)):
+        rows_of = [begins[pl.ds(quarter * per + k, 1)] for k in range(per)]
+        from_row[n] = jnp.concatenate(rows_of, 1)
+        tok_row[n] = quarter * size + lax.broadcasted_iota(jnp.int32, (1, size), 1)
+        columns = [
+            jnp.transpose(jnp.broadcast_to(row.astype(f32), (HP, HP)))[:, :1] for row in rows_of
+        ]
+        column = jnp.concatenate(columns, 0)
+        token = quarter * size + lax.broadcasted_iota(jnp.int32, (size, 1), 0)
+        from_col[n] = column.astype(jnp.int32)
+        tok_col[n] = token
+        angle = (token.astype(f32) - column) * freq_ref[0:1]
+        sine = jnp.sin(angle)
+        cos_ref[n] = jnp.where(lane < HD, jnp.cos(angle), 0.0)
+        sin_ref[n] = jnp.where(lane < HD // 2, -sine, jnp.where(lane < HD, sine, 0.0))
     for p in range(shares):
         own, other = table[last, p, :2, :share], land[last, p, :2, :share]
         at = slice(p * share, (p + 1) * share)
@@ -1349,25 +1394,42 @@
     background.finish()
 
 
-def start_call(grid, plan, joins, early, shards, gains):
+def start_call(grid, plan, joins, early, shards, gains, doc_ids, rows):
     depth, width = shards[0].shape[1], grid.Y * grid.C * shards[0].shape[1]
     units = shards[4].shape[2] // 4
     hops = len(doubling(grid)) + 1
     table = (hops + 1, grid.Y * grid.C * grid.Z, 8, HP)
-    return fused_call(
+    ladder = np.arange(HP) % (HD // 2)
+    frequency = np.power(np.float32(rope_base), (-2.0 * ladder / HD).astype(np.float32))
+    frequency = jnp.asarray(np.broadcast_to(frequency.astype(np.float32), (8, HP)))
+    docs = doc_ids.reshape(doc_ids.shape[0], -1, HP)
+    ints = jnp.int32
+    gain_all, cosine, sine_part, tok_row, from_row, tok_col, from_col = fused_call(
         grid, functools.partial(start_kernel, grid, joins, early), "start", plan,
-        (*shards, gains), [VMEM] * 8, shaped(((2, 2, width), f32)), (VMEM,),
+        (*shards, gains, docs, frequency), [VMEM] * 10,
+        shaped(
+            ((2, 2, width), f32), ((4, rows, HP), f32), ((4, rows, HP), f32), ((4, 1, rows), ints),
+            ((4, 1, rows), ints), ((4, rows, 1), ints), ((4, rows, 1), ints),
+        ),
+        (VMEM,) * 7,
         [
-            pltpu.VMEM((2, depth, BLOCK), bf16),
+            pltpu.VMEM((2, depth * 3 // 2, BLOCK), bf16),
             pltpu.VMEM((4, 3, depth, units), bf16),
             pltpu.SemaphoreType.DMA((2, 6)),
             pltpu.SemaphoreType.DMA((2,)),
             pltpu.VMEM(table, f32),
             pltpu.VMEM(table, f32),
             pltpu.SemaphoreType.DMA((2, hops + 1)),
+            pltpu.VMEM(docs.shape, ints),
+            pltpu.VMEM(docs.shape[1:], ints),
+            pltpu.SemaphoreType.DMA((2, 1)),
         ],
         70,
-    )[0]
+    )
+    return gain_all, {
+        "cos": cosine, "sin": sine_part, "tok_row": tok_row, "from_row": from_row,
+        "tok_col": tok_col, "from_col": from_col,
+    }
 
 
 def tail_kernel(
@@ -1376,9 +1438,13 @@
 ):
     x, _, c, z = grid.me()
     mine = z // (grid.Z // 2) == c
-    depth = attn_own.shape[0]
-    rows = pl.ds(pl.multiple_of(c * depth, depth), depth)
-    other = pl.ds(pl.multiple_of((1 - c) * depth, depth), depth)
+    depth, share_rows = ffn_own.shape[2], attn_own.shape[0]
+
+    def part_of(core, size):
+        return pl.ds(pl.multiple_of(core * size, size), size)
+
+    rows, other = part_of(c, depth), part_of(1 - c, depth)
+    attn_rows, attn_other = part_of(c, share_rows), part_of(1 - c, share_rows)
     background.begin()
     others = doubling(grid)
     sib, over, diag = greet(grid, 3, cycle, others)
@@ -1394,11 +1460,11 @@
         for part in parts:
             background.do(alive, functools.partial(background.put, part, False))
         if heads:
-            keep = (term.at[rows], attn_own)
+            keep = (term.at[attn_rows], attn_own)
             moves = [
-                remote(term.at[other], attn_own, sems, 3, sib),
-                remote(term.at[rows], attn_came, sems, 4, over),
-                remote(term.at[other], attn_came, sems, 5, diag),
+                remote(term.at[attn_other], attn_own, sems, 3, sib),
+                remote(term.at[attn_rows], attn_came, sems, 4, over),
+                remote(term.at[attn_other], attn_came, sems, 5, diag),
             ]
         else:
             keep = (term.at[:, rows], ffn_own.at[c])
@@ -1426,14 +1492,15 @@
         return stay, moves
 
     done = {}
-    waiting = list(enumerate(ready))
+    waiting = [(n, rest) for n, *rest in ready]
     hops = sum_over(table, land, t_sems, [over, sib] + others)
     while waiting or background.now < len(background.stages):
         for n, (layer, heads, stage) in list(waiting):
-            if stage < background.now:
+            if stage < max(0, background.now - 1) or background.now >= len(background.stages):
                 background.arrived(stage)
                 done[heads] = home(n, layer, heads)
-                waiting.remove((n, (layer, heads, stage)))
+                waiting.remove((n, [layer, heads, stage]))
+                break
         next(hops, None)
         next(hops, None)
         if background.now < len(background.stages):
@@ -1468,7 +1535,7 @@
     return fused_call(
         grid, functools.partial(tail_kernel, grid, ready), "tail", plan, gain_rows, [VMEM] * 4,
         shaped(
-            *[((2, 3, depth, units), bf16)] * 2, *[((depth, BLOCK), bf16)] * 2, ((8, width), f32)
+            *[((2, 3, depth, units), bf16)] * 2, *[((depth * 3 // 2, BLOCK), bf16)] * 2, ((8, width), f32)
         ),
         (ANY,) * 4 + (VMEM,),
         [
@@ -1483,10 +1550,11 @@
 
 
 def finish_kernel(
-    ffn_own, ffn_came, attn_own, attn_came, query, key, value, out, gate, up, down
+    ffn_own, ffn_came, attn_own, attn_came, out_one, out_two, grad_one, grad_two,
+    produced, grads, query, key, value, out, gate, up, down,
 ):
     x = lax.axis_index("section")
-    units = ffn_own.shape[3]
+    depth, units = ffn_own.shape[2:]
 
     def put(side, ffn_ref, attn_ref):
         for core in range(2):
@@ -1496,14 +1564,18 @@
             down[at] = jnp.transpose(ffn_ref[core, 2].astype(f32))
 
         def head(n):
-            return attn_ref[:, n * HD : (n + 1) * HD].astype(f32)
+            if n < 4:
+                return attn_ref[:depth, n * HD : (n + 1) * HD].astype(f32)
+            return jnp.concatenate(
+                [attn_ref[depth:, k * HD : (k + 1) * HD].astype(f32) for k in (n - 4, n - 2)], 0
+            )
 
         for h in range(2):
             at = slice((2 * side + h) * HD, (2 * side + h + 1) * HD)
             query[:, at] = head(h)
             out[at] = jnp.transpose(head(4 + h))
-        key[:, side * HD : (side + 1) * HD] = head(2)
-        value[:, side * HD : (side + 1) * HD] = head(3)
+        key[side * HD : (side + 1) * HD] = jnp.transpose(head(2))
+        value[side * HD : (side + 1) * HD] = jnp.transpose(head(3))
 
     for layer in range(2):
 
@@ -1511,35 +1583,27 @@
         def _():
             put(layer, ffn_own, attn_own)
             put(1 - layer, ffn_came, attn_came)
-
-
-def finish_call(blocks, shards):
-    return pl.pallas_call(
+            produced[layer] = out_one[...]
+            produced[1 - layer] = out_two[...]
+            grads[layer] = grad_one[...].astype(f32)
+            grads[1 - layer] = grad_two[...].astype(f32)
+
+
+def finish_call(blocks, outs, grads, shards):
+    shape = (2,) + outs[0].shape
+    shapes = [shard.shape[1:] for shard in shards]
+    shapes[1:3] = [shape[::-1] for shape in shapes[1:3]]
+    produced, grads, query, key, value, *rest = pl.pallas_call(
         finish_kernel,
-        out_shape=tuple(jax.ShapeDtypeStruct(shard.shape[1:], f32) for shard in shards),
-        in_specs=[VMEM] * 4,
-        out_specs=(VMEM,) * 7,
+        out_shape=shaped((shape, bf16), (shape, f32))
+        + tuple(jax.ShapeDtypeStruct(one, f32) for one in shapes),
+        in_specs=[VMEM] * 8,
+        out_specs=(VMEM,) * 9,
         compiler_params=params(),
-        cost_estimate=cost(6),
+        cost_estimate=cost(8),
         name="finish",
-    )(*blocks)
-
-
-def turning(doc_row):
-    places = jnp.arange(doc_row.shape[-1], dtype=jnp.int32)
-    begins = jnp.concatenate([jnp.ones((1,), dtype=bool), doc_row[1:] != doc_row[:-1]], -1)
-    starts = lax.cummax(jnp.where(begins, places, 0), axis=0)
-    positions = (places - starts).astype(f32)
-    ladder = jnp.arange(HD // 2, dtype=f32)
-    frequency = rope_base ** (-2.0 * ladder / HD)
-    angles = positions[..., None] * frequency
-    cosine, sine_part = jnp.cos(angles), jnp.sin(angles)
-    blank = jnp.zeros((doc_row.shape[0], HP - HD), f32)
-    return (
-        starts,
-        jnp.concatenate([cosine, cosine, blank], -1),
-        jnp.concatenate([-sine_part, sine_part, blank], -1),
-    )
+    )(*blocks, *outs, *grads)
+    return produced, grads, query, key.T, value.T, *rest
 
 
 def after(value, *others):
@@ -1600,51 +1664,39 @@
         first, last = grid.send(block[0], route(0)), grid.send(block[1], route(1))
         return jnp.where(z // C == 0, first, last)
 
-    def leave(block, section):
-        def route(m):
+    def leave(lower_block, upper_block):
+        first = z // C == 0
+
+        def route(swap):
             def go(x, y, c, z):
-                if z // C != m:
-                    return None
+                section = (z // C + swap) % 2
                 return (section, y, z % C, 2 * c + (x + z) % 2)
 
             return go
 
-        return [grid.send(block, route(m)) for m in range(micro)]
+        same = grid.send(jnp.where(first, lower_block, upper_block), route(0))
+        swapped_over = grid.send(jnp.where(first, upper_block, lower_block), route(1))
+        return same, swapped_over
 
     rows_in = enter(inputs)
-    docs = grid.over_c(doc_ids)
-    docs = jnp.where(c == z % C, doc_ids, docs)[:, 0]
-    doc_row = lax.dynamic_index_in_dim(docs, z // C, 0, keepdims=False)
-    length = doc_row.shape[0]
-    starts, cosine, sine_part = turning(doc_row)
-    ids = place_id(grid)
-
-    def in_my_order(rows_of):
-        return jnp.stack(
-            [lax.dynamic_slice_in_dim(rows_of, ids[n] * rows, rows, 0) for n in range(4)]
-        )
-
-    facts = {
-        "tok": in_my_order(jnp.arange(length, dtype=jnp.int32)),
-        "from": in_my_order(starts),
-        "cos": in_my_order(cosine),
-        "sin": in_my_order(sine_part),
-    }
-
     halves = Z // 2
     tall = C * depth
     units = wg.shape[2] // 4
+    share_rows = depth * 3 // 2
     upper, lower = pl.ds(0, tall // 2), pl.ds(tall // 2, tall // 2)
-    attn_cuts = [((upper,), (upper,), None), ((lower,), None, (lower,))]
+    cores = [pl.ds(core * share_rows, share_rows) for core in range(2)]
+    attn_cuts = [((cores[0],), (cores[0],), None), ((cores[1],), None, (cores[1],))]
     ffn_cuts = [((m,), (m, upper), (m, lower)) for m in range(3)]
-    attn = [Gather(grid, (tall, BLOCK), attn_cuts, True) for _ in range(2)]
+    attn = [Gather(grid, (C * share_rows, BLOCK), attn_cuts, True) for _ in range(2)]
     ffn = [Gather(grid, (3, tall, units), ffn_cuts) for _ in range(2)]
     plan = Plan()
     joins = [[ring.begin(plan) for ring in rings] for rings in (attn, ffn)]
     attn[0].add(plan, 0)
     ffn[0].add(plan, max(0, len(plan.stages) - 2), 1)
     shards = (wq, wk, wv, wo, wg, wu, wd)
-    gain_all = start_call(grid, plan, joins, max(0, len(plan.stages) - 3), shards, gains)
+    gain_all, facts = start_call(
+        grid, plan, joins, max(0, len(plan.stages) - 3), shards, gains, doc_ids, rows
+    )
 
     hidden = rows_in
     kept = []
@@ -1653,7 +1705,7 @@
         hidden, keep = layer_forward(grid, hidden, attn[s], ffn[s], nexts, gain_all[s], facts)
         kept.append(keep)
     rows_cot = enter(after(cotangent, kept[1][2]))
-    outs = [leave(after(kept[1][0], hidden, rows_cot), 0), leave(after(hidden, rows_cot), 1)]
+    outs = leave(after(kept[1][0], hidden, rows_cot), after(hidden, rows_cot))
 
     def sum_ffn(terms):
         def block(m):
@@ -1667,50 +1719,46 @@
         return Scatter(grid, parts, (3, tall, units))
 
     def sum_attn(qkv_term, out_term):
-        size = tall // 2
-
-        def block(row, count):
+        def top(core):
             return lambda yy, zz: (
-                pl.ds(pl.multiple_of(yy * tall + row, size), size),
-                pl.ds(pl.multiple_of(zz % halves * count, HP), count),
+                pl.ds(pl.multiple_of((yy * C + core) * depth, depth), depth),
+                pl.ds(pl.multiple_of(zz % halves * BLOCK, BLOCK), BLOCK),
             )
 
+        def below(core):
+            return lambda yy, zz: (yy * C + core, zz % halves)
+
         parts = []
-        for cuts, rows_at, row in ((attn_cuts[0], upper, 0), (attn_cuts[1], lower, size)):
-            parts.append(
-                (
-                    cuts,
-                    [
-                        (qkv_term, block(row, 4 * HD), (rows_at, pl.ds(0, 4 * HD))),
-                        (out_term, block(row, 2 * HP), (rows_at, pl.ds(4 * HD, 2 * HP))),
-                    ],
-                )
-            )
-        return Scatter(grid, parts, (tall, BLOCK), True)
+        for core in range(C):
+            first = core * share_rows
+            places = [
+                (qkv_term, top(core), (pl.ds(first, depth),)),
+                (out_term, below(core), (pl.ds(first + depth, depth // 2),)),
+            ]
+            parts.append((attn_cuts[core], places))
+        return Scatter(grid, parts, (C * share_rows, BLOCK), True)
 
     upstream = rows_cot
     gain_terms, running = [None] * 2, []
-    leaving = outs[0] + outs[1]
+    waited, grads = outs, [None] * 2
     for s in (1, 0):
         upstream, gain_terms[s] = layer_backward(
-            grid, upstream, kept[s], attn[s], ffn[s], gain_all[s], facts, running, sum_ffn, sum_attn, leaving
+            grid, upstream, kept[s], attn[s], ffn[s], gain_all[s], facts, running, sum_ffn, sum_attn, waited
         )
-        leaving = leave(upstream, s)
-        if s == 1:
-            upper_grads = leaving
-    grads_in = [leaving, upper_grads]
-    produced = jnp.where(at_zero, jnp.stack(outs[0]), jnp.stack(outs[1]))
+        grads[s], waited = upstream, ()
+    grads_in = leave(*grads)
     plan = Plan()
     ready = []
-    for n in (1, 3, 0, 2):
+    for n in (3, 2, 1, 0):
         left = running[n].left()
         running[n].add(plan, 0, left, True)
         ready.append((1 - n // 2, n % 2 == 1, left - 1))
         running[n].total(plan)
+    order = sorted(range(4), key=lambda n: ready[n][2])
+    ready = [(n,) + ready[n] for n in order]
     *blocks, gain_sum = tail_call(grid, plan, ready, gain_terms[0] + gain_terms[1], depth, units)
-    grads_in = jnp.where(at_zero, jnp.stack(grads_in[0]), jnp.stack(grads_in[1])).astype(f32)
-
-    terms = finish_call(blocks, shards)
+
+    produced, grads_in, *terms = finish_call(blocks, outs, grads_in, shards)
     share = gains.shape[2]
     mine = (y * C + c) * Z + z
     gain_share = lax.dynamic_slice(gain_sum, (2 * x, mine * share), (2, share))[None]

time: 846 us -> 802 us (0.948)
  Pallas kernels: 781 us -> 759 us
    pallas_call x10, Pallas kernels: 776 us -> 750 us  [fused_call(): pl.pallas_call(whole, out_shape=tuple(outs) + tuple(plan.outs), in_specs=...]
    ppermute x13 -> x8, starting transfers between devices: 28.7 us -> 20.6 us  [send(): return lax.ppermute(block, AXES, pairs)]
  transfers between devices with their start and end apart: 13 -> 8, of which waited for: 0 -> 0; matrix products, arithmetic and copies ran while one was open for 2% -> 1% of each run, Pallas kernels for 46% -> 40%
where the time goes in v5:
time: 802 us; the launch traced here: 793 us
  Pallas kernels  759 us (95%)
  starting transfers between devices  20.6 us (3%)
  local copies, waits for them, and re-layouts  8.45 us (1%)
    pallas_call x10, Pallas kernels, fused_call(): pl.pallas_call(whole, out_shape=tuple(outs) + tuple(plan.outs), in_specs=...  750 us
    ppermute x8, starting transfers between devices, send(): return lax.ppermute(block, AXES, pairs)  20.6 us
  transfers between devices with their start and end apart: 8, of which 0 were waited for; matrix products, arithmetic and copies ran while one was open for 1% of the time, Pallas kernels for 40%

profile of v5, /device:TPU:1, one launch (start us, length us, event | category | flops | bytes accessed | tf_op | source)
XLA Modules:
  0.0 792.5 jit_solution(8414149711666202132)
XLA Ops:
  0.7 1.5 slice_bitcast_fusion.2
  2.2 0.7 collective-permute-start.1
  2.9 1.3 collective-permute-start
  4.2 0.8 copy.22.refs_1_
  5.1 0.8 copy.23.refs_2_
  5.9 0.6 jit_solution_.3.refs_9_
  6.5 100.2 %start.1 = (f32[2,2,1536]{2,1,0:T(2,128)}, f32[4,256,128]{2,1,0:T(8,128)}, f32[4,256,128]{2,1,0:T(8,128)}, s32[4,1,256]{2,1,0:T(1,128)}, s32[4,1,256]{2,1,0:T(1,...) custom-call(bf16[1,384,384]{2,1,0:T(8,128)(2,1)} %refs_0_.1, ...), custom_call_target="tpu_custom_call" | custom-call | flops 70000001024 | bytes 1048576 | tf_op jit(solution)/shard_map/start/pallas_call | solution.py:526
  106.7 1.4 slice_bitcast_fusion.4
  108.1 1.0 broadcast_select_fusion.5.refs_0_.refs_1_
  109.1 73.1 %attn.2 = (bf16[4,256,1536]{2,1,0:T(8,128)(2,1)}, bf16[4,4,256,128]{3,2,1,0:T(8,128)(2,1)}, bf16[2,4,256,128]{3,2,1,0:T(8,128)(2,1)}, bf16[2,4,256,128]{3,2,1,0:...) custom-call(bf16[256,1536]{1,0:T(8,128)(2,1)} %broadcast_select_fusi, ...), custom_call_target="tpu_custom_call" | custom-call | flops 60000002048 | bytes 1048576 | tf_op jit(solution)/shard_map/attn/pallas_call | solution.py:526
  182.2 67.9 %ffn.2 = (bf16[256,1536]{1,0:T(8,128)(2,1)}, bf16[4,256,1536]{2,1,0:T(8,128)(2,1)}, bf16[4,256,1024]{2,1,0:T(8,128)(2,1)}, bf16[4,256,1024]{2,1,0:T(8,128)(2,1)}...) custom-call(f32[256,1536]{1,0:T(8,128)} %get-tuple-element.129.refs_, ...), custom_call_target="tpu_custom_call" | custom-call | flops 44000002048 | bytes 1048576 | tf_op jit(solution)/shard_map/ffn/pallas_call | solution.py:526
  250.1 70.7 %attn.3 = (bf16[4,256,1536]{2,1,0:T(8,128)(2,1)}, bf16[4,4,256,128]{3,2,1,0:T(8,128)(2,1)}, bf16[2,4,256,128]{3,2,1,0:T(8,128)(2,1)}, bf16[2,4,256,128]{3,2,1,0:...) custom-call(bf16[256,1536]{1,0:T(8,128)(2,1)} %get-tuple-element.161, ...), custom_call_target="tpu_custom_call" | custom-call | flops 60000002048 | bytes 1048576 | tf_op jit(solution)/shard_map/attn/pallas_call | solution.py:526
  321.0 0.7 collective-permute-start.3
  321.7 1.5 collective-permute-start.2
  323.2 42.4 %ffn.3 = (bf16[256,1536]{1,0:T(8,128)(2,1)}, bf16[4,256,1536]{2,1,0:T(8,128)(2,1)}, bf16[4,256,1024]{2,1,0:T(8,128)(2,1)}, bf16[4,256,1024]{2,1,0:T(8,128)(2,1)}, bf16[4,256,1024]{2,1,0:T(8,128)(2,1)}) custom-call(f32[256,1536]{1,0:T(8,128)} %get-tuple-element.148.refs_0_.refs_1_, f32[1,1536]{1,0:T(1,128)} %get-tuple-element.224.refs_1_.refs_2_, ...), custom_call_target="tpu_custom_call" | custom-call | flops 44000002048 | bytes 1048576 | tf_op jit(solution)/shard_map/ffn/pallas_call | solution.py:526
  365.7 1.0 broadcast_select_fusion.4.refs_0_
  366.6 0.4 copy-done.1
  367.0 0.3 copy-done.3
  367.5 3.2 collective-permute-start.5
  370.7 4.2 collective-permute-start.4
  374.9 59.7 %ffn_back.2 = (f32[256,1536]{1,0:T(8,128)}, f32[8,1536]{1,0:T(8,128)}, bf16[3,1536,1024]{2,1,0:T(8,128)(2,1)}) custom-call(bf16[256,1536]{1,0:T(8,128)(2,1)} %broadcast_select_fusion.4.refs_0_, f32[256,1536]{1,0:T(8,128)} %get-tuple-element.148.refs_0_.refs_1_, f32[1,1536]{1,0:T(1,128)} %get-tuple-element.224.refs_1_.refs_2_, ...), custom_call_target="tpu_custom_call" | custom-call | flops 60000002048 | bytes 1048576 | tf_op jit(solution)/shard_map/ffn_back/pallas_call | solution.py:526
  434.7 73.6 %attn_back.2 = (bf16[256,1536]{1,0:T(8,128)(2,1)}, f32[8,1536]{1,0:T(8,128)}, bf16[1536,768]{1,0:T(8,128)(2,1)}, bf16[4,2,192,384]{3,2,1,0:T(8,128)(2,1)}, bf16[...) custom-call(f32[256,1536]{1,0:T(8,128)} %get-tuple-element.159.refs_0_, ...), custom_call_target="tpu_custom_call" | custom-call | flops 80000000000 | bytes 1048576 | tf_op jit(solution)/shard_map/attn_back/pallas_call | solution.py:526
  508.3 70.8 %ffn_back.3 = (f32[256,1536]{1,0:T(8,128)}, f32[8,1536]{1,0:T(8,128)}, bf16[3,1536,1024]{2,1,0:T(8,128)(2,1)}, bf16[3,768,256]{2,1,0:T(8,128)(2,1)}, bf16[3,768,...) custom-call(bf16[256,1536]{1,0:T(8,128)(2,1)} %get-tuple-element.172.refs_0_, ...), custom_call_target="tpu_custom_call" | custom-call | flops 60000002048 | bytes 1048576 | tf_op jit(solution)/shard_map/ffn_back/pallas_call | solution.py:526
  579.1 76.3 %attn_back.3 = (bf16[256,1536]{1,0:T(8,128)(2,1)}, f32[8,1536]{1,0:T(8,128)}, bf16[1536,768]{1,0:T(8,128)(2,1)}, bf16[4,2,192,384]{3,2,1,0:T(8,128)(2,1)}, bf16[...) custom-call(f32[256,1536]{1,0:T(8,128)} %get-tuple-element.181.refs_0_, ...), custom_call_target="tpu_custom_call" | custom-call | flops 80000000000 | bytes 1048576 | tf_op jit(solution)/shard_map/attn_back/pallas_call | solution.py:526
  655.5 1.2 broadcast_select_fusion
  656.7 7.1 collective-permute-start.7
  663.8 1.9 collective-permute-start.6
  665.7 115.4 %tail.1 = (bf16[2,3,384,256]{3,2,1,0:T(8,128)(2,1)}, bf16[2,3,384,256]{3,2,1,0:T(8,128)(2,1)}, bf16[576,384]{1,0:T(8,128)(2,1)}, bf16[576,384]{1,0:T(8,128)(2,1)}, f32[8,1536]{1,0:T(8,128)}) custom-call(f32[8,1536]{1,0:T(8,128)} %get-tuple-element.189.refs_0_, f32[8,1536]{1,0:T(8,128)} %get-tuple-element.190.refs_1_, f32[8,1536]{1,0:T(8,128)} %get-tuple-element.191.refs_2_, ...), custom_call_target="tpu_custom_call" | custom-call | flops 60000002048 | bytes 1048576 | tf_op jit(solution)/shard_map/tail/pallas_call | solution.py:526
  781.1 1.3 dynamic-slice_bitcast_fusion
  782.5 0.9 copy-done.9
  783.4 0.2 copy-done.10
  783.6 8.5 %finish.1 = (bf16[2,256,1536]{2,1,0:T(8,128)(2,1)}, f32[2,256,1536]{2,1,0:T(8,128)}, f32[384,384]{1,0:T(8,128)}, f32[192,384]{1,0:T(8,128)}, f32[192,384]{1,0:T(...) custom-call(bf16[2,3,384,256]{3,2,1,0:T(8,128)(2,1)} %get-tuple-element.201.ffn_ow, ...), custom_call_target="tpu_custom_call" | custom-call | flops 8000000000 | bytes 1048576 | tf_op jit(solution)/shard_map/finish/pallas_call | solution.py:1596
  (28 shorter events, 0.4 us)
Async XLA Ops:
  0.6 5.2 copy-start.6
  0.7 3.6 copy-start.4
  0.7 4.4 copy-start.5
  2.2 105.9 %collective-permute-start.1 = (bf16[256,1536]{1,0:T(8,128)(2,1)S(1)}, bf16[256,1536]{1,0:T(8,128)(2,1)S(1)}, u32[]{:S(2)}, u32[]{:S(2)}) collective-permute-start(bf16[256,1536]{1,0:T(8,128)(2,1)S(1)} %get-tuple-element.222), channel_id=1, source_target_pairs={{0,2},{2,6},{5,3},{7,7},{8,10},{10,14},{13,11},{15,15},{17,18},{19... | collective-permute-start | bytes 2359304 | tf_op jit(solution)/shard_map/ppermute | solution.py:49
  2.9 105.2 %collective-permute-start = (bf16[256,1536]{1,0:T(8,128)(2,1)S(1)}, bf16[256,1536]{1,0:T(8,128)(2,1)S(1)}, u32[]{:S(2)}, u32[]{:S(2)}) collective-permute-start(bf16[256,1536]{1,0:T(8,128)(2,1)S(1)} %get-tuple-element.223), channel_id=1, source_target_pairs={{0,0},{2,4},{5,1},{7,5},{8,8},{10,12},{13,9},{15,13},{17,16},{19,2... | collective-permute-start | bytes 2359304 | tf_op jit(solution)/shard_map/ppermute | solution.py:49
  250.1 70.7 %copy-start = (bf16[2,256,1536]{2,1,0:T(8,128)(2,1)S(1)}, bf16[2,256,1536]{2,1,0:T(8,128)(2,1)}, u32[]{:S(2)}) copy-start(bf16[2,256,1536]{2,1,0:T(8,128)(2,1)} %param.14) | copy-start | bytes 4718596
  321.0 44.7 %collective-permute-start.3 = (bf16[256,1536]{1,0:T(8,128)(2,1)S(1)}, bf16[256,1536]{1,0:T(8,128)(2,1)S(1)}, u32[]{:S(2)}, u32[]{:S(2)}) collective-permute-start(bf16[256,1536]{1,0:T(8,128)(2,1)S(1)} %get-tuple-element.220), channel_id=1, source_target_pairs={{0,2},{2,6},{5,3},{7,7},{8,10},{10,14},{13,11},{15,15},{17,18},{19... | collective-permute-start | bytes 2359304 | tf_op jit(solution)/shard_map/ppermute | solution.py:49
  321.7 44.0 %collective-permute-start.2 = (bf16[256,1536]{1,0:T(8,128)(2,1)S(1)}, bf16[256,1536]{1,0:T(8,128)(2,1)S(1)}, u32[]{:S(2)}, u32[]{:S(2)}) collective-permute-start(bf16[256,1536]{1,0:T(8,128)(2,1)S(1)} %get-tuple-element.221), channel_id=1, source_target_pairs={{0,0},{2,4},{5,1},{7,5},{8,8},{10,12},{13,9},{15,13},{17,16},{19,2... | collective-permute-start | bytes 2359304 | tf_op jit(solution)/shard_map/ppermute | solution.py:49
  365.6 1.4 copy-start.1
  365.7 1.6 copy-start.3
  367.5 67.1 %collective-permute-start.5 = (bf16[256,1536]{1,0:T(8,128)(2,1)S(1)}, bf16[256,1536]{1,0:T(8,128)(2,1)S(1)}, u32[]{:S(2)}, u32[]{:S(2)}) collective-permute-start(bf16[256,1536]{1,0:T(8,128)(2,1)S(1)} %get-tuple-element.218), channel_id=1, source_target_pairs={{0,16},{1,21},{2,0},{3,5},{4,18},{5,23},{6,2},{7,7},{8,24},{9,29},... | collective-permute-start | bytes 2359304 | tf_op jit(solution)/shard_map/ppermute | solution.py:49
  370.7 63.9 %collective-permute-start.4 = (bf16[256,1536]{1,0:T(8,128)(2,1)S(1)}, bf16[256,1536]{1,0:T(8,128)(2,1)S(1)}, u32[]{:S(2)}, u32[]{:S(2)}) collective-permute-start(bf16[256,1536]{1,0:T(8,128)(2,1)S(1)} %get-tuple-element.219), channel_id=1, source_target_pairs={{0,0},{1,5},{2,16},{3,21},{4,2},{5,7},{6,18},{7,23},{8,8},{9,13},{... | collective-permute-start | bytes 2359304 | tf_op jit(solution)/shard_map/ppermute | solution.py:49
  434.6 73.6 %copy-start.7 = (bf16[256,1536]{1,0:T(8,128)(2,1)}, bf16[256,1536]{1,0:T(8,128)(2,1)S(1)}, u32[]{:S(2)}) copy-start(bf16[256,1536]{1,0:T(8,128)(2,1)S(1)} %collective-permute-done.5.out_two) | copy-start | bytes 2359300
  434.7 73.6 %copy-start.8 = (bf16[256,1536]{1,0:T(8,128)(2,1)}, bf16[256,1536]{1,0:T(8,128)(2,1)S(1)}, u32[]{:S(2)}) copy-start(bf16[256,1536]{1,0:T(8,128)(2,1)S(1)} %collective-permute-done.4.out_one) | copy-start | bytes 2359300
  579.1 76.3 %copy-start.2 = (bf16[256,1536]{1,0:T(8,128)(2,1)S(1)}, bf16[256,1536]{1,0:T(8,128)(2,1)}, u32[]{:S(2)}) copy-start(bf16[256,1536]{1,0:T(8,128)(2,1)} %get-tuple-element.172.refs_0_) | copy-start | bytes 2359300
  656.7 125.7 %collective-permute-start.7 = (bf16[256,1536]{1,0:T(8,128)(2,1)S(1)}, bf16[256,1536]{1,0:T(8,128)(2,1)S(1)}, u32[]{:S(2)}, u32[]{:S(2)}) collective-permute-start(bf16[256,1536]{1,0:T(8,128)(2,1)S(1)} %get-tuple-element.216), channel_id=1, source_target_pairs={{0,16},{1,21},{2,0},{3,5},{4,18},{5,23},{6,2},{7,7},{8,24},{9,29},... | collective-permute-start | bytes 2359304 | tf_op jit(solution)/shard_map/ppermute | solution.py:49
  663.8 118.7 %collective-permute-start.6 = (bf16[256,1536]{1,0:T(8,128)(2,1)S(1)}, bf16[256,1536]{1,0:T(8,128)(2,1)S(1)}, u32[]{:S(2)}, u32[]{:S(2)}) collective-permute-start(bf16[256,1536]{1,0:T(8,128)(2,1)S(1)} %get-tuple-element.217), channel_id=1, source_target_pairs={{0,0},{1,5},{2,16},{3,21},{4,2},{5,7},{6,18},{7,23},{8,8},{9,13},{... | collective-permute-start | bytes 2359304 | tf_op jit(solution)/shard_map/ppermute | solution.py:49
  782.4 0.9 copy-start.9
  782.5 1.1 copy-start.10

commit v6 on v5

--- a/solution.py
+++ b/solution.py
@@ -884,33 +884,41 @@
     for copy in fetched:
         copy.wait()
 
-    def work(slot, start, size):
+    def work(slots, start, size):
         at = pl.ds(start, size)
+        tall = size * len(slots)
+
+        def rows_of(ref):
+            return jnp.concatenate([ref[slot, at] for slot in slots], 0)
+
+        def put(ref, cols, values):
+            for n, slot in enumerate(slots):
+                ref[slot, at, cols] = values[n * size : (n + 1) * size].astype(bf16)
 
         def tile(n, carry):
             cols = pl.ds(pl.multiple_of(n * STEP, STEP), STEP)
-            some = rows_ref[slot, at]
+            some = rows_of(rows_ref)
             gate = jnp.dot(some, held[0, :, cols], preferred_element_type=f32)
             up = jnp.dot(some, held[1, :, cols], preferred_element_type=f32)
-            gate_ref[slot, at, cols] = gate.astype(bf16)
-            up_ref[slot, at, cols] = up.astype(bf16)
-            hid_ref[slot, at, cols] = (gate * jax.nn.sigmoid(gate) * up).astype(bf16)
+            put(gate_ref, cols, gate)
+            put(up_ref, cols, up)
+            put(hid_ref, cols, gate * jax.nn.sigmoid(gate) * up)
             return carry
 
         lax.fori_loop(0, hidden // STEP, tile, 0)
 
         def tile_down(n, carry):
             cols = pl.ds(pl.multiple_of(n * STEP, STEP), STEP)
-            part[at, cols] = dot_nt(hid_ref[slot, at], held[2, cols])
+            part[:tall, cols] = dot_nt(rows_of(hid_ref), held[2, cols])
             return carry
 
         lax.fori_loop(0, width // STEP, tile_down, 0)
 
-    work(0, 0, rows)
+    work((0,), 0, rows)
     store(0)
     own[...] = mid_ref[...] + part[...]
     spread.near.wait_recv()
-    work(1, 0, rows)
+    work((1,), 0, rows)
     store(1)
     collect.give_near(part[...])
     background.advance()
@@ -921,10 +929,9 @@
         if k:
             background.advance()
         spread.relay[k].wait_recv()
-        work(3, k * size, size)
-        collect.give_side(k, part[cuts[k]])
-        work(2, k * size, size)
-        collect.give_over(k, part[cuts[k]])
+        work((3, 2), k * size, size)
+        collect.give_side(k, part[:size])
+        collect.give_over(k, part[size : 2 * size])
     store(2)
     store(3)
     background.advance()
@@ -1001,34 +1008,42 @@
     background.advance()
     wait_all(fetched + loads[:2])
 
-    def work(slot, start, size):
+    def work(slots, start, size):
         at = pl.ds(start, size)
+        tall = size * len(slots)
+
+        def rows_of(ref, cols=slice(None)):
+            return jnp.concatenate([ref[slot, at, cols] for slot in slots], 0)
+
+        def put(ref, cols, values):
+            for n, slot in enumerate(slots):
+                ref[slot, at, cols] = values[n * size : (n + 1) * size].astype(bf16)
 
         def tile(n, carry):
             cols = pl.ds(pl.multiple_of(n * STEP, STEP), STEP)
-            grad = jnp.dot(rows_ref[slot, at], held[2, :, cols], preferred_element_type=f32)
-            gate = gate_ref[slot, at, cols].astype(f32)
-            up = up_ref[slot, at, cols].astype(f32)
+            grad = jnp.dot(rows_of(rows_ref), held[2, :, cols], preferred_element_type=f32)
+            gate = rows_of(gate_ref, cols).astype(f32)
+            up = rows_of(up_ref, cols).astype(f32)
             sig = jax.nn.sigmoid(gate)
-            dgate_ref[slot, at, cols] = (grad * up * sig * (1.0 + gate * (1.0 - sig))).astype(bf16)
-            dup_ref[slot, at, cols] = (grad * gate * sig).astype(bf16)
+            put(dgate_ref, cols, grad * up * sig * (1.0 + gate * (1.0 - sig)))
+            put(dup_ref, cols, grad * gate * sig)
             return carry
 
         lax.fori_loop(0, hidden // STEP, tile, 0)
 
         def tile_back(n, carry):
             cols = pl.ds(pl.multiple_of(n * STEP, STEP), STEP)
-            part[at, cols] = dot_nt(dgate_ref[slot, at], held[0, cols]) + dot_nt(
-                dup_ref[slot, at], held[1, cols]
+            part[:tall, cols] = dot_nt(rows_of(dgate_ref), held[0, cols]) + dot_nt(
+                rows_of(dup_ref), held[1, cols]
             )
             return carry
 
         lax.fori_loop(0, width // STEP, tile_back, 0)
 
-    work(0, 0, rows)
+    work((0,), 0, rows)
     own[...] = part[...]
     spread.near.wait_recv()
-    work(1, 0, rows)
+    work((1,), 0, rows)
     collect.give_near(part[...])
     background.advance()
     cuts = pieces_of(rows)
@@ -1038,10 +1053,9 @@
         if k:
             background.advance()
         spread.relay[k].wait_recv()
-        work(3, k * size, size)
-        collect.give_side(k, part[cuts[k]])
-        work(2, k * size, size)
-        collect.give_over(k, part[cuts[k]])
+        work((3, 2), k * size, size)
+        collect.give_side(k, part[:size])
+        collect.give_over(k, part[size : 2 * size])
     background.advance()
     wait_all(loads[2:])
     outs = []

time: 802 us -> 800 us (level)
  no operation moved by 1% of the time
where the time goes in v6:
time: 800 us; the launch traced here: 791 us
  Pallas kernels  760 us (95%)
  starting transfers between devices  18.1 us (2%)
  local copies, waits for them, and re-layouts  8.45 us (1%)
    pallas_call x10, Pallas kernels, fused_call(): pl.pallas_call(whole, out_shape=tuple(outs) + tuple(plan.outs), in_specs=...  751 us
    ppermute x8, starting transfers between devices, send(): return lax.ppermute(block, AXES, pairs)  18.1 us
  transfers between devices with their start and end apart: 8, of which 0 were waited for; matrix products, arithmetic and copies ran while one was open for 1% of the time, Pallas kernels for 40%

profile of v6, /device:TPU:1, one launch (start us, length us, event | category | flops | bytes accessed | tf_op | source)
XLA Modules:
  0.0 791.0 jit_solution(1047026799380219745)
XLA Ops:
  0.7 1.5 slice_bitcast_fusion.2
  2.2 0.7 collective-permute-start.1
  2.9 1.3 collective-permute-start
  4.2 0.8 copy.22.refs_1_
  5.1 0.8 copy.23.refs_2_
  5.9 0.6 jit_solution_.3.refs_9_
  6.5 100.2 %start.1 = (f32[2,2,1536]{2,1,0:T(2,128)}, f32[4,256,128]{2,1,0:T(8,128)}, f32[4,256,128]{2,1,0:T(8,128)}, s32[4,1,256]{2,1,0:T(1,128)}, s32[4,1,256]{2,1,0:T(1,...) custom-call(bf16[1,384,384]{2,1,0:T(8,128)(2,1)} %refs_0_.1, ...), custom_call_target="tpu_custom_call" | custom-call | flops 70000001024 | bytes 1048576 | tf_op jit(solution)/shard_map/start/pallas_call | solution.py:526
  106.7 1.4 slice_bitcast_fusion.4
  108.1 1.0 broadcast_select_fusion.5.refs_0_.refs_1_
  109.1 73.1 %attn.2 = (bf16[4,256,1536]{2,1,0:T(8,128)(2,1)}, bf16[4,4,256,128]{3,2,1,0:T(8,128)(2,1)}, bf16[2,4,256,128]{3,2,1,0:T(8,128)(2,1)}, bf16[2,4,256,128]{3,2,1,0:...) custom-call(bf16[256,1536]{1,0:T(8,128)(2,1)} %broadcast_select_fusi, ...), custom_call_target="tpu_custom_call" | custom-call | flops 60000002048 | bytes 1048576 | tf_op jit(solution)/shard_map/attn/pallas_call | solution.py:526
  182.2 66.2 %ffn.2 = (bf16[256,1536]{1,0:T(8,128)(2,1)}, bf16[4,256,1536]{2,1,0:T(8,128)(2,1)}, bf16[4,256,1024]{2,1,0:T(8,128)(2,1)}, bf16[4,256,1024]{2,1,0:T(8,128)(2,1)}...) custom-call(f32[256,1536]{1,0:T(8,128)} %get-tuple-element.129.refs_, ...), custom_call_target="tpu_custom_call" | custom-call | flops 44000002048 | bytes 1048576 | tf_op jit(solution)/shard_map/ffn/pallas_call | solution.py:526
  248.4 72.5 %attn.3 = (bf16[4,256,1536]{2,1,0:T(8,128)(2,1)}, bf16[4,4,256,128]{3,2,1,0:T(8,128)(2,1)}, bf16[2,4,256,128]{3,2,1,0:T(8,128)(2,1)}, bf16[2,4,256,128]{3,2,1,0:...) custom-call(bf16[256,1536]{1,0:T(8,128)(2,1)} %get-tuple-element.161, ...), custom_call_target="tpu_custom_call" | custom-call | flops 60000002048 | bytes 1048576 | tf_op jit(solution)/shard_map/attn/pallas_call | solution.py:526
  321.0 0.7 collective-permute-start.3
  321.7 1.5 collective-permute-start.2
  323.2 43.2 %ffn.3 = (bf16[256,1536]{1,0:T(8,128)(2,1)}, bf16[4,256,1536]{2,1,0:T(8,128)(2,1)}, bf16[4,256,1024]{2,1,0:T(8,128)(2,1)}, bf16[4,256,1024]{2,1,0:T(8,128)(2,1)}, bf16[4,256,1024]{2,1,0:T(8,128)(2,1)}) custom-call(f32[256,1536]{1,0:T(8,128)} %get-tuple-element.148.refs_0_.refs_1_, f32[1,1536]{1,0:T(1,128)} %get-tuple-element.224.refs_1_.refs_2_, ...), custom_call_target="tpu_custom_call" | custom-call | flops 44000002048 | bytes 1048576 | tf_op jit(solution)/shard_map/ffn/pallas_call | solution.py:526
  366.5 1.0 broadcast_select_fusion.4.refs_0_
  367.4 0.4 copy-done.1
  367.8 0.3 copy-done.3
  368.3 1.9 collective-permute-start.5
  370.2 4.5 collective-permute-start.4
  374.8 57.9 %ffn_back.2 = (f32[256,1536]{1,0:T(8,128)}, f32[8,1536]{1,0:T(8,128)}, bf16[3,1536,1024]{2,1,0:T(8,128)(2,1)}) custom-call(bf16[256,1536]{1,0:T(8,128)(2,1)} %broadcast_select_fusion.4.refs_0_, f32[256,1536]{1,0:T(8,128)} %get-tuple-element.148.refs_0_.refs_1_, f32[1,1536]{1,0:T(1,128)} %get-tuple-element.224.refs_1_.refs_2_, ...), custom_call_target="tpu_custom_call" | custom-call | flops 60000002048 | bytes 1048576 | tf_op jit(solution)/shard_map/ffn_back/pallas_call | solution.py:526
  432.7 73.8 %attn_back.2 = (bf16[256,1536]{1,0:T(8,128)(2,1)}, f32[8,1536]{1,0:T(8,128)}, bf16[1536,768]{1,0:T(8,128)(2,1)}, bf16[4,2,192,384]{3,2,1,0:T(8,128)(2,1)}, bf16[...) custom-call(f32[256,1536]{1,0:T(8,128)} %get-tuple-element.159.refs_0_, ...), custom_call_target="tpu_custom_call" | custom-call | flops 80000000000 | bytes 1048576 | tf_op jit(solution)/shard_map/attn_back/pallas_call | solution.py:526
  506.6 69.3 %ffn_back.3 = (f32[256,1536]{1,0:T(8,128)}, f32[8,1536]{1,0:T(8,128)}, bf16[3,1536,1024]{2,1,0:T(8,128)(2,1)}, bf16[3,768,256]{2,1,0:T(8,128)(2,1)}, bf16[3,768,...) custom-call(bf16[256,1536]{1,0:T(8,128)(2,1)} %get-tuple-element.172.refs_0_, ...), custom_call_target="tpu_custom_call" | custom-call | flops 60000002048 | bytes 1048576 | tf_op jit(solution)/shard_map/ffn_back/pallas_call | solution.py:526
  575.9 78.2 %attn_back.3 = (bf16[256,1536]{1,0:T(8,128)(2,1)}, f32[8,1536]{1,0:T(8,128)}, bf16[1536,768]{1,0:T(8,128)(2,1)}, bf16[4,2,192,384]{3,2,1,0:T(8,128)(2,1)}, bf16[...) custom-call(f32[256,1536]{1,0:T(8,128)} %get-tuple-element.181.refs_0_, ...), custom_call_target="tpu_custom_call" | custom-call | flops 80000000000 | bytes 1048576 | tf_op jit(solution)/shard_map/attn_back/pallas_call | solution.py:526
  654.2 1.2 broadcast_select_fusion
  655.4 5.5 collective-permute-start.7
  660.9 1.9 collective-permute-start.6
  662.8 116.8 %tail.1 = (bf16[2,3,384,256]{3,2,1,0:T(8,128)(2,1)}, bf16[2,3,384,256]{3,2,1,0:T(8,128)(2,1)}, bf16[576,384]{1,0:T(8,128)(2,1)}, bf16[576,384]{1,0:T(8,128)(2,1)}, f32[8,1536]{1,0:T(8,128)}) custom-call(f32[8,1536]{1,0:T(8,128)} %get-tuple-element.189.refs_0_, f32[8,1536]{1,0:T(8,128)} %get-tuple-element.190.refs_1_, f32[8,1536]{1,0:T(8,128)} %get-tuple-element.191.refs_2_, ...), custom_call_target="tpu_custom_call" | custom-call | flops 60000002048 | bytes 1048576 | tf_op jit(solution)/shard_map/tail/pallas_call | solution.py:526
  779.6 1.3 dynamic-slice_bitcast_fusion
  781.0 0.9 copy-done.9
  781.9 0.2 copy-done.10
  782.1 8.5 %finish.1 = (bf16[2,256,1536]{2,1,0:T(8,128)(2,1)}, f32[2,256,1536]{2,1,0:T(8,128)}, f32[384,384]{1,0:T(8,128)}, f32[192,384]{1,0:T(8,128)}, f32[192,384]{1,0:T(...) custom-call(bf16[2,3,384,256]{3,2,1,0:T(8,128)(2,1)} %get-tuple-element.201.ffn_ow, ...), custom_call_target="tpu_custom_call" | custom-call | flops 8000000000 | bytes 1048576 | tf_op jit(solution)/shard_map/finish/pallas_call | solution.py:1610
  (28 shorter events, 0.4 us)
Async XLA Ops:
  0.6 5.2 copy-start.6
  0.7 3.6 copy-start.4
  0.7 4.4 copy-start.5
  2.2 105.9 %collective-permute-start.1 = (bf16[256,1536]{1,0:T(8,128)(2,1)S(1)}, bf16[256,1536]{1,0:T(8,128)(2,1)S(1)}, u32[]{:S(2)}, u32[]{:S(2)}) collective-permute-start(bf16[256,1536]{1,0:T(8,128)(2,1)S(1)} %get-tuple-element.222), channel_id=1, source_target_pairs={{0,2},{2,6},{5,3},{7,7},{8,10},{10,14},{13,11},{15,15},{17,18},{19... | collective-permute-start | bytes 2359304 | tf_op jit(solution)/shard_map/ppermute | solution.py:49
  2.9 105.2 %collective-permute-start = (bf16[256,1536]{1,0:T(8,128)(2,1)S(1)}, bf16[256,1536]{1,0:T(8,128)(2,1)S(1)}, u32[]{:S(2)}, u32[]{:S(2)}) collective-permute-start(bf16[256,1536]{1,0:T(8,128)(2,1)S(1)} %get-tuple-element.223), channel_id=1, source_target_pairs={{0,0},{2,4},{5,1},{7,5},{8,8},{10,12},{13,9},{15,13},{17,16},{19,2... | collective-permute-start | bytes 2359304 | tf_op jit(solution)/shard_map/ppermute | solution.py:49
  248.4 72.5 %copy-start = (bf16[2,256,1536]{2,1,0:T(8,128)(2,1)S(1)}, bf16[2,256,1536]{2,1,0:T(8,128)(2,1)}, u32[]{:S(2)}) copy-start(bf16[2,256,1536]{2,1,0:T(8,128)(2,1)} %param.14) | copy-start | bytes 4718596
  321.0 45.5 %collective-permute-start.3 = (bf16[256,1536]{1,0:T(8,128)(2,1)S(1)}, bf16[256,1536]{1,0:T(8,128)(2,1)S(1)}, u32[]{:S(2)}, u32[]{:S(2)}) collective-permute-start(bf16[256,1536]{1,0:T(8,128)(2,1)S(1)} %get-tuple-element.220), channel_id=1, source_target_pairs={{0,2},{2,6},{5,3},{7,7},{8,10},{10,14},{13,11},{15,15},{17,18},{19... | collective-permute-start | bytes 2359304 | tf_op jit(solution)/shard_map/ppermute | solution.py:49
  321.7 44.8 %collective-permute-start.2 = (bf16[256,1536]{1,0:T(8,128)(2,1)S(1)}, bf16[256,1536]{1,0:T(8,128)(2,1)S(1)}, u32[]{:S(2)}, u32[]{:S(2)}) collective-permute-start(bf16[256,1536]{1,0:T(8,128)(2,1)S(1)} %get-tuple-element.221), channel_id=1, source_target_pairs={{0,0},{2,4},{5,1},{7,5},{8,8},{10,12},{13,9},{15,13},{17,16},{19,2... | collective-permute-start | bytes 2359304 | tf_op jit(solution)/shard_map/ppermute | solution.py:49
  366.4 1.4 copy-start.1
  366.4 1.6 copy-start.3
  368.3 64.4 %collective-permute-start.5 = (bf16[256,1536]{1,0:T(8,128)(2,1)S(1)}, bf16[256,1536]{1,0:T(8,128)(2,1)S(1)}, u32[]{:S(2)}, u32[]{:S(2)}) collective-permute-start(bf16[256,1536]{1,0:T(8,128)(2,1)S(1)} %get-tuple-element.218), channel_id=1, source_target_pairs={{0,16},{1,21},{2,0},{3,5},{4,18},{5,23},{6,2},{7,7},{8,24},{9,29},... | collective-permute-start | bytes 2359304 | tf_op jit(solution)/shard_map/ppermute | solution.py:49
  370.2 62.5 %collective-permute-start.4 = (bf16[256,1536]{1,0:T(8,128)(2,1)S(1)}, bf16[256,1536]{1,0:T(8,128)(2,1)S(1)}, u32[]{:S(2)}, u32[]{:S(2)}) collective-permute-start(bf16[256,1536]{1,0:T(8,128)(2,1)S(1)} %get-tuple-element.219), channel_id=1, source_target_pairs={{0,0},{1,5},{2,16},{3,21},{4,2},{5,7},{6,18},{7,23},{8,8},{9,13},{... | collective-permute-start | bytes 2359304 | tf_op jit(solution)/shard_map/ppermute | solution.py:49
  432.7 73.9 %copy-start.7 = (bf16[256,1536]{1,0:T(8,128)(2,1)}, bf16[256,1536]{1,0:T(8,128)(2,1)S(1)}, u32[]{:S(2)}) copy-start(bf16[256,1536]{1,0:T(8,128)(2,1)S(1)} %collective-permute-done.5.out_two) | copy-start | bytes 2359300
  432.7 73.9 %copy-start.8 = (bf16[256,1536]{1,0:T(8,128)(2,1)}, bf16[256,1536]{1,0:T(8,128)(2,1)S(1)}, u32[]{:S(2)}) copy-start(bf16[256,1536]{1,0:T(8,128)(2,1)S(1)} %collective-permute-done.4.out_one) | copy-start | bytes 2359300
  575.9 78.2 %copy-start.2 = (bf16[256,1536]{1,0:T(8,128)(2,1)S(1)}, bf16[256,1536]{1,0:T(8,128)(2,1)}, u32[]{:S(2)}) copy-start(bf16[256,1536]{1,0:T(8,128)(2,1)} %get-tuple-element.172.refs_0_) | copy-start | bytes 2359300
  655.4 125.6 %collective-permute-start.7 = (bf16[256,1536]{1,0:T(8,128)(2,1)S(1)}, bf16[256,1536]{1,0:T(8,128)(2,1)S(1)}, u32[]{:S(2)}, u32[]{:S(2)}) collective-permute-start(bf16[256,1536]{1,0:T(8,128)(2,1)S(1)} %get-tuple-element.216), channel_id=1, source_target_pairs={{0,16},{1,21},{2,0},{3,5},{4,18},{5,23},{6,2},{7,7},{8,24},{9,29},... | collective-permute-start | bytes 2359304 | tf_op jit(solution)/shard_map/ppermute | solution.py:49
  660.9 120.1 %collective-permute-start.6 = (bf16[256,1536]{1,0:T(8,128)(2,1)S(1)}, bf16[256,1536]{1,0:T(8,128)(2,1)S(1)}, u32[]{:S(2)}, u32[]{:S(2)}) collective-permute-start(bf16[256,1536]{1,0:T(8,128)(2,1)S(1)} %get-tuple-element.217), channel_id=1, source_target_pairs={{0,0},{1,5},{2,16},{3,21},{4,2},{5,7},{6,18},{7,23},{8,8},{9,13},{... | collective-permute-start | bytes 2359304 | tf_op jit(solution)/shard_map/ppermute | solution.py:49
  781.0 0.9 copy-start.9
  781.0 1.1 copy-start.10

commit v7 on v6

--- a/solution.py
+++ b/solution.py
@@ -1642,7 +1642,7 @@
 def layer_backward(grid, grad_out, kept, attn, ffn, gain_pair, facts, running, sum_ffn, sum_attn, leaving):
     hidden_in, kept_attn, middle, whole2, gate, up, hidden = kept
     plan = Plan()
-    for ring in running:
+    for ring in reversed(running):
         ring.add(plan, 0, min(4, ring.left()))
     grad_middle, gain_two, terms = ffn_back_call(
         grid, plan, grad_out, middle, gain_pair[1:2], gate, up, hidden, whole2, ffn.found

time: 800 us -> 796 us (level)
  no operation moved by 1% of the time
where the time goes in v7:
time: 796 us; the launch traced here: 787 us
  Pallas kernels  756 us (95%)
  starting transfers between devices  17.4 us (2%)
  local copies, waits for them, and re-layouts  8.45 us (1%)
    pallas_call x10, Pallas kernels, fused_call(): pl.pallas_call(whole, out_shape=tuple(outs) + tuple(plan.outs), in_specs=...  748 us
    ppermute x8, starting transfers between devices, send(): return lax.ppermute(block, AXES, pairs)  17.4 us
  transfers between devices with their start and end apart: 8, of which 0 were waited for; matrix products, arithmetic and copies ran while one was open for 1% of the time, Pallas kernels for 40%

profile of v7, /device:TPU:1, one launch (start us, length us, event | category | flops | bytes accessed | tf_op | source)
XLA Modules:
  0.0 786.8 jit_solution(11629226765421625746)
XLA Ops:
  0.7 1.5 slice_bitcast_fusion.2
  2.2 0.7 collective-permute-start.1
  2.9 1.3 collective-permute-start
  4.2 0.8 copy.22.refs_1_
  5.1 0.8 copy.23.refs_2_
  5.9 0.6 jit_solution_.3.refs_9_
  6.5 100.2 %start.1 = (f32[2,2,1536]{2,1,0:T(2,128)}, f32[4,256,128]{2,1,0:T(8,128)}, f32[4,256,128]{2,1,0:T(8,128)}, s32[4,1,256]{2,1,0:T(1,128)}, s32[4,1,256]{2,1,0:T(1,...) custom-call(bf16[1,384,384]{2,1,0:T(8,128)(2,1)} %refs_0_.1, ...), custom_call_target="tpu_custom_call" | custom-call | flops 70000001024 | bytes 1048576 | tf_op jit(solution)/shard_map/start/pallas_call | solution.py:526
  106.7 1.4 slice_bitcast_fusion.4
  108.1 1.0 broadcast_select_fusion.5.refs_0_.refs_1_
  109.1 73.1 %attn.2 = (bf16[4,256,1536]{2,1,0:T(8,128)(2,1)}, bf16[4,4,256,128]{3,2,1,0:T(8,128)(2,1)}, bf16[2,4,256,128]{3,2,1,0:T(8,128)(2,1)}, bf16[2,4,256,128]{3,2,1,0:...) custom-call(bf16[256,1536]{1,0:T(8,128)(2,1)} %broadcast_select_fusi, ...), custom_call_target="tpu_custom_call" | custom-call | flops 60000002048 | bytes 1048576 | tf_op jit(solution)/shard_map/attn/pallas_call | solution.py:526
  182.2 66.2 %ffn.2 = (bf16[256,1536]{1,0:T(8,128)(2,1)}, bf16[4,256,1536]{2,1,0:T(8,128)(2,1)}, bf16[4,256,1024]{2,1,0:T(8,128)(2,1)}, bf16[4,256,1024]{2,1,0:T(8,128)(2,1)}...) custom-call(f32[256,1536]{1,0:T(8,128)} %get-tuple-element.129.refs_, ...), custom_call_target="tpu_custom_call" | custom-call | flops 44000002048 | bytes 1048576 | tf_op jit(solution)/shard_map/ffn/pallas_call | solution.py:526
  248.4 72.5 %attn.3 = (bf16[4,256,1536]{2,1,0:T(8,128)(2,1)}, bf16[4,4,256,128]{3,2,1,0:T(8,128)(2,1)}, bf16[2,4,256,128]{3,2,1,0:T(8,128)(2,1)}, bf16[2,4,256,128]{3,2,1,0:...) custom-call(bf16[256,1536]{1,0:T(8,128)(2,1)} %get-tuple-element.161, ...), custom_call_target="tpu_custom_call" | custom-call | flops 60000002048 | bytes 1048576 | tf_op jit(solution)/shard_map/attn/pallas_call | solution.py:526
  321.0 0.7 collective-permute-start.3
  321.7 1.5 collective-permute-start.2
  323.2 43.2 %ffn.3 = (bf16[256,1536]{1,0:T(8,128)(2,1)}, bf16[4,256,1536]{2,1,0:T(8,128)(2,1)}, bf16[4,256,1024]{2,1,0:T(8,128)(2,1)}, bf16[4,256,1024]{2,1,0:T(8,128)(2,1)}, bf16[4,256,1024]{2,1,0:T(8,128)(2,1)}) custom-call(f32[256,1536]{1,0:T(8,128)} %get-tuple-element.148.refs_0_.refs_1_, f32[1,1536]{1,0:T(1,128)} %get-tuple-element.224.refs_1_.refs_2_, ...), custom_call_target="tpu_custom_call" | custom-call | flops 44000002048 | bytes 1048576 | tf_op jit(solution)/shard_map/ffn/pallas_call | solution.py:526
  366.5 1.0 broadcast_select_fusion.4.refs_0_
  367.4 0.4 copy-done.1
  367.8 0.3 copy-done.3
  368.3 1.9 collective-permute-start.5
  370.2 4.5 collective-permute-start.4
  374.8 57.9 %ffn_back.2 = (f32[256,1536]{1,0:T(8,128)}, f32[8,1536]{1,0:T(8,128)}, bf16[3,1536,1024]{2,1,0:T(8,128)(2,1)}) custom-call(bf16[256,1536]{1,0:T(8,128)(2,1)} %broadcast_select_fusion.4.refs_0_, f32[256,1536]{1,0:T(8,128)} %get-tuple-element.148.refs_0_.refs_1_, f32[1,1536]{1,0:T(1,128)} %get-tuple-element.224.refs_1_.refs_2_, ...), custom_call_target="tpu_custom_call" | custom-call | flops 60000002048 | bytes 1048576 | tf_op jit(solution)/shard_map/ffn_back/pallas_call | solution.py:526
  432.7 73.8 %attn_back.2 = (bf16[256,1536]{1,0:T(8,128)(2,1)}, f32[8,1536]{1,0:T(8,128)}, bf16[1536,768]{1,0:T(8,128)(2,1)}, bf16[4,2,192,384]{3,2,1,0:T(8,128)(2,1)}, bf16[...) custom-call(f32[256,1536]{1,0:T(8,128)} %get-tuple-element.159.refs_0_, ...), custom_call_target="tpu_custom_call" | custom-call | flops 80000000000 | bytes 1048576 | tf_op jit(solution)/shard_map/attn_back/pallas_call | solution.py:526
  506.6 66.3 %ffn_back.3 = (f32[256,1536]{1,0:T(8,128)}, f32[8,1536]{1,0:T(8,128)}, bf16[3,1536,1024]{2,1,0:T(8,128)(2,1)}, bf16[1152,384]{1,0:T(8,128)(2,1)}, bf16[1152,384]...) custom-call(bf16[256,1536]{1,0:T(8,128)(2,1)} %get-tuple-element.172.refs_0_, ...), custom_call_target="tpu_custom_call" | custom-call | flops 60000002048 | bytes 1048576 | tf_op jit(solution)/shard_map/ffn_back/pallas_call | solution.py:526
  572.9 79.6 %attn_back.3 = (bf16[256,1536]{1,0:T(8,128)(2,1)}, f32[8,1536]{1,0:T(8,128)}, bf16[1536,768]{1,0:T(8,128)(2,1)}, bf16[4,2,192,384]{3,2,1,0:T(8,128)(2,1)}, bf16[...) custom-call(f32[256,1536]{1,0:T(8,128)} %get-tuple-element.181.refs_0_, ...), custom_call_target="tpu_custom_call" | custom-call | flops 80000000000 | bytes 1048576 | tf_op jit(solution)/shard_map/attn_back/pallas_call | solution.py:526
  652.5 1.2 broadcast_select_fusion
  653.8 4.6 collective-permute-start.7
  658.4 2.2 collective-permute-start.6
  660.5 114.8 %tail.1 = (bf16[2,3,384,256]{3,2,1,0:T(8,128)(2,1)}, bf16[2,3,384,256]{3,2,1,0:T(8,128)(2,1)}, bf16[576,384]{1,0:T(8,128)(2,1)}, bf16[576,384]{1,0:T(8,128)(2,1)}, f32[8,1536]{1,0:T(8,128)}) custom-call(f32[8,1536]{1,0:T(8,128)} %get-tuple-element.189.refs_0_, f32[8,1536]{1,0:T(8,128)} %get-tuple-element.190.refs_1_, f32[8,1536]{1,0:T(8,128)} %get-tuple-element.191.refs_2_, ...), custom_call_target="tpu_custom_call" | custom-call | flops 60000002048 | bytes 1048576 | tf_op jit(solution)/shard_map/tail/pallas_call | solution.py:526
  775.4 1.3 dynamic-slice_bitcast_fusion
  776.7 0.9 copy-done.9
  777.6 0.2 copy-done.10
  777.9 8.5 %finish.1 = (bf16[2,256,1536]{2,1,0:T(8,128)(2,1)}, f32[2,256,1536]{2,1,0:T(8,128)}, f32[384,384]{1,0:T(8,128)}, f32[192,384]{1,0:T(8,128)}, f32[192,384]{1,0:T(...) custom-call(bf16[2,3,384,256]{3,2,1,0:T(8,128)(2,1)} %get-tuple-element.201.ffn_ow, ...), custom_call_target="tpu_custom_call" | custom-call | flops 8000000000 | bytes 1048576 | tf_op jit(solution)/shard_map/finish/pallas_call | solution.py:1610
  (28 shorter events, 0.4 us)
Async XLA Ops:
  0.6 5.2 copy-start.6
  0.7 3.6 copy-start.4
  0.7 4.4 copy-start.5
  2.2 105.9 %collective-permute-start.1 = (bf16[256,1536]{1,0:T(8,128)(2,1)S(1)}, bf16[256,1536]{1,0:T(8,128)(2,1)S(1)}, u32[]{:S(2)}, u32[]{:S(2)}) collective-permute-start(bf16[256,1536]{1,0:T(8,128)(2,1)S(1)} %get-tuple-element.222), channel_id=1, source_target_pairs={{0,2},{2,6},{5,3},{7,7},{8,10},{10,14},{13,11},{15,15},{17,18},{19... | collective-permute-start | bytes 2359304 | tf_op jit(solution)/shard_map/ppermute | solution.py:49
  2.9 105.2 %collective-permute-start = (bf16[256,1536]{1,0:T(8,128)(2,1)S(1)}, bf16[256,1536]{1,0:T(8,128)(2,1)S(1)}, u32[]{:S(2)}, u32[]{:S(2)}) collective-permute-start(bf16[256,1536]{1,0:T(8,128)(2,1)S(1)} %get-tuple-element.223), channel_id=1, source_target_pairs={{0,0},{2,4},{5,1},{7,5},{8,8},{10,12},{13,9},{15,13},{17,16},{19,2... | collective-permute-start | bytes 2359304 | tf_op jit(solution)/shard_map/ppermute | solution.py:49
  248.4 72.5 %copy-start = (bf16[2,256,1536]{2,1,0:T(8,128)(2,1)S(1)}, bf16[2,256,1536]{2,1,0:T(8,128)(2,1)}, u32[]{:S(2)}) copy-start(bf16[2,256,1536]{2,1,0:T(8,128)(2,1)} %param.14) | copy-start | bytes 4718596
  321.0 45.5 %collective-permute-start.3 = (bf16[256,1536]{1,0:T(8,128)(2,1)S(1)}, bf16[256,1536]{1,0:T(8,128)(2,1)S(1)}, u32[]{:S(2)}, u32[]{:S(2)}) collective-permute-start(bf16[256,1536]{1,0:T(8,128)(2,1)S(1)} %get-tuple-element.220), channel_id=1, source_target_pairs={{0,2},{2,6},{5,3},{7,7},{8,10},{10,14},{13,11},{15,15},{17,18},{19... | collective-permute-start | bytes 2359304 | tf_op jit(solution)/shard_map/ppermute | solution.py:49
  321.7 44.8 %collective-permute-start.2 = (bf16[256,1536]{1,0:T(8,128)(2,1)S(1)}, bf16[256,1536]{1,0:T(8,128)(2,1)S(1)}, u32[]{:S(2)}, u32[]{:S(2)}) collective-permute-start(bf16[256,1536]{1,0:T(8,128)(2,1)S(1)} %get-tuple-element.221), channel_id=1, source_target_pairs={{0,0},{2,4},{5,1},{7,5},{8,8},{10,12},{13,9},{15,13},{17,16},{19,2... | collective-permute-start | bytes 2359304 | tf_op jit(solution)/shard_map/ppermute | solution.py:49
  366.4 1.4 copy-start.1
  366.4 1.6 copy-start.3
  368.3 64.4 %collective-permute-start.5 = (bf16[256,1536]{1,0:T(8,128)(2,1)S(1)}, bf16[256,1536]{1,0:T(8,128)(2,1)S(1)}, u32[]{:S(2)}, u32[]{:S(2)}) collective-permute-start(bf16[256,1536]{1,0:T(8,128)(2,1)S(1)} %get-tuple-element.218), channel_id=1, source_target_pairs={{0,16},{1,21},{2,0},{3,5},{4,18},{5,23},{6,2},{7,7},{8,24},{9,29},... | collective-permute-start | bytes 2359304 | tf_op jit(solution)/shard_map/ppermute | solution.py:49
  370.2 62.5 %collective-permute-start.4 = (bf16[256,1536]{1,0:T(8,128)(2,1)S(1)}, bf16[256,1536]{1,0:T(8,128)(2,1)S(1)}, u32[]{:S(2)}, u32[]{:S(2)}) collective-permute-start(bf16[256,1536]{1,0:T(8,128)(2,1)S(1)} %get-tuple-element.219), channel_id=1, source_target_pairs={{0,0},{1,5},{2,16},{3,21},{4,2},{5,7},{6,18},{7,23},{8,8},{9,13},{... | collective-permute-start | bytes 2359304 | tf_op jit(solution)/shard_map/ppermute | solution.py:49
  432.7 73.9 %copy-start.7 = (bf16[256,1536]{1,0:T(8,128)(2,1)}, bf16[256,1536]{1,0:T(8,128)(2,1)S(1)}, u32[]{:S(2)}) copy-start(bf16[256,1536]{1,0:T(8,128)(2,1)S(1)} %collective-permute-done.5.out_two) | copy-start | bytes 2359300
  432.7 73.9 %copy-start.8 = (bf16[256,1536]{1,0:T(8,128)(2,1)}, bf16[256,1536]{1,0:T(8,128)(2,1)S(1)}, u32[]{:S(2)}) copy-start(bf16[256,1536]{1,0:T(8,128)(2,1)S(1)} %collective-permute-done.4.out_one) | copy-start | bytes 2359300
  572.9 79.6 %copy-start.2 = (bf16[256,1536]{1,0:T(8,128)(2,1)S(1)}, bf16[256,1536]{1,0:T(8,128)(2,1)}, u32[]{:S(2)}) copy-start(bf16[256,1536]{1,0:T(8,128)(2,1)} %get-tuple-element.172.refs_0_) | copy-start | bytes 2359300
  653.8 122.9 %collective-permute-start.7 = (bf16[256,1536]{1,0:T(8,128)(2,1)S(1)}, bf16[256,1536]{1,0:T(8,128)(2,1)S(1)}, u32[]{:S(2)}, u32[]{:S(2)}) collective-permute-start(bf16[256,1536]{1,0:T(8,128)(2,1)S(1)} %get-tuple-element.216), channel_id=1, source_target_pairs={{0,16},{1,21},{2,0},{3,5},{4,18},{5,23},{6,2},{7,7},{8,24},{9,29},... | collective-permute-start | bytes 2359304 | tf_op jit(solution)/shard_map/ppermute | solution.py:49
  658.4 118.4 %collective-permute-start.6 = (bf16[256,1536]{1,0:T(8,128)(2,1)S(1)}, bf16[256,1536]{1,0:T(8,128)(2,1)S(1)}, u32[]{:S(2)}, u32[]{:S(2)}) collective-permute-start(bf16[256,1536]{1,0:T(8,128)(2,1)S(1)} %get-tuple-element.217), channel_id=1, source_target_pairs={{0,0},{1,5},{2,16},{3,21},{4,2},{5,7},{6,18},{7,23},{8,8},{9,13},{... | collective-permute-start | bytes 2359304 | tf_op jit(solution)/shard_map/ppermute | solution.py:49
  776.7 0.9 copy-start.9
  776.7 1.1 copy-start.10
